TPU v7x, 32 devices: a whole 2x2x4 slice. The times are simulated.
32 devices in a mesh: dp: 8 (over z, x), dim: 4 (over y, core).
Axes of the slice: x: 2, y: 2, z: 4, core: 2. Of those that a mesh axis runs over, the one named last changes fastest.
Arguments:
- attribute_vectors: bfloat16 [128, 512, 256], P('dp', 'dim'), may hold values from -6 to 6
- upstream: bfloat16 [128, 512, 256], P('dp', 'dim'), may hold values from -6 to 6
- compress: bfloat16 [256, 64], replicated, may hold values from -0.375 to 0.375
- interact_proj: bfloat16 [64, 512], P(None, 'dim'), may hold values from -0.75 to 0.75
- linear_mix: bfloat16 [256, 256], replicated, may hold values from -0.375 to 0.375
- row_owner: int32 [32768, 1], P('dp'), may hold values from 0 to 7; in each aligned block of 4096 rows (0 to 4095, 4096 to 8191, ...) at most 2048 rows name the same one
- row_slot: int32 [32768], P('dp'), may hold values from 0 to 255
Outputs:
- table_grad: float32 [512, 2048], P('dim', 'dp')
Inputs may be any that keep to these rules, and one draw needn't show every extreme that they name: `row_owner`: in each aligned block of 4096 rows (the rows of one device) no owner is named by more than 2048 rows, a bound that some block reaches.
All inputs are finite; a program needn't handle non-finite values.
Results may differ from a plain program's by a relative error of at most 0.0035.
Values may be sent and summed in bfloat16 or wider, within the bound.
No kernel may reach another device: no remote copies, remote signals or barrier semaphores. Data moves between devices by JAX's collectives and lax.ppermute only.
A program may use at most 64 MiB of HBM per device.

v0:
```python
import math

import jax
import jax.numpy as jnp
from jax import lax
from jax.sharding import PartitionSpec as P

SHARD = 256


def layer_back(totals, upstream_n):
    centred = totals - jnp.mean(totals, axis=-1, keepdims=True)
    inverse = 1.0 / jnp.sqrt(jnp.mean(centred * centred, axis=-1, keepdims=True) + 1e-05)
    normed = centred * inverse
    return inverse * (
        upstream_n
        - jnp.mean(upstream_n, axis=-1, keepdims=True)
        - normed * jnp.mean(upstream_n * normed, axis=-1, keepdims=True)
    )


def finish_grad(
    attribute_vectors, upstream, compress, linear_mix, reduced_lookup_vectors, pairwise_gradient
):
    leading_product_term = jnp.einsum(
        "sxh,shl->slx",
        pairwise_gradient,
        reduced_lookup_vectors,
        preferred_element_type=jnp.float32,
    )
    compressor_gradient = jnp.einsum(
        "itm,ipt->imp", pairwise_gradient, attribute_vectors, preferred_element_type=jnp.float32
    ).astype(jnp.bfloat16)
    trailing_product_term = jnp.einsum(
        "hu,zux->zxh", compress, compressor_gradient, preferred_element_type=jnp.float32
    )
    linear_term = jnp.einsum(
        "bdg,fg->bdf", upstream, linear_mix, preferred_element_type=jnp.float32
    )
    return (
        upstream.astype(jnp.float32) + linear_term + leading_product_term + trailing_product_term
    ).astype(jnp.bfloat16)


def shards(attribute_vectors, upstream, compress, interact_proj, linear_mix, row_owner, row_slot):
    reduced_lookup_vectors = jnp.einsum(
        "qy,piq->pyi", compress, attribute_vectors, preferred_element_type=jnp.float32
    ).astype(jnp.bfloat16)
    partial_feature_totals = jnp.einsum(
        "pzt,pvz->ptv",
        attribute_vectors,
        reduced_lookup_vectors,
        preferred_element_type=jnp.float32,
    )
    normed_part = jnp.einsum(
        "bdf,kd->bfk", upstream, interact_proj, preferred_element_type=jnp.float32
    )
    sums_all, standardized_entire = lax.psum((partial_feature_totals, normed_part), "dim")
    pairwise_gradient = layer_back(sums_all, standardized_entire).astype(jnp.bfloat16)
    feature_grad = finish_grad(
        attribute_vectors, upstream, compress, linear_mix, reduced_lookup_vectors, pairwise_gradient
    )
    local_width = feature_grad.shape[1]
    row_count = feature_grad.shape[0] * feature_grad.shape[2]
    grad_rows = jnp.transpose(feature_grad, (1, 0, 2)).reshape(local_width, row_count)
    peer_count = lax.axis_size("dp")
    owners = row_owner[:, 0]
    capacity = 4 * row_count // peer_count
    owner_hits = (owners[:, None] == jnp.arange(peer_count, dtype=jnp.int32)[None, :]).astype(
        jnp.int32
    )
    position = jnp.sum((jnp.cumsum(owner_hits, axis=0) - owner_hits) * owner_hits, axis=1)
    target = owners * capacity + position
    buffer_size = peer_count * capacity
    send_rows = jnp.zeros((local_width, buffer_size), jnp.bfloat16).at[:, target].set(grad_rows)
    send_slots = jnp.full((1, buffer_size), -1, jnp.int32).at[0, target].set(row_slot)
    got_rows, got_slots = (
        lax.all_to_all(send_rows, "dp", split_axis=1, concat_axis=1, tiled=True),
        lax.all_to_all(send_slots, "dp", split_axis=1, concat_axis=1, tiled=True),
    )
    block_size = math.gcd(buffer_size, 2048)
    table_index = jnp.arange(SHARD, dtype=jnp.int32)

    def accumulate(block_index, cumulative_tally):
        offset = block_index * block_size
        block_rows = lax.dynamic_slice_in_dim(got_rows, offset, block_size, 1)
        block_slots = lax.dynamic_slice_in_dim(got_slots, offset, block_size, 1)[0]
        onehot = (block_slots[:, None] == table_index[None, :]).astype(jnp.bfloat16)
        return cumulative_tally + jnp.dot(block_rows, onehot, preferred_element_type=jnp.float32)

    table_grad = lax.fori_loop(
        0, buffer_size // block_size, accumulate, jnp.zeros((local_width, SHARD), jnp.float32)
    )
    return table_grad


def solution(mesh):
    placed = (
        P("dp", "dim", None),
        P("dp", "dim", None),
        P(),
        P(None, "dim"),
        P(),
        P("dp", None),
        P("dp"),
    )
    return jax.shard_map(
        shards, mesh=mesh, in_specs=placed, out_specs=P("dim", "dp"), check_vma=False
    )
```

profile of v0, /device:TPU:0, one launch (start us, length us, event | category | flops | bytes accessed | tf_op | source)
XLA Modules:
  0.0 214.4 jit_solution(15420274427450918533)
XLA Ops:
  6.5 1.2 copy-done
  7.8 1.2 convolution_convert_fusion.1
  9.0 1.3 convolution_bitcast_fusion
  10.3 1.3 fusion.22
  11.6 2.3 %reduce-window.6 = s32[8,32,128]{2,1,0:T(8,128)S(1)} reduce-window(s32[8,32,128]{2,1,0:T(8,128)S(1)} %fusion.16, s32[]{:T(128)} %constant.48.clone.1), window={size=1x1x128 pad=0_0x0_0x127_0}, to_apply=%region_0.0 | reduce-window | flops 4161536 | bytes 262148 | tf_op jit(solution)/shard_map/reduce-window
  13.9 0.3 slice_reduce_fusion
  14.2 0.2 reduce-window.9
  14.8 0.1 and_reduce_fusion
  15.0 16.3 %scatter_custom_fusion.1 = s32[16384]{0:T(1024)} fusion(s32[4096]{0:T(1024)S(1)} %broadcast_select_fusion, s32[4096]{0:T(1024)} %param.15, s32[]{:T(128)} %constant.55.clone.1), kind=kCustom, calls=%fused_computation.38 | custom fusion | bytes 66048
  31.3 7.3 %all-to-all-start.1 = ((s32[1,8,2048]{2,0,1:T(1,128)}), s32[1,8,2048]{2,0,1:T(1,128)S(1)}, u32[]{:S(2)}, u32[]{:S(2)}) async-start(s32[1,8,2048]{2,0,1:T(1,128)} %bitcast.14), calls=%async_computation.1 | async-start | bytes 131072 | tf_op jit(solution)/shard_map/all_to_all | solution.py:79
  38.5 1.8 fusion.14
  40.4 25.7 %all-reduce.4.cloned.1.call-done = (f32[16,256,64]{1,2,0:T(8,128)}, f32[16,256,64]{1,2,0:T(8,128)}) async-done(((f32[16,256,64]{1,2,0:T(8,128)}, f32[16,256,64]{1,2,0:T(8,128)}), (f32[16,256,64]{1,2,0:T(8,128)}, f32[16,256,64]{1,2,0:T(8,128)})) %all-reduce.4.cloned.1.call-update) | async-done | bytes 2097168 | tf_op jit(solution)/shard_map/psum | solution.py:58
  66.0 1.4 reduce_sum.49
  67.5 1.4 multiply_reduce_fusion.1
  68.9 1.6 fusion.24
  70.5 1.1 multiply_convert_fusion
  71.7 3.2 %fusion.10 = f32[16,128,256]{2,1,0:T(8,128)} fusion(bf16[16,256,64]{1,2,0:T(8,128)(2,1)} %multiply_convert_fusion, bf16[16,128,256]{2,1,0:T(8,128)(2,1)S(1)} %copy-done, bf16[256,64]{0,1:T(8,128)(2,1)S(1)} %copy-done.7), kind=kOutput, calls=%fused_computation.17 | convolution fusion | flops 134348800 | bytes 3702784 | tf_op jit(solution)/shard_map/hu,zux->zxh/dot_general | solution.py:34
  74.9 3.7 %fusion.9 = bf16[128,16,256]{2,0,1:T(8,128)(2,1)} fusion(f32[16,128,256]{2,1,0:T(8,128)} %fusion.10, bf16[16,128,64]{1,2,0:T(8,128)(2,1)S(1)} %convolution_convert_fusion.1, bf16[16,256,64]{1,2,0:T(8,128)(2,1)S(1)} %copy-done.3, f32[16,128,256]{2,1,0:T(8,128)} %fusion.14, bf16[16,128,256]{2,1,0:T(8,128)(2,1)S(1)} %copy-done.2), kind=kOutput, calls=%fused_computation.13 | convolution fusion | flops 69730304 | bytes 7077888 | tf_op jit(solution)/shard_map/sxh,shl->slx/dot_general | solution.py:25
  78.6 1.6 copy.11
  80.3 13.6 %scatter_custom_fusion = bf16[128,16384]{0,1:T(8,128)(2,1)} fusion(s32[4096]{0:T(1024)S(1)} %bitcast.63, bf16[4096,128]{1,0:T(8,128)(2,1)S(1)} %bitcast.58, bf16[]{:T(256)} %constant.50.clone.1), kind=kCustom, calls=%fused_computation.11 | custom fusion | bytes 4194306 | tf_op jit(solution)/shard_map/scatter | solution.py:75
  93.8 5.5 %all-to-all-start = ((bf16[128,8,2048]{0,2,1:T(8,128)(2,1)}), bf16[128,8,2048]{0,2,1:T(8,128)(2,1)}, u32[]{:S(2)}, u32[]{:S(2)}) async-start(bf16[128,8,2048]{0,2,1:T(8,128)(2,1)} %bitcast.57), calls=%async_computation | async-start | bytes 8388608 | tf_op jit(solution)/shard_map/all_to_all | solution.py:78
  99.3 93.2 %all-to-all-done = bf16[128,8,2048]{0,2,1:T(8,128)(2,1)} async-done(((bf16[128,8,2048]{0,2,1:T(8,128)(2,1)}), bf16[128,8,2048]{0,2,1:T(8,128)(2,1)}, u32[]{:S(2)}, u32[]{:S(2)}) %all-to-all-start) | async-done | bytes 4194336 | tf_op jit(solution)/shard_map/all_to_all | solution.py:78
  192.6 14.3 %while.14 = (s32[]{:T(128)}, f32[128,256]{1,0:T(8,128)S(1)}, bf16[128,16384]{0,1:T(8,128)(2,1)}, s32[1,16384]{1,0:T(1,128)S(1)}, s32[]{:T(128)}, /*index=5*/s32[]{:T(128)}, s32[]{:T(128)}, s32[]{:T(128)}) while((s32[]{:T(128)}, f32[128,256]{1,0:T(8,128)S(1)}, bf16[128,16384]{0,1:T(8,128)(2,1)}, s32[1,16384]{1,0:T(1,128)S(1)}, ...), condition=%wide.region_12.13_spmd.clone, body=%wide.region_11.12_spmd.clone.sunk | while | flops 134807552 | bytes 811157 | solution.py:91
  192.6 1.7 fusion.37
  194.4 1.7 fusion.37
  196.1 1.7 fusion.37
  197.9 1.7 fusion.37
  199.7 1.7 fusion.37
  201.5 1.7 fusion.37
  203.3 1.7 fusion.37
  205.1 1.7 fusion.37
  206.9 0.6 copy-done.11
  (43 shorter events, 0.5 us)
Async XLA Ops:
  6.5 1.2 copy-start
  6.5 3.8 %copy-start.2 = (bf16[16,128,256]{2,1,0:T(8,128)(2,1)S(1)}, bf16[16,128,256]{2,1,0:T(8,128)(2,1)}, u32[]{:S(2)}) copy-start(bf16[16,128,256]{2,1,0:T(8,128)(2,1)} %param.10) | copy-start | bytes 3145732
  6.5 3.8 %copy-start.8 = (bf16[64,128]{1,0:T(8,128)(2,1)S(1)}, bf16[64,128]{1,0:T(8,128)(2,1)}, u32[]{:S(2)}) copy-start(bf16[64,128]{1,0:T(8,128)(2,1)} %param.12) | copy-start | bytes 49156
  6.5 59.5 %all-reduce.4.cloned.1.call-start = ((), (), s32[]{:S(2)}) async-start(), calls=%async_computation.2 | async-start | bytes 4194304 | tf_op jit(solution)/shard_map/psum | solution.py:58
  10.3 1.3 copy-start.5
  11.6 3.1 %copy-start.9 = (s32[2]{0:T(128)S(1)}, s32[2]{0:T(128)}, u32[]{:S(2)}) copy-start(s32[2]{0:T(128)} %constant.58) | copy-start | bytes 28
  11.6 3.3 %copy-start.10 = (s32[2]{0:T(128)S(1)}, s32[2]{0:T(128)}, u32[]{:S(2)}) copy-start(s32[2]{0:T(128)} %constant.61) | copy-start | bytes 28
  11.6 27.0 %copy-start.6 = (bf16[256,256]{1,0:T(8,128)(2,1)S(1)}, bf16[256,256]{1,0:T(8,128)(2,1)}, u32[]{:S(2)}) copy-start(bf16[256,256]{1,0:T(8,128)(2,1)} %param.13) | copy-start | bytes 393220
  31.3 62.6 %all-to-all-start.1 = ((s32[1,8,2048]{2,0,1:T(1,128)}), s32[1,8,2048]{2,0,1:T(1,128)S(1)}, u32[]{:S(2)}, u32[]{:S(2)}) async-start(s32[1,8,2048]{2,0,1:T(1,128)} %bitcast.14), calls=%async_computation.1 | async-start | bytes 131072 | tf_op jit(solution)/shard_map/all_to_all | solution.py:79
  66.0 2.9 %copy-start.1 = (f32[16,256,64]{1,2,0:T(8,128)S(1)}, f32[16,256,64]{1,2,0:T(8,128)}, u32[]{:S(2)}) copy-start(f32[16,256,64]{1,2,0:T(8,128)} %get-tuple-element.128) | copy-start | bytes 3145732
  67.4 3.1 %copy-start.4 = (f32[16,256,64]{1,2,0:T(8,128)S(1)}, f32[16,256,64]{1,2,0:T(8,128)}, u32[]{:S(2)}) copy-start(f32[16,256,64]{1,2,0:T(8,128)} %get-tuple-element.127) | copy-start | bytes 3145732
  68.9 2.7 %copy-start.7 = (bf16[256,64]{0,1:T(8,128)(2,1)S(1)}, bf16[256,64]{0,1:T(8,128)(2,1)}, u32[]{:S(2)}) copy-start(bf16[256,64]{0,1:T(8,128)(2,1)} %param.11) | copy-start | bytes 98308
  71.7 3.2 %copy-start.3 = (bf16[16,256,64]{1,2,0:T(8,128)(2,1)S(1)}, bf16[16,256,64]{1,2,0:T(8,128)(2,1)}, u32[]{:S(2)}) copy-start(bf16[16,256,64]{1,2,0:T(8,128)(2,1)} %multiply_convert_fusion) | copy-start | bytes 1572868
  93.8 98.7 %all-to-all-start = ((bf16[128,8,2048]{0,2,1:T(8,128)(2,1)}), bf16[128,8,2048]{0,2,1:T(8,128)(2,1)}, u32[]{:S(2)}, u32[]{:S(2)}) async-start(bf16[128,8,2048]{0,2,1:T(8,128)(2,1)} %bitcast.57), calls=%async_computation | async-start | bytes 8388608 | tf_op jit(solution)/shard_map/all_to_all | solution.py:78
  206.9 0.7 copy-start.11
Sparse Core Ops, SparseCore 0:
  11.7 54.2 all-reduce.3
where the time goes:
time: 215 us; the launch traced here: 214 us
  waiting for transfers between devices  119 us (55%)
  local copies, waits for them, and re-layouts  33.7 us (16%)
  matrix products  26.6 us (12%)
  between operations  13.6 us (6%)
  starting transfers between devices  12.8 us (6%)
  other arithmetic  8.58 us (4%)
    all_to_all x1, waiting for transfers between devices, shards(): lax.all_to_all(send_rows, 'dp', split_axis=1, concat_axis=1, tiled=True)  93.2 us
    psum x1, waiting for transfers between devices, shards(): lax.psum((partial_feature_totals, normed_part), 'dim')  25.7 us
    unnamed x25, local copies, waits for them, and re-layouts  18.2 us
    dot_general x8, matrix products, accumulate(): jnp.dot(block_rows, onehot, preferred_element_type=jnp.float32)  14 us
    scatter x1, local copies, waits for them, and re-layouts, shards(): jnp.zeros((local_width, buffer_size), jnp.bfloat16).at[:, target]  13.6 us
    all_to_all x1, starting transfers between devices, shards(): lax.all_to_all(send_slots, 'dp', split_axis=1, concat_axis=1, tiled=True)  7.25 us
    all_to_all x1, starting transfers between devices, shards(): lax.all_to_all(send_rows, 'dp', split_axis=1, concat_axis=1, tiled=True)  5.51 us
  transfers between devices with their start and end apart: 3, of which 2 were waited for; matrix products, arithmetic and copies ran while one was open for 23% of the time, Pallas kernels for 0%

commit v1 on v0

v1 whole, which is shorter than its diff:
```python
import functools

import jax
import jax.numpy as jnp
from jax import lax
from jax.experimental import pallas as pl
from jax.experimental.pallas import tpu as pltpu
from jax.sharding import PartitionSpec as P

SHARD = 256
F32, BF16 = jnp.float32, jnp.bfloat16


def dot_nt(a, b):
    return lax.dot_general(a, b, (((1,), (1,)), ((), ())), preferred_element_type=F32)


def dot_nn(a, b):
    return lax.dot_general(a, b, (((1,), (0,)), ((), ())), preferred_element_type=F32)


def transposed(ref):
    return ref[...].astype(F32).T.astype(BF16)


def partial_sums_kernel(pieces_ref, av_ref, up_ref, compress_ref, proj_ref, send_ref, keep_ref, comp_t):
    step = pl.program_id(0)

    @pl.when(step == 0)
    def _():
        comp_t[...] = transposed(compress_ref)

    count = av_ref.shape[0]
    half = pl.num_programs(0) // 2
    rank = comp_t.shape[0]
    for b in range(count):
        reduced = dot_nt(comp_t[...], av_ref[b]).astype(BF16)
        sums = dot_nn(reduced, av_ref[b])
        sums = sums - jnp.mean(sums, axis=0, keepdims=True)
        grads = dot_nn(proj_ref[...], up_ref[b])
        grads = grads - jnp.mean(grads, axis=0, keepdims=True)

        @pl.when(step < half)
        def _():
            send_ref[b, :rank] = sums
            send_ref[b, rank:] = grads

        @pl.when(step >= half)
        def _():
            keep_ref[b, :rank] = sums
            keep_ref[b, rank:] = grads


def partial_sums(pieces, av, up, compress, proj):
    samples, width, features = av.shape
    count = pieces.shape[0]
    piece = samples // count
    rank = compress.shape[1]
    half = count // 2
    block = (piece, width, features)
    out_block = (piece, 2 * rank, features)
    return pl.pallas_call(
        partial_sums_kernel,
        grid_spec=pltpu.PrefetchScalarGridSpec(
            num_scalar_prefetch=1,
            grid=(count,),
            in_specs=[
                pl.BlockSpec(block, lambda i, q: (q[i], 0, 0)),
                pl.BlockSpec(block, lambda i, q: (q[i], 0, 0)),
                pl.BlockSpec(compress.shape, lambda i, q: (0, 0)),
                pl.BlockSpec(proj.shape, lambda i, q: (0, 0)),
            ],
            out_specs=[
                pl.BlockSpec(out_block, lambda i, q: (jnp.minimum(i, half - 1), 0, 0)),
                pl.BlockSpec(out_block, lambda i, q: (jnp.maximum(i - half, 0), 0, 0)),
            ],
            scratch_shapes=[pltpu.VMEM((rank, features), BF16)],
        ),
        out_shape=[jax.ShapeDtypeStruct((half * piece, 2 * rank, features), F32)] * 2,
        compiler_params=pltpu.CompilerParams(vmem_limit_bytes=16 * 2**20),
        name="partial_sums",
    )(pieces, av, up, compress, proj)


def layer_back_kernel(keep_ref, got_ref, pair_ref):
    rank = keep_ref.shape[1] // 2
    for b in range(keep_ref.shape[0]):
        total = keep_ref[b] + got_ref[b].astype(F32)
        centred, grads = total[:rank], total[rank:]
        inverse = 1.0 / jnp.sqrt(jnp.mean(centred * centred, axis=0, keepdims=True) + 1e-05)
        normed = centred * inverse
        moment = jnp.mean(grads * normed, axis=0, keepdims=True)
        pair_ref[b] = (inverse * (grads - normed * moment)).astype(BF16)


def layer_back(keep, got):
    samples, twice, features = keep.shape
    return pl.pallas_call(
        layer_back_kernel,
        out_shape=jax.ShapeDtypeStruct((samples, twice // 2, features), BF16),
        compiler_params=pltpu.CompilerParams(vmem_limit_bytes=16 * 2**20),
        name="layer_back",
    )(keep, got)


def table_kernel(owners, starts, pieces_ref, av_ref, up_ref, compress_ref, mix_ref, owner_ref, slot_ref, *rest):
    pair_refs = rest[: len(starts)]
    out_ref, comp_pair, masked, onehot, total = rest[len(starts):]
    step = pl.program_id(0)
    count, width, features = av_ref.shape
    rank = compress_ref.shape[1]

    @pl.when(step == 0)
    def _():
        comp_t = transposed(compress_ref)
        for b in range(count):
            comp_pair[b, :rank] = comp_t
            comp_pair[b, 2 * rank:] = comp_t
        total[...] = jnp.zeros_like(total)

    for pair_ref, start in zip(pair_refs, starts):
        for at in range(pair_ref.shape[0] // count):
            @pl.when(step == start + at)
            def _():
                comp_pair[:, rank:2 * rank] = pair_ref[at * count:(at + 1) * count]

    up = up_ref[...].reshape(count * width, features)
    linear = up.astype(F32) + dot_nt(up, mix_ref[...])
    first = pieces_ref[step] * count
    slots = lax.broadcasted_iota(jnp.int32, (SHARD, features), 0)
    for b in range(count):
        both = dot_nt(av_ref[b], comp_pair[b, :2 * rank]).astype(BF16)
        grad = linear[b * width:(b + 1) * width] + dot_nn(both, comp_pair[b, rank:])
        grad = grad.astype(BF16)
        owner = owner_ref[pl.ds(first + b, 1), :]
        columns = slice(b * features, (b + 1) * features)
        for o in range(owners):
            mask = jnp.where(owner == o, 1.0, 0.0).astype(BF16)
            masked[o * width:(o + 1) * width, columns] = grad * mask
        hit = slots == slot_ref[pl.ds(first + b, 1), :]
        onehot[:, columns] = jnp.where(hit, 1.0, 0.0).astype(BF16)
    total[...] += dot_nt(masked[...], onehot[...])

    @pl.when(step == pl.num_programs(0) - 1)
    def _():
        out_ref[...] = total[...].reshape(out_ref.shape).astype(BF16)


def table_partial(owners, pieces, av, up, compress, mix, owner, slot, pairs):
    samples, width, features = av.shape
    count = pieces.shape[0]
    piece = samples // count
    rank = compress.shape[1]
    starts, start = [], 0
    for pair in pairs:
        starts.append(start)
        start += pair.shape[0] // piece
    block = pl.BlockSpec((piece, width, features), lambda i, q: (q[i], 0, 0))

    def whole(a):
        return pl.BlockSpec(a.shape, lambda i, q: (0,) * a.ndim)

    return pl.pallas_call(
        functools.partial(table_kernel, owners, starts),
        grid_spec=pltpu.PrefetchScalarGridSpec(
            num_scalar_prefetch=1,
            grid=(count,),
            in_specs=[block, block] + [whole(a) for a in (compress, mix, owner, slot, *pairs)],
            out_specs=pl.BlockSpec((owners, width, SHARD), lambda i, q: (0, 0, 0)),
            scratch_shapes=[
                pltpu.VMEM((piece, 3 * rank, features), BF16),
                pltpu.VMEM((owners * width, piece * features), BF16),
                pltpu.VMEM((SHARD, piece * features), BF16),
                pltpu.VMEM((owners * width, SHARD), F32),
            ],
        ),
        out_shape=jax.ShapeDtypeStruct((owners, width, SHARD), BF16),
        compiler_params=pltpu.CompilerParams(vmem_limit_bytes=24 * 2**20),
        name="table_partial",
    )(pieces, av, up, compress, mix, owner, slot, *pairs)


def shards(attribute_vectors, upstream, compress, interact_proj, linear_mix, row_owner, row_slot):
    owners = lax.axis_size("dp")
    peers = lax.axis_size("dim")
    me = lax.axis_index("dim")
    samples, width, features = attribute_vectors.shape
    piece = samples // peers

    def swap(x, bit):
        return lax.ppermute(x, "dim", [(i, i ^ bit) for i in range(peers)])

    bits = [1 << t for t in range(peers.bit_length() - 1)]
    order = [0]
    for bit in reversed(bits):
        order += [j ^ bit for j in order]
    order = jnp.asarray(order, jnp.int32)
    pieces = order ^ me.astype(jnp.int32)
    send_first = jnp.roll(order, peers // 2) ^ me.astype(jnp.int32)

    send, keep = partial_sums(send_first, attribute_vectors, upstream, compress, interact_proj)
    got = swap(send, bits[0])
    for bit in bits[1:]:
        keep = keep + got.astype(F32)
        half = keep.shape[0] // 2
        got = swap(keep[half:].astype(BF16), bit)
        keep = keep[:half]
    pair = layer_back(keep, got)
    pairs = [pair]
    for bit in reversed(bits):
        pairs += [swap(jnp.concatenate(pairs) if len(pairs) > 1 else pairs[0], bit)]

    table = table_partial(
        owners,
        pieces,
        attribute_vectors,
        upstream,
        compress,
        linear_mix,
        row_owner.reshape(samples, features),
        row_slot.reshape(samples, features),
        pairs,
    )
    got = lax.all_to_all(table, "dp", split_axis=0, concat_axis=0, tiled=True)
    return jnp.sum(got.astype(F32), axis=0)


def solution(mesh):
    placed = (
        P("dp", "dim", None),
        P("dp", "dim", None),
        P(),
        P(None, "dim"),
        P(),
        P("dp", None),
        P("dp"),
    )
    return jax.shard_map(
        shards, mesh=mesh, in_specs=placed, out_specs=P("dim", "dp"), check_vma=False
    )
```

time: 215 us -> 57.7 us (0.27)
  waiting for transfers between devices: 119 us -> 12.1 us
  local copies, waits for them, and re-layouts: 33.7 us -> 5.95 us
  matrix products: 26.6 us -> 0 us
  blocking collectives: 0 us -> 20.9 us
  between operations: 13.6 us -> 0.14 us
  Pallas kernels: 0 us -> 11.3 us
  starting transfers between devices: 12.8 us -> 5.35 us
  other arithmetic: 8.58 us -> 1.58 us
    all_to_all x2 -> x0, waiting for transfers between devices: 93.2 us -> none  [the longest x1 93.2 us: shards(): lax.all_to_all(send_rows, 'dp', split_axis=1, concat_axis=1, tiled=True)]
    dot_general x14 -> x0, matrix products: 26.6 us -> none  [the longest x8 14 us: accumulate(): jnp.dot(block_rows, onehot, preferred_element_type=jnp.float32)]
    psum x1 -> x0, waiting for transfers between devices: 25.7 us -> none  [shards(): lax.psum((partial_feature_totals, normed_part), 'dim')]
    all_to_all x0 -> x1, blocking collectives: none -> 20.9 us  [shards(): got = lax.all_to_all(table, 'dp', split_axis=0, concat_axis=0, tiled=True)]
    scatter x1 -> x0, local copies, waits for them, and re-layouts: 13.6 us -> none  [shards(): jnp.zeros((local_width, buffer_size), jnp.bfloat16).at[:, target]]
    all_to_all x2 -> x0, starting transfers between devices: 12.8 us -> none  [the longest x1 7.25 us: shards(): lax.all_to_all(send_slots, 'dp', split_axis=1, concat_axis=1, tiled=True)]
    unnamed x25 -> x22, local copies, waits for them, and re-layouts: 18.2 us -> 5.87 us
    ppermute x0 -> x4, waiting for transfers between devices: none -> 12.1 us  [swap(): return lax.ppermute(x, 'dim', [(i, i ^ bit) for i in range(peers)])]
  transfers between devices with their start and end apart: 3 -> 4, of which waited for: 2 -> 3; matrix products, arithmetic and copies ran while one was open for 23% -> 2% of each run, Pallas kernels for 0% -> 0%
where the time goes in v1:
time: 57.7 us; the launch traced here: 57.4 us
  blocking collectives  20.9 us (36%)
  waiting for transfers between devices  12.1 us (21%)
  Pallas kernels  11.3 us (20%)
  local copies, waits for them, and re-layouts  5.95 us (10%)
  starting transfers between devices  5.35 us (9%)
  other arithmetic  1.58 us (3%)
    all_to_all x1, blocking collectives, shards(): got = lax.all_to_all(table, 'dp', split_axis=0, concat_axis=0, tiled=True)  20.9 us
    ppermute x4, waiting for transfers between devices, swap(): return lax.ppermute(x, 'dim', [(i, i ^ bit) for i in range(peers)])  12.1 us
    unnamed x22, local copies, waits for them, and re-layouts  5.87 us
    pallas_call x1, Pallas kernels, partial_sums(): pl.pallas_call(partial_sums_kernel, grid_spec=pltpu.PrefetchScalarGridSpe...  5.74 us
    pallas_call x1, Pallas kernels, table_partial(): pl.pallas_call(functools.partial(table_kernel, owners, starts), grid_spec...  5.41 us
    ppermute x4, starting transfers between devices, swap(): return lax.ppermute(x, 'dim', [(i, i ^ bit) for i in range(peers)])  5.35 us
  transfers between devices with their start and end apart: 4, of which 3 were waited for; matrix products, arithmetic and copies ran while one was open for 2% of the time, Pallas kernels for 0%

profile of v1, /device:TPU:0, one launch (start us, length us, event | category | flops | bytes accessed | tf_op | source)
XLA Modules:
  0.0 57.4 jit_solution(17888752092953805942)
XLA Ops:
  0.0 0.9 %copy.10.compress_ref = bf16[256,64]{1,0:T(8,128)(2,1)S(1)} copy(bf16[256,64]{0,1:T(8,128)(2,1)} %param.10) | data formatting | bytes 65536 | tf_op args[2]
  0.9 0.0 copy-start.9
  0.9 0.6 %copy-done.9 = s32[4]{0:T(128)S(1)} copy-done((s32[4]{0:T(128)S(1)}, s32[4]{0:T(128)}, u32[]{:S(2)}) %copy-start.9) | copy-done | bytes 40
  1.6 0.0 copy-done.5
  1.6 1.2 %copy-done = bf16[16,128,256]{2,1,0:T(8,128)(2,1)S(1)} copy-done((bf16[16,128,256]{2,1,0:T(8,128)(2,1)S(1)}, bf16[16,128,256]{2,1,0:T(8,128)(2,1)}, u32[]{:S(2)}) %copy-start) | copy-done | bytes 1048600
  2.8 1.2 %copy-done.2 = bf16[16,128,256]{2,1,0:T(8,128)(2,1)S(1)} copy-done((bf16[16,128,256]{2,1,0:T(8,128)(2,1)S(1)}, bf16[16,128,256]{2,1,0:T(8,128)(2,1)}, u32[]{:S(2)}) %copy-start.2) | copy-done | bytes 1048600
  4.0 5.7 %partial_sums.1 = (f32[8,128,256]{2,1,0:T(8,128)S(1)}, f32[8,128,256]{2,1,0:T(8,128)S(1)}) custom-call(s32[4]{0:T(128)S(1)} %broadcast_xor_fusion.pieces_ref, bf16[16,128,256]{2,1,0:T(8,128)(2,1)S(1)} %copy-done, bf16[16,128,256]{2,1,0:T(8,128)(2,1)S(1)} %copy-done.2, bf16[256,64]{1,0:T(8,128)(2,1)S(1)} %copy.10.compress_ref, bf16[64,128]{1,0:T(8,128)(2,1)S(1)} %copy-done.5), custom_call_target="tpu_custom_call" | custom-call | tf_op jit(solution)/shard_map/partial_sums/pallas_call | solution.py:62
  9.8 0.5 collective-permute-start
  10.3 2.3 %collective-permute-done = f32[8,128,256]{2,1,0:T(8,128)S(1)} collective-permute-done((f32[8,128,256]{2,1,0:T(8,128)S(1)}, f32[8,128,256]{2,1,0:T(8,128)S(1)}, u32[]{:S(2)}, u32[]{:S(2)}) %collective-permute-start) | collective-permute-done | bytes 1048608 | tf_op jit(solution)/shard_map/ppermute | solution.py:191
  12.6 0.1 add.3
  12.7 0.0 copy-start.1
  12.8 0.0 copy-start.3
  12.8 3.0 %collective-permute-start.1 = (bf16[4,128,256]{2,1,0:T(8,128)(2,1)S(1)}, bf16[4,128,256]{2,1,0:T(8,128)(2,1)S(1)}, u32[]{:S(2)}, u32[]{:S(2)}) collective-permute-start(bf16[4,128,256]{2,1,0:T(8,128)(2,1)S(1)} %slice.22), channel_id=1, source_target_pairs={{0,2},{1,3},{2,0},{3,1},{4,6},{5,7},{6,4},{7,5},{8,10},{9,11},{10,... | collective-permute-start | bytes 786440 | tf_op jit(solution)/shard_map/ppermute | solution.py:191
  15.8 6.6 %collective-permute-done.1.got_ref = bf16[4,128,256]{2,1,0:T(8,128)(2,1)S(1)} collective-permute-done((bf16[4,128,256]{2,1,0:T(8,128)(2,1)S(1)}, bf16[4,128,256]{2,1,0:T(8,128)(2,1)S(1)}, u32[]{:S(2)}, u32[]{:S(2)}) %collective-permute-start.1) | collective-permute-done | bytes 262176 | tf_op jit(solution)/shard_map/ppermute | solution.py:191
  22.3 0.1 layer_back.1.rest_0_
  22.5 0.0 copy-start.6
  22.5 1.8 %collective-permute-start.2 = (bf16[4,64,256]{2,1,0:T(8,128)(2,1)S(1)}, bf16[4,64,256]{2,1,0:T(8,128)(2,1)S(1)}, u32[]{:S(2)}, u32[]{:S(2)}) collective-permute-start(bf16[4,64,256]{2,1,0:T(8,128)(2,1)S(1)} %layer_back.1.rest_0_), channel_id=1, source_target_pairs={{0,2},{1,3},{2,0},{3,1},{4,6},{5,7},{6,4},{7,5},{8,10},{9,11},{10,... | collective-permute-start | bytes 393224 | tf_op jit(solution)/shard_map/ppermute | solution.py:191
  24.3 3.3 %collective-permute-done.2.rest_1_ = bf16[4,64,256]{2,1,0:T(8,128)(2,1)S(1)} collective-permute-done((bf16[4,64,256]{2,1,0:T(8,128)(2,1)S(1)}, bf16[4,64,256]{2,1,0:T(8,128)(2,1)S(1)}, u32[]{:S(2)}, u32[]{:S(2)}) %collective-permute-start.2) | collective-permute-done | bytes 131104 | tf_op jit(solution)/shard_map/ppermute | solution.py:191
  27.6 0.1 collective-permute-start.3
  27.7 0.5 broadcast.3
  28.2 0.0 copy-done.6
  28.2 0.7 %reduce.3 = s32[4096]{0:T(1024)S(1)} reduce(s32[4096,1]{0,1:T(1,128)S(1)} %copy-done.6, s32[]{:T(128)} %broadcast.3), dimensions={1}, to_apply=%param.13.reduce_sub_computation.3 | reduce | bytes 32772 | tf_op args[5]
  28.9 0.0 copy-start.7
  28.9 0.7 %copy-done.7 = s32[4096]{0:T(1024)S(1)} copy-done((s32[4096]{0:T(1024)S(1)}, s32[4096]{0:T(1024)}, u32[]{:S(2)}) %copy-start.7) | copy-done | bytes 16408
  29.6 0.6 %copy-done.8 = s32[4]{0:T(128)S(1)} copy-done((s32[4]{0:T(128)S(1)}, s32[4]{0:T(128)}, u32[]{:S(2)}) %copy-start.8) | copy-done | bytes 40
  30.3 0.0 collective-permute-done.3.rest_2_
  30.3 0.0 copy-done.1
  30.3 0.0 copy-done.3
  30.3 0.0 copy-done.4
  30.3 5.4 %table_partial.1 = bf16[8,128,256]{2,1,0:T(8,128)(2,1)S(1)} custom-call(s32[4]{0:T(128)S(1)} %broadcast_xor_fusion.1.pieces_ref, bf16[16,128,256]{2,1,0:T(8,128)(2,1)S(1)} %copy-done.1, bf16[16,128,256]{2,1,0:T(8,128)(2,1)S(1)} %copy-done.3, bf16[256,64]{1,0:T(8,128)(2,1)S(1)} %copy.10.compress_ref, bf16[256,256]{1,0:T(8,128)(2,1)S(1)} %copy-done.4, ...), custom_call_target="tpu_custom_call" | custom-call | tf_op jit(solution)/shard_map/table_partial/pallas_call | solution.py:163
  35.7 20.9 %all_to_all.5 = bf16[8,128,256]{2,1,0:T(8,128)(2,1)S(1)} all-to-all(bf16[8,128,256]{2,1,0:T(8,128)(2,1)S(1)} %table_partial.1), channel_id=1, replica_groups=mesh['dp'=8,'dim'=4] {'dp'}, dimensions={0} | all-to-all | bytes 1048576 | tf_op jit(solution)/shard_map/all_to_all | solution.py:224
  56.6 0.7 %convert_reduce_fusion = f32[128,256]{1,0:T(8,128)} fusion(bf16[8,128,256]{2,1,0:T(8,128)(2,1)S(1)} %all_to_all.5), kind=kLoop, calls=%fused_computation | loop fusion | flops 491520 | bytes 655360 | tf_op jit(solution)/shard_map/reduce_sum | solution.py:225
  (12 shorter events, 0.1 us)
Async XLA Ops:
  0.0 1.6 %copy-start.5 = (bf16[64,128]{1,0:T(8,128)(2,1)S(1)}, bf16[64,128]{1,0:T(8,128)(2,1)}, u32[]{:S(2)}) copy-start(bf16[64,128]{1,0:T(8,128)(2,1)} %proj_ref.1) | copy-start | bytes 49156
  0.9 0.7 %copy-start.9 = (s32[4]{0:T(128)S(1)}, s32[4]{0:T(128)}, u32[]{:S(2)}) copy-start(s32[4]{0:T(128)} %constant.11) | copy-start | bytes 52
  1.6 1.2 %copy-start = (bf16[16,128,256]{2,1,0:T(8,128)(2,1)S(1)}, bf16[16,128,256]{2,1,0:T(8,128)(2,1)}, u32[]{:S(2)}) copy-start(bf16[16,128,256]{2,1,0:T(8,128)(2,1)} %av_ref.3) | copy-start | bytes 3145732
  2.8 1.2 %copy-start.2 = (bf16[16,128,256]{2,1,0:T(8,128)(2,1)S(1)}, bf16[16,128,256]{2,1,0:T(8,128)(2,1)}, u32[]{:S(2)}) copy-start(bf16[16,128,256]{2,1,0:T(8,128)(2,1)} %up_ref.3) | copy-start | bytes 3145732
  9.8 2.8 %collective-permute-start = (f32[8,128,256]{2,1,0:T(8,128)S(1)}, f32[8,128,256]{2,1,0:T(8,128)S(1)}, u32[]{:S(2)}, u32[]{:S(2)}) collective-permute-start(f32[8,128,256]{2,1,0:T(8,128)S(1)} %get-tuple-element.8), channel_id=1, source_target_pairs={{0,1},{1,0},{2,3},{3,2},{4,5},{5,4},{6,7},{7,6},{8,9},{9,8},{10,11... | collective-permute-start | bytes 3145736 | tf_op jit(solution)/shard_map/ppermute | solution.py:191
  12.7 17.5 %copy-start.1 = (bf16[16,128,256]{2,1,0:T(8,128)(2,1)S(1)}, bf16[16,128,256]{2,1,0:T(8,128)(2,1)}, u32[]{:S(2)}) copy-start(bf16[16,128,256]{2,1,0:T(8,128)(2,1)} %av_ref.3) | copy-start | bytes 3145732
  12.8 17.5 %copy-start.3 = (bf16[16,128,256]{2,1,0:T(8,128)(2,1)S(1)}, bf16[16,128,256]{2,1,0:T(8,128)(2,1)}, u32[]{:S(2)}) copy-start(bf16[16,128,256]{2,1,0:T(8,128)(2,1)} %up_ref.3) | copy-start | bytes 3145732
  12.8 9.6 %collective-permute-start.1 = (bf16[4,128,256]{2,1,0:T(8,128)(2,1)S(1)}, bf16[4,128,256]{2,1,0:T(8,128)(2,1)S(1)}, u32[]{:S(2)}, u32[]{:S(2)}) collective-permute-start(bf16[4,128,256]{2,1,0:T(8,128)(2,1)S(1)} %slice.22), channel_id=1, source_target_pairs={{0,2},{1,3},{2,0},{3,1},{4,6},{5,7},{6,4},{7,5},{8,10},{9,11},{10,... | collective-permute-start | bytes 786440 | tf_op jit(solution)/shard_map/ppermute | solution.py:191
  22.5 5.7 %copy-start.6 = (s32[4096,1]{0,1:T(1,128)S(1)}, s32[4096,1]{0,1:T(1,128)}, u32[]{:S(2)}) copy-start(s32[4096,1]{0,1:T(1,128)} %param.13) | copy-start | bytes 49156
  22.5 5.1 %collective-permute-start.2 = (bf16[4,64,256]{2,1,0:T(8,128)(2,1)S(1)}, bf16[4,64,256]{2,1,0:T(8,128)(2,1)S(1)}, u32[]{:S(2)}, u32[]{:S(2)}) collective-permute-start(bf16[4,64,256]{2,1,0:T(8,128)(2,1)S(1)} %layer_back.1.rest_0_), channel_id=1, source_target_pairs={{0,2},{1,3},{2,0},{3,1},{4,6},{5,7},{6,4},{7,5},{8,10},{9,11},{10,... | collective-permute-start | bytes 393224 | tf_op jit(solution)/shard_map/ppermute | solution.py:191
  27.6 2.7 %copy-start.4 = (bf16[256,256]{1,0:T(8,128)(2,1)S(1)}, bf16[256,256]{1,0:T(8,128)(2,1)}, u32[]{:S(2)}) copy-start(bf16[256,256]{1,0:T(8,128)(2,1)} %mix_ref.1) | copy-start | bytes 393220
  27.6 2.7 %collective-permute-start.3 = (bf16[8,64,256]{2,1,0:T(8,128)(2,1)S(1)}, bf16[8,64,256]{2,1,0:T(8,128)(2,1)S(1)}, u32[]{:S(2)}, u32[]{:S(2)}) collective-permute-start(bf16[8,64,256]{2,1,0:T(8,128)(2,1)S(1)} %pad_maximum_fusion), channel_id=1, source_target_pairs={{0,1},{1,0},{2,3},{3,2},{4,5},{5,4},{6,7},{7,6},{8,9},{9,8},{10,11... | collective-permute-start | bytes 786440 | tf_op jit(solution)/shard_map/ppermute | solution.py:191
  28.9 0.7 %copy-start.7 = (s32[4096]{0:T(1024)S(1)}, s32[4096]{0:T(1024)}, u32[]{:S(2)}) copy-start(s32[4096]{0:T(1024)} %param.14) | copy-start | bytes 49156
  29.6 0.7 %copy-start.8 = (s32[4]{0:T(128)S(1)}, s32[4]{0:T(128)}, u32[]{:S(2)}) copy-start(s32[4]{0:T(128)} %constant.8.clone) | copy-start | bytes 52

commit v2 on v0

v2 whole, which is shorter than its diff:
```python
import functools

import jax
import jax.numpy as jnp
from jax import lax
from jax.experimental import pallas as pl
from jax.experimental.pallas import tpu as pltpu
from jax.sharding import PartitionSpec as P

SHARD = 256
F32, BF16 = jnp.float32, jnp.bfloat16
LIMIT = 20 * 2**20
LOAD_LIMIT = 50 * 2**20
VMEM = pl.BlockSpec(memory_space=pltpu.VMEM)


def dot_nt(a, b):
    return lax.dot_general(a, b, (((1,), (1,)), ((), ())), preferred_element_type=F32)


def dot_nn(a, b):
    return lax.dot_general(a, b, (((1,), (0,)), ((), ())), preferred_element_type=F32)


def bits_of(size):
    return [1 << t for t in range(size.bit_length() - 1)]


def halves(bits):
    numbers = [0]
    for bit in reversed(bits):
        numbers += [n ^ bit for n in numbers]
    return numbers


def cost(flops, moved):
    return pl.CostEstimate(flops=flops, bytes_accessed=moved, transcendentals=0)


def width_sums(comp_t_ref, proj_ref, av_ref, up_ref, places, out_refs):
    rank = comp_t_ref.shape[0]
    for n, place in enumerate(places):
        out_ref, at = out_refs[2 * n // len(places)], n % (len(places) // 2)
        reduced = dot_nt(comp_t_ref[...], av_ref[place]).astype(BF16)
        sums = dot_nn(reduced, av_ref[place])
        out_ref[at, :rank] = sums - jnp.mean(sums, axis=0, keepdims=True)
        grads = dot_nn(proj_ref[...], up_ref[place])
        out_ref[at, rank:] = grads - jnp.mean(grads, axis=0, keepdims=True)


def load_kernel(order, groups, av_hbm, up_hbm, comp_t_ref, proj_ref, send_ref, keep_ref, av_ref, up_ref, av_sem, up_sem):
    me = lax.axis_index("dim")
    samples = av_ref.shape[0]
    piece = samples // len(order)
    share = piece // groups
    copies = []
    for g in range(groups):
        for n, j in enumerate(order):
            source = pl.ds((me ^ j) * piece + g * share, share)
            place = (g * len(order) + n) * share
            at = g * len(order) + n
            pair = (
                pltpu.make_async_copy(av_hbm.at[source], av_ref.at[pl.ds(place, share)], av_sem.at[at]),
                pltpu.make_async_copy(up_hbm.at[source], up_ref.at[pl.ds(place, share)], up_sem.at[at]),
            )
            pair[0].start()
            pair[1].start()
            copies.append(pair)
    first = len(order)
    for pair in copies[:first]:
        pair[0].wait()
        pair[1].wait()
    width_sums(comp_t_ref, proj_ref, av_ref, up_ref, range(first * share), (send_ref, keep_ref))
    for pair in copies[first:]:
        pair[0].wait()
        pair[1].wait()


def sums_kernel(places, av_ref, up_ref, comp_t_ref, proj_ref, send_ref, keep_ref):
    width_sums(comp_t_ref, proj_ref, av_ref, up_ref, places, (send_ref, keep_ref))


def load_and_sum(order, groups, av, up, comp_t, proj):
    samples, width, features = av.shape
    rank = comp_t.shape[0]
    half = jax.ShapeDtypeStruct((samples // groups // 2, 2 * rank, features), F32)
    hbm = pl.BlockSpec(memory_space=pltpu.HBM)
    count = groups * len(order)
    return pl.pallas_call(
        functools.partial(load_kernel, order, groups),
        in_specs=[hbm, hbm, VMEM, VMEM],
        out_specs=[VMEM] * 4,
        out_shape=[half, half, jax.ShapeDtypeStruct(av.shape, BF16), jax.ShapeDtypeStruct(up.shape, BF16)],
        scratch_shapes=[pltpu.SemaphoreType.DMA((count,)), pltpu.SemaphoreType.DMA((count,))],
        compiler_params=pltpu.CompilerParams(vmem_limit_bytes=LOAD_LIMIT),
        cost_estimate=cost(2 * 3 * samples // groups * width * features * rank, 4 * av.size),
        name="load_and_sum",
    )(av, up, comp_t, proj)


def sum_group(places, av, up, comp_t, proj):
    samples, width, features = av.shape
    rank = comp_t.shape[0]
    half = jax.ShapeDtypeStruct((len(places) // 2, 2 * rank, features), F32)
    return pl.pallas_call(
        functools.partial(sums_kernel, places),
        in_specs=[VMEM] * 4,
        out_specs=[VMEM] * 2,
        out_shape=[half, half],
        compiler_params=pltpu.CompilerParams(vmem_limit_bytes=LIMIT),
        cost_estimate=cost(2 * 3 * len(places) * width * features * rank, 8 * half.size),
        name="sum_group",
    )(av, up, comp_t, proj)


def layer_back_kernel(keep_ref, got_ref, pair_ref):
    rank = keep_ref.shape[1] // 2
    for b in range(keep_ref.shape[0]):
        total = keep_ref[b] + got_ref[b].astype(F32)
        centred, grads = total[:rank], total[rank:]
        inverse = 1.0 / jnp.sqrt(jnp.mean(centred * centred, axis=0, keepdims=True) + 1e-05)
        normed = centred * inverse
        moment = jnp.mean(grads * normed, axis=0, keepdims=True)
        pair_ref[b] = (inverse * (grads - normed * moment)).astype(BF16)


def layer_back(keep, got):
    samples, twice, features = keep.shape
    return pl.pallas_call(
        layer_back_kernel,
        in_specs=[VMEM] * 2,
        out_specs=VMEM,
        out_shape=jax.ShapeDtypeStruct((samples, twice // 2, features), BF16),
        compiler_params=pltpu.CompilerParams(vmem_limit_bytes=LIMIT),
        cost_estimate=cost(16 * keep.size, 8 * keep.size),
        name="layer_back",
    )(keep, got)


def table_kernel(jobs, owners, chained, pairs, has_total, *refs):
    av_ref, up_ref, comp_t_ref, mix_ref, owner_ref, slot_ref = refs[:6]
    pair_refs, refs = refs[6:6 + pairs], refs[6 + pairs:]
    if has_total:
        total_ref, refs = refs[0], refs[1:]
    outs, (masked, onehot) = refs[:-2], refs[-2:]
    _, width, features = av_ref.shape
    me, here = lax.axis_index("dim"), lax.axis_index("dp")
    slots = lax.broadcasted_iota(jnp.int32, (SHARD, features), 0)
    comp_t = comp_t_ref[...]
    for n, (place, j, offset, piece, pair, at) in enumerate(jobs):
        back = pair_refs[pair][at]
        up = up_ref[place]
        both = dot_nt(av_ref[place], jnp.concatenate([comp_t, back])).astype(BF16)
        grad = up.astype(F32) + dot_nt(up, mix_ref[...])
        grad = (grad + dot_nn(both, jnp.concatenate([back, comp_t]))).astype(BF16)
        lookups = pl.ds(pl.multiple_of(((me ^ j) * piece + offset) * features, features), features)
        owner = owner_ref[:, lookups] ^ here
        columns = slice(n * features, (n + 1) * features)
        for o in range(owners):
            mask = jnp.where(owner == o, 1.0, 0.0).astype(BF16)
            masked[o * width:(o + 1) * width, columns] = grad * mask
        hit = slots == slot_ref[:, lookups]
        onehot[:, columns] = jnp.where(hit, 1.0, 0.0).astype(BF16)
    added = dot_nt(masked[...], onehot[...])
    if has_total:
        added = added + total_ref[...]
    if chained is None:
        outs[0][...] = added
        return
    part = width // len(chained)
    for c, chain in enumerate(chained):
        for n, o in enumerate(halves(chain[1:])):
            at = (o ^ chain[0]) * width + c * part
            outs[2 * c][n] = added[at:at + part].astype(BF16)
            at = o * width + c * part
            outs[2 * c + 1][n] = added[at:at + part]


def table_part(jobs, owners, chained, av, up, comp_t, mix, owner, slot, pairs, total):
    _, width, features = av.shape
    rank = comp_t.shape[0]
    if chained is None:
        shapes = [jax.ShapeDtypeStruct((owners * width, SHARD), F32)]
    else:
        part = (owners // 2, width // len(chained), SHARD)
        shapes = [jax.ShapeDtypeStruct(part, t) for _ in chained for t in (BF16, F32)]
    args = [av, up, comp_t, mix, owner, slot, *pairs] + ([] if total is None else [total])
    lookups = len(jobs) * features
    return pl.pallas_call(
        functools.partial(table_kernel, jobs, owners, chained, len(pairs), total is not None),
        in_specs=[VMEM] * len(args),
        out_specs=[VMEM] * len(shapes),
        out_shape=shapes,
        scratch_shapes=[
            pltpu.VMEM((owners * width, lookups), BF16),
            pltpu.VMEM((SHARD, lookups), BF16),
        ],
        compiler_params=pltpu.CompilerParams(vmem_limit_bytes=LIMIT),
        cost_estimate=cost(
            2 * lookups * width * (features + 4 * rank + owners * SHARD),
            2 * lookups * width * owners,
        ),
        name="table_part",
    )(*args)


def finish_kernel(*refs):
    *ins, out_ref = refs
    part = out_ref.shape[0] // (len(ins) // 2)
    for c in range(len(ins) // 2):
        out_ref[c * part:(c + 1) * part] = ins[2 * c][0] + ins[2 * c + 1][0].astype(F32)


def finish(sums, width):
    args = [a for pair in sums for a in pair]
    return pl.pallas_call(
        finish_kernel,
        in_specs=[VMEM] * len(args),
        out_specs=VMEM,
        out_shape=jax.ShapeDtypeStruct((width, SHARD), F32),
        compiler_params=pltpu.CompilerParams(vmem_limit_bytes=LIMIT),
        name="finish",
    )(*args)


def swap(x, axis, bit):
    return lax.ppermute(x, axis, [(i, i ^ bit) for i in range(lax.axis_size(axis))])


def shards(attribute_vectors, upstream, compress, interact_proj, linear_mix, row_owner, row_slot):
    owners, peers = lax.axis_size("dp"), lax.axis_size("dim")
    samples, width, features = attribute_vectors.shape
    piece = samples // peers
    groups = min(2, piece)
    share = piece // groups
    comp_t = compress.T

    bits = bits_of(peers)
    held = halves(bits)
    order = held[peers // 2:] + held[:peers // 2]
    place_of = {j: n for n, j in enumerate(order)}

    send, keep, av, up = load_and_sum(order, groups, attribute_vectors, upstream, comp_t, interact_proj)
    parts = [(send, keep)]
    for g in range(1, groups):
        places = range(g * peers * share, (g + 1) * peers * share)
        parts.append(sum_group(places, av, up, comp_t, interact_proj))

    total = None
    owner, slot = row_owner.reshape(1, -1), row_slot.reshape(1, -1)
    low = bits_of(owners)[:(owners.bit_length() - 1) // 2]
    high = bits_of(owners)[len(low):]
    chains = [low + high, high[:1] + low + high[1:]]
    for g, (send, keep) in enumerate(parts):
        got = swap(send, "dim", bits[0])
        for bit in bits[1:]:
            keep = keep + got.astype(F32)
            half = keep.shape[0] // 2
            got = swap(keep[half:].astype(BF16), "dim", bit)
            keep = keep[:half]
        pairs, have = [layer_back(keep, got)], [0]
        for bit in reversed(bits):
            pairs += [swap(pair, "dim", bit) for pair in pairs]
            have += [j ^ bit for j in have]
        jobs = []
        for at, j in enumerate(have):
            for s in range(share):
                jobs.append(((g * peers + place_of[j]) * share + s, j, g * share + s, piece, at, s))
        chained = chains if g == groups - 1 else None
        outs = table_part(
            jobs, owners, chained, av, up, comp_t, linear_mix, owner, slot, pairs, total
        )
        total = outs[0]

    sums = []
    for c, chain in enumerate(chains):
        send, keep = outs[2 * c], outs[2 * c + 1]
        got = swap(send, "dp", chain[0])
        for bit in chain[1:]:
            keep = keep + got.astype(F32)
            half = keep.shape[0] // 2
            got = swap(keep[half:].astype(BF16), "dp", bit)
            keep = keep[:half]
        sums.append((keep, got))
    return finish(sums, width)


def solution(mesh):
    placed = (
        P("dp", "dim", None),
        P("dp", "dim", None),
        P(),
        P(None, "dim"),
        P(),
        P("dp", None),
        P("dp"),
    )
    return jax.shard_map(
        shards, mesh=mesh, in_specs=placed, out_specs=P("dim", "dp"), check_vma=False
    )
```

time: 215 us -> 43.3 us (0.20)
  waiting for transfers between devices: 119 us -> 13.1 us
  local copies, waits for them, and re-layouts: 33.7 us -> 1.6 us
  matrix products: 26.6 us -> 0 us
  between operations: 13.6 us -> 0.2 us
  other arithmetic: 8.58 us -> 0.22 us
  starting transfers between devices: 12.8 us -> 20.7 us
  Pallas kernels: 0 us -> 7.3 us
    all_to_all x2 -> x0, waiting for transfers between devices: 93.2 us -> none  [the longest x1 93.2 us: shards(): lax.all_to_all(send_rows, 'dp', split_axis=1, concat_axis=1, tiled=True)]
    dot_general x14 -> x0, matrix products: 26.6 us -> none  [the longest x8 14 us: accumulate(): jnp.dot(block_rows, onehot, preferred_element_type=jnp.float32)]
    psum x1 -> x0, waiting for transfers between devices: 25.7 us -> none  [shards(): lax.psum((partial_feature_totals, normed_part), 'dim')]
    ppermute x0 -> x16, starting transfers between devices: none -> 20.7 us  [swap(): lax.ppermute(x, axis, [(i, i ^ bit) for i in range(lax.axis_size(axis))])]
    unnamed x25 -> x10, local copies, waits for them, and re-layouts: 18.2 us -> 1.49 us
    scatter x1 -> x0, local copies, waits for them, and re-layouts: 13.6 us -> none  [shards(): jnp.zeros((local_width, buffer_size), jnp.bfloat16).at[:, target]]
    ppermute x0 -> x16, waiting for transfers between devices: none -> 13.1 us  [swap(): lax.ppermute(x, axis, [(i, i ^ bit) for i in range(lax.axis_size(axis))])]
    all_to_all x2 -> x0, starting transfers between devices: 12.8 us -> none  [the longest x1 7.25 us: shards(): lax.all_to_all(send_slots, 'dp', split_axis=1, concat_axis=1, tiled=True)]
  transfers between devices with their start and end apart: 3 -> 16, of which waited for: 2 -> 8; matrix products, arithmetic and copies ran while one was open for 23% -> 1% of each run, Pallas kernels for 0% -> 6%
where the time goes in v2:
time: 43.3 us; the launch traced here: 43.1 us
  starting transfers between devices  20.7 us (48%)
  waiting for transfers between devices  13.1 us (30%)
  Pallas kernels  7.3 us (17%)
  local copies, waits for them, and re-layouts  1.6 us (4%)
    ppermute x16, starting transfers between devices, swap(): lax.ppermute(x, axis, [(i, i ^ bit) for i in range(lax.axis_size(axis))])  20.7 us
    ppermute x16, waiting for transfers between devices, swap(): lax.ppermute(x, axis, [(i, i ^ bit) for i in range(lax.axis_size(axis))])  13.1 us
    pallas_call x2, Pallas kernels, table_part(): pl.pallas_call(functools.partial(table_kernel, jobs, owners, chained, len...  3.86 us
    pallas_call x1, Pallas kernels, load_and_sum(): pl.pallas_call(functools.partial(load_kernel, order, groups), in_specs=[h...  2.02 us
    unnamed x10, local copies, waits for them, and re-layouts  1.49 us
  transfers between devices with their start and end apart: 16, of which 8 were waited for; matrix products, arithmetic and copies ran while one was open for 1% of the time, Pallas kernels for 6%

profile of v2, /device:TPU:0, one launch (start us, length us, event | category | flops | bytes accessed | tf_op | source)
XLA Modules:
  0.0 43.1 jit_solution(6095645806313674473)
XLA Ops:
  0.0 0.8 %copy-done = bf16[256,64]{0,1:T(8,128)(2,1)S(1)} copy-done((bf16[256,64]{0,1:T(8,128)(2,1)S(1)}, bf16[256,64]{0,1:T(8,128)(2,1)}, u32[]{:S(2)}) %copy-start) | copy-done | bytes 32792
  0.8 0.7 %copy-done.1 = bf16[64,128]{1,0:T(8,128)(2,1)S(1)} copy-done((bf16[64,128]{1,0:T(8,128)(2,1)S(1)}, bf16[64,128]{1,0:T(8,128)(2,1)}, u32[]{:S(2)}) %copy-start.1) | copy-done | bytes 16408
  1.5 2.0 %load_and_sum.1 = (f32[4,128,256]{2,1,0:T(8,128)S(1)}, f32[4,128,256]{2,1,0:T(8,128)S(1)}, bf16[16,128,256]{2,1,0:T(8,128)(2,1)S(1)}, bf16[16,128,256]{2,1,0:T(8,128)(2,1)S(1)}) custom-call(bf16[16,128,256]{2,1,0:T(8,128)(2,1)} %av_hbm.1, bf16[16,128,256]{2,1,0:T(8,128)(2,1)} %up_hbm.1, bf16[64,256]{1,0:T(8,128)(2,1)S(1)} %bitcast.3, ...), custom_call_target="tpu_custom_call" | custom-call | flops 100663296 | bytes 2097152 | tf_op jit(solution)/shard_map/load_and_sum/pallas_call | solution.py:89
  3.5 0.5 %collective-permute-start.5 = (f32[4,128,256]{2,1,0:T(8,128)S(1)}, f32[4,128,256]{2,1,0:T(8,128)S(1)}, u32[]{:S(2)}, u32[]{:S(2)}) collective-permute-start(f32[4,128,256]{2,1,0:T(8,128)S(1)} %get-tuple-element.20), channel_id=1, source_target_pairs={{0,1},{1,0},{2,3},{3,2},{4,5},{5,4},{6,7},{7,6},{8,9},{9,8},{10,11... | collective-permute-start | bytes 1572872 | tf_op jit(solution)/shard_map/ppermute | solution.py:227
  4.0 0.6 %sum_group.1 = (f32[4,128,256]{2,1,0:T(8,128)S(1)}, f32[4,128,256]{2,1,0:T(8,128)S(1)}) custom-call(bf16[16,128,256]{2,1,0:T(8,128)(2,1)S(1)} %get-tuple-element.15.av_ref.refs_0_, bf16[16,128,256]{2,1,0:T(8,128)(2,1)S(1)} %get-tuple-element.16.up_ref.refs_1_, bf16[64,256]{1,0:T(8,128)(2,1)S(1)} %bitcast.4, bf16[64,128]{1,0:T(8,128)(2,1)S(1)} %copy-done.1), custom_call_target="tpu_custom_call" | custom-call | flops 100663296 | bytes 1048576 | tf_op jit(solution)/shard_map/sum_group/pallas_call | solution.py:105
  4.6 0.1 collective-permute-start
  4.7 0.8 %collective-permute-done.5 = f32[4,128,256]{2,1,0:T(8,128)S(1)} collective-permute-done((f32[4,128,256]{2,1,0:T(8,128)S(1)}, f32[4,128,256]{2,1,0:T(8,128)S(1)}, u32[]{:S(2)}, u32[]{:S(2)}) %collective-permute-start.5) | collective-permute-done | bytes 524320 | tf_op jit(solution)/shard_map/ppermute | solution.py:227
  5.6 0.1 add.19
  5.6 3.0 %collective-permute-start.6 = (bf16[2,128,256]{2,1,0:T(8,128)(2,1)S(1)}, bf16[2,128,256]{2,1,0:T(8,128)(2,1)S(1)}, u32[]{:S(2)}, u32[]{:S(2)}) collective-permute-start(bf16[2,128,256]{2,1,0:T(8,128)(2,1)S(1)} %slice.74), channel_id=1, source_target_pairs={{0,2},{1,3},{2,0},{3,1},{4,6},{5,7},{6,4},{7,5},{8,10},{9,11},{10,... | collective-permute-start | bytes 393224 | tf_op jit(solution)/shard_map/ppermute | solution.py:227
  8.6 0.1 add.18
  8.7 0.7 %collective-permute-start.1 = (bf16[2,128,256]{2,1,0:T(8,128)(2,1)S(1)}, bf16[2,128,256]{2,1,0:T(8,128)(2,1)S(1)}, u32[]{:S(2)}, u32[]{:S(2)}) collective-permute-start(bf16[2,128,256]{2,1,0:T(8,128)(2,1)S(1)} %slice.75), channel_id=1, source_target_pairs={{0,2},{1,3},{2,0},{3,1},{4,6},{5,7},{6,4},{7,5},{8,10},{9,11},{10,... | collective-permute-start | bytes 393224 | tf_op jit(solution)/shard_map/ppermute | solution.py:227
  9.4 3.5 %collective-permute-done.6.got_ref = bf16[2,128,256]{2,1,0:T(8,128)(2,1)S(1)} collective-permute-done((bf16[2,128,256]{2,1,0:T(8,128)(2,1)S(1)}, bf16[2,128,256]{2,1,0:T(8,128)(2,1)S(1)}, u32[]{:S(2)}, u32[]{:S(2)}) %collective-permute-start.6) | collective-permute-done | bytes 131104 | tf_op jit(solution)/shard_map/ppermute | solution.py:227
  12.9 0.1 layer_back.3.refs_6_
  13.0 2.1 %collective-permute-start.7 = (bf16[2,64,256]{2,1,0:T(8,128)(2,1)S(1)}, bf16[2,64,256]{2,1,0:T(8,128)(2,1)S(1)}, u32[]{:S(2)}, u32[]{:S(2)}) collective-permute-start(bf16[2,64,256]{2,1,0:T(8,128)(2,1)S(1)} %layer_back.3.refs_6_), channel_id=1, source_target_pairs={{0,2},{1,3},{2,0},{3,1},{4,6},{5,7},{6,4},{7,5},{8,10},{9,11},{10,... | collective-permute-start | bytes 196616 | tf_op jit(solution)/shard_map/ppermute | solution.py:227
  15.2 0.4 collective-permute-done.1.got_ref
  15.6 0.1 layer_back.2.refs_6_
  15.7 2.1 %collective-permute-start.2 = (bf16[2,64,256]{2,1,0:T(8,128)(2,1)S(1)}, bf16[2,64,256]{2,1,0:T(8,128)(2,1)S(1)}, u32[]{:S(2)}, u32[]{:S(2)}) collective-permute-start(bf16[2,64,256]{2,1,0:T(8,128)(2,1)S(1)} %layer_back.2.refs_6_), channel_id=1, source_target_pairs={{0,2},{1,3},{2,0},{3,1},{4,6},{5,7},{6,4},{7,5},{8,10},{9,11},{10,... | collective-permute-start | bytes 196616 | tf_op jit(solution)/shard_map/ppermute | solution.py:227
  17.8 0.5 %collective-permute-start.9 = (bf16[2,64,256]{2,1,0:T(8,128)(2,1)S(1)}, bf16[2,64,256]{2,1,0:T(8,128)(2,1)S(1)}, u32[]{:S(2)}, u32[]{:S(2)}) collective-permute-start(bf16[2,64,256]{2,1,0:T(8,128)(2,1)S(1)} %collective-permute-done.7.refs_7_), channel_id=1, source_target_pairs={{0,1},{1,0},{2,3},{3,2},{4,5},{5,4},{6,7},{7,6},{8,9},{9,8},{10,11... | collective-permute-start | bytes 196616 | tf_op jit(solution)/shard_map/ppermute | solution.py:227
  18.3 1.7 %collective-permute-done.2.refs_7_ = bf16[2,64,256]{2,1,0:T(8,128)(2,1)S(1)} collective-permute-done((bf16[2,64,256]{2,1,0:T(8,128)(2,1)S(1)}, bf16[2,64,256]{2,1,0:T(8,128)(2,1)S(1)}, u32[]{:S(2)}, u32[]{:S(2)}) %collective-permute-start.2) | collective-permute-done | bytes 65568 | tf_op jit(solution)/shard_map/ppermute | solution.py:227
  20.1 1.9 %table_part.2.refs_10_ = f32[1024,256]{1,0:T(8,128)S(1)} custom-call(bf16[16,128,256]{2,1,0:T(8,128)(2,1)S(1)} %get-tuple-element.15.av_ref.refs_0_, bf16[16,128,256]{2,1,0:T(8,128)(2,1)S(1)} %get-tuple-element.16.up_ref.refs_1_, bf16[64,256]{1,0:T(8,128)(2,1)S(1)} %bitcast.5, bf16[256,256]{1,0:T(8,128)(2,1)S(1)} %copy-done.2, s32[1,4096]{1,0:T(1,128)S(1)} %bitcast.7, ...), custom_call_target="tpu_custom_call" | custom-call | flops 1342177280 | bytes 4194304 | tf_op jit(solution)/shard_map/table_part/pallas_call | solution.py:189
  22.0 1.9 %table_part.3 = (bf16[4,64,256]{2,1,0:T(8,128)(2,1)S(1)}, f32[4,64,256]{2,1,0:T(8,128)S(1)}, bf16[4,64,256]{2,1,0:T(8,128)(2,1)S(1)}, f32[4,64,256]{2,1,0:T(8,128)S(1)}) custom-call(bf16[16,128,256]{2,1,0:T(8,128)(2,1)S(1)} %get-tuple-element.15.av_ref.refs_0_, bf16[16,128,256]{2,1,0:T(8,128)(2,1)S(1)} %get-tuple-element.16.up_ref.refs_1_, ...), custom_call_target="tpu_custom_call" | custom-call | flops 1342177280 | bytes 4194304 | tf_op jit(solution)/shard_map/table_part/pallas_call | solution.py:189
  24.0 2.1 %collective-permute-start.10 = (bf16[4,64,256]{2,1,0:T(8,128)(2,1)S(1)}, bf16[4,64,256]{2,1,0:T(8,128)(2,1)S(1)}, u32[]{:S(2)}, u32[]{:S(2)}) collective-permute-start(bf16[4,64,256]{2,1,0:T(8,128)(2,1)S(1)} %get-tuple-element.22), channel_id=1, source_target_pairs={{0,4},{4,0},{8,12},{12,8},{16,20},{20,16},{24,28},{28,24},{1,5},{5... | collective-permute-start | bytes 393224 | tf_op jit(solution)/shard_map/ppermute | solution.py:227
  26.0 1.6 %collective-permute-start.13 = (bf16[4,64,256]{2,1,0:T(8,128)(2,1)S(1)}, bf16[4,64,256]{2,1,0:T(8,128)(2,1)S(1)}, u32[]{:S(2)}, u32[]{:S(2)}) collective-permute-start(bf16[4,64,256]{2,1,0:T(8,128)(2,1)S(1)} %get-tuple-element.24), channel_id=1, source_target_pairs={{0,8},{4,12},{8,0},{12,4},{16,24},{20,28},{24,16},{28,20},{1,9},{5... | collective-permute-start | bytes 393224 | tf_op jit(solution)/shard_map/ppermute | solution.py:227
  27.6 2.6 %collective-permute-done.10 = bf16[4,64,256]{2,1,0:T(8,128)(2,1)S(1)} collective-permute-done((bf16[4,64,256]{2,1,0:T(8,128)(2,1)S(1)}, bf16[4,64,256]{2,1,0:T(8,128)(2,1)S(1)}, u32[]{:S(2)}, u32[]{:S(2)}) %collective-permute-start.10) | collective-permute-done | bytes 131104 | tf_op jit(solution)/shard_map/ppermute | solution.py:227
  30.2 1.9 %collective-permute-start.11 = (bf16[2,64,256]{2,1,0:T(8,128)(2,1)S(1)}, bf16[2,64,256]{2,1,0:T(8,128)(2,1)S(1)}, u32[]{:S(2)}, u32[]{:S(2)}) collective-permute-start(bf16[2,64,256]{2,1,0:T(8,128)(2,1)S(1)} %slice.77), channel_id=1, source_target_pairs={{0,8},{4,12},{8,0},{12,4},{16,24},{20,28},{24,16},{28,20},{1,9},{5... | collective-permute-start | bytes 196616 | tf_op jit(solution)/shard_map/ppermute | solution.py:227
  32.2 1.6 %collective-permute-start.14 = (bf16[2,64,256]{2,1,0:T(8,128)(2,1)S(1)}, bf16[2,64,256]{2,1,0:T(8,128)(2,1)S(1)}, u32[]{:S(2)}, u32[]{:S(2)}) collective-permute-start(bf16[2,64,256]{2,1,0:T(8,128)(2,1)S(1)} %slice.76), channel_id=1, source_target_pairs={{0,4},{4,0},{8,12},{12,8},{16,20},{20,16},{24,28},{28,24},{1,5},{5... | collective-permute-start | bytes 196616 | tf_op jit(solution)/shard_map/ppermute | solution.py:227
  33.7 0.8 %collective-permute-done.11 = bf16[2,64,256]{2,1,0:T(8,128)(2,1)S(1)} collective-permute-done((bf16[2,64,256]{2,1,0:T(8,128)(2,1)S(1)}, bf16[2,64,256]{2,1,0:T(8,128)(2,1)S(1)}, u32[]{:S(2)}, u32[]{:S(2)}) %collective-permute-start.11) | collective-permute-done | bytes 65568 | tf_op jit(solution)/shard_map/ppermute | solution.py:227
  34.6 2.9 %collective-permute-start.12 = (bf16[1,64,256]{2,1,0:T(8,128)(2,1)S(1)}, bf16[1,64,256]{2,1,0:T(8,128)(2,1)S(1)}, u32[]{:S(2)}, u32[]{:S(2)}) collective-permute-start(bf16[1,64,256]{2,1,0:T(8,128)(2,1)S(1)} %slice.79), channel_id=1, source_target_pairs={{0,16},{4,20},{8,24},{12,28},{16,0},{20,4},{24,8},{28,12},{1,17},{... | collective-permute-start | bytes 98312 | tf_op jit(solution)/shard_map/ppermute | solution.py:227
  37.5 1.7 %collective-permute-start.15 = (bf16[1,64,256]{2,1,0:T(8,128)(2,1)S(1)}, bf16[1,64,256]{2,1,0:T(8,128)(2,1)S(1)}, u32[]{:S(2)}, u32[]{:S(2)}) collective-permute-start(bf16[1,64,256]{2,1,0:T(8,128)(2,1)S(1)} %slice.78), channel_id=1, source_target_pairs={{0,16},{4,20},{8,24},{12,28},{16,0},{20,4},{24,8},{28,12},{1,17},{... | collective-permute-start | bytes 98312 | tf_op jit(solution)/shard_map/ppermute | solution.py:227
  39.2 0.4 collective-permute-done.12.refs_1_
  39.6 2.8 %collective-permute-done.15.refs_3_ = bf16[1,64,256]{2,1,0:T(8,128)(2,1)S(1)} collective-permute-done((bf16[1,64,256]{2,1,0:T(8,128)(2,1)S(1)}, bf16[1,64,256]{2,1,0:T(8,128)(2,1)S(1)}, u32[]{:S(2)}, u32[]{:S(2)}) %collective-permute-start.15) | collective-permute-done | bytes 32800 | tf_op jit(solution)/shard_map/ppermute | solution.py:227
  42.4 0.7 %finish.1 = f32[128,256]{1,0:T(8,128)} custom-call(f32[1,64,256]{2,1,0:T(8,128)S(1)} %slice.60.refs_0_, bf16[1,64,256]{2,1,0:T(8,128)(2,1)S(1)} %collective-permute-done.12.refs_1_, f32[1,64,256]{2,1,0:T(8,128)S(1)} %slice.64.refs_2_, bf16[1,64,256]{2,1,0:T(8,128)(2,1)S(1)} %collective-permute-done.15.refs_3_), custom_call_target="tpu_custom_call" | custom-call | tf_op jit(solution)/shard_map/finish/pallas_call | solution.py:216
  (33 shorter events, 0.2 us)
Async XLA Ops:
  0.0 0.8 %copy-start = (bf16[256,64]{0,1:T(8,128)(2,1)S(1)}, bf16[256,64]{0,1:T(8,128)(2,1)}, u32[]{:S(2)}) copy-start(bf16[256,64]{0,1:T(8,128)(2,1)} %param.9) | copy-start | bytes 98308
  0.8 0.7 %copy-start.1 = (bf16[64,128]{1,0:T(8,128)(2,1)S(1)}, bf16[64,128]{1,0:T(8,128)(2,1)}, u32[]{:S(2)}) copy-start(bf16[64,128]{1,0:T(8,128)(2,1)} %proj_ref.3) | copy-start | bytes 49156
  3.5 2.1 %collective-permute-start.5 = (f32[4,128,256]{2,1,0:T(8,128)S(1)}, f32[4,128,256]{2,1,0:T(8,128)S(1)}, u32[]{:S(2)}, u32[]{:S(2)}) collective-permute-start(f32[4,128,256]{2,1,0:T(8,128)S(1)} %get-tuple-element.20), channel_id=1, source_target_pairs={{0,1},{1,0},{2,3},{3,2},{4,5},{5,4},{6,7},{7,6},{8,9},{9,8},{10,11... | collective-permute-start | bytes 1572872 | tf_op jit(solution)/shard_map/ppermute | solution.py:227
  4.6 4.0 %collective-permute-start = (f32[4,128,256]{2,1,0:T(8,128)S(1)}, f32[4,128,256]{2,1,0:T(8,128)S(1)}, u32[]{:S(2)}, u32[]{:S(2)}) collective-permute-start(f32[4,128,256]{2,1,0:T(8,128)S(1)} %get-tuple-element.18), channel_id=1, source_target_pairs={{0,1},{1,0},{2,3},{3,2},{4,5},{5,4},{6,7},{7,6},{8,9},{9,8},{10,11... | collective-permute-start | bytes 1572872 | tf_op jit(solution)/shard_map/ppermute | solution.py:227
  5.6 7.2 %collective-permute-start.6 = (bf16[2,128,256]{2,1,0:T(8,128)(2,1)S(1)}, bf16[2,128,256]{2,1,0:T(8,128)(2,1)S(1)}, u32[]{:S(2)}, u32[]{:S(2)}) collective-permute-start(bf16[2,128,256]{2,1,0:T(8,128)(2,1)S(1)} %slice.74), channel_id=1, source_target_pairs={{0,2},{1,3},{2,0},{3,1},{4,6},{5,7},{6,4},{7,5},{8,10},{9,11},{10,... | collective-permute-start | bytes 393224 | tf_op jit(solution)/shard_map/ppermute | solution.py:227
  8.7 6.9 %collective-permute-start.1 = (bf16[2,128,256]{2,1,0:T(8,128)(2,1)S(1)}, bf16[2,128,256]{2,1,0:T(8,128)(2,1)S(1)}, u32[]{:S(2)}, u32[]{:S(2)}) collective-permute-start(bf16[2,128,256]{2,1,0:T(8,128)(2,1)S(1)} %slice.75), channel_id=1, source_target_pairs={{0,2},{1,3},{2,0},{3,1},{4,6},{5,7},{6,4},{7,5},{8,10},{9,11},{10,... | collective-permute-start | bytes 393224 | tf_op jit(solution)/shard_map/ppermute | solution.py:227
  13.0 4.8 %collective-permute-start.7 = (bf16[2,64,256]{2,1,0:T(8,128)(2,1)S(1)}, bf16[2,64,256]{2,1,0:T(8,128)(2,1)S(1)}, u32[]{:S(2)}, u32[]{:S(2)}) collective-permute-start(bf16[2,64,256]{2,1,0:T(8,128)(2,1)S(1)} %layer_back.3.refs_6_), channel_id=1, source_target_pairs={{0,2},{1,3},{2,0},{3,1},{4,6},{5,7},{6,4},{7,5},{8,10},{9,11},{10,... | collective-permute-start | bytes 196616 | tf_op jit(solution)/shard_map/ppermute | solution.py:227
  15.1 4.9 %copy-start.2 = (bf16[256,256]{1,0:T(8,128)(2,1)S(1)}, bf16[256,256]{1,0:T(8,128)(2,1)}, u32[]{:S(2)}) copy-start(bf16[256,256]{1,0:T(8,128)(2,1)} %refs_3_.3) | copy-start | bytes 393220
  15.1 4.9 %copy-start.3 = (s32[4096,1]{0,1:T(1,128)S(1)}, s32[4096,1]{0,1:T(1,128)}, u32[]{:S(2)}) copy-start(s32[4096,1]{0,1:T(1,128)} %param.12) | copy-start | bytes 49156
  15.1 4.9 %copy-start.4 = (s32[4096]{0:T(1024)S(1)}, s32[4096]{0:T(1024)}, u32[]{:S(2)}) copy-start(s32[4096]{0:T(1024)} %param.13) | copy-start | bytes 49156
  15.7 4.4 %collective-permute-start.2 = (bf16[2,64,256]{2,1,0:T(8,128)(2,1)S(1)}, bf16[2,64,256]{2,1,0:T(8,128)(2,1)S(1)}, u32[]{:S(2)}, u32[]{:S(2)}) collective-permute-start(bf16[2,64,256]{2,1,0:T(8,128)(2,1)S(1)} %layer_back.2.refs_6_), channel_id=1, source_target_pairs={{0,2},{1,3},{2,0},{3,1},{4,6},{5,7},{6,4},{7,5},{8,10},{9,11},{10,... | collective-permute-start | bytes 196616 | tf_op jit(solution)/shard_map/ppermute | solution.py:227
  17.8 2.3 %collective-permute-start.8 = (bf16[2,64,256]{2,1,0:T(8,128)(2,1)S(1)}, bf16[2,64,256]{2,1,0:T(8,128)(2,1)S(1)}, u32[]{:S(2)}, u32[]{:S(2)}) collective-permute-start(bf16[2,64,256]{2,1,0:T(8,128)(2,1)S(1)} %layer_back.3.refs_6_), channel_id=1, source_target_pairs={{0,1},{1,0},{2,3},{3,2},{4,5},{5,4},{6,7},{7,6},{8,9},{9,8},{10,11... | collective-permute-start | bytes 196616 | tf_op jit(solution)/shard_map/ppermute | solution.py:227
  17.8 2.2 %collective-permute-start.9 = (bf16[2,64,256]{2,1,0:T(8,128)(2,1)S(1)}, bf16[2,64,256]{2,1,0:T(8,128)(2,1)S(1)}, u32[]{:S(2)}, u32[]{:S(2)}) collective-permute-start(bf16[2,64,256]{2,1,0:T(8,128)(2,1)S(1)} %collective-permute-done.7.refs_7_), channel_id=1, source_target_pairs={{0,1},{1,0},{2,3},{3,2},{4,5},{5,4},{6,7},{7,6},{8,9},{9,8},{10,11... | collective-permute-start | bytes 196616 | tf_op jit(solution)/shard_map/ppermute | solution.py:227
  18.3 3.7 %collective-permute-start.3 = (bf16[2,64,256]{2,1,0:T(8,128)(2,1)S(1)}, bf16[2,64,256]{2,1,0:T(8,128)(2,1)S(1)}, u32[]{:S(2)}, u32[]{:S(2)}) collective-permute-start(bf16[2,64,256]{2,1,0:T(8,128)(2,1)S(1)} %layer_back.2.refs_6_), channel_id=1, source_target_pairs={{0,1},{1,0},{2,3},{3,2},{4,5},{5,4},{6,7},{7,6},{8,9},{9,8},{10,11... | collective-permute-start | bytes 196616 | tf_op jit(solution)/shard_map/ppermute | solution.py:227
  20.0 2.0 %collective-permute-start.4 = (bf16[2,64,256]{2,1,0:T(8,128)(2,1)S(1)}, bf16[2,64,256]{2,1,0:T(8,128)(2,1)S(1)}, u32[]{:S(2)}, u32[]{:S(2)}) collective-permute-start(bf16[2,64,256]{2,1,0:T(8,128)(2,1)S(1)} %collective-permute-done.2.refs_7_), channel_id=1, source_target_pairs={{0,1},{1,0},{2,3},{3,2},{4,5},{5,4},{6,7},{7,6},{8,9},{9,8},{10,11... | collective-permute-start | bytes 196616 | tf_op jit(solution)/shard_map/ppermute | solution.py:227
  24.0 6.2 %collective-permute-start.10 = (bf16[4,64,256]{2,1,0:T(8,128)(2,1)S(1)}, bf16[4,64,256]{2,1,0:T(8,128)(2,1)S(1)}, u32[]{:S(2)}, u32[]{:S(2)}) collective-permute-start(bf16[4,64,256]{2,1,0:T(8,128)(2,1)S(1)} %get-tuple-element.22), channel_id=1, source_target_pairs={{0,4},{4,0},{8,12},{12,8},{16,20},{20,16},{24,28},{28,24},{1,5},{5... | collective-permute-start | bytes 393224 | tf_op jit(solution)/shard_map/ppermute | solution.py:227
  26.0 6.1 %collective-permute-start.13 = (bf16[4,64,256]{2,1,0:T(8,128)(2,1)S(1)}, bf16[4,64,256]{2,1,0:T(8,128)(2,1)S(1)}, u32[]{:S(2)}, u32[]{:S(2)}) collective-permute-start(bf16[4,64,256]{2,1,0:T(8,128)(2,1)S(1)} %get-tuple-element.24), channel_id=1, source_target_pairs={{0,8},{4,12},{8,0},{12,4},{16,24},{20,28},{24,16},{28,20},{1,9},{5... | collective-permute-start | bytes 393224 | tf_op jit(solution)/shard_map/ppermute | solution.py:227
  30.2 4.3 %collective-permute-start.11 = (bf16[2,64,256]{2,1,0:T(8,128)(2,1)S(1)}, bf16[2,64,256]{2,1,0:T(8,128)(2,1)S(1)}, u32[]{:S(2)}, u32[]{:S(2)}) collective-permute-start(bf16[2,64,256]{2,1,0:T(8,128)(2,1)S(1)} %slice.77), channel_id=1, source_target_pairs={{0,8},{4,12},{8,0},{12,4},{16,24},{20,28},{24,16},{28,20},{1,9},{5... | collective-permute-start | bytes 196616 | tf_op jit(solution)/shard_map/ppermute | solution.py:227
  32.2 5.3 %collective-permute-start.14 = (bf16[2,64,256]{2,1,0:T(8,128)(2,1)S(1)}, bf16[2,64,256]{2,1,0:T(8,128)(2,1)S(1)}, u32[]{:S(2)}, u32[]{:S(2)}) collective-permute-start(bf16[2,64,256]{2,1,0:T(8,128)(2,1)S(1)} %slice.76), channel_id=1, source_target_pairs={{0,4},{4,0},{8,12},{12,8},{16,20},{20,16},{24,28},{28,24},{1,5},{5... | collective-permute-start | bytes 196616 | tf_op jit(solution)/shard_map/ppermute | solution.py:227
  34.6 5.0 %collective-permute-start.12 = (bf16[1,64,256]{2,1,0:T(8,128)(2,1)S(1)}, bf16[1,64,256]{2,1,0:T(8,128)(2,1)S(1)}, u32[]{:S(2)}, u32[]{:S(2)}) collective-permute-start(bf16[1,64,256]{2,1,0:T(8,128)(2,1)S(1)} %slice.79), channel_id=1, source_target_pairs={{0,16},{4,20},{8,24},{12,28},{16,0},{20,4},{24,8},{28,12},{1,17},{... | collective-permute-start | bytes 98312 | tf_op jit(solution)/shard_map/ppermute | solution.py:227
  37.5 4.9 %collective-permute-start.15 = (bf16[1,64,256]{2,1,0:T(8,128)(2,1)S(1)}, bf16[1,64,256]{2,1,0:T(8,128)(2,1)S(1)}, u32[]{:S(2)}, u32[]{:S(2)}) collective-permute-start(bf16[1,64,256]{2,1,0:T(8,128)(2,1)S(1)} %slice.78), channel_id=1, source_target_pairs={{0,16},{4,20},{8,24},{12,28},{16,0},{20,4},{24,8},{28,12},{1,17},{... | collective-permute-start | bytes 98312 | tf_op jit(solution)/shard_map/ppermute | solution.py:227

commit v3 on v0

v3 whole, which is shorter than its diff:
```python
import functools

import jax
import jax.numpy as jnp
from jax import lax
from jax.experimental import pallas as pl
from jax.experimental.pallas import tpu as pltpu
from jax.sharding import PartitionSpec as P

SHARD = 256
F32, BF16 = jnp.float32, jnp.bfloat16
LIMIT = 20 * 2**20
LOAD_LIMIT = 51 * 2**20
VMEM = pl.BlockSpec(memory_space=pltpu.VMEM)
HBM = pl.BlockSpec(memory_space=pltpu.HBM)


def dot_nt(a, b):
    return lax.dot_general(a, b, (((1,), (1,)), ((), ())), preferred_element_type=F32)


def dot_nn(a, b):
    return lax.dot_general(a, b, (((1,), (0,)), ((), ())), preferred_element_type=F32)


def bits_of(size):
    return [1 << t for t in range(size.bit_length() - 1)]


def halves(bits):
    numbers = [0]
    for bit in reversed(bits):
        numbers += [n ^ bit for n in numbers]
    return numbers


def call(kernel, name, args, shapes, flops, limit=LIMIT, specs=None, scratch=()):
    moved = sum(a.size * a.dtype.itemsize for a in (*args, *shapes))
    return pl.pallas_call(
        kernel,
        in_specs=specs or [VMEM] * len(args),
        out_specs=[VMEM] * len(shapes),
        out_shape=list(shapes),
        scratch_shapes=list(scratch),
        compiler_params=pltpu.CompilerParams(vmem_limit_bytes=limit),
        cost_estimate=pl.CostEstimate(flops=flops, bytes_accessed=moved, transcendentals=0),
        name=name,
    )(*args)


def width_sums(comp_t_ref, proj_ref, av_ref, up_ref, place, out_ref, at):
    rank = comp_t_ref.shape[0]
    reduced = dot_nt(comp_t_ref[...], av_ref[place]).astype(BF16)
    sums = dot_nn(reduced, av_ref[place])
    out_ref[at, :rank] = sums - jnp.mean(sums, axis=0, keepdims=True)
    grads = dot_nn(proj_ref[...], up_ref[place])
    out_ref[at, rank:] = grads - jnp.mean(grads, axis=0, keepdims=True)


def load_kernel(order, av_hbm, up_hbm, comp_hbm, proj_hbm, out_ref, av_ref, up_ref, comp_t_ref, proj_ref, sems):
    me = lax.axis_index("dim")
    piece = av_ref.shape[0] // len(order)
    copies = [
        pltpu.make_async_copy(comp_hbm, comp_t_ref, sems.at[0]),
        pltpu.make_async_copy(proj_hbm, proj_ref, sems.at[1]),
    ]
    for n, j in enumerate(order):
        source = pl.ds((me ^ j) * piece, piece)
        to = pl.ds(n * piece, piece)
        copies.append(pltpu.make_async_copy(av_hbm.at[source], av_ref.at[to], sems.at[2 + 2 * n]))
        copies.append(pltpu.make_async_copy(up_hbm.at[source], up_ref.at[to], sems.at[3 + 2 * n]))
    for copy in copies:
        copy.start()
    first = 2 + 2 * (len(order) // 4)
    for copy in copies[:first]:
        copy.wait()
    for at in range(out_ref.shape[0]):
        width_sums(comp_t_ref, proj_ref, av_ref, up_ref, at, out_ref, at)
    for copy in copies[first:]:
        copy.wait()


def sums_kernel(start, av_ref, up_ref, comp_t_ref, proj_ref, *out_refs):
    for out_ref in out_refs:
        for at in range(out_ref.shape[0]):
            width_sums(comp_t_ref, proj_ref, av_ref, up_ref, start + at, out_ref, at)
        start += out_ref.shape[0]


def prepare_kernel(start, av_ref, up_ref, comp_t_ref, proj_ref, mix_ref, slot_ref, out_ref, linear_ref, onehot_ref):
    sums_kernel(start, av_ref, up_ref, comp_t_ref, proj_ref, out_ref)
    samples, width, features = up_ref.shape
    for b in range(samples):
        up = up_ref[b]
        linear_ref[b] = up.astype(F32) + dot_nt(up, mix_ref[...])
    slots = lax.broadcasted_iota(jnp.int32, (SHARD, features), 0)
    for at in range(0, samples * features, features):
        hit = slots == slot_ref[:, at:at + features]
        onehot_ref[:, at:at + features] = jnp.where(hit, 1.0, 0.0).astype(BF16)


def layer_back_kernel(*refs):
    *terms, pair_ref = refs
    rank = pair_ref.shape[1]
    for b in range(pair_ref.shape[0]):
        total = sum(term[b].astype(F32) for term in terms)
        centred, grads = total[:rank], total[rank:]
        inverse = 1.0 / jnp.sqrt(jnp.mean(centred * centred, axis=0, keepdims=True) + 1e-05)
        normed = centred * inverse
        moment = jnp.mean(grads * normed, axis=0, keepdims=True)
        pair_ref[b] = (inverse * (grads - normed * moment)).astype(BF16)


def table_kernel(jobs, chains, last, pairs, has_total, *refs):
    av_ref, comp_t_ref, linear_ref, owner_ref, onehot_ref = refs[:5]
    pair_refs, refs = refs[5:5 + pairs], refs[5 + pairs:]
    if has_total:
        total_ref, refs = refs[0], refs[1:]
    outs, (masked, onehot) = refs[:-2], refs[-2:]
    _, width, features = av_ref.shape
    me, here = lax.axis_index("dim"), lax.axis_index("dp")
    odd = me % 2 == 1
    comp_t = comp_t_ref[...]
    ids = [here ^ jnp.where(odd, b, a) for a, b in zip(*[halves(chain) for chain in chains])]
    for n, (place, j, offset, piece, pair, at) in enumerate(jobs):
        back = pair_refs[pair][at]
        both = dot_nt(av_ref[place], jnp.concatenate([comp_t, back])).astype(BF16)
        grad = linear_ref[place] + dot_nn(both, jnp.concatenate([back, comp_t]))
        grad = grad.astype(BF16)
        lookups = pl.ds(pl.multiple_of(((me ^ j) * piece + offset) * features, features), features)
        owner = owner_ref[:, lookups]
        columns = slice(n * features, (n + 1) * features)
        for o, number in enumerate(ids):
            mask = jnp.where(owner == number, 1.0, 0.0).astype(BF16)
            masked[o * width:(o + 1) * width, columns] = grad * mask
        onehot[:, columns] = onehot_ref[:, lookups]
    added = dot_nt(masked[...], onehot[...])
    if has_total:
        added = added + total_ref[...]
    if not last:
        outs[0][...] = added
        return
    half = len(ids) // 2
    for n in range(half):
        outs[0][n] = added[(half + n) * width:(half + n + 1) * width].astype(BF16)
        outs[1][n] = added[n * width:(n + 1) * width]


def table_part(jobs, chains, last, av, comp_t, linear, owner, onehot, pairs, total):
    _, width, features = av.shape
    rank = comp_t.shape[0]
    owners = 1 << len(chains[0])
    if last:
        shapes = [jax.ShapeDtypeStruct((owners // 2, width, SHARD), t) for t in (BF16, F32)]
    else:
        shapes = [jax.ShapeDtypeStruct((owners * width, SHARD), F32)]
    args = [av, comp_t, linear, owner, onehot, *pairs] + ([] if total is None else [total])
    lookups = len(jobs) * features
    return call(
        functools.partial(table_kernel, jobs, chains, last, len(pairs), total is not None),
        "table_part",
        args,
        shapes,
        2 * lookups * width * (4 * rank + owners * SHARD),
        scratch=[pltpu.VMEM((owners * width, lookups), BF16), pltpu.VMEM((SHARD, lookups), BF16)],
    )


def finish_kernel(keep_ref, got_ref, out_ref):
    out_ref[...] = keep_ref[0] + got_ref[0].astype(F32)


def swap(x, bit):
    return lax.ppermute(x, "dim", [(i, i ^ bit) for i in range(lax.axis_size("dim"))])


def swap_rows(x, chains, step):
    owners, peers = lax.axis_size("dp"), lax.axis_size("dim")
    return lax.ppermute(
        x,
        ("dp", "dim"),
        [
            (a * peers + b, (a ^ chains[b % 2][step]) * peers + b)
            for a in range(owners)
            for b in range(peers)
        ],
    )


def shards(attribute_vectors, upstream, compress, interact_proj, linear_mix, row_owner, row_slot):
    owners, peers = lax.axis_size("dp"), lax.axis_size("dim")
    samples, width, features = attribute_vectors.shape
    rank = compress.shape[1]
    piece = samples // peers
    quarter = samples // 4
    shape = jax.ShapeDtypeStruct
    part = shape((quarter, 2 * rank, features), F32)
    sample_flops = 6 * width * features * rank

    bits = bits_of(peers)
    held = halves(bits)
    count = peers // 4
    order = held[3 * count:] + held[2 * count:3 * count] + held[count:2 * count] + held[:count]
    place_of = {j: n for n, j in enumerate(order)}

    send_high, av, up, comp_t, proj = call(
        functools.partial(load_kernel, order),
        "load_and_sum",
        (attribute_vectors, upstream, compress.T, interact_proj),
        [
            part,
            shape(upstream.shape, BF16),
            shape(upstream.shape, BF16),
            shape((rank, features), BF16),
            shape(interact_proj.shape, BF16),
        ],
        quarter * sample_flops,
        limit=LOAD_LIMIT,
        specs=[HBM] * 4,
        scratch=[pltpu.SemaphoreType.DMA((2 * peers + 2,))],
    )
    args = (av, up, comp_t, proj)
    got_high = swap(send_high, bits[0])
    send_low, keep_high = call(
        functools.partial(sums_kernel, quarter), "sums", args, [part] * 2, 2 * quarter * sample_flops
    )
    got_low = swap(send_low, bits[0])
    got = swap((keep_high + got_high).astype(BF16), bits[1])
    keep_low, linear, onehot = call(
        functools.partial(prepare_kernel, 3 * quarter),
        "prepare",
        (*args, linear_mix, row_slot.reshape(1, -1)),
        [part, shape(up.shape, F32), shape((SHARD, samples * features), BF16)],
        2 * samples * width * features * features,
    )
    terms = [keep_low, got_low, got]
    for bit in bits[2:]:
        keep = sum(term.astype(F32) for term in terms)
        half = keep.shape[0] // 2
        terms = [keep[:half], swap(keep[half:].astype(BF16), bit)]
    (pair,) = call(
        layer_back_kernel, "layer_back", terms, [shape((piece, rank, features), BF16)], 16 * terms[0].size
    )
    pairs, have = [pair], [0]
    for bit in reversed(bits):
        pairs += [swap(pair, bit) for pair in pairs]
        have += [j ^ bit for j in have]
    pairs = dict(zip(have, pairs))

    low = bits_of(owners)[:(owners.bit_length() - 1) // 2]
    high = bits_of(owners)[len(low):]
    chains = [low + high, high[:1] + low + high[1:]]
    stages = [[0, bits[0]]]
    for bit in reversed(bits[1:]):
        new = [j ^ bit for stage in stages for j in stage]
        stages += [[j for j in new if not j & bits[0]], [j for j in new if j & bits[0]]]
    total = None
    for stage in stages:
        jobs = [
            (place_of[j] * piece + s, j, s, piece, at, s)
            for at, j in enumerate(stage)
            for s in range(piece)
        ]
        outs = table_part(
            jobs, chains, stage is stages[-1], av, comp_t, linear, row_owner.reshape(1, -1), onehot,
            [pairs[j] for j in stage], total,
        )
        total = outs[0]

    send, keep = outs
    got = swap_rows(send, chains, 0)
    for step in range(1, len(chains[0])):
        keep = keep + got.astype(F32)
        half = keep.shape[0] // 2
        got = swap_rows(keep[half:].astype(BF16), chains, step)
        keep = keep[:half]
    (out,) = call(finish_kernel, "finish", (keep, got), [shape((width, SHARD), F32)], width * SHARD)
    return out


def solution(mesh):
    placed = (
        P("dp", "dim", None),
        P("dp", "dim", None),
        P(),
        P(None, "dim"),
        P(),
        P("dp", None),
        P("dp"),
    )
    return jax.shard_map(
        shards, mesh=mesh, in_specs=placed, out_specs=P("dim", "dp"), check_vma=False
    )
```

time: 215 us -> 41.9 us (0.19)
  waiting for transfers between devices: 119 us -> 19.3 us
  local copies, waits for them, and re-layouts: 33.7 us -> 1.53 us
  matrix products: 26.6 us -> 0 us
  between operations: 13.6 us -> 0.13 us
  Pallas kernels: 0 us -> 8.78 us
  other arithmetic: 8.58 us -> 0.16 us
    all_to_all x2 -> x0, waiting for transfers between devices: 93.2 us -> none  [the longest x1 93.2 us: shards(): lax.all_to_all(send_rows, 'dp', split_axis=1, concat_axis=1, tiled=True)]
    dot_general x14 -> x0, matrix products: 26.6 us -> none  [the longest x8 14 us: accumulate(): jnp.dot(block_rows, onehot, preferred_element_type=jnp.float32)]
    psum x1 -> x0, waiting for transfers between devices: 25.7 us -> none  [shards(): lax.psum((partial_feature_totals, normed_part), 'dim')]
    ppermute x0 -> x9, waiting for transfers between devices: none -> 19.3 us  [the longest x3 10.4 us: swap_rows(): lax.ppermute(x, ('dp', 'dim'), [(a * peers + b, (a ^ chains[b % 2][step])...]
    unnamed x25 -> x10, local copies, waits for them, and re-layouts: 18.2 us -> 1.49 us
    scatter x1 -> x0, local copies, waits for them, and re-layouts: 13.6 us -> none  [shards(): jnp.zeros((local_width, buffer_size), jnp.bfloat16).at[:, target]]
    all_to_all x2 -> x0, starting transfers between devices: 12.8 us -> none  [the longest x1 7.25 us: shards(): lax.all_to_all(send_slots, 'dp', split_axis=1, concat_axis=1, tiled=True)]
    ppermute x0 -> x9, starting transfers between devices: none -> 11.7 us  [the longest x3 6.33 us: swap_rows(): lax.ppermute(x, ('dp', 'dim'), [(a * peers + b, (a ^ chains[b % 2][step])...]
  transfers between devices with their start and end apart: 3 -> 9, of which waited for: 2 -> 6; matrix products, arithmetic and copies ran while one was open for 23% -> 0% of each run, Pallas kernels for 0% -> 13%
where the time goes in v3:
time: 41.9 us; the launch traced here: 41.6 us
  waiting for transfers between devices  19.3 us (46%)
  starting transfers between devices  11.7 us (28%)
  Pallas kernels  8.78 us (21%)
  local copies, waits for them, and re-layouts  1.53 us (4%)
    ppermute x3, waiting for transfers between devices, swap_rows(): lax.ppermute(x, ('dp', 'dim'), [(a * peers + b, (a ^ chains[b % 2][step])...  10.4 us
    ppermute x6, waiting for transfers between devices, swap(): lax.ppermute(x, 'dim', [(i, i ^ bit) for i in range(lax.axis_size('dim'))])  8.95 us
    pallas_call x8, Pallas kernels, call(): pl.pallas_call(kernel, in_specs=specs or [VMEM] * len(args), out_specs=[V...  8.78 us
    ppermute x3, starting transfers between devices, swap_rows(): lax.ppermute(x, ('dp', 'dim'), [(a * peers + b, (a ^ chains[b % 2][step])...  6.33 us
    ppermute x6, starting transfers between devices, swap(): lax.ppermute(x, 'dim', [(i, i ^ bit) for i in range(lax.axis_size('dim'))])  5.4 us
    unnamed x10, local copies, waits for them, and re-layouts  1.49 us
  transfers between devices with their start and end apart: 9, of which 6 were waited for; matrix products, arithmetic and copies ran while one was open for 0% of the time, Pallas kernels for 13%

profile of v3, /device:TPU:0, one launch (start us, length us, event | category | flops | bytes accessed | tf_op | source)
XLA Modules:
  0.0 41.6 jit_solution(4522540042894290669)
XLA Ops:
  0.0 0.8 %copy-done.2 = bf16[256,64]{0,1:T(8,128)(2,1)S(1)} copy-done((bf16[256,64]{0,1:T(8,128)(2,1)S(1)}, bf16[256,64]{0,1:T(8,128)(2,1)}, u32[]{:S(2)}) %copy-start.2) | copy-done | bytes 32792
  0.8 0.7 %copy-done.3 = bf16[64,128]{1,0:T(8,128)(2,1)S(1)} copy-done((bf16[64,128]{1,0:T(8,128)(2,1)S(1)}, bf16[64,128]{1,0:T(8,128)(2,1)}, u32[]{:S(2)}) %copy-start.3) | copy-done | bytes 16408
  1.5 1.6 %load_and_sum.1 = (f32[4,128,256]{2,1,0:T(8,128)S(1)}, bf16[16,128,256]{2,1,0:T(8,128)(2,1)S(1)}, bf16[16,128,256]{2,1,0:T(8,128)(2,1)S(1)}, bf16[64,256]{1,0:T(8,128)(2,1)S(1)}, bf16[64,128]{1,0:T(8,128)(2,1)S(1)}) custom-call(bf16[16,128,256]{2,1,0:T(8,128)(2,1)} %av_hbm.1, bf16[16,128,256]{2,1,0:T(8,128)(2,1)} %up_hbm.1, bf16[64,256]{1,0:T(8,128)(2,1)S(1)} %bitcast.6, ...), custom_call_target="tpu_custom_call" | custom-call | flops 50331648 | bytes 4816896 | tf_op jit(solution)/shard_map/load_and_sum/pallas_call | solution.py:39
  3.1 0.0 copy-start.1
  3.1 0.0 copy-start.4
  3.1 0.5 %collective-permute-start.1 = (f32[4,128,256]{2,1,0:T(8,128)S(1)}, f32[4,128,256]{2,1,0:T(8,128)S(1)}, u32[]{:S(2)}, u32[]{:S(2)}) collective-permute-start(f32[4,128,256]{2,1,0:T(8,128)S(1)} %get-tuple-element.26), channel_id=1, source_target_pairs={{0,1},{1,0},{2,3},{3,2},{4,5},{5,4},{6,7},{7,6},{8,9},{9,8},{10,11... | collective-permute-start | bytes 1572872 | tf_op jit(solution)/shard_map/ppermute | solution.py:174
  3.6 0.6 %sums.1 = (f32[4,128,256]{2,1,0:T(8,128)S(1)}, f32[4,128,256]{2,1,0:T(8,128)S(1)}) custom-call(bf16[16,128,256]{2,1,0:T(8,128)(2,1)S(1)} %get-tuple-element.17.av_ref.refs_0_, bf16[16,128,256]{2,1,0:T(8,128)(2,1)S(1)} %get-tuple-element.19.up_ref, bf16[64,256]{1,0:T(8,128)(2,1)S(1)} %get-tuple-element.18.comp_t_ref.refs_1_, ...), custom_call_target="tpu_custom_call" | custom-call | flops 100663296 | bytes 3194880 | tf_op jit(solution)/shard_map/sums/pallas_call | solution.py:39
  4.2 0.1 collective-permute-start
  4.4 0.8 %collective-permute-done.1 = f32[4,128,256]{2,1,0:T(8,128)S(1)} collective-permute-done((f32[4,128,256]{2,1,0:T(8,128)S(1)}, f32[4,128,256]{2,1,0:T(8,128)S(1)}, u32[]{:S(2)}, u32[]{:S(2)}) %collective-permute-start.1) | collective-permute-done | bytes 524320 | tf_op jit(solution)/shard_map/ppermute | solution.py:174
  5.2 0.1 add_convert_fusion
  5.3 0.0 copy-start
  5.3 3.0 %collective-permute-start.2 = (bf16[4,128,256]{2,1,0:T(8,128)(2,1)S(1)}, bf16[4,128,256]{2,1,0:T(8,128)(2,1)S(1)}, u32[]{:S(2)}, u32[]{:S(2)}) collective-permute-start(bf16[4,128,256]{2,1,0:T(8,128)(2,1)S(1)} %add_convert_fusion), channel_id=1, source_target_pairs={{0,2},{1,3},{2,0},{3,1},{4,6},{5,7},{6,4},{7,5},{8,10},{9,11},{10,... | collective-permute-start | bytes 786440 | tf_op jit(solution)/shard_map/ppermute | solution.py:174
  8.2 1.8 %prepare.1 = (f32[4,128,256]{2,1,0:T(8,128)S(1)}, f32[16,128,256]{2,1,0:T(8,128)S(1)}, bf16[256,4096]{1,0:T(8,128)(2,1)S(1)}) custom-call(bf16[16,128,256]{2,1,0:T(8,128)(2,1)S(1)} %get-tuple-element.17.av_ref.refs_0_, bf16[16,128,256]{2,1,0:T(8,128)(2,1)S(1)} %get-tuple-element.19.up_ref, bf16[64,256]{1,0:T(8,128)(2,1)S(1)} %get-tuple-element.18.comp_t_ref.refs_1_, ...), custom_call_target="tpu_custom_call" | custom-call | flops 268435456 | bytes 7012352 | tf_op jit(solution)/shard_map/prepare/pallas_call | solution.py:39
  10.0 0.0 collective-permute-done.refs_1_
  10.0 4.8 %collective-permute-done.2.refs_2_ = bf16[4,128,256]{2,1,0:T(8,128)(2,1)S(1)} collective-permute-done((bf16[4,128,256]{2,1,0:T(8,128)(2,1)S(1)}, bf16[4,128,256]{2,1,0:T(8,128)(2,1)S(1)}, u32[]{:S(2)}, u32[]{:S(2)}) %collective-permute-start.2) | collective-permute-done | bytes 262176 | tf_op jit(solution)/shard_map/ppermute | solution.py:174
  14.8 0.2 layer_back.1.refs_5_
  15.0 1.8 %collective-permute-start.3 = (bf16[4,64,256]{2,1,0:T(8,128)(2,1)S(1)}, bf16[4,64,256]{2,1,0:T(8,128)(2,1)S(1)}, u32[]{:S(2)}, u32[]{:S(2)}) collective-permute-start(bf16[4,64,256]{2,1,0:T(8,128)(2,1)S(1)} %layer_back.1.refs_5_), channel_id=1, source_target_pairs={{0,2},{1,3},{2,0},{3,1},{4,6},{5,7},{6,4},{7,5},{8,10},{9,11},{10,... | collective-permute-start | bytes 393224 | tf_op jit(solution)/shard_map/ppermute | solution.py:174
  16.8 3.3 %collective-permute-done.3.refs_5_ = bf16[4,64,256]{2,1,0:T(8,128)(2,1)S(1)} collective-permute-done((bf16[4,64,256]{2,1,0:T(8,128)(2,1)S(1)}, bf16[4,64,256]{2,1,0:T(8,128)(2,1)S(1)}, u32[]{:S(2)}, u32[]{:S(2)}) %collective-permute-start.3) | collective-permute-done | bytes 131104 | tf_op jit(solution)/shard_map/ppermute | solution.py:174
  20.1 0.0 collective-permute-start.4
  20.1 0.0 collective-permute-done.5.refs_6_
  20.1 1.8 %table_part.3.refs_6_ = f32[1024,256]{1,0:T(8,128)S(1)} custom-call(bf16[16,128,256]{2,1,0:T(8,128)(2,1)S(1)} %get-tuple-element.17.av_ref.refs_0_, bf16[64,256]{1,0:T(8,128)(2,1)S(1)} %get-tuple-element.18.comp_t_ref.refs_1_, f32[16,128,256]{2,1,0:T(8,128)S(1)} %get-tuple-element.21.refs_2_, s32[1,4096]{1,0:T(1,128)S(1)} %bitcast.3, ...), custom_call_target="tpu_custom_call" | custom-call | flops 1207959552 | bytes 6602752 | tf_op jit(solution)/shard_map/table_part/pallas_call | solution.py:39
  21.9 1.1 %table_part.4.refs_6_ = f32[1024,256]{1,0:T(8,128)S(1)} custom-call(bf16[16,128,256]{2,1,0:T(8,128)(2,1)S(1)} %get-tuple-element.17.av_ref.refs_0_, bf16[64,256]{1,0:T(8,128)(2,1)S(1)} %get-tuple-element.18.comp_t_ref.refs_1_, f32[16,128,256]{2,1,0:T(8,128)S(1)} %get-tuple-element.21.refs_2_, s32[1,4096]{1,0:T(1,128)S(1)} %bitcast.4, ...), custom_call_target="tpu_custom_call" | custom-call | flops 603979776 | bytes 7520256 | tf_op jit(solution)/shard_map/table_part/pallas_call | solution.py:39
  23.0 0.0 collective-permute-done.4.refs_5_
  23.0 1.1 %table_part.5 = (bf16[4,128,256]{2,1,0:T(8,128)(2,1)S(1)}, f32[4,128,256]{2,1,0:T(8,128)S(1)}) custom-call(bf16[16,128,256]{2,1,0:T(8,128)(2,1)S(1)} %get-tuple-element.17.av_ref.refs_0_, bf16[64,256]{1,0:T(8,128)(2,1)S(1)} %get-tuple-element.18.comp_t_ref.refs_1_, f32[16,128,256]{2,1,0:T(8,128)S(1)} %get-tuple-element.21.refs_2_, s32[1,4096]{1,0:T(1,128)S(1)} %bitcast.5, ...), custom_call_target="tpu_custom_call" | custom-call | flops 603979776 | bytes 7258112 | tf_op jit(solution)/shard_map/table_part/pallas_call | solution.py:39
  24.1 1.7 %collective-permute-start.6 = (bf16[4,128,256]{2,1,0:T(8,128)(2,1)S(1)}, bf16[4,128,256]{2,1,0:T(8,128)(2,1)S(1)}, u32[]{:S(2)}, u32[]{:S(2)}) collective-permute-start(bf16[4,128,256]{2,1,0:T(8,128)(2,1)S(1)} %get-tuple-element.28), channel_id=1, source_target_pairs={{0,4},{1,9},{2,6},{3,11},{4,0},{5,13},{6,2},{7,15},{8,12},{9,1},{1... | collective-permute-start | bytes 786440 | tf_op jit(solution)/shard_map/ppermute | solution.py:179
  25.8 4.7 %collective-permute-done.6 = bf16[4,128,256]{2,1,0:T(8,128)(2,1)S(1)} collective-permute-done((bf16[4,128,256]{2,1,0:T(8,128)(2,1)S(1)}, bf16[4,128,256]{2,1,0:T(8,128)(2,1)S(1)}, u32[]{:S(2)}, u32[]{:S(2)}) %collective-permute-start.6) | collective-permute-done | bytes 262176 | tf_op jit(solution)/shard_map/ppermute | solution.py:179
  30.6 0.1 convert_add_fusion
  30.7 1.8 %collective-permute-start.7 = (bf16[2,128,256]{2,1,0:T(8,128)(2,1)S(1)}, bf16[2,128,256]{2,1,0:T(8,128)(2,1)S(1)}, u32[]{:S(2)}, u32[]{:S(2)}) collective-permute-start(bf16[2,128,256]{2,1,0:T(8,128)(2,1)S(1)} %slice.25), channel_id=1, source_target_pairs={{0,8},{1,5},{2,10},{3,7},{4,12},{5,1},{6,14},{7,3},{8,0},{9,13},{1... | collective-permute-start | bytes 393224 | tf_op jit(solution)/shard_map/ppermute | solution.py:179
  32.5 3.2 %collective-permute-done.7 = bf16[2,128,256]{2,1,0:T(8,128)(2,1)S(1)} collective-permute-done((bf16[2,128,256]{2,1,0:T(8,128)(2,1)S(1)}, bf16[2,128,256]{2,1,0:T(8,128)(2,1)S(1)}, u32[]{:S(2)}, u32[]{:S(2)}) %collective-permute-start.7) | collective-permute-done | bytes 131104 | tf_op jit(solution)/shard_map/ppermute | solution.py:179
  35.7 2.8 %collective-permute-start.8 = (bf16[1,128,256]{2,1,0:T(8,128)(2,1)S(1)}, bf16[1,128,256]{2,1,0:T(8,128)(2,1)S(1)}, u32[]{:S(2)}, u32[]{:S(2)}) collective-permute-start(bf16[1,128,256]{2,1,0:T(8,128)(2,1)S(1)} %slice.26), channel_id=1, source_target_pairs={{0,16},{1,17},{2,18},{3,19},{4,20},{5,21},{6,22},{7,23},{8,24},{9,... | collective-permute-start | bytes 196616 | tf_op jit(solution)/shard_map/ppermute | solution.py:179
  38.6 2.4 %collective-permute-done.8.got_ref = bf16[1,128,256]{2,1,0:T(8,128)(2,1)S(1)} collective-permute-done((bf16[1,128,256]{2,1,0:T(8,128)(2,1)S(1)}, bf16[1,128,256]{2,1,0:T(8,128)(2,1)S(1)}, u32[]{:S(2)}, u32[]{:S(2)}) %collective-permute-start.8) | collective-permute-done | bytes 65568 | tf_op jit(solution)/shard_map/ppermute | solution.py:179
  41.0 0.7 %finish.1 = f32[128,256]{1,0:T(8,128)} custom-call(f32[1,128,256]{2,1,0:T(8,128)S(1)} %slice.20.keep_ref, bf16[1,128,256]{2,1,0:T(8,128)(2,1)S(1)} %collective-permute-done.8.got_ref), custom_call_target="tpu_custom_call" | custom-call | flops 32768 | bytes 327680 | tf_op jit(solution)/shard_map/finish/pallas_call | solution.py:39
  (10 shorter events, 0.1 us)
Async XLA Ops:
  0.0 0.8 %copy-start.2 = (bf16[256,64]{0,1:T(8,128)(2,1)S(1)}, bf16[256,64]{0,1:T(8,128)(2,1)}, u32[]{:S(2)}) copy-start(bf16[256,64]{0,1:T(8,128)(2,1)} %param.9) | copy-start | bytes 98308
  0.8 0.7 %copy-start.3 = (bf16[64,128]{1,0:T(8,128)(2,1)S(1)}, bf16[64,128]{1,0:T(8,128)(2,1)}, u32[]{:S(2)}) copy-start(bf16[64,128]{1,0:T(8,128)(2,1)} %proj_hbm.1) | copy-start | bytes 49156
  3.1 5.1 %copy-start.1 = (bf16[256,256]{1,0:T(8,128)(2,1)S(1)}, bf16[256,256]{1,0:T(8,128)(2,1)}, u32[]{:S(2)}) copy-start(bf16[256,256]{1,0:T(8,128)(2,1)} %mix_ref.1) | copy-start | bytes 393220
  3.1 5.1 %copy-start.4 = (s32[4096]{0:T(1024)S(1)}, s32[4096]{0:T(1024)}, u32[]{:S(2)}) copy-start(s32[4096]{0:T(1024)} %param.13) | copy-start | bytes 49156
  3.1 2.1 %collective-permute-start.1 = (f32[4,128,256]{2,1,0:T(8,128)S(1)}, f32[4,128,256]{2,1,0:T(8,128)S(1)}, u32[]{:S(2)}, u32[]{:S(2)}) collective-permute-start(f32[4,128,256]{2,1,0:T(8,128)S(1)} %get-tuple-element.26), channel_id=1, source_target_pairs={{0,1},{1,0},{2,3},{3,2},{4,5},{5,4},{6,7},{7,6},{8,9},{9,8},{10,11... | collective-permute-start | bytes 1572872 | tf_op jit(solution)/shard_map/ppermute | solution.py:174
  4.2 5.8 %collective-permute-start = (f32[4,128,256]{2,1,0:T(8,128)S(1)}, f32[4,128,256]{2,1,0:T(8,128)S(1)}, u32[]{:S(2)}, u32[]{:S(2)}) collective-permute-start(f32[4,128,256]{2,1,0:T(8,128)S(1)} %get-tuple-element.24), channel_id=1, source_target_pairs={{0,1},{1,0},{2,3},{3,2},{4,5},{5,4},{6,7},{7,6},{8,9},{9,8},{10,11... | collective-permute-start | bytes 1572872 | tf_op jit(solution)/shard_map/ppermute | solution.py:174
  5.3 14.8 %copy-start = (s32[4096,1]{0,1:T(1,128)S(1)}, s32[4096,1]{0,1:T(1,128)}, u32[]{:S(2)}) copy-start(s32[4096,1]{0,1:T(1,128)} %param.12) | copy-start | bytes 49156
  5.3 9.6 %collective-permute-start.2 = (bf16[4,128,256]{2,1,0:T(8,128)(2,1)S(1)}, bf16[4,128,256]{2,1,0:T(8,128)(2,1)S(1)}, u32[]{:S(2)}, u32[]{:S(2)}) collective-permute-start(bf16[4,128,256]{2,1,0:T(8,128)(2,1)S(1)} %add_convert_fusion), channel_id=1, source_target_pairs={{0,2},{1,3},{2,0},{3,1},{4,6},{5,7},{6,4},{7,5},{8,10},{9,11},{10,... | collective-permute-start | bytes 786440 | tf_op jit(solution)/shard_map/ppermute | solution.py:174
  15.0 5.1 %collective-permute-start.3 = (bf16[4,64,256]{2,1,0:T(8,128)(2,1)S(1)}, bf16[4,64,256]{2,1,0:T(8,128)(2,1)S(1)}, u32[]{:S(2)}, u32[]{:S(2)}) collective-permute-start(bf16[4,64,256]{2,1,0:T(8,128)(2,1)S(1)} %layer_back.1.refs_5_), channel_id=1, source_target_pairs={{0,2},{1,3},{2,0},{3,1},{4,6},{5,7},{6,4},{7,5},{8,10},{9,11},{10,... | collective-permute-start | bytes 393224 | tf_op jit(solution)/shard_map/ppermute | solution.py:174
  16.8 3.3 %collective-permute-start.5 = (bf16[4,64,256]{2,1,0:T(8,128)(2,1)S(1)}, bf16[4,64,256]{2,1,0:T(8,128)(2,1)S(1)}, u32[]{:S(2)}, u32[]{:S(2)}) collective-permute-start(bf16[4,64,256]{2,1,0:T(8,128)(2,1)S(1)} %layer_back.1.refs_5_), channel_id=1, source_target_pairs={{0,1},{1,0},{2,3},{3,2},{4,5},{5,4},{6,7},{7,6},{8,9},{9,8},{10,11... | collective-permute-start | bytes 393224 | tf_op jit(solution)/shard_map/ppermute | solution.py:174
  20.1 2.9 %collective-permute-start.4 = (bf16[4,64,256]{2,1,0:T(8,128)(2,1)S(1)}, bf16[4,64,256]{2,1,0:T(8,128)(2,1)S(1)}, u32[]{:S(2)}, u32[]{:S(2)}) collective-permute-start(bf16[4,64,256]{2,1,0:T(8,128)(2,1)S(1)} %collective-permute-done.3.refs_5_), channel_id=1, source_target_pairs={{0,1},{1,0},{2,3},{3,2},{4,5},{5,4},{6,7},{7,6},{8,9},{9,8},{10,11... | collective-permute-start | bytes 393224 | tf_op jit(solution)/shard_map/ppermute | solution.py:174
  24.1 6.4 %collective-permute-start.6 = (bf16[4,128,256]{2,1,0:T(8,128)(2,1)S(1)}, bf16[4,128,256]{2,1,0:T(8,128)(2,1)S(1)}, u32[]{:S(2)}, u32[]{:S(2)}) collective-permute-start(bf16[4,128,256]{2,1,0:T(8,128)(2,1)S(1)} %get-tuple-element.28), channel_id=1, source_target_pairs={{0,4},{1,9},{2,6},{3,11},{4,0},{5,13},{6,2},{7,15},{8,12},{9,1},{1... | collective-permute-start | bytes 786440 | tf_op jit(solution)/shard_map/ppermute | solution.py:179
  30.7 5.0 %collective-permute-start.7 = (bf16[2,128,256]{2,1,0:T(8,128)(2,1)S(1)}, bf16[2,128,256]{2,1,0:T(8,128)(2,1)S(1)}, u32[]{:S(2)}, u32[]{:S(2)}) collective-permute-start(bf16[2,128,256]{2,1,0:T(8,128)(2,1)S(1)} %slice.25), channel_id=1, source_target_pairs={{0,8},{1,5},{2,10},{3,7},{4,12},{5,1},{6,14},{7,3},{8,0},{9,13},{1... | collective-permute-start | bytes 393224 | tf_op jit(solution)/shard_map/ppermute | solution.py:179
  35.7 5.2 %collective-permute-start.8 = (bf16[1,128,256]{2,1,0:T(8,128)(2,1)S(1)}, bf16[1,128,256]{2,1,0:T(8,128)(2,1)S(1)}, u32[]{:S(2)}, u32[]{:S(2)}) collective-permute-start(bf16[1,128,256]{2,1,0:T(8,128)(2,1)S(1)} %slice.26), channel_id=1, source_target_pairs={{0,16},{1,17},{2,18},{3,19},{4,20},{5,21},{6,22},{7,23},{8,24},{9,... | collective-permute-start | bytes 196616 | tf_op jit(solution)/shard_map/ppermute | solution.py:179

commit v4 on v3

v4 whole, which is shorter than its diff:
```python
import functools

import jax
import jax.numpy as jnp
from jax import lax
from jax.experimental import pallas as pl
from jax.experimental.pallas import tpu as pltpu
from jax.sharding import PartitionSpec as P

SHARD = 256
F32, BF16 = jnp.float32, jnp.bfloat16
LIMIT = 20 * 2**20
LOAD_LIMIT = 52600 * 2**10
VMEM = pl.BlockSpec(memory_space=pltpu.VMEM)
HBM = pl.BlockSpec(memory_space=pltpu.HBM)


def dot_nt(a, b):
    return lax.dot_general(a, b, (((1,), (1,)), ((), ())), preferred_element_type=F32)


def dot_nn(a, b):
    return lax.dot_general(a, b, (((1,), (0,)), ((), ())), preferred_element_type=F32)


def bits_of(size):
    return [1 << t for t in range(size.bit_length() - 1)]


def halves(bits):
    numbers = [0]
    for bit in reversed(bits):
        numbers += [n ^ bit for n in numbers]
    return numbers


def call(kernel, name, args, shapes, flops, limit=LIMIT, specs=None, scratch=()):
    moved = sum(a.size * a.dtype.itemsize for a in (*args, *shapes))
    return pl.pallas_call(
        kernel,
        in_specs=specs or [VMEM] * len(args),
        out_specs=[VMEM] * len(shapes),
        out_shape=list(shapes),
        scratch_shapes=list(scratch),
        compiler_params=pltpu.CompilerParams(vmem_limit_bytes=limit),
        cost_estimate=pl.CostEstimate(flops=flops, bytes_accessed=moved, transcendentals=0),
        name=name,
    )(*args)


def width_sums(comp_t_ref, proj_ref, av_ref, up_ref, place, out_ref, at):
    rank = comp_t_ref.shape[0]
    reduced = dot_nt(comp_t_ref[...], av_ref[place]).astype(BF16)
    sums = dot_nn(reduced, av_ref[place])
    out_ref[at, :rank] = sums - jnp.mean(sums, axis=0, keepdims=True)
    grads = dot_nn(proj_ref[...], up_ref[place])
    out_ref[at, rank:] = grads - jnp.mean(grads, axis=0, keepdims=True)


def load_kernel(order, av_hbm, up_hbm, av_ref, up_ref, sems):
    me = lax.axis_index("dim")
    piece = av_ref.shape[0] // len(order)
    copies = []
    for n, j in enumerate(order):
        source = pl.ds((me ^ j) * piece, piece)
        to = pl.ds(n * piece, piece)
        copies.append(pltpu.make_async_copy(av_hbm.at[source], av_ref.at[to], sems.at[2 * n]))
        copies.append(pltpu.make_async_copy(up_hbm.at[source], up_ref.at[to], sems.at[2 * n + 1]))
    for copy in copies:
        copy.start()
    for copy in copies:
        copy.wait()


def sums_kernel(start, av_ref, up_ref, comp_t_ref, proj_ref, *out_refs):
    for out_ref in out_refs:
        for at in range(out_ref.shape[0]):
            width_sums(comp_t_ref, proj_ref, av_ref, up_ref, start + at, out_ref, at)
        start += out_ref.shape[0]


def prepare_kernel(start, av_ref, up_ref, comp_t_ref, proj_ref, mix_ref, slot_ref, out_ref, linear_ref, onehot_ref):
    sums_kernel(start, av_ref, up_ref, comp_t_ref, proj_ref, out_ref)
    samples, width, features = up_ref.shape
    for b in range(samples):
        up = up_ref[b]
        linear_ref[b] = up.astype(F32) + dot_nt(up, mix_ref[...])
    slots = lax.broadcasted_iota(jnp.int32, (SHARD, features), 0)
    for at in range(0, samples * features, features):
        hit = slots == slot_ref[:, at:at + features]
        onehot_ref[:, at:at + features] = jnp.where(hit, 1.0, 0.0).astype(BF16)


def layer_back_kernel(*refs):
    *terms, pair_ref = refs
    rank = pair_ref.shape[1]
    for b in range(pair_ref.shape[0]):
        total = sum(term[b].astype(F32) for term in terms)
        centred, grads = total[:rank], total[rank:]
        inverse = 1.0 / jnp.sqrt(jnp.mean(centred * centred, axis=0, keepdims=True) + 1e-05)
        normed = centred * inverse
        moment = jnp.mean(grads * normed, axis=0, keepdims=True)
        pair_ref[b] = (inverse * (grads - normed * moment)).astype(BF16)


def add_lookups(grad, owner_ref, at, numbers, masked, columns):
    width, features = grad.shape
    owner = owner_ref[:, pl.ds(pl.multiple_of(at * features, features), features)]
    for o, number in enumerate(numbers):
        mask = jnp.where(owner == number, 1.0, 0.0).astype(BF16)
        masked[o * width:(o + 1) * width, columns] = grad * mask


def feature_grad(av, back, comp_t, linear):
    both = dot_nt(av, jnp.concatenate([comp_t, back])).astype(BF16)
    return (linear + dot_nn(both, jnp.concatenate([back, comp_t]))).astype(BF16)


def table_kernel(jobs, owners, last, pairs, has_total, *refs):
    av_ref, comp_t_ref, linear_ref, owner_ref, onehot_ref = refs[:5]
    pair_refs, refs = refs[5:5 + pairs], refs[5 + pairs:]
    if has_total:
        total_ref, refs = refs[0], refs[1:]
    outs, (masked, onehot) = refs[:-2], refs[-2:]
    _, width, features = av_ref.shape
    me, here = lax.axis_index("dim"), lax.axis_index("dp")
    comp_t = comp_t_ref[...]
    numbers = [here ^ m for m in owners]
    for n, (place, j, offset, piece, pair, at) in enumerate(jobs):
        grad = feature_grad(av_ref[place], pair_refs[pair][at], comp_t, linear_ref[place])
        at = (me ^ j) * piece + offset
        columns = slice(n * features, (n + 1) * features)
        add_lookups(grad, owner_ref, at, numbers, masked, columns)
        lookups = pl.ds(pl.multiple_of(at * features, features), features)
        onehot[:, columns] = onehot_ref[:, lookups]
    added = dot_nt(masked[...], onehot[...])
    if has_total:
        added = added + total_ref[...]
    if not last:
        outs[0][...] = added
        return
    half = width // len(last)
    for c, chain in enumerate(last):
        for n, o in enumerate(halves(chain[1:])):
            at = (o ^ chain[0]) * width + c * half
            outs[2 * c][n] = added[at:at + half].astype(BF16)
            at = o * width + c * half
            outs[2 * c + 1][n] = added[at:at + half]


def table_part(jobs, owners, last, av, comp_t, linear, owner, onehot, pairs, total):
    _, width, features = av.shape
    rank = comp_t.shape[0]
    shape = jax.ShapeDtypeStruct
    lookups = len(jobs) * features
    if last:
        part = (len(owners) // 2, width // len(last), SHARD)
        shapes = [shape(part, t) for _ in last for t in (BF16, F32)]
    else:
        shapes = [shape((len(owners) * width, SHARD), F32)]
    args = [av, comp_t, linear, owner, onehot, *pairs] + ([] if total is None else [total])
    return call(
        functools.partial(table_kernel, jobs, owners, last, len(pairs), total is not None),
        "table_part",
        args,
        shapes,
        2 * lookups * width * (4 * rank + len(owners) * SHARD),
        scratch=[pltpu.VMEM((len(owners) * width, lookups), BF16), pltpu.VMEM((SHARD, lookups), BF16)],
    )


def fold_kernel(*refs):
    *terms, send_ref, keep_ref = refs
    half = keep_ref.shape[0]
    start = 0
    for keep, got in zip(terms[::2], terms[1::2]):
        stop = start + keep.shape[1]
        send_ref[:, start:stop] = (keep[half:] + got[half:].astype(F32)).astype(BF16)
        keep_ref[:, start:stop] = keep[:half] + got[:half].astype(F32)
        start = stop


def fold(terms):
    count, _, slots = terms[0].shape
    part = (count // 2, sum(keep.shape[1] for keep in terms[::2]), slots)
    shapes = [jax.ShapeDtypeStruct(part, t) for t in (BF16, F32)]
    return call(fold_kernel, "fold", terms, shapes, terms[0].size)


def finish_kernel(*refs):
    *terms, out_ref = refs
    start = 0
    for keep, got in zip(terms[::2], terms[1::2]):
        stop = start + keep.shape[1]
        out_ref[start:stop] = keep[0] + got[0].astype(F32)
        start = stop


def swap(x, bit, axis="dim"):
    return lax.ppermute(x, axis, [(i, i ^ bit) for i in range(lax.axis_size(axis))])


def shards(attribute_vectors, upstream, compress, interact_proj, linear_mix, row_owner, row_slot):
    owners, peers = lax.axis_size("dp"), lax.axis_size("dim")
    samples, width, features = attribute_vectors.shape
    rank = compress.shape[1]
    piece = samples // peers
    quarter = samples // 4
    shape = jax.ShapeDtypeStruct
    part = shape((quarter, 2 * rank, features), F32)
    sample_flops = 6 * width * features * rank

    bits = bits_of(peers)
    held = halves(bits)
    count = peers // 4
    order = held[3 * count:] + held[2 * count:3 * count] + held[count:2 * count] + held[:count]
    place_of = {j: n for n, j in enumerate(order)}

    av, up = call(
        functools.partial(load_kernel, order),
        "load",
        (attribute_vectors, upstream),
        [shape(upstream.shape, BF16)] * 2,
        0,
        limit=LOAD_LIMIT,
        specs=[HBM] * 2,
        scratch=[pltpu.SemaphoreType.DMA((2 * peers,))],
    )
    comp_t = compress.T
    args = (av, up, comp_t, interact_proj)
    (send_high,) = call(
        functools.partial(sums_kernel, 0), "sums", args, [part], quarter * sample_flops
    )
    got_high = swap(send_high, bits[0])
    send_low, keep_high = call(
        functools.partial(sums_kernel, quarter), "sums", args, [part] * 2, 2 * quarter * sample_flops
    )
    got_low = swap(send_low, bits[0])
    got = swap((keep_high + got_high).astype(BF16), bits[1])
    keep_low, linear, onehot = call(
        functools.partial(prepare_kernel, 3 * quarter),
        "prepare",
        (*args, linear_mix, row_slot.reshape(1, -1)),
        [part, shape(up.shape, F32), shape((SHARD, samples * features), BF16)],
        2 * samples * width * features * features,
    )
    terms = [keep_low, got_low, got]
    for bit in bits[2:]:
        keep = sum(term.astype(F32) for term in terms)
        half = keep.shape[0] // 2
        terms = [keep[:half], swap(keep[half:].astype(BF16), bit)]
    (pair,) = call(
        layer_back_kernel, "layer_back", terms, [shape((piece, rank, features), BF16)], 16 * terms[0].size
    )
    owner = row_owner.reshape(1, -1)
    numbers = list(range(owners))

    def jobs_of(stage):
        return [
            (place_of[j] * piece + s, j, s, piece, at, s) for at, j in enumerate(stage) for s in range(piece)
        ]

    pairs = {0: pair}
    total = None
    for bit in reversed(bits[1:]):
        pairs.update({j ^ bit: swap(got, bit) for j, got in pairs.items()})
    stages = []
    for n, j in enumerate(list(pairs)):
        if n == 1:
            stage = list(stages[0])
            (total,) = table_part(
                jobs_of(stage), numbers, None, av, comp_t, linear, owner, onehot, [pairs[i] for i in stage], total
            )
            pairs[j], total = lax.optimization_barrier((pairs[j], total))
        pairs[j ^ bits[0]] = swap(pairs[j], bits[0])
        stages += [[j, j ^ bits[0]]] if n == 0 else [[j], [j ^ bits[0]]]
    for stage in stages[1:-1]:
        (total,) = table_part(
            jobs_of(stage), numbers, None, av, comp_t, linear, owner, onehot, [pairs[j] for j in stage], total
        )
    stage = stages[-1]
    low = bits_of(owners)[:(owners.bit_length() - 1) // 2]
    high = bits_of(owners)[len(low):]
    chains = [low + high, high[:1] + low + high[1:]]
    outs = table_part(
        jobs_of(stage), numbers, chains, av, comp_t, linear, owner, onehot, [pairs[j] for j in stage], total
    )
    sums = []
    for chain, send, keep in zip(chains, outs[::2], outs[1::2]):
        got = swap(send, chain[0], "dp")
        for bit in chain[1:len(low) + 1]:
            send, keep = fold([keep, got])
            got = swap(send, bit, "dp")
        sums += [keep, got]
    for bit in high[1:]:
        send, keep = fold(sums)
        sums = [keep, swap(send, bit, "dp")]
    (out,) = call(finish_kernel, "finish", sums, [shape((width, SHARD), F32)], width * SHARD)
    return out


def solution(mesh):
    placed = (
        P("dp", "dim", None),
        P("dp", "dim", None),
        P(),
        P(None, "dim"),
        P(),
        P("dp", None),
        P("dp"),
    )
    return jax.shard_map(
        shards, mesh=mesh, in_specs=placed, out_specs=P("dim", "dp"), check_vma=False
    )
```

time: 41.9 us -> 41.2 us (0.983)
  starting transfers between devices: 11.7 us -> 14.9 us
  waiting for transfers between devices: 19.3 us -> 16.6 us
  local copies, waits for them, and re-layouts: 1.53 us -> 0.03 us
  Pallas kernels: 8.78 us -> 9.25 us
    ppermute x9 -> x11, starting transfers between devices: 11.7 us -> 14.9 us  [swap(): lax.ppermute(x, axis, [(i, i ^ bit) for i in range(lax.axis_size(axis))])]
    ppermute x9 -> x11, waiting for transfers between devices: 19.3 us -> 16.6 us  [swap(): lax.ppermute(x, axis, [(i, i ^ bit) for i in range(lax.axis_size(axis))])]
    unnamed x10, local copies, waits for them, and re-layouts: 1.49 us -> 0.03 us
    pallas_call x8 -> x12, Pallas kernels: 8.78 us -> 9.25 us  [call(): pl.pallas_call(kernel, in_specs=specs or [VMEM] * len(args), out_specs=[V...]
  transfers between devices with their start and end apart: 9 -> 11, of which waited for: 6 -> 8; matrix products, arithmetic and copies ran while one was open for 0% -> 0% of each run, Pallas kernels for 13% -> 13%
where the time goes in v4:
time: 41.2 us; the launch traced here: 41 us
  waiting for transfers between devices  16.6 us (40%)
  starting transfers between devices  14.9 us (36%)
  Pallas kernels  9.25 us (22%)
    ppermute x11, waiting for transfers between devices, swap(): lax.ppermute(x, axis, [(i, i ^ bit) for i in range(lax.axis_size(axis))])  16.6 us
    ppermute x11, starting transfers between devices, swap(): lax.ppermute(x, axis, [(i, i ^ bit) for i in range(lax.axis_size(axis))])  14.9 us
    pallas_call x12, Pallas kernels, call(): pl.pallas_call(kernel, in_specs=specs or [VMEM] * len(args), out_specs=[V...  9.25 us
  transfers between devices with their start and end apart: 11, of which 8 were waited for; matrix products, arithmetic and copies ran while one was open for 0% of the time, Pallas kernels for 13%

profile of v4, /device:TPU:0, one launch (start us, length us, event | category | flops | bytes accessed | tf_op | source)
XLA Modules:
  0.0 41.0 jit_solution(10979413180681799533)
XLA Ops:
  0.0 1.6 %load.1 = (bf16[16,128,256]{2,1,0:T(8,128)(2,1)S(1)}, bf16[16,128,256]{2,1,0:T(8,128)(2,1)S(1)}) custom-call(bf16[16,128,256]{2,1,0:T(8,128)(2,1)} %av_hbm.1, bf16[16,128,256]{2,1,0:T(8,128)(2,1)} %up_hbm.1), custom_call_target="tpu_custom_call" | custom-call | bytes 4194304 | tf_op jit(solution)/shard_map/load/pallas_call | solution.py:39
  1.6 0.4 %sums.3 = f32[4,128,256]{2,1,0:T(8,128)S(1)} custom-call(bf16[16,128,256]{2,1,0:T(8,128)(2,1)S(1)} %get-tuple-element.24.av_ref.refs_0_, bf16[16,128,256]{2,1,0:T(8,128)(2,1)S(1)} %get-tuple-element.25.up_ref, bf16[64,256]{1,0:T(8,128)(2,1)S(1)} %bitcast.3, bf16[64,128]{1,0:T(8,128)(2,1)S(1)} %copy-done.1), custom_call_target="tpu_custom_call" | custom-call | flops 50331648 | bytes 2670592 | tf_op jit(solution)/shard_map/sums/pallas_call | solution.py:39
  2.0 0.0 copy-start.3
  2.1 0.0 copy-start.4
  2.1 0.5 %collective-permute-start.1 = (f32[4,128,256]{2,1,0:T(8,128)S(1)}, f32[4,128,256]{2,1,0:T(8,128)S(1)}, u32[]{:S(2)}, u32[]{:S(2)}) collective-permute-start(f32[4,128,256]{2,1,0:T(8,128)S(1)} %sums.3), channel_id=1, source_target_pairs={{0,1},{1,0},{2,3},{3,2},{4,5},{5,4},{6,7},{7,6},{8,9},{9,8},{10,11... | collective-permute-start | bytes 1572872 | tf_op jit(solution)/shard_map/ppermute | solution.py:200
  2.6 0.6 %sums.2 = (f32[4,128,256]{2,1,0:T(8,128)S(1)}, f32[4,128,256]{2,1,0:T(8,128)S(1)}) custom-call(bf16[16,128,256]{2,1,0:T(8,128)(2,1)S(1)} %get-tuple-element.24.av_ref.refs_0_, bf16[16,128,256]{2,1,0:T(8,128)(2,1)S(1)} %get-tuple-element.25.up_ref, bf16[64,256]{1,0:T(8,128)(2,1)S(1)} %bitcast.4, bf16[64,128]{1,0:T(8,128)(2,1)S(1)} %copy-done.1), custom_call_target="tpu_custom_call" | custom-call | flops 100663296 | bytes 3194880 | tf_op jit(solution)/shard_map/sums/pallas_call | solution.py:39
  3.2 0.1 collective-permute-start
  3.3 0.8 %collective-permute-done.1 = f32[4,128,256]{2,1,0:T(8,128)S(1)} collective-permute-done((f32[4,128,256]{2,1,0:T(8,128)S(1)}, f32[4,128,256]{2,1,0:T(8,128)S(1)}, u32[]{:S(2)}, u32[]{:S(2)}) %collective-permute-start.1) | collective-permute-done | bytes 524320 | tf_op jit(solution)/shard_map/ppermute | solution.py:200
  4.1 0.1 add_convert_fusion
  4.2 0.0 copy-start.2
  4.2 3.0 %collective-permute-start.2 = (bf16[4,128,256]{2,1,0:T(8,128)(2,1)S(1)}, bf16[4,128,256]{2,1,0:T(8,128)(2,1)S(1)}, u32[]{:S(2)}, u32[]{:S(2)}) collective-permute-start(bf16[4,128,256]{2,1,0:T(8,128)(2,1)S(1)} %add_convert_fusion), channel_id=1, source_target_pairs={{0,2},{1,3},{2,0},{3,1},{4,6},{5,7},{6,4},{7,5},{8,10},{9,11},{10,... | collective-permute-start | bytes 786440 | tf_op jit(solution)/shard_map/ppermute | solution.py:200
  7.2 1.8 %prepare.1 = (f32[4,128,256]{2,1,0:T(8,128)S(1)}, f32[16,128,256]{2,1,0:T(8,128)S(1)}, bf16[256,4096]{1,0:T(8,128)(2,1)S(1)}) custom-call(bf16[16,128,256]{2,1,0:T(8,128)(2,1)S(1)} %get-tuple-element.24.av_ref.refs_0_, bf16[16,128,256]{2,1,0:T(8,128)(2,1)S(1)} %get-tuple-element.25.up_ref, bf16[64,256]{1,0:T(8,128)(2,1)S(1)} %bitcast.5, ...), custom_call_target="tpu_custom_call" | custom-call | flops 268435456 | bytes 7012352 | tf_op jit(solution)/shard_map/prepare/pallas_call | solution.py:39
  9.0 4.8 %collective-permute-done.2.refs_2_ = bf16[4,128,256]{2,1,0:T(8,128)(2,1)S(1)} collective-permute-done((bf16[4,128,256]{2,1,0:T(8,128)(2,1)S(1)}, bf16[4,128,256]{2,1,0:T(8,128)(2,1)S(1)}, u32[]{:S(2)}, u32[]{:S(2)}) %collective-permute-start.2) | collective-permute-done | bytes 262176 | tf_op jit(solution)/shard_map/ppermute | solution.py:200
  13.8 0.2 layer_back.1.refs_5_
  13.9 0.1 collective-permute-start.4
  14.0 1.8 %collective-permute-start.3 = (bf16[4,64,256]{2,1,0:T(8,128)(2,1)S(1)}, bf16[4,64,256]{2,1,0:T(8,128)(2,1)S(1)}, u32[]{:S(2)}, u32[]{:S(2)}) collective-permute-start(bf16[4,64,256]{2,1,0:T(8,128)(2,1)S(1)} %layer_back.1.refs_5_), channel_id=1, source_target_pairs={{0,2},{1,3},{2,0},{3,1},{4,6},{5,7},{6,4},{7,5},{8,10},{9,11},{10,... | collective-permute-start | bytes 393224 | tf_op jit(solution)/shard_map/ppermute | solution.py:200
  15.8 0.0 collective-permute-done.4.refs_6_
  15.8 1.8 %table_part.3.refs_6_ = f32[1024,256]{1,0:T(8,128)S(1)} custom-call(bf16[16,128,256]{2,1,0:T(8,128)(2,1)S(1)} %get-tuple-element.24.av_ref.refs_0_, bf16[64,256]{1,0:T(8,128)(2,1)S(1)} %bitcast.6, f32[16,128,256]{2,1,0:T(8,128)S(1)} %get-tuple-element.26.refs_2_, s32[1,4096]{1,0:T(1,128)S(1)} %bitcast.9, bf16[256,4096]{1,0:T(8,128)(2,1)S(1)} %get-tuple-element.27.refs_4_, ...), custom_call_target="tpu_custom_call" | custom-call | flops 1207959552 | bytes 6602752 | tf_op jit(solution)/shard_map/table_part/pallas_call | solution.py:39
  17.6 2.3 %collective-permute-done.3.refs_5_ = bf16[4,64,256]{2,1,0:T(8,128)(2,1)S(1)} collective-permute-done((bf16[4,64,256]{2,1,0:T(8,128)(2,1)S(1)}, bf16[4,64,256]{2,1,0:T(8,128)(2,1)S(1)}, u32[]{:S(2)}, u32[]{:S(2)}) %collective-permute-start.3) | collective-permute-done | bytes 131104 | tf_op jit(solution)/shard_map/ppermute | solution.py:200
  19.9 1.1 %table_part.4.refs_6_ = f32[1024,256]{1,0:T(8,128)S(1)} custom-call(bf16[16,128,256]{2,1,0:T(8,128)(2,1)S(1)} %get-tuple-element.24.av_ref.refs_0_, bf16[64,256]{1,0:T(8,128)(2,1)S(1)} %bitcast.7, f32[16,128,256]{2,1,0:T(8,128)S(1)} %get-tuple-element.26.refs_2_, s32[1,4096]{1,0:T(1,128)S(1)} %bitcast.10, bf16[256,4096]{1,0:T(8,128)(2,1)S(1)} %get-tuple-element.27.refs_4_, ...), custom_call_target="tpu_custom_call" | custom-call | flops 603979776 | bytes 7520256 | tf_op jit(solution)/shard_map/table_part/pallas_call | solution.py:39
  21.1 0.2 collective-permute-done.5.refs_5_
  21.3 1.1 %table_part.5 = (bf16[4,64,256]{2,1,0:T(8,128)(2,1)S(1)}, f32[4,64,256]{2,1,0:T(8,128)S(1)}, bf16[4,64,256]{2,1,0:T(8,128)(2,1)S(1)}, f32[4,64,256]{2,1,0:T(8,128)S(1)}) custom-call(bf16[16,128,256]{2,1,0:T(8,128)(2,1)S(1)} %get-tuple-element.24.av_ref.refs_0_, bf16[64,256]{1,0:T(8,128)(2,1)S(1)} %bitcast.8, f32[16,128,256]{2,1,0:T(8,128)S(1)} %get-tuple-element.26.refs_2_, ...), custom_call_target="tpu_custom_call" | custom-call | flops 603979776 | bytes 7258112 | tf_op jit(solution)/shard_map/table_part/pallas_call | solution.py:39
  22.4 1.8 %collective-permute-start.6 = (bf16[4,64,256]{2,1,0:T(8,128)(2,1)S(1)}, bf16[4,64,256]{2,1,0:T(8,128)(2,1)S(1)}, u32[]{:S(2)}, u32[]{:S(2)}) collective-permute-start(bf16[4,64,256]{2,1,0:T(8,128)(2,1)S(1)} %get-tuple-element.34), channel_id=1, source_target_pairs={{0,4},{4,0},{8,12},{12,8},{16,20},{20,16},{24,28},{28,24},{1,5},{5... | collective-permute-start | bytes 393224 | tf_op jit(solution)/shard_map/ppermute | solution.py:200
  24.2 1.6 %collective-permute-start.8 = (bf16[4,64,256]{2,1,0:T(8,128)(2,1)S(1)}, bf16[4,64,256]{2,1,0:T(8,128)(2,1)S(1)}, u32[]{:S(2)}, u32[]{:S(2)}) collective-permute-start(bf16[4,64,256]{2,1,0:T(8,128)(2,1)S(1)} %get-tuple-element.38), channel_id=1, source_target_pairs={{0,8},{4,12},{8,0},{12,4},{16,24},{20,28},{24,16},{28,20},{1,9},{5... | collective-permute-start | bytes 393224 | tf_op jit(solution)/shard_map/ppermute | solution.py:200
  25.8 2.4 %collective-permute-done.6.refs_1_ = bf16[4,64,256]{2,1,0:T(8,128)(2,1)S(1)} collective-permute-done((bf16[4,64,256]{2,1,0:T(8,128)(2,1)S(1)}, bf16[4,64,256]{2,1,0:T(8,128)(2,1)S(1)}, u32[]{:S(2)}, u32[]{:S(2)}) %collective-permute-start.6) | collective-permute-done | bytes 131104 | tf_op jit(solution)/shard_map/ppermute | solution.py:200
  28.2 1.9 %collective-permute-start.7 = (bf16[2,64,256]{2,1,0:T(8,128)(2,1)S(1)}, bf16[2,64,256]{2,1,0:T(8,128)(2,1)S(1)}, u32[]{:S(2)}, u32[]{:S(2)}) collective-permute-start(bf16[2,64,256]{2,1,0:T(8,128)(2,1)S(1)} %get-tuple-element.36), channel_id=1, source_target_pairs={{0,8},{4,12},{8,0},{12,4},{16,24},{20,28},{24,16},{28,20},{1,9},{5... | collective-permute-start | bytes 196616 | tf_op jit(solution)/shard_map/ppermute | solution.py:200
  30.1 1.6 %collective-permute-start.9 = (bf16[2,64,256]{2,1,0:T(8,128)(2,1)S(1)}, bf16[2,64,256]{2,1,0:T(8,128)(2,1)S(1)}, u32[]{:S(2)}, u32[]{:S(2)}) collective-permute-start(bf16[2,64,256]{2,1,0:T(8,128)(2,1)S(1)} %get-tuple-element.40), channel_id=1, source_target_pairs={{0,4},{4,0},{8,12},{12,8},{16,20},{20,16},{24,28},{28,24},{1,5},{5... | collective-permute-start | bytes 196616 | tf_op jit(solution)/shard_map/ppermute | solution.py:200
  31.6 0.9 %collective-permute-done.7.refs_1_ = bf16[2,64,256]{2,1,0:T(8,128)(2,1)S(1)} collective-permute-done((bf16[2,64,256]{2,1,0:T(8,128)(2,1)S(1)}, bf16[2,64,256]{2,1,0:T(8,128)(2,1)S(1)}, u32[]{:S(2)}, u32[]{:S(2)}) %collective-permute-start.7) | collective-permute-done | bytes 65568 | tf_op jit(solution)/shard_map/ppermute | solution.py:200
  32.5 1.9 %collective-permute-done.9.refs_3_ = bf16[2,64,256]{2,1,0:T(8,128)(2,1)S(1)} collective-permute-done((bf16[2,64,256]{2,1,0:T(8,128)(2,1)S(1)}, bf16[2,64,256]{2,1,0:T(8,128)(2,1)S(1)}, u32[]{:S(2)}, u32[]{:S(2)}) %collective-permute-start.9) | collective-permute-done | bytes 65568 | tf_op jit(solution)/shard_map/ppermute | solution.py:200
  34.4 2.6 %collective-permute-start.10 = (bf16[1,128,256]{2,1,0:T(8,128)(2,1)S(1)}, bf16[1,128,256]{2,1,0:T(8,128)(2,1)S(1)}, u32[]{:S(2)}, u32[]{:S(2)}) collective-permute-start(bf16[1,128,256]{2,1,0:T(8,128)(2,1)S(1)} %get-tuple-element.42), channel_id=1, source_target_pairs={{0,16},{4,20},{8,24},{12,28},{16,0},{20,4},{24,8},{28,12},{1,17},{... | collective-permute-start | bytes 196616 | tf_op jit(solution)/shard_map/ppermute | solution.py:200
  37.1 3.3 %collective-permute-done.10.refs_1_ = bf16[1,128,256]{2,1,0:T(8,128)(2,1)S(1)} collective-permute-done((bf16[1,128,256]{2,1,0:T(8,128)(2,1)S(1)}, bf16[1,128,256]{2,1,0:T(8,128)(2,1)S(1)}, u32[]{:S(2)}, u32[]{:S(2)}) %collective-permute-start.10) | collective-permute-done | bytes 65568 | tf_op jit(solution)/shard_map/ppermute | solution.py:200
  40.4 0.7 %finish.1 = f32[128,256]{1,0:T(8,128)} custom-call(f32[1,128,256]{2,1,0:T(8,128)S(1)} %get-tuple-element.41.refs_0_, bf16[1,128,256]{2,1,0:T(8,128)(2,1)S(1)} %collective-permute-done.10.refs_1_), custom_call_target="tpu_custom_call" | custom-call | flops 32768 | bytes 327680 | tf_op jit(solution)/shard_map/finish/pallas_call | solution.py:39
  (13 shorter events, 0.1 us)
Async XLA Ops:
  0.0 1.6 %copy-start.1 = (bf16[64,128]{1,0:T(8,128)(2,1)S(1)}, bf16[64,128]{1,0:T(8,128)(2,1)}, u32[]{:S(2)}) copy-start(bf16[64,128]{1,0:T(8,128)(2,1)} %proj_ref.5) | copy-start | bytes 49156
  0.0 1.6 %copy-start = (bf16[256,64]{0,1:T(8,128)(2,1)S(1)}, bf16[256,64]{0,1:T(8,128)(2,1)}, u32[]{:S(2)}) copy-start(bf16[256,64]{0,1:T(8,128)(2,1)} %param.9) | copy-start | bytes 98308
  2.0 5.1 %copy-start.3 = (bf16[256,256]{1,0:T(8,128)(2,1)S(1)}, bf16[256,256]{1,0:T(8,128)(2,1)}, u32[]{:S(2)}) copy-start(bf16[256,256]{1,0:T(8,128)(2,1)} %mix_ref.1) | copy-start | bytes 393220
  2.1 5.1 %copy-start.4 = (s32[4096]{0:T(1024)S(1)}, s32[4096]{0:T(1024)}, u32[]{:S(2)}) copy-start(s32[4096]{0:T(1024)} %param.13) | copy-start | bytes 49156
  2.1 2.1 %collective-permute-start.1 = (f32[4,128,256]{2,1,0:T(8,128)S(1)}, f32[4,128,256]{2,1,0:T(8,128)S(1)}, u32[]{:S(2)}, u32[]{:S(2)}) collective-permute-start(f32[4,128,256]{2,1,0:T(8,128)S(1)} %sums.3), channel_id=1, source_target_pairs={{0,1},{1,0},{2,3},{3,2},{4,5},{5,4},{6,7},{7,6},{8,9},{9,8},{10,11... | collective-permute-start | bytes 1572872 | tf_op jit(solution)/shard_map/ppermute | solution.py:200
  3.2 5.8 %collective-permute-start = (f32[4,128,256]{2,1,0:T(8,128)S(1)}, f32[4,128,256]{2,1,0:T(8,128)S(1)}, u32[]{:S(2)}, u32[]{:S(2)}) collective-permute-start(f32[4,128,256]{2,1,0:T(8,128)S(1)} %get-tuple-element.29), channel_id=1, source_target_pairs={{0,1},{1,0},{2,3},{3,2},{4,5},{5,4},{6,7},{7,6},{8,9},{9,8},{10,11... | collective-permute-start | bytes 1572872 | tf_op jit(solution)/shard_map/ppermute | solution.py:200
  4.2 11.6 %copy-start.2 = (s32[4096,1]{0,1:T(1,128)S(1)}, s32[4096,1]{0,1:T(1,128)}, u32[]{:S(2)}) copy-start(s32[4096,1]{0,1:T(1,128)} %param.12) | copy-start | bytes 49156
  4.2 9.6 %collective-permute-start.2 = (bf16[4,128,256]{2,1,0:T(8,128)(2,1)S(1)}, bf16[4,128,256]{2,1,0:T(8,128)(2,1)S(1)}, u32[]{:S(2)}, u32[]{:S(2)}) collective-permute-start(bf16[4,128,256]{2,1,0:T(8,128)(2,1)S(1)} %add_convert_fusion), channel_id=1, source_target_pairs={{0,2},{1,3},{2,0},{3,1},{4,6},{5,7},{6,4},{7,5},{8,10},{9,11},{10,... | collective-permute-start | bytes 786440 | tf_op jit(solution)/shard_map/ppermute | solution.py:200
  13.9 1.9 %collective-permute-start.4 = (bf16[4,64,256]{2,1,0:T(8,128)(2,1)S(1)}, bf16[4,64,256]{2,1,0:T(8,128)(2,1)S(1)}, u32[]{:S(2)}, u32[]{:S(2)}) collective-permute-start(bf16[4,64,256]{2,1,0:T(8,128)(2,1)S(1)} %layer_back.1.refs_5_), channel_id=1, source_target_pairs={{0,1},{1,0},{2,3},{3,2},{4,5},{5,4},{6,7},{7,6},{8,9},{9,8},{10,11... | collective-permute-start | bytes 393224 | tf_op jit(solution)/shard_map/ppermute | solution.py:200
  14.0 5.9 %collective-permute-start.3 = (bf16[4,64,256]{2,1,0:T(8,128)(2,1)S(1)}, bf16[4,64,256]{2,1,0:T(8,128)(2,1)S(1)}, u32[]{:S(2)}, u32[]{:S(2)}) collective-permute-start(bf16[4,64,256]{2,1,0:T(8,128)(2,1)S(1)} %layer_back.1.refs_5_), channel_id=1, source_target_pairs={{0,2},{1,3},{2,0},{3,1},{4,6},{5,7},{6,4},{7,5},{8,10},{9,11},{10,... | collective-permute-start | bytes 393224 | tf_op jit(solution)/shard_map/ppermute | solution.py:200
  19.9 1.3 %collective-permute-start.5 = (bf16[4,64,256]{2,1,0:T(8,128)(2,1)S(1)}, bf16[4,64,256]{2,1,0:T(8,128)(2,1)S(1)}, u32[]{:S(2)}, u32[]{:S(2)}) collective-permute-start(bf16[4,64,256]{2,1,0:T(8,128)(2,1)S(1)} %collective-permute-done.3.refs_5_), channel_id=1, source_target_pairs={{0,1},{1,0},{2,3},{3,2},{4,5},{5,4},{6,7},{7,6},{8,9},{9,8},{10,11... | collective-permute-start | bytes 393224 | tf_op jit(solution)/shard_map/ppermute | solution.py:200
  22.4 5.8 %collective-permute-start.6 = (bf16[4,64,256]{2,1,0:T(8,128)(2,1)S(1)}, bf16[4,64,256]{2,1,0:T(8,128)(2,1)S(1)}, u32[]{:S(2)}, u32[]{:S(2)}) collective-permute-start(bf16[4,64,256]{2,1,0:T(8,128)(2,1)S(1)} %get-tuple-element.34), channel_id=1, source_target_pairs={{0,4},{4,0},{8,12},{12,8},{16,20},{20,16},{24,28},{28,24},{1,5},{5... | collective-permute-start | bytes 393224 | tf_op jit(solution)/shard_map/ppermute | solution.py:200
  24.2 5.9 %collective-permute-start.8 = (bf16[4,64,256]{2,1,0:T(8,128)(2,1)S(1)}, bf16[4,64,256]{2,1,0:T(8,128)(2,1)S(1)}, u32[]{:S(2)}, u32[]{:S(2)}) collective-permute-start(bf16[4,64,256]{2,1,0:T(8,128)(2,1)S(1)} %get-tuple-element.38), channel_id=1, source_target_pairs={{0,8},{4,12},{8,0},{12,4},{16,24},{20,28},{24,16},{28,20},{1,9},{5... | collective-permute-start | bytes 393224 | tf_op jit(solution)/shard_map/ppermute | solution.py:200
  28.2 4.3 %collective-permute-start.7 = (bf16[2,64,256]{2,1,0:T(8,128)(2,1)S(1)}, bf16[2,64,256]{2,1,0:T(8,128)(2,1)S(1)}, u32[]{:S(2)}, u32[]{:S(2)}) collective-permute-start(bf16[2,64,256]{2,1,0:T(8,128)(2,1)S(1)} %get-tuple-element.36), channel_id=1, source_target_pairs={{0,8},{4,12},{8,0},{12,4},{16,24},{20,28},{24,16},{28,20},{1,9},{5... | collective-permute-start | bytes 196616 | tf_op jit(solution)/shard_map/ppermute | solution.py:200
  30.1 4.3 %collective-permute-start.9 = (bf16[2,64,256]{2,1,0:T(8,128)(2,1)S(1)}, bf16[2,64,256]{2,1,0:T(8,128)(2,1)S(1)}, u32[]{:S(2)}, u32[]{:S(2)}) collective-permute-start(bf16[2,64,256]{2,1,0:T(8,128)(2,1)S(1)} %get-tuple-element.40), channel_id=1, source_target_pairs={{0,4},{4,0},{8,12},{12,8},{16,20},{20,16},{24,28},{28,24},{1,5},{5... | collective-permute-start | bytes 196616 | tf_op jit(solution)/shard_map/ppermute | solution.py:200
  34.4 5.9 %collective-permute-start.10 = (bf16[1,128,256]{2,1,0:T(8,128)(2,1)S(1)}, bf16[1,128,256]{2,1,0:T(8,128)(2,1)S(1)}, u32[]{:S(2)}, u32[]{:S(2)}) collective-permute-start(bf16[1,128,256]{2,1,0:T(8,128)(2,1)S(1)} %get-tuple-element.42), channel_id=1, source_target_pairs={{0,16},{4,20},{8,24},{12,28},{16,0},{20,4},{24,8},{28,12},{1,17},{... | collective-permute-start | bytes 196616 | tf_op jit(solution)/shard_map/ppermute | solution.py:200

commit v5 on v4

v5 whole, which is shorter than its diff:
```python
import functools

import jax
import jax.numpy as jnp
from jax import lax
from jax.experimental import pallas as pl
from jax.experimental.pallas import tpu as pltpu
from jax.sharding import PartitionSpec as P

SHARD = 256
F32, BF16 = jnp.float32, jnp.bfloat16
LIMIT = 20 * 2**20
LOAD_LIMIT = 52600 * 2**10
VMEM = pl.BlockSpec(memory_space=pltpu.VMEM)
HBM = pl.BlockSpec(memory_space=pltpu.HBM)
shape = jax.ShapeDtypeStruct


def dot_nt(a, b):
    return lax.dot_general(a, b, (((1,), (1,)), ((), ())), preferred_element_type=F32)


def dot_nn(a, b):
    return lax.dot_general(a, b, (((1,), (0,)), ((), ())), preferred_element_type=F32)


def bits_of(size):
    return [1 << t for t in range(size.bit_length() - 1)]


def halves(bits):
    numbers = [0]
    for bit in reversed(bits):
        numbers += [n ^ bit for n in numbers]
    return numbers


def call(kernel, name, args, shapes, flops, limit=LIMIT, specs=None, scratch=()):
    moved = sum(a.size * a.dtype.itemsize for a in (*args, *shapes)) if flops > 1 else 1
    return pl.pallas_call(
        kernel,
        in_specs=specs or [VMEM] * len(args),
        out_specs=[VMEM] * len(shapes),
        out_shape=list(shapes),
        scratch_shapes=list(scratch),
        compiler_params=pltpu.CompilerParams(vmem_limit_bytes=limit),
        cost_estimate=pl.CostEstimate(flops=flops, bytes_accessed=moved, transcendentals=0),
        name=name,
    )(*args)


def load_kernel(order, piece, av_hbm, up_hbm, av_ref, up_ref, sems):
    me = lax.axis_index("dim")
    copies = []
    for n, j in enumerate(order):
        for s in range(piece):
            at = n * piece + s
            source = (me ^ j) * piece + s
            copies.append(pltpu.make_async_copy(av_hbm.at[source], av_ref.at[at], sems.at[2 * at]))
            copies.append(pltpu.make_async_copy(up_hbm.at[source], up_ref.at[at], sems.at[2 * at + 1]))
    for copy in copies:
        copy.start()
    for copy in copies:
        copy.wait()


def width_sums(comp_t_ref, proj_ref, av, up, out_ref, at):
    rank = comp_t_ref.shape[0]
    reduced = dot_nt(comp_t_ref[...], av).astype(BF16)
    sums = dot_nn(reduced, av)
    out_ref[at, :rank] = sums - jnp.mean(sums, axis=0, keepdims=True)
    grads = dot_nn(proj_ref[...], up)
    out_ref[at, rank:] = grads - jnp.mean(grads, axis=0, keepdims=True)


def sums_kernel(start, av_ref, up_ref, comp_t_ref, proj_ref, *out_refs):
    for out_ref in out_refs:
        for at in range(out_ref.shape[0]):
            width_sums(comp_t_ref, proj_ref, av_ref[start + at], up_ref[start + at], out_ref, at)
        start += out_ref.shape[0]


def prepare_kernel(
    order, piece, start, av_ref, up_ref, comp_t_ref, proj_ref, mix_ref, slot_ref, out_ref, linear_ref, onehot_ref
):
    sums_kernel(start, av_ref, up_ref, comp_t_ref, proj_ref, out_ref)
    me = lax.axis_index("dim")
    features = up_ref.shape[2]
    slots = lax.broadcasted_iota(jnp.int32, (SHARD, features), 0)
    for n, j in enumerate(order):
        for s in range(piece):
            at = n * piece + s
            up = up_ref[at]
            linear_ref[at] = up.astype(F32) + dot_nt(up, mix_ref[...])
            hit = slots == slot_ref[:, lookups_of(me, j, piece, s, features)]
            onehot_ref[:, at * features:(at + 1) * features] = jnp.where(hit, 1.0, 0.0).astype(BF16)


def lookups_of(me, j, piece, s, features):
    return pl.ds(pl.multiple_of(((me ^ j) * piece + s) * features, features), features)


def add_kernel(keep_ref, got_ref, *out_refs):
    start = 0
    for out_ref in out_refs:
        stop = start + out_ref.shape[0]
        out_ref[...] = (keep_ref[start:stop] + got_ref[start:stop]).astype(out_ref.dtype)
        start = stop


def layer_back_kernel(starts, *refs):
    *terms, pair_ref = refs
    rank = pair_ref.shape[1]
    for b in range(pair_ref.shape[0]):
        total = sum(term[start + b].astype(F32) for start, term in zip(starts, terms))
        centred, grads = total[:rank], total[rank:]
        inverse = 1.0 / jnp.sqrt(jnp.mean(centred * centred, axis=0, keepdims=True) + 1e-05)
        normed = centred * inverse
        moment = jnp.mean(grads * normed, axis=0, keepdims=True)
        pair_ref[b] = (inverse * (grads - normed * moment)).astype(BF16)


def table_kernel(jobs, piece, rows, chain, has_total, *refs):
    av_ref, comp_t_ref, linear_ref, owner_ref, onehot_ref = refs[:5]
    pair_refs, refs = refs[5:5 + len(jobs)], refs[5 + len(jobs):]
    if has_total:
        total_ref, refs = refs[0], refs[1:]
    *outs, masked = refs
    _, width, features = av_ref.shape
    me, here = lax.axis_index("dim"), lax.axis_index("dp")
    comp_t = comp_t_ref[...]
    count = rows[1] - rows[0]
    owners = masked.shape[0] // count
    share = pair_refs[0].shape[0]
    added = None
    for (j, place, offset), pair_ref in zip(jobs, pair_refs):
        for s in range(share):
            at = place + s
            back = pair_ref[s]
            both = dot_nt(av_ref[at, rows[0]:rows[1]], jnp.concatenate([comp_t, back])).astype(BF16)
            grad = linear_ref[at, rows[0]:rows[1]] + dot_nn(both, jnp.concatenate([back, comp_t]))
            grad = grad.astype(BF16)
            owner = owner_ref[:, lookups_of(me, j, piece, offset + s, features)] ^ here
            for o in range(owners):
                mask = jnp.where(owner == o, 1.0, 0.0).astype(BF16)
                masked[o * count:(o + 1) * count, s * features:(s + 1) * features] = grad * mask
        part = dot_nt(masked[...], onehot_ref[:, place * features:(place + share) * features])
        added = part if added is None else added + part
    if chain is None:
        outs[0][...] = added + total_ref[...] if has_total else added
        return

    def block(o):
        own = added[o * count:(o + 1) * count]
        return own + total_ref[o * width + rows[0]:o * width + rows[1]] if has_total else own

    for n, o in enumerate(halves(chain[1:])):
        outs[0][n] = block(o ^ chain[0]).astype(BF16)
        outs[1][n] = block(o)


def table_part(jobs, piece, rows, owners, chain, arrays, pairs, total):
    _, width, features = arrays[0].shape
    rank = arrays[1].shape[0]
    count = rows[1] - rows[0]
    share = pairs[0].shape[0]
    if chain is None:
        shapes = [shape((owners * width, SHARD), F32)]
    else:
        shapes = [shape((owners // 2, count, SHARD), t) for t in (BF16, F32)]
    return call(
        functools.partial(table_kernel, jobs, piece, rows, chain, total is not None),
        "table_part",
        [*arrays, *pairs] + ([] if total is None else [total]),
        shapes,
        1,
        scratch=[pltpu.VMEM((owners * count, share * features), BF16)],
    )


def fold_kernel(*refs):
    *terms, send_ref, keep_ref = refs
    half = keep_ref.shape[0]
    start = 0
    for keep, got in zip(terms[::2], terms[1::2]):
        stop = start + keep.shape[1]
        send_ref[:, start:stop] = (keep[half:] + got[half:].astype(F32)).astype(BF16)
        keep_ref[:, start:stop] = keep[:half] + got[:half].astype(F32)
        start = stop


def fold(terms):
    count, _, slots = terms[0].shape
    part = (count // 2, sum(keep.shape[1] for keep in terms[::2]), slots)
    return call(fold_kernel, "fold", terms, [shape(part, t) for t in (BF16, F32)], terms[0].size)


def finish_kernel(*refs):
    *terms, out_ref = refs
    start = 0
    for keep, got in zip(terms[::2], terms[1::2]):
        stop = start + keep.shape[1]
        out_ref[start:stop] = keep[0] + got[0].astype(F32)
        start = stop


def swap(x, bit, axis="dim"):
    return lax.ppermute(x, axis, [(i, i ^ bit) for i in range(lax.axis_size(axis))])


def after(x, *others):
    return lax.optimization_barrier((x, *others))[0]


def shards(attribute_vectors, upstream, compress, interact_proj, linear_mix, row_owner, row_slot):
    owners, peers = lax.axis_size("dp"), lax.axis_size("dim")
    samples, width, features = attribute_vectors.shape
    rank = compress.shape[1]
    piece = samples // peers
    quarter = samples // 4
    groups = 2 if peers == 4 else 1
    share = piece // groups
    sample_flops = 6 * width * features * rank

    bits = bits_of(peers)
    held = halves(bits)
    count = peers // 4
    order = held[3 * count:] + held[2 * count:3 * count] + held[count:2 * count] + held[:count]
    place_of = {j: n * piece for n, j in enumerate(order)}

    comp_t = compress.T
    owner, slot = row_owner.reshape(1, -1), row_slot.reshape(1, -1)
    part = shape((quarter, 2 * rank, features), F32)

    av, up = call(
        functools.partial(load_kernel, order, piece),
        "load",
        (attribute_vectors, upstream),
        [shape(upstream.shape, BF16)] * 2,
        0,
        limit=LOAD_LIMIT,
        specs=[HBM] * 2,
        scratch=[pltpu.SemaphoreType.DMA((2 * samples,))],
    )
    args = (av, up, comp_t, interact_proj)
    (send_high,) = call(
        functools.partial(sums_kernel, 0), "sums", args, [part], quarter * sample_flops
    )
    got_high = swap(send_high, bits[0])
    send_low, keep_high = call(
        functools.partial(sums_kernel, quarter), "sums", args, [part] * 2, 2 * quarter * sample_flops
    )
    got_low = swap(send_low, bits[0])
    sent = call(
        add_kernel,
        "add",
        (keep_high, got_high),
        [shape((quarter // groups, 2 * rank, features), BF16)] * groups,
        keep_high.size,
    )
    got = [swap(x, bits[1]) for x in sent]
    keep_low, linear, onehot = call(
        functools.partial(prepare_kernel, order, piece, 3 * quarter),
        "prepare",
        (*args, linear_mix, slot),
        [part, shape((samples, width, features), F32), shape((SHARD, samples * features), BF16)],
        2 * samples * width * features * features,
    )
    arrays = (av, comp_t, linear, owner, onehot)

    def layer_back(terms, starts):
        return call(
            functools.partial(layer_back_kernel, starts),
            "layer_back",
            terms,
            [shape((share, rank, features), BF16)],
            32 * share * rank * features,
        )[0]

    def table(total, *stage, rows=(0, width), chain=None):
        jobs = [(j, place_of[j] + g * share, g * share) for g, j in stage]
        outs = table_part(jobs, piece, rows, owners, chain, arrays, [pairs[g][j] for g, j in stage], total)
        return outs if chain else outs[0]

    pairs = [{} for _ in range(groups)]
    total = None
    if groups == 2:
        core, y = bits
        far = core ^ y
        pairs[0][0] = layer_back([keep_low, got_low, got[0]], [0, 0, 0])
        pairs[0][y] = swap(pairs[0][0], y)
        pairs[1][0] = layer_back([keep_low, got_low, after(got[1], pairs[0][0])], [share, share, 0])
        pairs[1][y] = swap(pairs[1][0], y)
        pairs[0][y] = after(pairs[0][y], pairs[1][0])
        pairs[0][core] = swap(after(pairs[0][0], pairs[0][y]), core)
        pairs[0][far] = swap(pairs[0][y], core)
        total = table(total, (0, 0), (0, y), (0, core), (0, far))
        pairs[1][y] = after(pairs[1][y], total)
        pairs[1][core] = swap(after(pairs[1][0], pairs[1][y]), core)
        pairs[1][far] = swap(pairs[1][y], core)
        total = table(total, (1, 0), (1, y))
        last = [(1, core), (1, far)]
    else:
        terms, starts = [keep_low, got_low, got[0]], [0, 0, 0]
        for bit in bits[2:]:
            keep = sum(term.astype(F32) for term in terms)
            half = keep.shape[0] // 2
            terms, starts = [keep[:half], swap(keep[half:].astype(BF16), bit)], [0, 0]
        pairs[0][0] = layer_back(terms, starts)
        for bit in reversed(bits):
            pairs[0].update({j ^ bit: swap(pair, bit) for j, pair in pairs[0].items()})
        *stage, last = [(0, j) for j in pairs[0]]
        for job in stage:
            total = table(total, job)
        last = [last]

    low = bits_of(owners)[:(owners.bit_length() - 1) // 2]
    high = bits_of(owners)[len(low):]
    chains = [low + high, high[:1] + low + high[1:]]
    sums = []
    for c, chain in enumerate(chains):
        rows = (c * width // 2, (c + 1) * width // 2)
        send, keep = table(total, *last, rows=rows, chain=chain)
        sums.append([keep, swap(send, chain[0], "dp")])
    for step in range(1, len(low) + 1):
        for c, chain in enumerate(chains):
            send, keep = fold(sums[c])
            sums[c] = [keep, swap(send, chain[step], "dp")]
    sums = sums[0] + sums[1]
    for bit in high[1:]:
        send, keep = fold(sums)
        sums = [keep, swap(send, bit, "dp")]
    (out,) = call(finish_kernel, "finish", sums, [shape((width, SHARD), F32)], width * SHARD)
    return out


def solution(mesh):
    placed = (
        P("dp", "dim", None),
        P("dp", "dim", None),
        P(),
        P(None, "dim"),
        P(),
        P("dp", None),
        P("dp"),
    )
    return jax.shard_map(
        shards, mesh=mesh, in_specs=placed, out_specs=P("dim", "dp"), check_vma=False
    )
```

time: 41.2 us -> 43.8 us (1.063)
  Pallas kernels: 9.25 us -> 11.6 us
  starting transfers between devices: 14.9 us -> 17.2 us
  waiting for transfers between devices: 16.6 us -> 14.6 us
    pallas_call x12 -> x15, Pallas kernels: 9.25 us -> 11.6 us  [call(): pl.pallas_call(kernel, in_specs=specs or [VMEM] * len(args), out_specs=[V...]
    ppermute x11 -> x15, starting transfers between devices: 14.9 us -> 17.2 us  [swap(): lax.ppermute(x, axis, [(i, i ^ bit) for i in range(lax.axis_size(axis))])]
    ppermute x11 -> x15, waiting for transfers between devices: 16.6 us -> 14.6 us  [swap(): lax.ppermute(x, axis, [(i, i ^ bit) for i in range(lax.axis_size(axis))])]
  transfers between devices with their start and end apart: 11 -> 15, of which waited for: 8 -> 9; matrix products, arithmetic and copies ran while one was open for 0% -> 0% of each run, Pallas kernels for 13% -> 17%
where the time goes in v5:
time: 43.8 us; the launch traced here: 43.6 us
  starting transfers between devices  17.2 us (39%)
  waiting for transfers between devices  14.6 us (33%)
  Pallas kernels  11.6 us (26%)
    ppermute x15, starting transfers between devices, swap(): lax.ppermute(x, axis, [(i, i ^ bit) for i in range(lax.axis_size(axis))])  17.2 us
    ppermute x15, waiting for transfers between devices, swap(): lax.ppermute(x, axis, [(i, i ^ bit) for i in range(lax.axis_size(axis))])  14.6 us
    pallas_call x15, Pallas kernels, call(): pl.pallas_call(kernel, in_specs=specs or [VMEM] * len(args), out_specs=[V...  11.6 us
  transfers between devices with their start and end apart: 15, of which 9 were waited for; matrix products, arithmetic and copies ran while one was open for 0% of the time, Pallas kernels for 17%

profile of v5, /device:TPU:0, one launch (start us, length us, event | category | flops | bytes accessed | tf_op | source)
XLA Modules:
  0.0 43.6 jit_solution(1589254588283966085)
XLA Ops:
  0.0 1.9 %load.1 = (bf16[16,128,256]{2,1,0:T(8,128)(2,1)S(1)}, bf16[16,128,256]{2,1,0:T(8,128)(2,1)S(1)}) custom-call(bf16[16,128,256]{2,1,0:T(8,128)(2,1)} %av_hbm.1, bf16[16,128,256]{2,1,0:T(8,128)(2,1)} %up_hbm.1), custom_call_target="tpu_custom_call" | custom-call | bytes 1 | tf_op jit(solution)/shard_map/load/pallas_call | solution.py:40
  1.9 0.4 sums.3
  2.3 0.5 %collective-permute-start.1 = (f32[4,128,256]{2,1,0:T(8,128)S(1)}, f32[4,128,256]{2,1,0:T(8,128)S(1)}, u32[]{:S(2)}, u32[]{:S(2)}) collective-permute-start(f32[4,128,256]{2,1,0:T(8,128)S(1)} %sums.3), channel_id=1, source_target_pairs={{0,1},{1,0},{2,3},{3,2},{4,5},{5,4},{6,7},{7,6},{8,9},{9,8},{10,11... | collective-permute-start | bytes 1572872 | tf_op jit(solution)/shard_map/ppermute | solution.py:208
  2.9 0.6 %sums.2 = (f32[4,128,256]{2,1,0:T(8,128)S(1)}, f32[4,128,256]{2,1,0:T(8,128)S(1)}) custom-call(bf16[16,128,256]{2,1,0:T(8,128)(2,1)S(1)} %get-tuple-element.29.av_ref.refs_0_, bf16[16,128,256]{2,1,0:T(8,128)(2,1)S(1)} %get-tuple-element.30.up_ref, bf16[64,256]{1,0:T(8,128)(2,1)S(1)} %bitcast.4, bf16[64,128]{1,0:T(8,128)(2,1)S(1)} %copy-done.2), custom_call_target="tpu_custom_call" | custom-call | flops 100663296 | bytes 3194880 | tf_op jit(solution)/shard_map/sums/pallas_call | solution.py:40
  3.4 0.1 collective-permute-start
  3.6 0.8 %collective-permute-done.1.got_ref = f32[4,128,256]{2,1,0:T(8,128)S(1)} collective-permute-done((f32[4,128,256]{2,1,0:T(8,128)S(1)}, f32[4,128,256]{2,1,0:T(8,128)S(1)}, u32[]{:S(2)}, u32[]{:S(2)}) %collective-permute-start.1) | collective-permute-done | bytes 524320 | tf_op jit(solution)/shard_map/ppermute | solution.py:208
  4.4 3.0 %collective-permute-start.3 = (bf16[2,128,256]{2,1,0:T(8,128)(2,1)S(1)}, bf16[2,128,256]{2,1,0:T(8,128)(2,1)S(1)}, u32[]{:S(2)}, u32[]{:S(2)}) collective-permute-start(bf16[2,128,256]{2,1,0:T(8,128)(2,1)S(1)} %get-tuple-element.37), channel_id=1, source_target_pairs={{0,2},{1,3},{2,0},{3,1},{4,6},{5,7},{6,4},{7,5},{8,10},{9,11},{10,... | collective-permute-start | bytes 393224 | tf_op jit(solution)/shard_map/ppermute | solution.py:208
  7.5 1.6 %prepare.1 = (f32[4,128,256]{2,1,0:T(8,128)S(1)}, f32[16,128,256]{2,1,0:T(8,128)S(1)}, bf16[256,4096]{1,0:T(8,128)(2,1)S(1)}) custom-call(bf16[16,128,256]{2,1,0:T(8,128)(2,1)S(1)} %get-tuple-element.29.av_ref.refs_0_, bf16[16,128,256]{2,1,0:T(8,128)(2,1)S(1)} %get-tuple-element.30.up_ref, bf16[64,256]{1,0:T(8,128)(2,1)S(1)} %bitcast.5, ...), custom_call_target="tpu_custom_call" | custom-call | flops 268435456 | bytes 7012352 | tf_op jit(solution)/shard_map/prepare/pallas_call | solution.py:40
  9.1 2.6 %collective-permute-done.3.refs_2_ = bf16[2,128,256]{2,1,0:T(8,128)(2,1)S(1)} collective-permute-done((bf16[2,128,256]{2,1,0:T(8,128)(2,1)S(1)}, bf16[2,128,256]{2,1,0:T(8,128)(2,1)S(1)}, u32[]{:S(2)}, u32[]{:S(2)}) %collective-permute-start.3) | collective-permute-done | bytes 131104 | tf_op jit(solution)/shard_map/ppermute | solution.py:208
  11.7 0.1 layer_back.2.refs_5_
  11.8 2.1 %collective-permute-start.5 = (bf16[2,64,256]{2,1,0:T(8,128)(2,1)S(1)}, bf16[2,64,256]{2,1,0:T(8,128)(2,1)S(1)}, u32[]{:S(2)}, u32[]{:S(2)}) collective-permute-start(bf16[2,64,256]{2,1,0:T(8,128)(2,1)S(1)} %layer_back.2.refs_5_), channel_id=1, source_target_pairs={{0,2},{1,3},{2,0},{3,1},{4,6},{5,7},{6,4},{7,5},{8,10},{9,11},{10,... | collective-permute-start | bytes 196616 | tf_op jit(solution)/shard_map/ppermute | solution.py:208
  13.9 0.4 %collective-permute-done.2.refs_2_ = bf16[2,128,256]{2,1,0:T(8,128)(2,1)S(1)} collective-permute-done((bf16[2,128,256]{2,1,0:T(8,128)(2,1)S(1)}, bf16[2,128,256]{2,1,0:T(8,128)(2,1)S(1)}, u32[]{:S(2)}, u32[]{:S(2)}) %collective-permute-start.2) | collective-permute-done | bytes 131104 | tf_op jit(solution)/shard_map/ppermute | solution.py:208
  14.3 0.1 layer_back.3.refs_5_
  14.5 1.7 %collective-permute-done.5.refs_6_ = bf16[2,64,256]{2,1,0:T(8,128)(2,1)S(1)} collective-permute-done((bf16[2,64,256]{2,1,0:T(8,128)(2,1)S(1)}, bf16[2,64,256]{2,1,0:T(8,128)(2,1)S(1)}, u32[]{:S(2)}, u32[]{:S(2)}) %collective-permute-start.5) | collective-permute-done | bytes 65568 | tf_op jit(solution)/shard_map/ppermute | solution.py:208
  16.2 0.5 %collective-permute-start.7 = (bf16[2,64,256]{2,1,0:T(8,128)(2,1)S(1)}, bf16[2,64,256]{2,1,0:T(8,128)(2,1)S(1)}, u32[]{:S(2)}, u32[]{:S(2)}) collective-permute-start(bf16[2,64,256]{2,1,0:T(8,128)(2,1)S(1)} %collective-permute-done.5.refs_6_), channel_id=1, source_target_pairs={{0,1},{1,0},{2,3},{3,2},{4,5},{5,4},{6,7},{7,6},{8,9},{9,8},{10,11... | collective-permute-start | bytes 196616 | tf_op jit(solution)/shard_map/ppermute | solution.py:208
  16.7 2.0 %collective-permute-start.4 = (bf16[2,64,256]{2,1,0:T(8,128)(2,1)S(1)}, bf16[2,64,256]{2,1,0:T(8,128)(2,1)S(1)}, u32[]{:S(2)}, u32[]{:S(2)}) collective-permute-start(bf16[2,64,256]{2,1,0:T(8,128)(2,1)S(1)} %layer_back.3.refs_5_), channel_id=1, source_target_pairs={{0,2},{1,3},{2,0},{3,1},{4,6},{5,7},{6,4},{7,5},{8,10},{9,11},{10,... | collective-permute-start | bytes 196616 | tf_op jit(solution)/shard_map/ppermute | solution.py:208
  18.7 2.9 %table_part.4.refs_7_ = f32[1024,256]{1,0:T(8,128)S(1)} custom-call(bf16[16,128,256]{2,1,0:T(8,128)(2,1)S(1)} %get-tuple-element.29.av_ref.refs_0_, bf16[64,256]{1,0:T(8,128)(2,1)S(1)} %bitcast.6, f32[16,128,256]{2,1,0:T(8,128)S(1)} %get-tuple-element.31.refs_2_, s32[1,4096]{1,0:T(1,128)S(1)} %bitcast.10, bf16[256,4096]{1,0:T(8,128)(2,1)S(1)} %get-tuple-element.32.refs_4_, ...), custom_call_target="tpu_custom_call" | custom-call | flops 1 | bytes 1 | tf_op jit(solution)/shard_map/table_part/pallas_call | solution.py:40
  21.7 0.5 %collective-permute-start.9 = (bf16[2,64,256]{2,1,0:T(8,128)(2,1)S(1)}, bf16[2,64,256]{2,1,0:T(8,128)(2,1)S(1)}, u32[]{:S(2)}, u32[]{:S(2)}) collective-permute-start(bf16[2,64,256]{2,1,0:T(8,128)(2,1)S(1)} %collective-permute-done.4.refs_6_), channel_id=1, source_target_pairs={{0,1},{1,0},{2,3},{3,2},{4,5},{5,4},{6,7},{7,6},{8,9},{9,8},{10,11... | collective-permute-start | bytes 196616 | tf_op jit(solution)/shard_map/ppermute | solution.py:208
  22.2 1.2 %table_part.5.refs_7_ = f32[1024,256]{1,0:T(8,128)S(1)} custom-call(bf16[16,128,256]{2,1,0:T(8,128)(2,1)S(1)} %get-tuple-element.29.av_ref.refs_0_, bf16[64,256]{1,0:T(8,128)(2,1)S(1)} %bitcast.7, f32[16,128,256]{2,1,0:T(8,128)S(1)} %get-tuple-element.31.refs_2_, s32[1,4096]{1,0:T(1,128)S(1)} %bitcast.11, bf16[256,4096]{1,0:T(8,128)(2,1)S(1)} %get-tuple-element.32.refs_4_, ...), custom_call_target="tpu_custom_call" | custom-call | flops 1 | bytes 1 | tf_op jit(solution)/shard_map/table_part/pallas_call | solution.py:40
  23.4 1.1 %table_part.7 = (bf16[4,64,256]{2,1,0:T(8,128)(2,1)S(1)}, f32[4,64,256]{2,1,0:T(8,128)S(1)}) custom-call(bf16[16,128,256]{2,1,0:T(8,128)(2,1)S(1)} %get-tuple-element.29.av_ref.refs_0_, bf16[64,256]{1,0:T(8,128)(2,1)S(1)} %bitcast.8, f32[16,128,256]{2,1,0:T(8,128)S(1)} %get-tuple-element.31.refs_2_, s32[1,4096]{1,0:T(1,128)S(1)} %bitcast.12, ...), custom_call_target="tpu_custom_call" | custom-call | flops 1 | bytes 1 | tf_op jit(solution)/shard_map/table_part/pallas_call | solution.py:40
  24.4 1.7 %collective-permute-start.12 = (bf16[4,64,256]{2,1,0:T(8,128)(2,1)S(1)}, bf16[4,64,256]{2,1,0:T(8,128)(2,1)S(1)}, u32[]{:S(2)}, u32[]{:S(2)}) collective-permute-start(bf16[4,64,256]{2,1,0:T(8,128)(2,1)S(1)} %get-tuple-element.48), channel_id=1, source_target_pairs={{0,8},{4,12},{8,0},{12,4},{16,24},{20,28},{24,16},{28,20},{1,9},{5... | collective-permute-start | bytes 393224 | tf_op jit(solution)/shard_map/ppermute | solution.py:208
  26.1 1.1 %table_part.6 = (bf16[4,64,256]{2,1,0:T(8,128)(2,1)S(1)}, f32[4,64,256]{2,1,0:T(8,128)S(1)}) custom-call(bf16[16,128,256]{2,1,0:T(8,128)(2,1)S(1)} %get-tuple-element.29.av_ref.refs_0_, bf16[64,256]{1,0:T(8,128)(2,1)S(1)} %bitcast.9, f32[16,128,256]{2,1,0:T(8,128)S(1)} %get-tuple-element.31.refs_2_, s32[1,4096]{1,0:T(1,128)S(1)} %bitcast.13, ...), custom_call_target="tpu_custom_call" | custom-call | flops 1 | bytes 1 | tf_op jit(solution)/shard_map/table_part/pallas_call | solution.py:40
  27.2 1.6 %collective-permute-start.10 = (bf16[4,64,256]{2,1,0:T(8,128)(2,1)S(1)}, bf16[4,64,256]{2,1,0:T(8,128)(2,1)S(1)}, u32[]{:S(2)}, u32[]{:S(2)}) collective-permute-start(bf16[4,64,256]{2,1,0:T(8,128)(2,1)S(1)} %get-tuple-element.44), channel_id=1, source_target_pairs={{0,4},{4,0},{8,12},{12,8},{16,20},{20,16},{24,28},{28,24},{1,5},{5... | collective-permute-start | bytes 393224 | tf_op jit(solution)/shard_map/ppermute | solution.py:208
  28.7 1.2 %collective-permute-done.12.refs_1_ = bf16[4,64,256]{2,1,0:T(8,128)(2,1)S(1)} collective-permute-done((bf16[4,64,256]{2,1,0:T(8,128)(2,1)S(1)}, bf16[4,64,256]{2,1,0:T(8,128)(2,1)S(1)}, u32[]{:S(2)}, u32[]{:S(2)}) %collective-permute-start.12) | collective-permute-done | bytes 131104 | tf_op jit(solution)/shard_map/ppermute | solution.py:208
  30.0 1.6 %collective-permute-start.13 = (bf16[2,64,256]{2,1,0:T(8,128)(2,1)S(1)}, bf16[2,64,256]{2,1,0:T(8,128)(2,1)S(1)}, u32[]{:S(2)}, u32[]{:S(2)}) collective-permute-start(bf16[2,64,256]{2,1,0:T(8,128)(2,1)S(1)} %get-tuple-element.50), channel_id=1, source_target_pairs={{0,4},{4,0},{8,12},{12,8},{16,20},{20,16},{24,28},{28,24},{1,5},{5... | collective-permute-start | bytes 196616 | tf_op jit(solution)/shard_map/ppermute | solution.py:208
  31.6 1.4 %collective-permute-done.10.refs_1_ = bf16[4,64,256]{2,1,0:T(8,128)(2,1)S(1)} collective-permute-done((bf16[4,64,256]{2,1,0:T(8,128)(2,1)S(1)}, bf16[4,64,256]{2,1,0:T(8,128)(2,1)S(1)}, u32[]{:S(2)}, u32[]{:S(2)}) %collective-permute-start.10) | collective-permute-done | bytes 131104 | tf_op jit(solution)/shard_map/ppermute | solution.py:208
  33.0 0.3 collective-permute-start.11
  33.3 1.1 %collective-permute-done.13.refs_3_ = bf16[2,64,256]{2,1,0:T(8,128)(2,1)S(1)} collective-permute-done((bf16[2,64,256]{2,1,0:T(8,128)(2,1)S(1)}, bf16[2,64,256]{2,1,0:T(8,128)(2,1)S(1)}, u32[]{:S(2)}, u32[]{:S(2)}) %collective-permute-start.13) | collective-permute-done | bytes 65568 | tf_op jit(solution)/shard_map/ppermute | solution.py:208
  34.3 3.0 %collective-permute-done.11.refs_1_ = bf16[2,64,256]{2,1,0:T(8,128)(2,1)S(1)} collective-permute-done((bf16[2,64,256]{2,1,0:T(8,128)(2,1)S(1)}, bf16[2,64,256]{2,1,0:T(8,128)(2,1)S(1)}, u32[]{:S(2)}, u32[]{:S(2)}) %collective-permute-start.11) | collective-permute-done | bytes 65568 | tf_op jit(solution)/shard_map/ppermute | solution.py:208
  37.4 3.3 %collective-permute-start.14 = (bf16[1,128,256]{2,1,0:T(8,128)(2,1)S(1)}, bf16[1,128,256]{2,1,0:T(8,128)(2,1)S(1)}, u32[]{:S(2)}, u32[]{:S(2)}) collective-permute-start(bf16[1,128,256]{2,1,0:T(8,128)(2,1)S(1)} %get-tuple-element.52), channel_id=1, source_target_pairs={{0,16},{4,20},{8,24},{12,28},{16,0},{20,4},{24,8},{28,12},{1,17},{... | collective-permute-start | bytes 196616 | tf_op jit(solution)/shard_map/ppermute | solution.py:208
  40.6 2.3 %collective-permute-done.14.refs_1_ = bf16[1,128,256]{2,1,0:T(8,128)(2,1)S(1)} collective-permute-done((bf16[1,128,256]{2,1,0:T(8,128)(2,1)S(1)}, bf16[1,128,256]{2,1,0:T(8,128)(2,1)S(1)}, u32[]{:S(2)}, u32[]{:S(2)}) %collective-permute-start.14) | collective-permute-done | bytes 65568 | tf_op jit(solution)/shard_map/ppermute | solution.py:208
  42.9 0.7 %finish.1 = f32[128,256]{1,0:T(8,128)} custom-call(f32[1,128,256]{2,1,0:T(8,128)S(1)} %get-tuple-element.51.refs_0_, bf16[1,128,256]{2,1,0:T(8,128)(2,1)S(1)} %collective-permute-done.14.refs_1_), custom_call_target="tpu_custom_call" | custom-call | flops 32768 | bytes 327680 | tf_op jit(solution)/shard_map/finish/pallas_call | solution.py:40
  (23 shorter events, 0.3 us)
Async XLA Ops:
  0.0 1.9 %copy-start.2 = (bf16[64,128]{1,0:T(8,128)(2,1)S(1)}, bf16[64,128]{1,0:T(8,128)(2,1)}, u32[]{:S(2)}) copy-start(bf16[64,128]{1,0:T(8,128)(2,1)} %proj_ref.5) | copy-start | bytes 49156
  0.0 1.9 %copy-start = (bf16[256,64]{0,1:T(8,128)(2,1)S(1)}, bf16[256,64]{0,1:T(8,128)(2,1)}, u32[]{:S(2)}) copy-start(bf16[256,64]{0,1:T(8,128)(2,1)} %param.9) | copy-start | bytes 98308
  2.3 5.2 %copy-start.3 = (bf16[256,256]{1,0:T(8,128)(2,1)S(1)}, bf16[256,256]{1,0:T(8,128)(2,1)}, u32[]{:S(2)}) copy-start(bf16[256,256]{1,0:T(8,128)(2,1)} %mix_ref.1) | copy-start | bytes 393220
  2.3 5.2 %copy-start.4 = (s32[4096]{0:T(1024)S(1)}, s32[4096]{0:T(1024)}, u32[]{:S(2)}) copy-start(s32[4096]{0:T(1024)} %param.13) | copy-start | bytes 49156
  2.3 2.1 %collective-permute-start.1 = (f32[4,128,256]{2,1,0:T(8,128)S(1)}, f32[4,128,256]{2,1,0:T(8,128)S(1)}, u32[]{:S(2)}, u32[]{:S(2)}) collective-permute-start(f32[4,128,256]{2,1,0:T(8,128)S(1)} %sums.3), channel_id=1, source_target_pairs={{0,1},{1,0},{2,3},{3,2},{4,5},{5,4},{6,7},{7,6},{8,9},{9,8},{10,11... | collective-permute-start | bytes 1572872 | tf_op jit(solution)/shard_map/ppermute | solution.py:208
  3.4 5.6 %collective-permute-start = (f32[4,128,256]{2,1,0:T(8,128)S(1)}, f32[4,128,256]{2,1,0:T(8,128)S(1)}, u32[]{:S(2)}, u32[]{:S(2)}) collective-permute-start(f32[4,128,256]{2,1,0:T(8,128)S(1)} %get-tuple-element.34), channel_id=1, source_target_pairs={{0,1},{1,0},{2,3},{3,2},{4,5},{5,4},{6,7},{7,6},{8,9},{9,8},{10,11... | collective-permute-start | bytes 1572872 | tf_op jit(solution)/shard_map/ppermute | solution.py:208
  4.4 7.2 %collective-permute-start.3 = (bf16[2,128,256]{2,1,0:T(8,128)(2,1)S(1)}, bf16[2,128,256]{2,1,0:T(8,128)(2,1)S(1)}, u32[]{:S(2)}, u32[]{:S(2)}) collective-permute-start(bf16[2,128,256]{2,1,0:T(8,128)(2,1)S(1)} %get-tuple-element.37), channel_id=1, source_target_pairs={{0,2},{1,3},{2,0},{3,1},{4,6},{5,7},{6,4},{7,5},{8,10},{9,11},{10,... | collective-permute-start | bytes 393224 | tf_op jit(solution)/shard_map/ppermute | solution.py:208
  7.4 7.0 %collective-permute-start.2 = (bf16[2,128,256]{2,1,0:T(8,128)(2,1)S(1)}, bf16[2,128,256]{2,1,0:T(8,128)(2,1)S(1)}, u32[]{:S(2)}, u32[]{:S(2)}) collective-permute-start(bf16[2,128,256]{2,1,0:T(8,128)(2,1)S(1)} %get-tuple-element.36), channel_id=1, source_target_pairs={{0,2},{1,3},{2,0},{3,1},{4,6},{5,7},{6,4},{7,5},{8,10},{9,11},{10,... | collective-permute-start | bytes 393224 | tf_op jit(solution)/shard_map/ppermute | solution.py:208
  7.5 11.2 %copy-start.1 = (s32[4096,1]{0,1:T(1,128)S(1)}, s32[4096,1]{0,1:T(1,128)}, u32[]{:S(2)}) copy-start(s32[4096,1]{0,1:T(1,128)} %param.12) | copy-start | bytes 49156
  11.8 4.4 %collective-permute-start.5 = (bf16[2,64,256]{2,1,0:T(8,128)(2,1)S(1)}, bf16[2,64,256]{2,1,0:T(8,128)(2,1)S(1)}, u32[]{:S(2)}, u32[]{:S(2)}) collective-permute-start(bf16[2,64,256]{2,1,0:T(8,128)(2,1)S(1)} %layer_back.2.refs_5_), channel_id=1, source_target_pairs={{0,2},{1,3},{2,0},{3,1},{4,6},{5,7},{6,4},{7,5},{8,10},{9,11},{10,... | collective-permute-start | bytes 196616 | tf_op jit(solution)/shard_map/ppermute | solution.py:208
  16.2 2.5 %collective-permute-start.6 = (bf16[2,64,256]{2,1,0:T(8,128)(2,1)S(1)}, bf16[2,64,256]{2,1,0:T(8,128)(2,1)S(1)}, u32[]{:S(2)}, u32[]{:S(2)}) collective-permute-start(bf16[2,64,256]{2,1,0:T(8,128)(2,1)S(1)} %layer_back.2.refs_5_), channel_id=1, source_target_pairs={{0,1},{1,0},{2,3},{3,2},{4,5},{5,4},{6,7},{7,6},{8,9},{9,8},{10,11... | collective-permute-start | bytes 196616 | tf_op jit(solution)/shard_map/ppermute | solution.py:208
  16.2 2.5 %collective-permute-start.7 = (bf16[2,64,256]{2,1,0:T(8,128)(2,1)S(1)}, bf16[2,64,256]{2,1,0:T(8,128)(2,1)S(1)}, u32[]{:S(2)}, u32[]{:S(2)}) collective-permute-start(bf16[2,64,256]{2,1,0:T(8,128)(2,1)S(1)} %collective-permute-done.5.refs_6_), channel_id=1, source_target_pairs={{0,1},{1,0},{2,3},{3,2},{4,5},{5,4},{6,7},{7,6},{8,9},{9,8},{10,11... | collective-permute-start | bytes 196616 | tf_op jit(solution)/shard_map/ppermute | solution.py:208
  16.7 4.9 %collective-permute-start.4 = (bf16[2,64,256]{2,1,0:T(8,128)(2,1)S(1)}, bf16[2,64,256]{2,1,0:T(8,128)(2,1)S(1)}, u32[]{:S(2)}, u32[]{:S(2)}) collective-permute-start(bf16[2,64,256]{2,1,0:T(8,128)(2,1)S(1)} %layer_back.3.refs_5_), channel_id=1, source_target_pairs={{0,2},{1,3},{2,0},{3,1},{4,6},{5,7},{6,4},{7,5},{8,10},{9,11},{10,... | collective-permute-start | bytes 196616 | tf_op jit(solution)/shard_map/ppermute | solution.py:208
  21.6 1.8 %collective-permute-start.8 = (bf16[2,64,256]{2,1,0:T(8,128)(2,1)S(1)}, bf16[2,64,256]{2,1,0:T(8,128)(2,1)S(1)}, u32[]{:S(2)}, u32[]{:S(2)}) collective-permute-start(bf16[2,64,256]{2,1,0:T(8,128)(2,1)S(1)} %layer_back.3.refs_5_), channel_id=1, source_target_pairs={{0,1},{1,0},{2,3},{3,2},{4,5},{5,4},{6,7},{7,6},{8,9},{9,8},{10,11... | collective-permute-start | bytes 196616 | tf_op jit(solution)/shard_map/ppermute | solution.py:208
  21.7 1.7 %collective-permute-start.9 = (bf16[2,64,256]{2,1,0:T(8,128)(2,1)S(1)}, bf16[2,64,256]{2,1,0:T(8,128)(2,1)S(1)}, u32[]{:S(2)}, u32[]{:S(2)}) collective-permute-start(bf16[2,64,256]{2,1,0:T(8,128)(2,1)S(1)} %collective-permute-done.4.refs_6_), channel_id=1, source_target_pairs={{0,1},{1,0},{2,3},{3,2},{4,5},{5,4},{6,7},{7,6},{8,9},{9,8},{10,11... | collective-permute-start | bytes 196616 | tf_op jit(solution)/shard_map/ppermute | solution.py:208
  24.4 5.5 %collective-permute-start.12 = (bf16[4,64,256]{2,1,0:T(8,128)(2,1)S(1)}, bf16[4,64,256]{2,1,0:T(8,128)(2,1)S(1)}, u32[]{:S(2)}, u32[]{:S(2)}) collective-permute-start(bf16[4,64,256]{2,1,0:T(8,128)(2,1)S(1)} %get-tuple-element.48), channel_id=1, source_target_pairs={{0,8},{4,12},{8,0},{12,4},{16,24},{20,28},{24,16},{28,20},{1,9},{5... | collective-permute-start | bytes 393224 | tf_op jit(solution)/shard_map/ppermute | solution.py:208
  27.2 5.8 %collective-permute-start.10 = (bf16[4,64,256]{2,1,0:T(8,128)(2,1)S(1)}, bf16[4,64,256]{2,1,0:T(8,128)(2,1)S(1)}, u32[]{:S(2)}, u32[]{:S(2)}) collective-permute-start(bf16[4,64,256]{2,1,0:T(8,128)(2,1)S(1)} %get-tuple-element.44), channel_id=1, source_target_pairs={{0,4},{4,0},{8,12},{12,8},{16,20},{20,16},{24,28},{28,24},{1,5},{5... | collective-permute-start | bytes 393224 | tf_op jit(solution)/shard_map/ppermute | solution.py:208
  30.0 4.3 %collective-permute-start.13 = (bf16[2,64,256]{2,1,0:T(8,128)(2,1)S(1)}, bf16[2,64,256]{2,1,0:T(8,128)(2,1)S(1)}, u32[]{:S(2)}, u32[]{:S(2)}) collective-permute-start(bf16[2,64,256]{2,1,0:T(8,128)(2,1)S(1)} %get-tuple-element.50), channel_id=1, source_target_pairs={{0,4},{4,0},{8,12},{12,8},{16,20},{20,16},{24,28},{28,24},{1,5},{5... | collective-permute-start | bytes 196616 | tf_op jit(solution)/shard_map/ppermute | solution.py:208
  33.0 4.3 %collective-permute-start.11 = (bf16[2,64,256]{2,1,0:T(8,128)(2,1)S(1)}, bf16[2,64,256]{2,1,0:T(8,128)(2,1)S(1)}, u32[]{:S(2)}, u32[]{:S(2)}) collective-permute-start(bf16[2,64,256]{2,1,0:T(8,128)(2,1)S(1)} %get-tuple-element.46), channel_id=1, source_target_pairs={{0,8},{4,12},{8,0},{12,4},{16,24},{20,28},{24,16},{28,20},{1,9},{5... | collective-permute-start | bytes 196616 | tf_op jit(solution)/shard_map/ppermute | solution.py:208
  37.4 5.6 %collective-permute-start.14 = (bf16[1,128,256]{2,1,0:T(8,128)(2,1)S(1)}, bf16[1,128,256]{2,1,0:T(8,128)(2,1)S(1)}, u32[]{:S(2)}, u32[]{:S(2)}) collective-permute-start(bf16[1,128,256]{2,1,0:T(8,128)(2,1)S(1)} %get-tuple-element.52), channel_id=1, source_target_pairs={{0,16},{4,20},{8,24},{12,28},{16,0},{20,4},{24,8},{28,12},{1,17},{... | collective-permute-start | bytes 196616 | tf_op jit(solution)/shard_map/ppermute | solution.py:208

commit v6 on v4

v6 whole, which is shorter than its diff:
```python
import functools

import jax
import jax.numpy as jnp
from jax import lax
from jax.experimental import pallas as pl
from jax.experimental.pallas import tpu as pltpu
from jax.sharding import PartitionSpec as P

SHARD = 256
F32, BF16 = jnp.float32, jnp.bfloat16
LIMIT = 20 * 2**20
LOAD_LIMIT = 52600 * 2**10
VMEM = pl.BlockSpec(memory_space=pltpu.VMEM)
HBM = pl.BlockSpec(memory_space=pltpu.HBM)
shape = jax.ShapeDtypeStruct


def dot_nt(a, b):
    return lax.dot_general(a, b, (((1,), (1,)), ((), ())), preferred_element_type=F32)


def dot_nn(a, b):
    return lax.dot_general(a, b, (((1,), (0,)), ((), ())), preferred_element_type=F32)


def bits_of(size):
    return [1 << t for t in range(size.bit_length() - 1)]


def halves(bits):
    numbers = [0]
    for bit in reversed(bits):
        numbers += [n ^ bit for n in numbers]
    return numbers


def call(kernel, name, args, shapes, flops, limit=LIMIT, specs=None, scratch=()):
    moved = sum(a.size * a.dtype.itemsize for a in (*args, *shapes))
    return pl.pallas_call(
        kernel,
        in_specs=specs or [VMEM] * len(args),
        out_specs=[VMEM] * len(shapes),
        out_shape=list(shapes),
        scratch_shapes=list(scratch),
        compiler_params=pltpu.CompilerParams(vmem_limit_bytes=limit),
        cost_estimate=pl.CostEstimate(flops=flops, bytes_accessed=moved, transcendentals=0),
        name=name,
    )(*args)


def load_kernel(piece, av_hbm, up_hbm, av_ref, up_ref, sems):
    me = lax.axis_index("dim")
    copies = []
    for j in range(av_ref.shape[0] // piece):
        source, to = pl.ds((me ^ j) * piece, piece), pl.ds(j * piece, piece)
        copies.append(pltpu.make_async_copy(av_hbm.at[source], av_ref.at[to], sems.at[2 * j]))
        copies.append(pltpu.make_async_copy(up_hbm.at[source], up_ref.at[to], sems.at[2 * j + 1]))
    for copy in copies:
        copy.start()
    for copy in copies:
        copy.wait()


def width_sums(comp_t_ref, proj_ref, av, up, out_ref, at):
    rank = comp_t_ref.shape[0]
    reduced = dot_nt(comp_t_ref[...], av).astype(BF16)
    sums = dot_nn(reduced, av)
    out_ref[at, :rank] = sums - jnp.mean(sums, axis=0, keepdims=True)
    grads = dot_nn(proj_ref[...], up)
    out_ref[at, rank:] = grads - jnp.mean(grads, axis=0, keepdims=True)


def sums_kernel(orders, piece, av_ref, up_ref, comp_t_ref, proj_ref, *out_refs):
    for order, out_ref in zip(orders, out_refs):
        for n in range(len(order) * piece):
            at = order[n // piece] * piece + n % piece
            width_sums(comp_t_ref, proj_ref, av_ref[at], up_ref[at], out_ref, n)


def prepare_kernel(low, piece, av_ref, up_ref, comp_t_ref, proj_ref, mix_ref, slot_ref, out_ref, linear_ref, onehot_ref):
    sums_kernel([low], piece, av_ref, up_ref, comp_t_ref, proj_ref, out_ref)
    me = lax.axis_index("dim")
    samples, _, features = up_ref.shape
    slots = lax.broadcasted_iota(jnp.int32, (SHARD, features), 0)
    for at in range(samples):
        b = at ^ (me * piece)
        up = up_ref[at]
        linear_ref[at] = up.astype(F32) + dot_nt(up, mix_ref[...])
        hit = slots == slot_ref[:, pl.ds(pl.multiple_of(b * features, features), features)]
        onehot_ref[at * features:(at + 1) * features] = jnp.where(hit, 1.0, 0.0).T.astype(BF16)


def add_kernel(keep_ref, got_ref, out_ref):
    out_ref[...] = (keep_ref[...] + got_ref[...]).astype(out_ref.dtype)


def add(keep, got):
    return call(add_kernel, "add", (keep, got), [shape(keep.shape, BF16)], keep.size)[0]


def layer_back_kernel(*refs):
    *terms, pair_ref = refs
    rank = pair_ref.shape[1]
    for b in range(pair_ref.shape[0]):
        total = sum(term[b].astype(F32) for term in terms)
        centred, grads = total[:rank], total[rank:]
        inverse = 1.0 / jnp.sqrt(jnp.mean(centred * centred, axis=0, keepdims=True) + 1e-05)
        normed = centred * inverse
        moment = jnp.mean(grads * normed, axis=0, keepdims=True)
        pair_ref[b] = (inverse * (grads - normed * moment)).astype(BF16)


def table_kernel(start, piece, chains, count, has_total, *refs):
    av_ref, comp_t_ref, linear_ref, owner_ref, onehot_ref = refs[:5]
    pair_refs, refs = refs[5:5 + count], refs[5 + count:]
    if has_total:
        total_ref, refs = refs[0], refs[1:]
    *outs, masked = refs
    _, width, features = av_ref.shape
    me, here = lax.axis_index("dim"), lax.axis_index("dp")
    comp_t = comp_t_ref[...]
    owners = masked.shape[0] // width
    for n in range(count * piece):
        at = start + n
        b = at ^ (me * piece)
        back = pair_refs[n // piece][n % piece]
        both = dot_nt(av_ref[at], jnp.concatenate([comp_t, back])).astype(BF16)
        grad = linear_ref[at] + dot_nn(both, jnp.concatenate([back, comp_t]))
        grad = grad.astype(BF16)
        owner = owner_ref[:, pl.ds(pl.multiple_of(b * features, features), features)] ^ here
        for o in range(owners):
            mask = jnp.where(owner == o, 1.0, 0.0).astype(BF16)
            masked[o * width:(o + 1) * width, n * features:(n + 1) * features] = grad * mask
    added = dot_nn(masked[...], onehot_ref[start * features:(start + count * piece) * features])
    if has_total:
        added = added + total_ref[...]
    if chains is None:
        outs[0][...] = added
        return
    half = width // len(chains)
    for c, chain in enumerate(chains):
        for n, o in enumerate(halves(chain[1:])):
            at = (o ^ chain[0]) * width + c * half
            outs[2 * c][n] = added[at:at + half].astype(BF16)
            at = o * width + c * half
            outs[2 * c + 1][n] = added[at:at + half]


def table_part(j, piece, owners, chains, arrays, pairs, total):
    _, width, features = arrays[0].shape
    lookups = len(pairs) * piece * features
    if chains is None:
        shapes = [shape((owners * width, SHARD), F32)]
    else:
        part = (owners // 2, width // len(chains), SHARD)
        shapes = [shape(part, t) for _ in chains for t in (BF16, F32)]
    return call(
        functools.partial(table_kernel, j * piece, piece, chains, len(pairs), total is not None),
        "table_part",
        [*arrays, *pairs] + ([] if total is None else [total]),
        shapes,
        2 * lookups * width * owners * SHARD,
        scratch=[pltpu.VMEM((owners * width, lookups), BF16)],
    )


def fold_kernel(*refs):
    *terms, send_ref, keep_ref = refs
    half = keep_ref.shape[0]
    start = 0
    for keep, got in zip(terms[::2], terms[1::2]):
        stop = start + keep.shape[1]
        send_ref[:, start:stop] = (keep[half:] + got[half:].astype(F32)).astype(BF16)
        keep_ref[:, start:stop] = keep[:half] + got[:half].astype(F32)
        start = stop


def fold(terms):
    count, _, slots = terms[0].shape
    part = (count // 2, sum(keep.shape[1] for keep in terms[::2]), slots)
    return call(fold_kernel, "fold", terms, [shape(part, t) for t in (BF16, F32)], terms[0].size)


def finish_kernel(*refs):
    *terms, out_ref = refs
    start = 0
    for keep, got in zip(terms[::2], terms[1::2]):
        stop = start + keep.shape[1]
        out_ref[start:stop] = keep[0] + got[0].astype(F32)
        start = stop


def swap(x, bit, axis="dim"):
    return lax.ppermute(x, axis, [(i, i ^ bit) for i in range(lax.axis_size(axis))])


def after(x, *others):
    return lax.optimization_barrier((x, *others))[0]


def shards(attribute_vectors, upstream, compress, interact_proj, linear_mix, row_owner, row_slot):
    owners, peers = lax.axis_size("dp"), lax.axis_size("dim")
    samples, width, features = attribute_vectors.shape
    rank = compress.shape[1]
    piece = samples // peers
    quarter = samples // 4
    sample_flops = 6 * width * features * rank

    bits = bits_of(peers)
    core = bits[0]
    held = halves(bits)
    count = peers // 4
    low, high = held[:count], held[count:2 * count]

    owner, slot = row_owner.reshape(1, -1), row_slot.reshape(1, -1)
    part = shape((quarter, 2 * rank, features), F32)
    comp_t, proj = compress.T, interact_proj
    av, up = call(
        functools.partial(load_kernel, piece),
        "load",
        (attribute_vectors, upstream),
        [shape(upstream.shape, BF16)] * 2,
        0,
        limit=LOAD_LIMIT,
        specs=[HBM] * 2,
        scratch=[pltpu.SemaphoreType.DMA((2 * peers,))],
    )
    args = (av, up, comp_t, proj)
    (send_high,) = call(
        functools.partial(sums_kernel, [[j ^ core for j in high]], piece),
        "first_sums",
        args,
        [part],
        quarter * sample_flops,
    )
    got_high = swap(send_high, core)
    keep_high, send_low = call(
        functools.partial(sums_kernel, [high, [j ^ core for j in low]], piece),
        "sums",
        args,
        [part] * 2,
        2 * quarter * sample_flops,
    )
    got_low = swap(send_low, core)
    got = swap(add(keep_high, got_high), bits[1])
    keep_low, linear, onehot = call(
        functools.partial(prepare_kernel, low, piece),
        "prepare",
        (*args, linear_mix, slot),
        [part, shape(up.shape, F32), shape((samples * features, SHARD), BF16)],
        2 * samples * width * features * features,
    )
    arrays = (av, comp_t, linear, owner, onehot)

    terms = [keep_low, got_low, got]
    for bit in bits[2:]:
        keep = sum(term.astype(F32) for term in terms)
        half = keep.shape[0] // 2
        terms = [keep[:half], swap(keep[half:].astype(BF16), bit)]
    (pair,) = call(
        layer_back_kernel,
        "layer_back",
        terms,
        [shape((piece, rank, features), BF16)],
        32 * piece * rank * features,
    )

    low_bits = bits_of(owners)[:(owners.bit_length() - 1) // 2]
    high_bits = bits_of(owners)[len(low_bits):]
    chains = [low_bits + high_bits, high_bits[:1] + low_bits + high_bits[1:]]
    pairs = {0: pair}
    (total,) = table_part(0, piece, owners, None, arrays, [pair], None)
    for bit in reversed(bits[1:]):
        pairs.update({j ^ bit: swap(got, bit) for j, got in pairs.items()})
    for j in list(pairs):
        pairs[j] = after(pairs[j], total) if j else pair
        pairs[j ^ core] = swap(pairs[j], core)
    middle = [pairs[j] for j in range(1, peers - 1)]
    (total,) = table_part(1, piece, owners, None, arrays, middle, total)
    outs = table_part(peers - 1, piece, owners, chains, arrays, [pairs[peers - 1]], total)

    sums = [[outs[2 * c + 1], swap(outs[2 * c], chain[0], "dp")] for c, chain in enumerate(chains)]
    for step in range(1, len(low_bits) + 1):
        for c, chain in enumerate(chains):
            send, keep = fold(sums[c])
            sums[c] = [keep, swap(send, chain[step], "dp")]
    sums = sums[0] + sums[1]
    for bit in high_bits[1:]:
        send, keep = fold(sums)
        sums = [keep, swap(send, bit, "dp")]
    (out,) = call(finish_kernel, "finish", sums, [shape((width, SHARD), F32)], width * SHARD)
    return out


def solution(mesh):
    placed = (
        P("dp", "dim", None),
        P("dp", "dim", None),
        P(),
        P(None, "dim"),
        P(),
        P("dp", None),
        P("dp"),
    )
    return jax.shard_map(
        shards, mesh=mesh, in_specs=placed, out_specs=P("dim", "dp"), check_vma=False
    )
```

time: 41.2 us -> 40.8 us (level)
  waiting for transfers between devices: 16.6 us -> 17.1 us
  Pallas kernels: 9.25 us -> 8.77 us
    pallas_call x12 -> x13, Pallas kernels: 9.25 us -> 8.77 us  [call(): pl.pallas_call(kernel, in_specs=specs or [VMEM] * len(args), out_specs=[V...]
  transfers between devices with their start and end apart: 11 -> 11, of which waited for: 8 -> 7; matrix products, arithmetic and copies ran while one was open for 0% -> 0% of each run, Pallas kernels for 13% -> 12%
where the time goes in v6:
time: 40.8 us; the launch traced here: 40.7 us
  waiting for transfers between devices  17.1 us (42%)
  starting transfers between devices  14.7 us (36%)
  Pallas kernels  8.77 us (21%)
    ppermute x11, waiting for transfers between devices, swap(): lax.ppermute(x, axis, [(i, i ^ bit) for i in range(lax.axis_size(axis))])  17.1 us
    ppermute x11, starting transfers between devices, swap(): lax.ppermute(x, axis, [(i, i ^ bit) for i in range(lax.axis_size(axis))])  14.7 us
    pallas_call x13, Pallas kernels, call(): pl.pallas_call(kernel, in_specs=specs or [VMEM] * len(args), out_specs=[V...  8.77 us
  transfers between devices with their start and end apart: 11, of which 7 were waited for; matrix products, arithmetic and copies ran while one was open for 0% of the time, Pallas kernels for 12%

profile of v6, /device:TPU:0, one launch (start us, length us, event | category | flops | bytes accessed | tf_op | source)
XLA Modules:
  0.0 40.7 jit_solution(17752366771335830749)
XLA Ops:
  0.0 1.6 %load.1 = (bf16[16,128,256]{2,1,0:T(8,128)(2,1)S(1)}, bf16[16,128,256]{2,1,0:T(8,128)(2,1)S(1)}) custom-call(bf16[16,128,256]{2,1,0:T(8,128)(2,1)} %av_hbm.1, bf16[16,128,256]{2,1,0:T(8,128)(2,1)} %up_hbm.1), custom_call_target="tpu_custom_call" | custom-call | bytes 4194304 | tf_op jit(solution)/shard_map/load/pallas_call | solution.py:40
  1.6 0.4 %first_sums.1 = f32[4,128,256]{2,1,0:T(8,128)S(1)} custom-call(bf16[16,128,256]{2,1,0:T(8,128)(2,1)S(1)} %get-tuple-element.23.av_ref.refs_0_, bf16[16,128,256]{2,1,0:T(8,128)(2,1)S(1)} %get-tuple-element.24.up_ref, bf16[64,256]{1,0:T(8,128)(2,1)S(1)} %bitcast.3, bf16[64,128]{1,0:T(8,128)(2,1)S(1)} %copy-done.1), custom_call_target="tpu_custom_call" | custom-call | flops 50331648 | bytes 2670592 | tf_op jit(solution)/shard_map/first_sums/pallas_call | solution.py:40
  2.0 0.0 copy-start.3
  2.1 0.0 copy-start.4
  2.1 0.5 %collective-permute-start.1 = (f32[4,128,256]{2,1,0:T(8,128)S(1)}, f32[4,128,256]{2,1,0:T(8,128)S(1)}, u32[]{:S(2)}, u32[]{:S(2)}) collective-permute-start(f32[4,128,256]{2,1,0:T(8,128)S(1)} %first_sums.1), channel_id=1, source_target_pairs={{0,1},{1,0},{2,3},{3,2},{4,5},{5,4},{6,7},{7,6},{8,9},{9,8},{10,11... | collective-permute-start | bytes 1572872 | tf_op jit(solution)/shard_map/ppermute | solution.py:195
  2.6 0.6 %sums.1 = (f32[4,128,256]{2,1,0:T(8,128)S(1)}, f32[4,128,256]{2,1,0:T(8,128)S(1)}) custom-call(bf16[16,128,256]{2,1,0:T(8,128)(2,1)S(1)} %get-tuple-element.23.av_ref.refs_0_, bf16[16,128,256]{2,1,0:T(8,128)(2,1)S(1)} %get-tuple-element.24.up_ref, bf16[64,256]{1,0:T(8,128)(2,1)S(1)} %bitcast.4, bf16[64,128]{1,0:T(8,128)(2,1)S(1)} %copy-done.1), custom_call_target="tpu_custom_call" | custom-call | flops 100663296 | bytes 3194880 | tf_op jit(solution)/shard_map/sums/pallas_call | solution.py:40
  3.2 0.1 collective-permute-start
  3.3 0.8 %collective-permute-done.1.got_ref = f32[4,128,256]{2,1,0:T(8,128)S(1)} collective-permute-done((f32[4,128,256]{2,1,0:T(8,128)S(1)}, f32[4,128,256]{2,1,0:T(8,128)S(1)}, u32[]{:S(2)}, u32[]{:S(2)}) %collective-permute-start.1) | collective-permute-done | bytes 524320 | tf_op jit(solution)/shard_map/ppermute | solution.py:195
  4.2 0.0 copy-start.2
  4.2 3.0 %collective-permute-start.2 = (bf16[4,128,256]{2,1,0:T(8,128)(2,1)S(1)}, bf16[4,128,256]{2,1,0:T(8,128)(2,1)S(1)}, u32[]{:S(2)}, u32[]{:S(2)}) collective-permute-start(bf16[4,128,256]{2,1,0:T(8,128)(2,1)S(1)} %add.1), channel_id=1, source_target_pairs={{0,2},{1,3},{2,0},{3,1},{4,6},{5,7},{6,4},{7,5},{8,10},{9,11},{10,... | collective-permute-start | bytes 786440 | tf_op jit(solution)/shard_map/ppermute | solution.py:195
  7.1 1.3 %prepare.1 = (f32[4,128,256]{2,1,0:T(8,128)S(1)}, f32[16,128,256]{2,1,0:T(8,128)S(1)}, bf16[4096,256]{1,0:T(8,128)(2,1)S(1)}) custom-call(bf16[16,128,256]{2,1,0:T(8,128)(2,1)S(1)} %get-tuple-element.23.av_ref.refs_0_, bf16[16,128,256]{2,1,0:T(8,128)(2,1)S(1)} %get-tuple-element.24.up_ref, bf16[64,256]{1,0:T(8,128)(2,1)S(1)} %bitcast.5, ...), custom_call_target="tpu_custom_call" | custom-call | flops 268435456 | bytes 7012352 | tf_op jit(solution)/shard_map/prepare/pallas_call | solution.py:40
  8.4 0.0 collective-permute-done.refs_1_
  8.4 5.3 %collective-permute-done.2.refs_2_ = bf16[4,128,256]{2,1,0:T(8,128)(2,1)S(1)} collective-permute-done((bf16[4,128,256]{2,1,0:T(8,128)(2,1)S(1)}, bf16[4,128,256]{2,1,0:T(8,128)(2,1)S(1)}, u32[]{:S(2)}, u32[]{:S(2)}) %collective-permute-start.2) | collective-permute-done | bytes 262176 | tf_op jit(solution)/shard_map/ppermute | solution.py:195
  13.7 0.2 layer_back.1.refs_5_
  13.9 1.8 %collective-permute-start.3 = (bf16[4,64,256]{2,1,0:T(8,128)(2,1)S(1)}, bf16[4,64,256]{2,1,0:T(8,128)(2,1)S(1)}, u32[]{:S(2)}, u32[]{:S(2)}) collective-permute-start(bf16[4,64,256]{2,1,0:T(8,128)(2,1)S(1)} %layer_back.1.refs_5_), channel_id=1, source_target_pairs={{0,2},{1,3},{2,0},{3,1},{4,6},{5,7},{6,4},{7,5},{8,10},{9,11},{10,... | collective-permute-start | bytes 393224 | tf_op jit(solution)/shard_map/ppermute | solution.py:195
  15.7 1.1 %table_part.3.refs_7_ = f32[1024,256]{1,0:T(8,128)S(1)} custom-call(bf16[16,128,256]{2,1,0:T(8,128)(2,1)S(1)} %get-tuple-element.23.av_ref.refs_0_, bf16[64,256]{1,0:T(8,128)(2,1)S(1)} %bitcast.6, f32[16,128,256]{2,1,0:T(8,128)S(1)} %get-tuple-element.25.refs_2_, s32[1,4096]{1,0:T(1,128)S(1)} %bitcast.9, bf16[4096,256]{1,0:T(8,128)(2,1)S(1)} %get-tuple-element.26.refs_4_, ...), custom_call_target="tpu_custom_call" | custom-call | flops 536870912 | bytes 6471680 | tf_op jit(solution)/shard_map/table_part/pallas_call | solution.py:40
  16.8 2.2 %collective-permute-done.3.refs_6_ = bf16[4,64,256]{2,1,0:T(8,128)(2,1)S(1)} collective-permute-done((bf16[4,64,256]{2,1,0:T(8,128)(2,1)S(1)}, bf16[4,64,256]{2,1,0:T(8,128)(2,1)S(1)}, u32[]{:S(2)}, u32[]{:S(2)}) %collective-permute-start.3) | collective-permute-done | bytes 131104 | tf_op jit(solution)/shard_map/ppermute | solution.py:195
  19.0 0.0 collective-permute-start.4
  19.0 0.0 collective-permute-done.5.refs_5_
  19.0 1.8 %table_part.4.refs_6_ = f32[1024,256]{1,0:T(8,128)S(1)} custom-call(bf16[16,128,256]{2,1,0:T(8,128)(2,1)S(1)} %get-tuple-element.23.av_ref.refs_0_, bf16[64,256]{1,0:T(8,128)(2,1)S(1)} %bitcast.7, f32[16,128,256]{2,1,0:T(8,128)S(1)} %get-tuple-element.25.refs_2_, s32[1,4096]{1,0:T(1,128)S(1)} %bitcast.10, bf16[4096,256]{1,0:T(8,128)(2,1)S(1)} %get-tuple-element.26.refs_4_, ...), custom_call_target="tpu_custom_call" | custom-call | flops 1073741824 | bytes 7651328 | tf_op jit(solution)/shard_map/table_part/pallas_call | solution.py:40
  20.8 0.0 collective-permute-done.4.refs_5_
  20.8 1.1 %table_part.5 = (bf16[4,64,256]{2,1,0:T(8,128)(2,1)S(1)}, f32[4,64,256]{2,1,0:T(8,128)S(1)}, bf16[4,64,256]{2,1,0:T(8,128)(2,1)S(1)}, f32[4,64,256]{2,1,0:T(8,128)S(1)}) custom-call(bf16[16,128,256]{2,1,0:T(8,128)(2,1)S(1)} %get-tuple-element.23.av_ref.refs_0_, bf16[64,256]{1,0:T(8,128)(2,1)S(1)} %bitcast.8, f32[16,128,256]{2,1,0:T(8,128)S(1)} %get-tuple-element.25.refs_2_, ...), custom_call_target="tpu_custom_call" | custom-call | flops 536870912 | bytes 7258112 | tf_op jit(solution)/shard_map/table_part/pallas_call | solution.py:40
  21.9 1.7 %collective-permute-start.6 = (bf16[4,64,256]{2,1,0:T(8,128)(2,1)S(1)}, bf16[4,64,256]{2,1,0:T(8,128)(2,1)S(1)}, u32[]{:S(2)}, u32[]{:S(2)}) collective-permute-start(bf16[4,64,256]{2,1,0:T(8,128)(2,1)S(1)} %get-tuple-element.32), channel_id=1, source_target_pairs={{0,4},{4,0},{8,12},{12,8},{16,20},{20,16},{24,28},{28,24},{1,5},{5... | collective-permute-start | bytes 393224 | tf_op jit(solution)/shard_map/ppermute | solution.py:195
  23.6 1.6 %collective-permute-start.8 = (bf16[4,64,256]{2,1,0:T(8,128)(2,1)S(1)}, bf16[4,64,256]{2,1,0:T(8,128)(2,1)S(1)}, u32[]{:S(2)}, u32[]{:S(2)}) collective-permute-start(bf16[4,64,256]{2,1,0:T(8,128)(2,1)S(1)} %get-tuple-element.36), channel_id=1, source_target_pairs={{0,8},{4,12},{8,0},{12,4},{16,24},{20,28},{24,16},{28,20},{1,9},{5... | collective-permute-start | bytes 393224 | tf_op jit(solution)/shard_map/ppermute | solution.py:195
  25.2 2.7 %collective-permute-done.6.refs_1_ = bf16[4,64,256]{2,1,0:T(8,128)(2,1)S(1)} collective-permute-done((bf16[4,64,256]{2,1,0:T(8,128)(2,1)S(1)}, bf16[4,64,256]{2,1,0:T(8,128)(2,1)S(1)}, u32[]{:S(2)}, u32[]{:S(2)}) %collective-permute-start.6) | collective-permute-done | bytes 131104 | tf_op jit(solution)/shard_map/ppermute | solution.py:195
  27.9 1.8 %collective-permute-start.7 = (bf16[2,64,256]{2,1,0:T(8,128)(2,1)S(1)}, bf16[2,64,256]{2,1,0:T(8,128)(2,1)S(1)}, u32[]{:S(2)}, u32[]{:S(2)}) collective-permute-start(bf16[2,64,256]{2,1,0:T(8,128)(2,1)S(1)} %get-tuple-element.34), channel_id=1, source_target_pairs={{0,8},{4,12},{8,0},{12,4},{16,24},{20,28},{24,16},{28,20},{1,9},{5... | collective-permute-start | bytes 196616 | tf_op jit(solution)/shard_map/ppermute | solution.py:195
  29.7 1.6 %collective-permute-start.9 = (bf16[2,64,256]{2,1,0:T(8,128)(2,1)S(1)}, bf16[2,64,256]{2,1,0:T(8,128)(2,1)S(1)}, u32[]{:S(2)}, u32[]{:S(2)}) collective-permute-start(bf16[2,64,256]{2,1,0:T(8,128)(2,1)S(1)} %get-tuple-element.38), channel_id=1, source_target_pairs={{0,4},{4,0},{8,12},{12,8},{16,20},{20,16},{24,28},{28,24},{1,5},{5... | collective-permute-start | bytes 196616 | tf_op jit(solution)/shard_map/ppermute | solution.py:195
  31.3 0.9 %collective-permute-done.7.refs_1_ = bf16[2,64,256]{2,1,0:T(8,128)(2,1)S(1)} collective-permute-done((bf16[2,64,256]{2,1,0:T(8,128)(2,1)S(1)}, bf16[2,64,256]{2,1,0:T(8,128)(2,1)S(1)}, u32[]{:S(2)}, u32[]{:S(2)}) %collective-permute-start.7) | collective-permute-done | bytes 65568 | tf_op jit(solution)/shard_map/ppermute | solution.py:195
  32.2 1.8 %collective-permute-done.9.refs_3_ = bf16[2,64,256]{2,1,0:T(8,128)(2,1)S(1)} collective-permute-done((bf16[2,64,256]{2,1,0:T(8,128)(2,1)S(1)}, bf16[2,64,256]{2,1,0:T(8,128)(2,1)S(1)}, u32[]{:S(2)}, u32[]{:S(2)}) %collective-permute-start.9) | collective-permute-done | bytes 65568 | tf_op jit(solution)/shard_map/ppermute | solution.py:195
  34.1 2.6 %collective-permute-start.10 = (bf16[1,128,256]{2,1,0:T(8,128)(2,1)S(1)}, bf16[1,128,256]{2,1,0:T(8,128)(2,1)S(1)}, u32[]{:S(2)}, u32[]{:S(2)}) collective-permute-start(bf16[1,128,256]{2,1,0:T(8,128)(2,1)S(1)} %get-tuple-element.40), channel_id=1, source_target_pairs={{0,16},{4,20},{8,24},{12,28},{16,0},{20,4},{24,8},{28,12},{1,17},{... | collective-permute-start | bytes 196616 | tf_op jit(solution)/shard_map/ppermute | solution.py:195
  36.7 3.3 %collective-permute-done.10.refs_1_ = bf16[1,128,256]{2,1,0:T(8,128)(2,1)S(1)} collective-permute-done((bf16[1,128,256]{2,1,0:T(8,128)(2,1)S(1)}, bf16[1,128,256]{2,1,0:T(8,128)(2,1)S(1)}, u32[]{:S(2)}, u32[]{:S(2)}) %collective-permute-start.10) | collective-permute-done | bytes 65568 | tf_op jit(solution)/shard_map/ppermute | solution.py:195
  40.0 0.7 %finish.1 = f32[128,256]{1,0:T(8,128)} custom-call(f32[1,128,256]{2,1,0:T(8,128)S(1)} %get-tuple-element.39.refs_0_, bf16[1,128,256]{2,1,0:T(8,128)(2,1)S(1)} %collective-permute-done.10.refs_1_), custom_call_target="tpu_custom_call" | custom-call | flops 32768 | bytes 327680 | tf_op jit(solution)/shard_map/finish/pallas_call | solution.py:40
  (13 shorter events, 0.1 us)
Async XLA Ops:
  0.0 1.6 %copy-start.1 = (bf16[64,128]{1,0:T(8,128)(2,1)S(1)}, bf16[64,128]{1,0:T(8,128)(2,1)}, u32[]{:S(2)}) copy-start(bf16[64,128]{1,0:T(8,128)(2,1)} %proj_ref.5) | copy-start | bytes 49156
  0.0 1.6 %copy-start = (bf16[256,64]{0,1:T(8,128)(2,1)S(1)}, bf16[256,64]{0,1:T(8,128)(2,1)}, u32[]{:S(2)}) copy-start(bf16[256,64]{0,1:T(8,128)(2,1)} %param.9) | copy-start | bytes 98308
  2.0 5.1 %copy-start.3 = (bf16[256,256]{1,0:T(8,128)(2,1)S(1)}, bf16[256,256]{1,0:T(8,128)(2,1)}, u32[]{:S(2)}) copy-start(bf16[256,256]{1,0:T(8,128)(2,1)} %mix_ref.1) | copy-start | bytes 393220
  2.1 5.1 %copy-start.4 = (s32[4096]{0:T(1024)S(1)}, s32[4096]{0:T(1024)}, u32[]{:S(2)}) copy-start(s32[4096]{0:T(1024)} %param.13) | copy-start | bytes 49156
  2.1 2.1 %collective-permute-start.1 = (f32[4,128,256]{2,1,0:T(8,128)S(1)}, f32[4,128,256]{2,1,0:T(8,128)S(1)}, u32[]{:S(2)}, u32[]{:S(2)}) collective-permute-start(f32[4,128,256]{2,1,0:T(8,128)S(1)} %first_sums.1), channel_id=1, source_target_pairs={{0,1},{1,0},{2,3},{3,2},{4,5},{5,4},{6,7},{7,6},{8,9},{9,8},{10,11... | collective-permute-start | bytes 1572872 | tf_op jit(solution)/shard_map/ppermute | solution.py:195
  3.2 5.3 %collective-permute-start = (f32[4,128,256]{2,1,0:T(8,128)S(1)}, f32[4,128,256]{2,1,0:T(8,128)S(1)}, u32[]{:S(2)}, u32[]{:S(2)}) collective-permute-start(f32[4,128,256]{2,1,0:T(8,128)S(1)} %get-tuple-element.28), channel_id=1, source_target_pairs={{0,1},{1,0},{2,3},{3,2},{4,5},{5,4},{6,7},{7,6},{8,9},{9,8},{10,11... | collective-permute-start | bytes 1572872 | tf_op jit(solution)/shard_map/ppermute | solution.py:195
  4.2 11.6 %copy-start.2 = (s32[4096,1]{0,1:T(1,128)S(1)}, s32[4096,1]{0,1:T(1,128)}, u32[]{:S(2)}) copy-start(s32[4096,1]{0,1:T(1,128)} %param.12) | copy-start | bytes 49156
  4.2 9.6 %collective-permute-start.2 = (bf16[4,128,256]{2,1,0:T(8,128)(2,1)S(1)}, bf16[4,128,256]{2,1,0:T(8,128)(2,1)S(1)}, u32[]{:S(2)}, u32[]{:S(2)}) collective-permute-start(bf16[4,128,256]{2,1,0:T(8,128)(2,1)S(1)} %add.1), channel_id=1, source_target_pairs={{0,2},{1,3},{2,0},{3,1},{4,6},{5,7},{6,4},{7,5},{8,10},{9,11},{10,... | collective-permute-start | bytes 786440 | tf_op jit(solution)/shard_map/ppermute | solution.py:195
  13.9 5.1 %collective-permute-start.3 = (bf16[4,64,256]{2,1,0:T(8,128)(2,1)S(1)}, bf16[4,64,256]{2,1,0:T(8,128)(2,1)S(1)}, u32[]{:S(2)}, u32[]{:S(2)}) collective-permute-start(bf16[4,64,256]{2,1,0:T(8,128)(2,1)S(1)} %layer_back.1.refs_5_), channel_id=1, source_target_pairs={{0,2},{1,3},{2,0},{3,1},{4,6},{5,7},{6,4},{7,5},{8,10},{9,11},{10,... | collective-permute-start | bytes 393224 | tf_op jit(solution)/shard_map/ppermute | solution.py:195
  15.7 3.3 %collective-permute-start.5 = (bf16[4,64,256]{2,1,0:T(8,128)(2,1)S(1)}, bf16[4,64,256]{2,1,0:T(8,128)(2,1)S(1)}, u32[]{:S(2)}, u32[]{:S(2)}) collective-permute-start(bf16[4,64,256]{2,1,0:T(8,128)(2,1)S(1)} %layer_back.1.refs_5_), channel_id=1, source_target_pairs={{0,1},{1,0},{2,3},{3,2},{4,5},{5,4},{6,7},{7,6},{8,9},{9,8},{10,11... | collective-permute-start | bytes 393224 | tf_op jit(solution)/shard_map/ppermute | solution.py:195
  19.0 1.8 %collective-permute-start.4 = (bf16[4,64,256]{2,1,0:T(8,128)(2,1)S(1)}, bf16[4,64,256]{2,1,0:T(8,128)(2,1)S(1)}, u32[]{:S(2)}, u32[]{:S(2)}) collective-permute-start(bf16[4,64,256]{2,1,0:T(8,128)(2,1)S(1)} %collective-permute-done.3.refs_6_), channel_id=1, source_target_pairs={{0,1},{1,0},{2,3},{3,2},{4,5},{5,4},{6,7},{7,6},{8,9},{9,8},{10,11... | collective-permute-start | bytes 393224 | tf_op jit(solution)/shard_map/ppermute | solution.py:195
  21.9 6.0 %collective-permute-start.6 = (bf16[4,64,256]{2,1,0:T(8,128)(2,1)S(1)}, bf16[4,64,256]{2,1,0:T(8,128)(2,1)S(1)}, u32[]{:S(2)}, u32[]{:S(2)}) collective-permute-start(bf16[4,64,256]{2,1,0:T(8,128)(2,1)S(1)} %get-tuple-element.32), channel_id=1, source_target_pairs={{0,4},{4,0},{8,12},{12,8},{16,20},{20,16},{24,28},{28,24},{1,5},{5... | collective-permute-start | bytes 393224 | tf_op jit(solution)/shard_map/ppermute | solution.py:195
  23.6 6.1 %collective-permute-start.8 = (bf16[4,64,256]{2,1,0:T(8,128)(2,1)S(1)}, bf16[4,64,256]{2,1,0:T(8,128)(2,1)S(1)}, u32[]{:S(2)}, u32[]{:S(2)}) collective-permute-start(bf16[4,64,256]{2,1,0:T(8,128)(2,1)S(1)} %get-tuple-element.36), channel_id=1, source_target_pairs={{0,8},{4,12},{8,0},{12,4},{16,24},{20,28},{24,16},{28,20},{1,9},{5... | collective-permute-start | bytes 393224 | tf_op jit(solution)/shard_map/ppermute | solution.py:195
  27.9 4.3 %collective-permute-start.7 = (bf16[2,64,256]{2,1,0:T(8,128)(2,1)S(1)}, bf16[2,64,256]{2,1,0:T(8,128)(2,1)S(1)}, u32[]{:S(2)}, u32[]{:S(2)}) collective-permute-start(bf16[2,64,256]{2,1,0:T(8,128)(2,1)S(1)} %get-tuple-element.34), channel_id=1, source_target_pairs={{0,8},{4,12},{8,0},{12,4},{16,24},{20,28},{24,16},{28,20},{1,9},{5... | collective-permute-start | bytes 196616 | tf_op jit(solution)/shard_map/ppermute | solution.py:195
  29.7 4.3 %collective-permute-start.9 = (bf16[2,64,256]{2,1,0:T(8,128)(2,1)S(1)}, bf16[2,64,256]{2,1,0:T(8,128)(2,1)S(1)}, u32[]{:S(2)}, u32[]{:S(2)}) collective-permute-start(bf16[2,64,256]{2,1,0:T(8,128)(2,1)S(1)} %get-tuple-element.38), channel_id=1, source_target_pairs={{0,4},{4,0},{8,12},{12,8},{16,20},{20,16},{24,28},{28,24},{1,5},{5... | collective-permute-start | bytes 196616 | tf_op jit(solution)/shard_map/ppermute | solution.py:195
  34.1 5.9 %collective-permute-start.10 = (bf16[1,128,256]{2,1,0:T(8,128)(2,1)S(1)}, bf16[1,128,256]{2,1,0:T(8,128)(2,1)S(1)}, u32[]{:S(2)}, u32[]{:S(2)}) collective-permute-start(bf16[1,128,256]{2,1,0:T(8,128)(2,1)S(1)} %get-tuple-element.40), channel_id=1, source_target_pairs={{0,16},{4,20},{8,24},{12,28},{16,0},{20,4},{24,8},{28,12},{1,17},{... | collective-permute-start | bytes 196616 | tf_op jit(solution)/shard_map/ppermute | solution.py:195

commit v7 on v6

--- a/solution.py
+++ b/solution.py
@@ -63,12 +63,13 @@
 
 
 def width_sums(comp_t_ref, proj_ref, av, up, out_ref, at):
+    kind = out_ref.dtype
     rank = comp_t_ref.shape[0]
     reduced = dot_nt(comp_t_ref[...], av).astype(BF16)
     sums = dot_nn(reduced, av)
-    out_ref[at, :rank] = sums - jnp.mean(sums, axis=0, keepdims=True)
+    out_ref[at, :rank] = (sums - jnp.mean(sums, axis=0, keepdims=True)).astype(kind)
     grads = dot_nn(proj_ref[...], up)
-    out_ref[at, rank:] = grads - jnp.mean(grads, axis=0, keepdims=True)
+    out_ref[at, rank:] = (grads - jnp.mean(grads, axis=0, keepdims=True)).astype(kind)
 
 
 def sums_kernel(orders, piece, av_ref, up_ref, comp_t_ref, proj_ref, *out_refs):
@@ -92,7 +93,7 @@
 
 
 def add_kernel(keep_ref, got_ref, out_ref):
-    out_ref[...] = (keep_ref[...] + got_ref[...]).astype(out_ref.dtype)
+    out_ref[...] = (keep_ref[...] + got_ref[...].astype(F32)).astype(out_ref.dtype)
 
 
 def add(keep, got):
@@ -111,7 +112,7 @@
         pair_ref[b] = (inverse * (grads - normed * moment)).astype(BF16)
 
 
-def table_kernel(start, piece, chains, count, has_total, *refs):
+def table_kernel(start, piece, last, count, has_total, *refs):
     av_ref, comp_t_ref, linear_ref, owner_ref, onehot_ref = refs[:5]
     pair_refs, refs = refs[5:5 + count], refs[5 + count:]
     if has_total:
@@ -135,28 +136,22 @@
     added = dot_nn(masked[...], onehot_ref[start * features:(start + count * piece) * features])
     if has_total:
         added = added + total_ref[...]
-    if chains is None:
+    if not last:
         outs[0][...] = added
         return
-    half = width // len(chains)
-    for c, chain in enumerate(chains):
-        for n, o in enumerate(halves(chain[1:])):
-            at = (o ^ chain[0]) * width + c * half
-            outs[2 * c][n] = added[at:at + half].astype(BF16)
-            at = o * width + c * half
-            outs[2 * c + 1][n] = added[at:at + half]
-
-
-def table_part(j, piece, owners, chains, arrays, pairs, total):
+    for m, out in enumerate(outs):
+        out[...] = added[m * width:(m + 1) * width].astype(out.dtype)
+
+
+def table_part(j, piece, owners, last, arrays, pairs, total):
     _, width, features = arrays[0].shape
     lookups = len(pairs) * piece * features
-    if chains is None:
+    if last:
+        shapes = [shape((width, SHARD), F32 if m == 0 else BF16) for m in range(owners)]
+    else:
         shapes = [shape((owners * width, SHARD), F32)]
-    else:
-        part = (owners // 2, width // len(chains), SHARD)
-        shapes = [shape(part, t) for _ in chains for t in (BF16, F32)]
     return call(
-        functools.partial(table_kernel, j * piece, piece, chains, len(pairs), total is not None),
+        functools.partial(table_kernel, j * piece, piece, last, len(pairs), total is not None),
         "table_part",
         [*arrays, *pairs] + ([] if total is None else [total]),
         shapes,
@@ -165,30 +160,9 @@
     )
 
 
-def fold_kernel(*refs):
-    *terms, send_ref, keep_ref = refs
-    half = keep_ref.shape[0]
-    start = 0
-    for keep, got in zip(terms[::2], terms[1::2]):
-        stop = start + keep.shape[1]
-        send_ref[:, start:stop] = (keep[half:] + got[half:].astype(F32)).astype(BF16)
-        keep_ref[:, start:stop] = keep[:half] + got[:half].astype(F32)
-        start = stop
-
-
-def fold(terms):
-    count, _, slots = terms[0].shape
-    part = (count // 2, sum(keep.shape[1] for keep in terms[::2]), slots)
-    return call(fold_kernel, "fold", terms, [shape(part, t) for t in (BF16, F32)], terms[0].size)
-
-
 def finish_kernel(*refs):
     *terms, out_ref = refs
-    start = 0
-    for keep, got in zip(terms[::2], terms[1::2]):
-        stop = start + keep.shape[1]
-        out_ref[start:stop] = keep[0] + got[0].astype(F32)
-        start = stop
+    out_ref[...] = sum(term[...].astype(F32) for term in terms)
 
 
 def swap(x, bit, axis="dim"):
@@ -231,7 +205,7 @@
         functools.partial(sums_kernel, [[j ^ core for j in high]], piece),
         "first_sums",
         args,
-        [part],
+        [shape(part.shape, BF16)],
         quarter * sample_flops,
     )
     got_high = swap(send_high, core)
@@ -266,30 +240,19 @@
         32 * piece * rank * features,
     )
 
-    low_bits = bits_of(owners)[:(owners.bit_length() - 1) // 2]
-    high_bits = bits_of(owners)[len(low_bits):]
-    chains = [low_bits + high_bits, high_bits[:1] + low_bits + high_bits[1:]]
     pairs = {0: pair}
-    (total,) = table_part(0, piece, owners, None, arrays, [pair], None)
+    (total,) = table_part(0, piece, owners, False, arrays, [pair], None)
     for bit in reversed(bits[1:]):
         pairs.update({j ^ bit: swap(got, bit) for j, got in pairs.items()})
     for j in list(pairs):
         pairs[j] = after(pairs[j], total) if j else pair
         pairs[j ^ core] = swap(pairs[j], core)
     middle = [pairs[j] for j in range(1, peers - 1)]
-    (total,) = table_part(1, piece, owners, None, arrays, middle, total)
-    outs = table_part(peers - 1, piece, owners, chains, arrays, [pairs[peers - 1]], total)
-
-    sums = [[outs[2 * c + 1], swap(outs[2 * c], chain[0], "dp")] for c, chain in enumerate(chains)]
-    for step in range(1, len(low_bits) + 1):
-        for c, chain in enumerate(chains):
-            send, keep = fold(sums[c])
-            sums[c] = [keep, swap(send, chain[step], "dp")]
-    sums = sums[0] + sums[1]
-    for bit in high_bits[1:]:
-        send, keep = fold(sums)
-        sums = [keep, swap(send, bit, "dp")]
-    (out,) = call(finish_kernel, "finish", sums, [shape((width, SHARD), F32)], width * SHARD)
+    (total,) = table_part(1, piece, owners, False, arrays, middle, total)
+    own, *sent = table_part(peers - 1, piece, owners, True, arrays, [pairs[peers - 1]], total)
+
+    got = [swap(sent[m - 1], m, "dp") for m in range(owners - 1, 0, -1)]
+    (out,) = call(finish_kernel, "finish", (own, *got), [shape(own.shape, F32)], owners * own.size)
     return out
 
 

time: 40.8 us -> 39.1 us (0.958)
  waiting for transfers between devices: 17.1 us -> 13.3 us
  starting transfers between devices: 14.7 us -> 16.8 us
    ppermute x11 -> x13, waiting for transfers between devices: 17.1 us -> 13.3 us  [swap(): lax.ppermute(x, axis, [(i, i ^ bit) for i in range(lax.axis_size(axis))])]
    ppermute x11 -> x13, starting transfers between devices: 14.7 us -> 16.8 us  [swap(): lax.ppermute(x, axis, [(i, i ^ bit) for i in range(lax.axis_size(axis))])]
    pallas_call x13 -> x10, Pallas kernels: 8.77 us -> 8.75 us  [call(): pl.pallas_call(kernel, in_specs=specs or [VMEM] * len(args), out_specs=[V...]
  transfers between devices with their start and end apart: 11 -> 13, of which waited for: 7 -> 7; matrix products, arithmetic and copies ran while one was open for 0% -> 0% of each run, Pallas kernels for 12% -> 12%
where the time goes in v7:
time: 39.1 us; the launch traced here: 39 us
  starting transfers between devices  16.8 us (43%)
  waiting for transfers between devices  13.3 us (34%)
  Pallas kernels  8.75 us (22%)
    ppermute x13, starting transfers between devices, swap(): lax.ppermute(x, axis, [(i, i ^ bit) for i in range(lax.axis_size(axis))])  16.8 us
    ppermute x13, waiting for transfers between devices, swap(): lax.ppermute(x, axis, [(i, i ^ bit) for i in range(lax.axis_size(axis))])  13.3 us
    pallas_call x10, Pallas kernels, call(): pl.pallas_call(kernel, in_specs=specs or [VMEM] * len(args), out_specs=[V...  8.75 us
  transfers between devices with their start and end apart: 13, of which 7 were waited for; matrix products, arithmetic and copies ran while one was open for 0% of the time, Pallas kernels for 12%

profile of v7, /device:TPU:0, one launch (start us, length us, event | category | flops | bytes accessed | tf_op | source)
XLA Modules:
  0.0 39.0 jit_solution(16233232368956172667)
XLA Ops:
  0.0 1.6 %load.1 = (bf16[16,128,256]{2,1,0:T(8,128)(2,1)S(1)}, bf16[16,128,256]{2,1,0:T(8,128)(2,1)S(1)}) custom-call(bf16[16,128,256]{2,1,0:T(8,128)(2,1)} %av_hbm.1, bf16[16,128,256]{2,1,0:T(8,128)(2,1)} %up_hbm.1), custom_call_target="tpu_custom_call" | custom-call | bytes 4194304 | tf_op jit(solution)/shard_map/load/pallas_call | solution.py:40
  1.6 0.4 %first_sums.1 = bf16[4,128,256]{2,1,0:T(8,128)(2,1)S(1)} custom-call(bf16[16,128,256]{2,1,0:T(8,128)(2,1)S(1)} %get-tuple-element.21.av_ref.refs_0_, bf16[16,128,256]{2,1,0:T(8,128)(2,1)S(1)} %get-tuple-element.22.up_ref, bf16[64,256]{1,0:T(8,128)(2,1)S(1)} %bitcast.3, bf16[64,128]{1,0:T(8,128)(2,1)S(1)} %copy-done.1), custom_call_target="tpu_custom_call" | custom-call | flops 50331648 | bytes 2408448 | tf_op jit(solution)/shard_map/first_sums/pallas_call | solution.py:40
  2.0 0.0 copy-start.3
  2.1 0.0 copy-start.4
  2.1 0.5 %collective-permute-start.1 = (bf16[4,128,256]{2,1,0:T(8,128)(2,1)S(1)}, bf16[4,128,256]{2,1,0:T(8,128)(2,1)S(1)}, u32[]{:S(2)}, u32[]{:S(2)}) collective-permute-start(bf16[4,128,256]{2,1,0:T(8,128)(2,1)S(1)} %first_sums.1), channel_id=1, source_target_pairs={{0,1},{1,0},{2,3},{3,2},{4,5},{5,4},{6,7},{7,6},{8,9},{9,8},{10,11... | collective-permute-start | bytes 786440 | tf_op jit(solution)/shard_map/ppermute | solution.py:169
  2.6 0.6 %sums.1 = (f32[4,128,256]{2,1,0:T(8,128)S(1)}, f32[4,128,256]{2,1,0:T(8,128)S(1)}) custom-call(bf16[16,128,256]{2,1,0:T(8,128)(2,1)S(1)} %get-tuple-element.21.av_ref.refs_0_, bf16[16,128,256]{2,1,0:T(8,128)(2,1)S(1)} %get-tuple-element.22.up_ref, bf16[64,256]{1,0:T(8,128)(2,1)S(1)} %bitcast.4, bf16[64,128]{1,0:T(8,128)(2,1)S(1)} %copy-done.1), custom_call_target="tpu_custom_call" | custom-call | flops 100663296 | bytes 3194880 | tf_op jit(solution)/shard_map/sums/pallas_call | solution.py:40
  3.2 0.1 collective-permute-start
  3.3 0.5 %collective-permute-done.1.got_ref = bf16[4,128,256]{2,1,0:T(8,128)(2,1)S(1)} collective-permute-done((bf16[4,128,256]{2,1,0:T(8,128)(2,1)S(1)}, bf16[4,128,256]{2,1,0:T(8,128)(2,1)S(1)}, u32[]{:S(2)}, u32[]{:S(2)}) %collective-permute-start.1) | collective-permute-done | bytes 262176 | tf_op jit(solution)/shard_map/ppermute | solution.py:169
  3.8 0.0 copy-start.2
  3.8 3.0 %collective-permute-start.2 = (bf16[4,128,256]{2,1,0:T(8,128)(2,1)S(1)}, bf16[4,128,256]{2,1,0:T(8,128)(2,1)S(1)}, u32[]{:S(2)}, u32[]{:S(2)}) collective-permute-start(bf16[4,128,256]{2,1,0:T(8,128)(2,1)S(1)} %add.1), channel_id=1, source_target_pairs={{0,2},{1,3},{2,0},{3,1},{4,6},{5,7},{6,4},{7,5},{8,10},{9,11},{10,... | collective-permute-start | bytes 786440 | tf_op jit(solution)/shard_map/ppermute | solution.py:169
  6.8 1.3 %prepare.1 = (f32[4,128,256]{2,1,0:T(8,128)S(1)}, f32[16,128,256]{2,1,0:T(8,128)S(1)}, bf16[4096,256]{1,0:T(8,128)(2,1)S(1)}) custom-call(bf16[16,128,256]{2,1,0:T(8,128)(2,1)S(1)} %get-tuple-element.21.av_ref.refs_0_, bf16[16,128,256]{2,1,0:T(8,128)(2,1)S(1)} %get-tuple-element.22.up_ref, bf16[64,256]{1,0:T(8,128)(2,1)S(1)} %bitcast.5, ...), custom_call_target="tpu_custom_call" | custom-call | flops 268435456 | bytes 7012352 | tf_op jit(solution)/shard_map/prepare/pallas_call | solution.py:40
  8.1 5.3 %collective-permute-done.2.refs_2_ = bf16[4,128,256]{2,1,0:T(8,128)(2,1)S(1)} collective-permute-done((bf16[4,128,256]{2,1,0:T(8,128)(2,1)S(1)}, bf16[4,128,256]{2,1,0:T(8,128)(2,1)S(1)}, u32[]{:S(2)}, u32[]{:S(2)}) %collective-permute-start.2) | collective-permute-done | bytes 262176 | tf_op jit(solution)/shard_map/ppermute | solution.py:169
  13.4 0.0 collective-permute-done.refs_1_
  13.4 0.2 layer_back.1.refs_5_
  13.5 1.8 %collective-permute-start.3 = (bf16[4,64,256]{2,1,0:T(8,128)(2,1)S(1)}, bf16[4,64,256]{2,1,0:T(8,128)(2,1)S(1)}, u32[]{:S(2)}, u32[]{:S(2)}) collective-permute-start(bf16[4,64,256]{2,1,0:T(8,128)(2,1)S(1)} %layer_back.1.refs_5_), channel_id=1, source_target_pairs={{0,2},{1,3},{2,0},{3,1},{4,6},{5,7},{6,4},{7,5},{8,10},{9,11},{10,... | collective-permute-start | bytes 393224 | tf_op jit(solution)/shard_map/ppermute | solution.py:169
  15.4 0.0 collective-permute-start.5
  15.4 1.1 %table_part.3.refs_7_ = f32[1024,256]{1,0:T(8,128)S(1)} custom-call(bf16[16,128,256]{2,1,0:T(8,128)(2,1)S(1)} %get-tuple-element.21.av_ref.refs_0_, bf16[64,256]{1,0:T(8,128)(2,1)S(1)} %bitcast.6, f32[16,128,256]{2,1,0:T(8,128)S(1)} %get-tuple-element.23.refs_2_, s32[1,4096]{1,0:T(1,128)S(1)} %bitcast.9, bf16[4096,256]{1,0:T(8,128)(2,1)S(1)} %get-tuple-element.24.refs_4_, ...), custom_call_target="tpu_custom_call" | custom-call | flops 536870912 | bytes 6471680 | tf_op jit(solution)/shard_map/table_part/pallas_call | solution.py:40
  16.5 2.2 %collective-permute-done.3.refs_6_ = bf16[4,64,256]{2,1,0:T(8,128)(2,1)S(1)} collective-permute-done((bf16[4,64,256]{2,1,0:T(8,128)(2,1)S(1)}, bf16[4,64,256]{2,1,0:T(8,128)(2,1)S(1)}, u32[]{:S(2)}, u32[]{:S(2)}) %collective-permute-start.3) | collective-permute-done | bytes 131104 | tf_op jit(solution)/shard_map/ppermute | solution.py:169
  18.6 1.7 %table_part.4.refs_6_ = f32[1024,256]{1,0:T(8,128)S(1)} custom-call(bf16[16,128,256]{2,1,0:T(8,128)(2,1)S(1)} %get-tuple-element.21.av_ref.refs_0_, bf16[64,256]{1,0:T(8,128)(2,1)S(1)} %bitcast.7, f32[16,128,256]{2,1,0:T(8,128)S(1)} %get-tuple-element.23.refs_2_, s32[1,4096]{1,0:T(1,128)S(1)} %bitcast.10, bf16[4096,256]{1,0:T(8,128)(2,1)S(1)} %get-tuple-element.24.refs_4_, ...), custom_call_target="tpu_custom_call" | custom-call | flops 1073741824 | bytes 7651328 | tf_op jit(solution)/shard_map/table_part/pallas_call | solution.py:40
  20.4 1.1 %table_part.5 = (f32[128,256]{1,0:T(8,128)S(1)}, bf16[128,256]{1,0:T(8,128)(2,1)S(1)}, bf16[128,256]{1,0:T(8,128)(2,1)S(1)}, bf16[128,256]{1,0:T(8,128)(2,1)S(1)...) custom-call(bf16[16,128,256]{2,1,0:T(8,128)(2,1)S(1)} %get-tuple-ele, ...), custom_call_target="tpu_custom_call" | custom-call | flops 536870912 | bytes 7061504 | tf_op jit(solution)/shard_map/table_part/pallas_call | solution.py:40
  21.5 4.8 %collective-permute-start.6 = (bf16[128,256]{1,0:T(8,128)(2,1)S(1)}, bf16[128,256]{1,0:T(8,128)(2,1)S(1)}, u32[]{:S(2)}, u32[]{:S(2)}) collective-permute-start(bf16[128,256]{1,0:T(8,128)(2,1)S(1)} %get-tuple-element.30), channel_id=1, source_target_pairs={{0,28},{4,24},{8,20},{12,16},{16,12},{20,8},{24,4},{28,0},{1,29},{... | collective-permute-start | bytes 196616 | tf_op jit(solution)/shard_map/ppermute | solution.py:169
  26.3 0.2 collective-permute-start.7
  26.5 0.8 %collective-permute-start.8 = (bf16[128,256]{1,0:T(8,128)(2,1)S(1)}, bf16[128,256]{1,0:T(8,128)(2,1)S(1)}, u32[]{:S(2)}, u32[]{:S(2)}) collective-permute-start(bf16[128,256]{1,0:T(8,128)(2,1)S(1)} %get-tuple-element.32), channel_id=1, source_target_pairs={{0,20},{4,16},{8,28},{12,24},{16,4},{20,0},{24,12},{28,8},{1,21},{... | collective-permute-start | bytes 196616 | tf_op jit(solution)/shard_map/ppermute | solution.py:169
  27.3 2.0 %collective-permute-start.9 = (bf16[128,256]{1,0:T(8,128)(2,1)S(1)}, bf16[128,256]{1,0:T(8,128)(2,1)S(1)}, u32[]{:S(2)}, u32[]{:S(2)}) collective-permute-start(bf16[128,256]{1,0:T(8,128)(2,1)S(1)} %get-tuple-element.33), channel_id=1, source_target_pairs={{0,16},{4,20},{8,24},{12,28},{16,0},{20,4},{24,8},{28,12},{1,17},{... | collective-permute-start | bytes 196616 | tf_op jit(solution)/shard_map/ppermute | solution.py:169
  29.3 2.3 %collective-permute-start.10 = (bf16[128,256]{1,0:T(8,128)(2,1)S(1)}, bf16[128,256]{1,0:T(8,128)(2,1)S(1)}, u32[]{:S(2)}, u32[]{:S(2)}) collective-permute-start(bf16[128,256]{1,0:T(8,128)(2,1)S(1)} %get-tuple-element.34), channel_id=1, source_target_pairs={{0,12},{4,8},{8,4},{12,0},{16,28},{20,24},{24,20},{28,16},{1,13},{... | collective-permute-start | bytes 196616 | tf_op jit(solution)/shard_map/ppermute | solution.py:169
  31.6 0.8 %collective-permute-start.11 = (bf16[128,256]{1,0:T(8,128)(2,1)S(1)}, bf16[128,256]{1,0:T(8,128)(2,1)S(1)}, u32[]{:S(2)}, u32[]{:S(2)}) collective-permute-start(bf16[128,256]{1,0:T(8,128)(2,1)S(1)} %get-tuple-element.35), channel_id=1, source_target_pairs={{0,8},{4,12},{8,0},{12,4},{16,24},{20,28},{24,16},{28,20},{1,9},{5... | collective-permute-start | bytes 196616 | tf_op jit(solution)/shard_map/ppermute | solution.py:169
  32.3 0.7 %collective-permute-done.7.refs_2_ = bf16[128,256]{1,0:T(8,128)(2,1)S(1)} collective-permute-done((bf16[128,256]{1,0:T(8,128)(2,1)S(1)}, bf16[128,256]{1,0:T(8,128)(2,1)S(1)}, u32[]{:S(2)}, u32[]{:S(2)}) %collective-permute-start.7) | collective-permute-done | bytes 65568 | tf_op jit(solution)/shard_map/ppermute | solution.py:169
  33.1 0.5 %collective-permute-start.12 = (bf16[128,256]{1,0:T(8,128)(2,1)S(1)}, bf16[128,256]{1,0:T(8,128)(2,1)S(1)}, u32[]{:S(2)}, u32[]{:S(2)}) collective-permute-start(bf16[128,256]{1,0:T(8,128)(2,1)S(1)} %get-tuple-element.36), channel_id=1, source_target_pairs={{0,4},{4,0},{8,12},{12,8},{16,20},{20,16},{24,28},{28,24},{1,5},{5... | collective-permute-start | bytes 196616 | tf_op jit(solution)/shard_map/ppermute | solution.py:169
  33.6 2.7 %collective-permute-done.8.refs_3_ = bf16[128,256]{1,0:T(8,128)(2,1)S(1)} collective-permute-done((bf16[128,256]{1,0:T(8,128)(2,1)S(1)}, bf16[128,256]{1,0:T(8,128)(2,1)S(1)}, u32[]{:S(2)}, u32[]{:S(2)}) %collective-permute-start.8) | collective-permute-done | bytes 65568 | tf_op jit(solution)/shard_map/ppermute | solution.py:169
  36.3 1.8 %collective-permute-done.9.refs_4_ = bf16[128,256]{1,0:T(8,128)(2,1)S(1)} collective-permute-done((bf16[128,256]{1,0:T(8,128)(2,1)S(1)}, bf16[128,256]{1,0:T(8,128)(2,1)S(1)}, u32[]{:S(2)}, u32[]{:S(2)}) %collective-permute-start.9) | collective-permute-done | bytes 65568 | tf_op jit(solution)/shard_map/ppermute | solution.py:169
  38.1 0.1 collective-permute-done.11.refs_6_
  38.3 0.7 %finish.1 = f32[128,256]{1,0:T(8,128)} custom-call(f32[128,256]{1,0:T(8,128)S(1)} %get-tuple-element.29.refs_0_, bf16[128,256]{1,0:T(8,128)(2,1)S(1)} %collective-permute-done.6.refs_1_, bf16[128,256]{1,0:T(8,128)(2,1)S(1)} %collective-permute-done.7.refs_2_, bf16[128,256]{1,0:T(8,128)(2,1)S(1)} %collective-permute-done.8.refs_3_, ...), custom_call_target="tpu_custom_call" | custom-call | flops 262144 | bytes 720896 | tf_op jit(solution)/shard_map/finish/pallas_call | solution.py:40
  (14 shorter events, 0.1 us)
Async XLA Ops:
  0.0 1.6 %copy-start.1 = (bf16[64,128]{1,0:T(8,128)(2,1)S(1)}, bf16[64,128]{1,0:T(8,128)(2,1)}, u32[]{:S(2)}) copy-start(bf16[64,128]{1,0:T(8,128)(2,1)} %proj_ref.5) | copy-start | bytes 49156
  0.0 1.6 %copy-start = (bf16[256,64]{0,1:T(8,128)(2,1)S(1)}, bf16[256,64]{0,1:T(8,128)(2,1)}, u32[]{:S(2)}) copy-start(bf16[256,64]{0,1:T(8,128)(2,1)} %param.9) | copy-start | bytes 98308
  2.0 4.7 %copy-start.3 = (bf16[256,256]{1,0:T(8,128)(2,1)S(1)}, bf16[256,256]{1,0:T(8,128)(2,1)}, u32[]{:S(2)}) copy-start(bf16[256,256]{1,0:T(8,128)(2,1)} %mix_ref.1) | copy-start | bytes 393220
  2.1 4.7 %copy-start.4 = (s32[4096]{0:T(1024)S(1)}, s32[4096]{0:T(1024)}, u32[]{:S(2)}) copy-start(s32[4096]{0:T(1024)} %param.13) | copy-start | bytes 49156
  2.1 1.7 %collective-permute-start.1 = (bf16[4,128,256]{2,1,0:T(8,128)(2,1)S(1)}, bf16[4,128,256]{2,1,0:T(8,128)(2,1)S(1)}, u32[]{:S(2)}, u32[]{:S(2)}) collective-permute-start(bf16[4,128,256]{2,1,0:T(8,128)(2,1)S(1)} %first_sums.1), channel_id=1, source_target_pairs={{0,1},{1,0},{2,3},{3,2},{4,5},{5,4},{6,7},{7,6},{8,9},{9,8},{10,11... | collective-permute-start | bytes 786440 | tf_op jit(solution)/shard_map/ppermute | solution.py:169
  3.2 10.2 %collective-permute-start = (f32[4,128,256]{2,1,0:T(8,128)S(1)}, f32[4,128,256]{2,1,0:T(8,128)S(1)}, u32[]{:S(2)}, u32[]{:S(2)}) collective-permute-start(f32[4,128,256]{2,1,0:T(8,128)S(1)} %get-tuple-element.26), channel_id=1, source_target_pairs={{0,1},{1,0},{2,3},{3,2},{4,5},{5,4},{6,7},{7,6},{8,9},{9,8},{10,11... | collective-permute-start | bytes 1572872 | tf_op jit(solution)/shard_map/ppermute | solution.py:169
  3.8 11.6 %copy-start.2 = (s32[4096,1]{0,1:T(1,128)S(1)}, s32[4096,1]{0,1:T(1,128)}, u32[]{:S(2)}) copy-start(s32[4096,1]{0,1:T(1,128)} %param.12) | copy-start | bytes 49156
  3.8 9.6 %collective-permute-start.2 = (bf16[4,128,256]{2,1,0:T(8,128)(2,1)S(1)}, bf16[4,128,256]{2,1,0:T(8,128)(2,1)S(1)}, u32[]{:S(2)}, u32[]{:S(2)}) collective-permute-start(bf16[4,128,256]{2,1,0:T(8,128)(2,1)S(1)} %add.1), channel_id=1, source_target_pairs={{0,2},{1,3},{2,0},{3,1},{4,6},{5,7},{6,4},{7,5},{8,10},{9,11},{10,... | collective-permute-start | bytes 786440 | tf_op jit(solution)/shard_map/ppermute | solution.py:169
  13.5 5.1 %collective-permute-start.3 = (bf16[4,64,256]{2,1,0:T(8,128)(2,1)S(1)}, bf16[4,64,256]{2,1,0:T(8,128)(2,1)S(1)}, u32[]{:S(2)}, u32[]{:S(2)}) collective-permute-start(bf16[4,64,256]{2,1,0:T(8,128)(2,1)S(1)} %layer_back.1.refs_5_), channel_id=1, source_target_pairs={{0,2},{1,3},{2,0},{3,1},{4,6},{5,7},{6,4},{7,5},{8,10},{9,11},{10,... | collective-permute-start | bytes 393224 | tf_op jit(solution)/shard_map/ppermute | solution.py:169
  15.4 3.3 %collective-permute-start.5 = (bf16[4,64,256]{2,1,0:T(8,128)(2,1)S(1)}, bf16[4,64,256]{2,1,0:T(8,128)(2,1)S(1)}, u32[]{:S(2)}, u32[]{:S(2)}) collective-permute-start(bf16[4,64,256]{2,1,0:T(8,128)(2,1)S(1)} %layer_back.1.refs_5_), channel_id=1, source_target_pairs={{0,1},{1,0},{2,3},{3,2},{4,5},{5,4},{6,7},{7,6},{8,9},{9,8},{10,11... | collective-permute-start | bytes 393224 | tf_op jit(solution)/shard_map/ppermute | solution.py:169
  18.6 1.8 %collective-permute-start.4 = (bf16[4,64,256]{2,1,0:T(8,128)(2,1)S(1)}, bf16[4,64,256]{2,1,0:T(8,128)(2,1)S(1)}, u32[]{:S(2)}, u32[]{:S(2)}) collective-permute-start(bf16[4,64,256]{2,1,0:T(8,128)(2,1)S(1)} %collective-permute-done.3.refs_6_), channel_id=1, source_target_pairs={{0,1},{1,0},{2,3},{3,2},{4,5},{5,4},{6,7},{7,6},{8,9},{9,8},{10,11... | collective-permute-start | bytes 393224 | tf_op jit(solution)/shard_map/ppermute | solution.py:169
  21.5 10.0 %collective-permute-start.6 = (bf16[128,256]{1,0:T(8,128)(2,1)S(1)}, bf16[128,256]{1,0:T(8,128)(2,1)S(1)}, u32[]{:S(2)}, u32[]{:S(2)}) collective-permute-start(bf16[128,256]{1,0:T(8,128)(2,1)S(1)} %get-tuple-element.30), channel_id=1, source_target_pairs={{0,28},{4,24},{8,20},{12,16},{16,12},{20,8},{24,4},{28,0},{1,29},{... | collective-permute-start | bytes 196616 | tf_op jit(solution)/shard_map/ppermute | solution.py:169
  26.3 6.8 %collective-permute-start.7 = (bf16[128,256]{1,0:T(8,128)(2,1)S(1)}, bf16[128,256]{1,0:T(8,128)(2,1)S(1)}, u32[]{:S(2)}, u32[]{:S(2)}) collective-permute-start(bf16[128,256]{1,0:T(8,128)(2,1)S(1)} %get-tuple-element.31), channel_id=1, source_target_pairs={{0,24},{4,28},{8,16},{12,20},{16,8},{20,12},{24,0},{28,4},{1,25},{... | collective-permute-start | bytes 196616 | tf_op jit(solution)/shard_map/ppermute | solution.py:169
  26.5 9.8 %collective-permute-start.8 = (bf16[128,256]{1,0:T(8,128)(2,1)S(1)}, bf16[128,256]{1,0:T(8,128)(2,1)S(1)}, u32[]{:S(2)}, u32[]{:S(2)}) collective-permute-start(bf16[128,256]{1,0:T(8,128)(2,1)S(1)} %get-tuple-element.32), channel_id=1, source_target_pairs={{0,20},{4,16},{8,28},{12,24},{16,4},{20,0},{24,12},{28,8},{1,21},{... | collective-permute-start | bytes 196616 | tf_op jit(solution)/shard_map/ppermute | solution.py:169
  27.3 10.9 %collective-permute-start.9 = (bf16[128,256]{1,0:T(8,128)(2,1)S(1)}, bf16[128,256]{1,0:T(8,128)(2,1)S(1)}, u32[]{:S(2)}, u32[]{:S(2)}) collective-permute-start(bf16[128,256]{1,0:T(8,128)(2,1)S(1)} %get-tuple-element.33), channel_id=1, source_target_pairs={{0,16},{4,20},{8,24},{12,28},{16,0},{20,4},{24,8},{28,12},{1,17},{... | collective-permute-start | bytes 196616 | tf_op jit(solution)/shard_map/ppermute | solution.py:169
  29.3 8.9 %collective-permute-start.10 = (bf16[128,256]{1,0:T(8,128)(2,1)S(1)}, bf16[128,256]{1,0:T(8,128)(2,1)S(1)}, u32[]{:S(2)}, u32[]{:S(2)}) collective-permute-start(bf16[128,256]{1,0:T(8,128)(2,1)S(1)} %get-tuple-element.34), channel_id=1, source_target_pairs={{0,12},{4,8},{8,4},{12,0},{16,28},{20,24},{24,20},{28,16},{1,13},{... | collective-permute-start | bytes 196616 | tf_op jit(solution)/shard_map/ppermute | solution.py:169
  31.6 6.7 %collective-permute-start.11 = (bf16[128,256]{1,0:T(8,128)(2,1)S(1)}, bf16[128,256]{1,0:T(8,128)(2,1)S(1)}, u32[]{:S(2)}, u32[]{:S(2)}) collective-permute-start(bf16[128,256]{1,0:T(8,128)(2,1)S(1)} %get-tuple-element.35), channel_id=1, source_target_pairs={{0,8},{4,12},{8,0},{12,4},{16,24},{20,28},{24,16},{28,20},{1,9},{5... | collective-permute-start | bytes 196616 | tf_op jit(solution)/shard_map/ppermute | solution.py:169
  33.1 5.2 %collective-permute-start.12 = (bf16[128,256]{1,0:T(8,128)(2,1)S(1)}, bf16[128,256]{1,0:T(8,128)(2,1)S(1)}, u32[]{:S(2)}, u32[]{:S(2)}) collective-permute-start(bf16[128,256]{1,0:T(8,128)(2,1)S(1)} %get-tuple-element.36), channel_id=1, source_target_pairs={{0,4},{4,0},{8,12},{12,8},{16,20},{20,16},{24,28},{28,24},{1,5},{5... | collective-permute-start | bytes 196616 | tf_op jit(solution)/shard_map/ppermute | solution.py:169

commit v8 on v7

--- a/solution.py
+++ b/solution.py
@@ -112,57 +112,81 @@
         pair_ref[b] = (inverse * (grads - normed * moment)).astype(BF16)
 
 
-def table_kernel(start, piece, last, count, has_total, *refs):
+def lookup_mask(owner_ref, piece, features, at):
+    b = at ^ (lax.axis_index("dim") * piece)
+    lookups = pl.ds(pl.multiple_of(b * features, features), features)
+    return owner_ref[:, lookups] ^ lax.axis_index("dp")
+
+
+def spread(grad, distance, owners, masked, n):
+    width, features = grad.shape
+    for o, m in enumerate(owners):
+        mask = jnp.where(distance == m, 1.0, 0.0).astype(BF16)
+        masked[o * width:(o + 1) * width, n * features:(n + 1) * features] = grad * mask
+
+
+def table_kernel(start, piece, owners, far, count, has_total, *refs):
     av_ref, comp_t_ref, linear_ref, owner_ref, onehot_ref = refs[:5]
     pair_refs, refs = refs[5:5 + count], refs[5 + count:]
     if has_total:
         total_ref, refs = refs[0], refs[1:]
     *outs, masked = refs
     _, width, features = av_ref.shape
-    me, here = lax.axis_index("dim"), lax.axis_index("dp")
     comp_t = comp_t_ref[...]
-    owners = masked.shape[0] // width
     for n in range(count * piece):
         at = start + n
-        b = at ^ (me * piece)
         back = pair_refs[n // piece][n % piece]
         both = dot_nt(av_ref[at], jnp.concatenate([comp_t, back])).astype(BF16)
         grad = linear_ref[at] + dot_nn(both, jnp.concatenate([back, comp_t]))
         grad = grad.astype(BF16)
-        owner = owner_ref[:, pl.ds(pl.multiple_of(b * features, features), features)] ^ here
-        for o in range(owners):
-            mask = jnp.where(owner == o, 1.0, 0.0).astype(BF16)
-            masked[o * width:(o + 1) * width, n * features:(n + 1) * features] = grad * mask
+        if far:
+            outs[-1][n] = grad
+        spread(grad, lookup_mask(owner_ref, piece, features, at), owners, masked, n)
     added = dot_nn(masked[...], onehot_ref[start * features:(start + count * piece) * features])
     if has_total:
-        added = added + total_ref[...]
-    if not last:
+        added = added + total_ref[owners[0] * width:(owners[-1] + 1) * width]
+    if not far:
         outs[0][...] = added
         return
-    for m, out in enumerate(outs):
-        out[...] = added[m * width:(m + 1) * width].astype(out.dtype)
-
-
-def table_part(j, piece, owners, last, arrays, pairs, total):
+    for o in range(len(owners)):
+        outs[o][...] = added[o * width:(o + 1) * width].astype(outs[o].dtype)
+
+
+def near_kernel(start, piece, owners, grad_ref, owner_ref, onehot_ref, total_ref, *refs):
+    *outs, masked = refs
+    count, width, features = grad_ref.shape
+    for n in range(count):
+        spread(grad_ref[n], lookup_mask(owner_ref, piece, features, start + n), owners, masked, n)
+    added = dot_nn(masked[...], onehot_ref[start * features:(start + count) * features])
+    added = added + total_ref[owners[0] * width:(owners[-1] + 1) * width]
+    for o, out in enumerate(outs):
+        out[...] = added[o * width:(o + 1) * width].astype(out.dtype)
+
+
+def table_part(j, piece, owners, far, arrays, pairs, total):
     _, width, features = arrays[0].shape
     lookups = len(pairs) * piece * features
-    if last:
-        shapes = [shape((width, SHARD), F32 if m == 0 else BF16) for m in range(owners)]
+    if far:
+        shapes = blocks(width, owners) + [shape((piece, width, features), BF16)]
     else:
-        shapes = [shape((owners * width, SHARD), F32)]
+        shapes = [shape((len(owners) * width, SHARD), F32)]
     return call(
-        functools.partial(table_kernel, j * piece, piece, last, len(pairs), total is not None),
+        functools.partial(table_kernel, j * piece, piece, owners, far, len(pairs), total is not None),
         "table_part",
         [*arrays, *pairs] + ([] if total is None else [total]),
         shapes,
-        2 * lookups * width * owners * SHARD,
-        scratch=[pltpu.VMEM((owners * width, lookups), BF16)],
-    )
-
-
-def finish_kernel(*refs):
+        2 * lookups * width * len(owners) * SHARD,
+        scratch=[pltpu.VMEM((len(owners) * width, lookups), BF16)],
+    )
+
+
+def blocks(width, owners):
+    return [shape((width, SHARD), BF16 if o else F32) for o in range(len(owners))]
+
+
+def collect_kernel(*refs):
     *terms, out_ref = refs
-    out_ref[...] = sum(term[...].astype(F32) for term in terms)
+    out_ref[...] = sum(term[...].astype(F32) for term in terms).astype(out_ref.dtype)
 
 
 def swap(x, bit, axis="dim"):
@@ -241,19 +265,35 @@
     )
 
     pairs = {0: pair}
-    (total,) = table_part(0, piece, owners, False, arrays, [pair], None)
+    everyone = list(range(owners))
+    near, far = everyone[:owners // 2], everyone[owners // 2:]
+    (total,) = table_part(0, piece, everyone, False, arrays, [pair], None)
     for bit in reversed(bits[1:]):
         pairs.update({j ^ bit: swap(got, bit) for j, got in pairs.items()})
     for j in list(pairs):
         pairs[j] = after(pairs[j], total) if j else pair
         pairs[j ^ core] = swap(pairs[j], core)
     middle = [pairs[j] for j in range(1, peers - 1)]
-    (total,) = table_part(1, piece, owners, False, arrays, middle, total)
-    own, *sent = table_part(peers - 1, piece, owners, True, arrays, [pairs[peers - 1]], total)
-
-    got = [swap(sent[m - 1], m, "dp") for m in range(owners - 1, 0, -1)]
-    (out,) = call(finish_kernel, "finish", (own, *got), [shape(own.shape, F32)], owners * own.size)
-    return out
+    (total,) = table_part(1, piece, everyone, False, arrays, middle, total)
+    last = peers - 1
+    *opposite, grad = table_part(last, piece, far, True, arrays, [pairs[last]], total)
+    own = call(
+        functools.partial(near_kernel, last * piece, piece, near),
+        "near_part",
+        (grad, owner, onehot, total),
+        blocks(width, near),
+        2 * piece * features * width * len(near) * SHARD,
+        scratch=[pltpu.VMEM((len(near) * width, piece * features), BF16)],
+    )
+
+    def collect(terms, kind):
+        return call(collect_kernel, "collect", terms, [shape((width, SHARD), kind)], width * SHARD)[0]
+
+    steps = near[:0:-1]
+    opposite = [opposite[0]] + [swap(opposite[m], m, "dp") for m in steps]
+    own = [own[0]] + [swap(own[m], m, "dp") for m in steps]
+    own.append(swap(collect(opposite, BF16), owners // 2, "dp"))
+    return collect(own, F32)
 
 
 def solution(mesh):

time: 39.1 us -> 36.5 us (0.934)
  starting transfers between devices: 16.8 us -> 14.7 us
  waiting for transfers between devices: 13.3 us -> 12.5 us
    ppermute x13, starting transfers between devices: 16.8 us -> 14.7 us  [swap(): lax.ppermute(x, axis, [(i, i ^ bit) for i in range(lax.axis_size(axis))])]
    ppermute x13, waiting for transfers between devices: 13.3 us -> 12.5 us  [swap(): lax.ppermute(x, axis, [(i, i ^ bit) for i in range(lax.axis_size(axis))])]
    pallas_call x10 -> x12, Pallas kernels: 8.75 us -> 8.92 us  [call(): pl.pallas_call(kernel, in_specs=specs or [VMEM] * len(args), out_specs=[V...]
  transfers between devices with their start and end apart: 13 -> 13, of which waited for: 7 -> 6; matrix products, arithmetic and copies ran while one was open for 0% -> 0% of each run, Pallas kernels for 12% -> 14%
where the time goes in v8:
time: 36.5 us; the launch traced here: 36.3 us
  starting transfers between devices  14.7 us (40%)
  waiting for transfers between devices  12.5 us (34%)
  Pallas kernels  8.92 us (24%)
    ppermute x13, starting transfers between devices, swap(): lax.ppermute(x, axis, [(i, i ^ bit) for i in range(lax.axis_size(axis))])  14.7 us
    ppermute x13, waiting for transfers between devices, swap(): lax.ppermute(x, axis, [(i, i ^ bit) for i in range(lax.axis_size(axis))])  12.5 us
    pallas_call x12, Pallas kernels, call(): pl.pallas_call(kernel, in_specs=specs or [VMEM] * len(args), out_specs=[V...  8.92 us
  transfers between devices with their start and end apart: 13, of which 6 were waited for; matrix products, arithmetic and copies ran while one was open for 0% of the time, Pallas kernels for 14%

profile of v8, /device:TPU:0, one launch (start us, length us, event | category | flops | bytes accessed | tf_op | source)
XLA Modules:
  0.0 36.3 jit_solution(8290289107701057119)
XLA Ops:
  0.0 1.6 %load.1 = (bf16[16,128,256]{2,1,0:T(8,128)(2,1)S(1)}, bf16[16,128,256]{2,1,0:T(8,128)(2,1)S(1)}) custom-call(bf16[16,128,256]{2,1,0:T(8,128)(2,1)} %av_hbm.1, bf16[16,128,256]{2,1,0:T(8,128)(2,1)} %up_hbm.1), custom_call_target="tpu_custom_call" | custom-call | bytes 4194304 | tf_op jit(solution)/shard_map/load/pallas_call | solution.py:40
  1.6 0.4 %first_sums.1 = bf16[4,128,256]{2,1,0:T(8,128)(2,1)S(1)} custom-call(bf16[16,128,256]{2,1,0:T(8,128)(2,1)S(1)} %get-tuple-element.22.av_ref.refs_0_, bf16[16,128,256]{2,1,0:T(8,128)(2,1)S(1)} %get-tuple-element.23.up_ref, bf16[64,256]{1,0:T(8,128)(2,1)S(1)} %bitcast.3, bf16[64,128]{1,0:T(8,128)(2,1)S(1)} %copy-done.2), custom_call_target="tpu_custom_call" | custom-call | flops 50331648 | bytes 2408448 | tf_op jit(solution)/shard_map/first_sums/pallas_call | solution.py:40
  2.0 0.0 copy-start.3
  2.1 0.0 copy-start.4
  2.1 0.5 %collective-permute-start.1 = (bf16[4,128,256]{2,1,0:T(8,128)(2,1)S(1)}, bf16[4,128,256]{2,1,0:T(8,128)(2,1)S(1)}, u32[]{:S(2)}, u32[]{:S(2)}) collective-permute-start(bf16[4,128,256]{2,1,0:T(8,128)(2,1)S(1)} %first_sums.1), channel_id=1, source_target_pairs={{0,1},{1,0},{2,3},{3,2},{4,5},{5,4},{6,7},{7,6},{8,9},{9,8},{10,11... | collective-permute-start | bytes 786440 | tf_op jit(solution)/shard_map/ppermute | solution.py:193
  2.6 0.6 %sums.1 = (f32[4,128,256]{2,1,0:T(8,128)S(1)}, f32[4,128,256]{2,1,0:T(8,128)S(1)}) custom-call(bf16[16,128,256]{2,1,0:T(8,128)(2,1)S(1)} %get-tuple-element.22.av_ref.refs_0_, bf16[16,128,256]{2,1,0:T(8,128)(2,1)S(1)} %get-tuple-element.23.up_ref, bf16[64,256]{1,0:T(8,128)(2,1)S(1)} %bitcast.4, bf16[64,128]{1,0:T(8,128)(2,1)S(1)} %copy-done.2), custom_call_target="tpu_custom_call" | custom-call | flops 100663296 | bytes 3194880 | tf_op jit(solution)/shard_map/sums/pallas_call | solution.py:40
  3.2 0.1 collective-permute-start
  3.3 0.5 %collective-permute-done.1.got_ref = bf16[4,128,256]{2,1,0:T(8,128)(2,1)S(1)} collective-permute-done((bf16[4,128,256]{2,1,0:T(8,128)(2,1)S(1)}, bf16[4,128,256]{2,1,0:T(8,128)(2,1)S(1)}, u32[]{:S(2)}, u32[]{:S(2)}) %collective-permute-start.1) | collective-permute-done | bytes 262176 | tf_op jit(solution)/shard_map/ppermute | solution.py:193
  3.8 0.0 copy-start.1
  3.8 3.0 %collective-permute-start.2 = (bf16[4,128,256]{2,1,0:T(8,128)(2,1)S(1)}, bf16[4,128,256]{2,1,0:T(8,128)(2,1)S(1)}, u32[]{:S(2)}, u32[]{:S(2)}) collective-permute-start(bf16[4,128,256]{2,1,0:T(8,128)(2,1)S(1)} %add.1), channel_id=1, source_target_pairs={{0,2},{1,3},{2,0},{3,1},{4,6},{5,7},{6,4},{7,5},{8,10},{9,11},{10,... | collective-permute-start | bytes 786440 | tf_op jit(solution)/shard_map/ppermute | solution.py:193
  6.8 1.3 %prepare.1 = (f32[4,128,256]{2,1,0:T(8,128)S(1)}, f32[16,128,256]{2,1,0:T(8,128)S(1)}, bf16[4096,256]{1,0:T(8,128)(2,1)S(1)}) custom-call(bf16[16,128,256]{2,1,0:T(8,128)(2,1)S(1)} %get-tuple-element.22.av_ref.refs_0_, bf16[16,128,256]{2,1,0:T(8,128)(2,1)S(1)} %get-tuple-element.23.up_ref, bf16[64,256]{1,0:T(8,128)(2,1)S(1)} %bitcast.5, ...), custom_call_target="tpu_custom_call" | custom-call | flops 268435456 | bytes 7012352 | tf_op jit(solution)/shard_map/prepare/pallas_call | solution.py:40
  8.1 5.3 %collective-permute-done.2.refs_2_ = bf16[4,128,256]{2,1,0:T(8,128)(2,1)S(1)} collective-permute-done((bf16[4,128,256]{2,1,0:T(8,128)(2,1)S(1)}, bf16[4,128,256]{2,1,0:T(8,128)(2,1)S(1)}, u32[]{:S(2)}, u32[]{:S(2)}) %collective-permute-start.2) | collective-permute-done | bytes 262176 | tf_op jit(solution)/shard_map/ppermute | solution.py:193
  13.4 0.0 collective-permute-done.refs_1_
  13.4 0.2 layer_back.1.refs_5_
  13.5 1.8 %collective-permute-start.3 = (bf16[4,64,256]{2,1,0:T(8,128)(2,1)S(1)}, bf16[4,64,256]{2,1,0:T(8,128)(2,1)S(1)}, u32[]{:S(2)}, u32[]{:S(2)}) collective-permute-start(bf16[4,64,256]{2,1,0:T(8,128)(2,1)S(1)} %layer_back.1.refs_5_), channel_id=1, source_target_pairs={{0,2},{1,3},{2,0},{3,1},{4,6},{5,7},{6,4},{7,5},{8,10},{9,11},{10,... | collective-permute-start | bytes 393224 | tf_op jit(solution)/shard_map/ppermute | solution.py:193
  15.4 1.1 %table_part.3.refs_7_ = f32[1024,256]{1,0:T(8,128)S(1)} custom-call(bf16[16,128,256]{2,1,0:T(8,128)(2,1)S(1)} %get-tuple-element.22.av_ref.refs_0_, bf16[64,256]{1,0:T(8,128)(2,1)S(1)} %bitcast.6, f32[16,128,256]{2,1,0:T(8,128)S(1)} %get-tuple-element.24.refs_2_, s32[1,4096]{1,0:T(1,128)S(1)} %bitcast.9, ...), custom_call_target="tpu_custom_call" | custom-call | flops 536870912 | bytes 6471680 | tf_op jit(solution)/shard_map/table_part/pallas_call | solution.py:40
  16.5 2.2 %collective-permute-done.3.refs_6_ = bf16[4,64,256]{2,1,0:T(8,128)(2,1)S(1)} collective-permute-done((bf16[4,64,256]{2,1,0:T(8,128)(2,1)S(1)}, bf16[4,64,256]{2,1,0:T(8,128)(2,1)S(1)}, u32[]{:S(2)}, u32[]{:S(2)}) %collective-permute-start.3) | collective-permute-done | bytes 131104 | tf_op jit(solution)/shard_map/ppermute | solution.py:193
  18.6 0.0 collective-permute-start.4
  18.6 1.7 %table_part.4.refs_6_.total_ref = f32[1024,256]{1,0:T(8,128)S(1)} custom-call(bf16[16,128,256]{2,1,0:T(8,128)(2,1)S(1)} %get-tuple-element.22.av_ref.refs_0_, bf16[64,256]{1,0:T(8,128)(2,1)S(1)} %bitcast.7, f32[16,128,256]{2,1,0:T(8,128)S(1)} %get-tuple-element.24.refs_2_, s32[1,4096]{1,0:T(1,128)S(1)} %bitcast.10, ...), custom_call_target="tpu_custom_call" | custom-call | flops 1073741824 | bytes 7651328 | tf_op jit(solution)/shard_map/table_part/pallas_call | solution.py:40
  20.4 0.8 %table_part.5 = (f32[128,256]{1,0:T(8,128)S(1)}, bf16[128,256]{1,0:T(8,128)(2,1)S(1)}, bf16[128,256]{1,0:T(8,128)(2,1)S(1)}, bf16[128,256]{1,0:T(8,128)(2,1)S(1)}, bf16[4,128,256]{2,1,0:T(8,128)(2,1)S(1)}) custom-call(bf16[16,128,256]{2,1,0:T(8,128)(2,1)S(1)} %get-tuple-element.22.av_ref.refs_0_, bf16[64,256]{1,0:T(8,128)(2,1)S(1)} %bitcast.8, ...), custom_call_target="tpu_custom_call" | custom-call | flops 268435456 | bytes 7061504 | tf_op jit(solution)/shard_map/table_part/pallas_call | solution.py:40
  21.2 2.7 %collective-permute-start.9 = (bf16[128,256]{1,0:T(8,128)(2,1)S(1)}, bf16[128,256]{1,0:T(8,128)(2,1)S(1)}, u32[]{:S(2)}, u32[]{:S(2)}) collective-permute-start(bf16[128,256]{1,0:T(8,128)(2,1)S(1)} %get-tuple-element.36), channel_id=1, source_target_pairs={{0,12},{4,8},{8,4},{12,0},{16,28},{20,24},{24,20},{28,16},{1,13},{... | collective-permute-start | bytes 196616 | tf_op jit(solution)/shard_map/ppermute | solution.py:193
  24.0 0.4 %collective-permute-start.10 = (bf16[128,256]{1,0:T(8,128)(2,1)S(1)}, bf16[128,256]{1,0:T(8,128)(2,1)S(1)}, u32[]{:S(2)}, u32[]{:S(2)}) collective-permute-start(bf16[128,256]{1,0:T(8,128)(2,1)S(1)} %get-tuple-element.37), channel_id=1, source_target_pairs={{0,8},{4,12},{8,0},{12,4},{16,24},{20,28},{24,16},{28,20},{1,9},{5... | collective-permute-start | bytes 196616 | tf_op jit(solution)/shard_map/ppermute | solution.py:193
  24.4 0.4 %collective-permute-start.11 = (bf16[128,256]{1,0:T(8,128)(2,1)S(1)}, bf16[128,256]{1,0:T(8,128)(2,1)S(1)}, u32[]{:S(2)}, u32[]{:S(2)}) collective-permute-start(bf16[128,256]{1,0:T(8,128)(2,1)S(1)} %get-tuple-element.38), channel_id=1, source_target_pairs={{0,4},{4,0},{8,12},{12,8},{16,20},{20,16},{24,28},{28,24},{1,5},{5... | collective-permute-start | bytes 196616 | tf_op jit(solution)/shard_map/ppermute | solution.py:193
  24.8 0.4 %near_part.1 = (f32[128,256]{1,0:T(8,128)S(1)}, bf16[128,256]{1,0:T(8,128)(2,1)S(1)}, bf16[128,256]{1,0:T(8,128)(2,1)S(1)}, bf16[128,256]{1,0:T(8,128)(2,1)S(1)}) custom-call(bf16[4,128,256]{2,1,0:T(8,128)(2,1)S(1)} %get-tuple-element.30.grad_ref, s32[1,4096]{1,0:T(1,128)S(1)} %bitcast.12, bf16[4096,256]{1,0:T(8,128)(2,1)S(1)} %get-tuple-element.25.refs_4_.onehot_ref, ...), custom_call_target="tpu_custom_call" | custom-call | flops 268435456 | bytes 3751936 | tf_op jit(solution)/shard_map/near_part/pallas_call | solution.py:40
  25.2 2.7 %collective-permute-start.6 = (bf16[128,256]{1,0:T(8,128)(2,1)S(1)}, bf16[128,256]{1,0:T(8,128)(2,1)S(1)}, u32[]{:S(2)}, u32[]{:S(2)}) collective-permute-start(bf16[128,256]{1,0:T(8,128)(2,1)S(1)} %get-tuple-element.32), channel_id=1, source_target_pairs={{0,12},{4,8},{8,4},{12,0},{16,28},{20,24},{24,20},{28,16},{1,13},{... | collective-permute-start | bytes 196616 | tf_op jit(solution)/shard_map/ppermute | solution.py:193
  28.0 0.4 %collective-permute-start.7 = (bf16[128,256]{1,0:T(8,128)(2,1)S(1)}, bf16[128,256]{1,0:T(8,128)(2,1)S(1)}, u32[]{:S(2)}, u32[]{:S(2)}) collective-permute-start(bf16[128,256]{1,0:T(8,128)(2,1)S(1)} %get-tuple-element.33), channel_id=1, source_target_pairs={{0,8},{4,12},{8,0},{12,4},{16,24},{20,28},{24,16},{28,20},{1,9},{5... | collective-permute-start | bytes 196616 | tf_op jit(solution)/shard_map/ppermute | solution.py:193
  28.4 0.4 %collective-permute-start.8 = (bf16[128,256]{1,0:T(8,128)(2,1)S(1)}, bf16[128,256]{1,0:T(8,128)(2,1)S(1)}, u32[]{:S(2)}, u32[]{:S(2)}) collective-permute-start(bf16[128,256]{1,0:T(8,128)(2,1)S(1)} %get-tuple-element.34), channel_id=1, source_target_pairs={{0,4},{4,0},{8,12},{12,8},{16,20},{20,16},{24,28},{28,24},{1,5},{5... | collective-permute-start | bytes 196616 | tf_op jit(solution)/shard_map/ppermute | solution.py:193
  28.8 0.6 %collective-permute-done.11.refs_3_ = bf16[128,256]{1,0:T(8,128)(2,1)S(1)} collective-permute-done((bf16[128,256]{1,0:T(8,128)(2,1)S(1)}, bf16[128,256]{1,0:T(8,128)(2,1)S(1)}, u32[]{:S(2)}, u32[]{:S(2)}) %collective-permute-start.11) | collective-permute-done | bytes 65568 | tf_op jit(solution)/shard_map/ppermute | solution.py:193
  29.4 2.2 %collective-permute-start.12 = (bf16[128,256]{1,0:T(8,128)(2,1)S(1)}, bf16[128,256]{1,0:T(8,128)(2,1)S(1)}, u32[]{:S(2)}, u32[]{:S(2)}) collective-permute-start(bf16[128,256]{1,0:T(8,128)(2,1)S(1)} %collect.2), channel_id=1, source_target_pairs={{0,16},{4,20},{8,24},{12,28},{16,0},{20,4},{24,8},{28,12},{1,17},{... | collective-permute-start | bytes 196616 | tf_op jit(solution)/shard_map/ppermute | solution.py:193
  31.7 1.1 %collective-permute-done.7.refs_2_ = bf16[128,256]{1,0:T(8,128)(2,1)S(1)} collective-permute-done((bf16[128,256]{1,0:T(8,128)(2,1)S(1)}, bf16[128,256]{1,0:T(8,128)(2,1)S(1)}, u32[]{:S(2)}, u32[]{:S(2)}) %collective-permute-start.7) | collective-permute-done | bytes 65568 | tf_op jit(solution)/shard_map/ppermute | solution.py:193
  32.8 2.8 %collective-permute-done.12.refs_4_ = bf16[128,256]{1,0:T(8,128)(2,1)S(1)} collective-permute-done((bf16[128,256]{1,0:T(8,128)(2,1)S(1)}, bf16[128,256]{1,0:T(8,128)(2,1)S(1)}, u32[]{:S(2)}, u32[]{:S(2)}) %collective-permute-start.12) | collective-permute-done | bytes 65568 | tf_op jit(solution)/shard_map/ppermute | solution.py:193
  35.6 0.7 %collect.3 = f32[128,256]{1,0:T(8,128)} custom-call(f32[128,256]{1,0:T(8,128)S(1)} %get-tuple-element.31.refs_0_, bf16[128,256]{1,0:T(8,128)(2,1)S(1)} %collective-permute-done.6.refs_1_, bf16[128,256]{1,0:T(8,128)(2,1)S(1)} %collective-permute-done.7.refs_2_, bf16[128,256]{1,0:T(8,128)(2,1)S(1)} %collective-permute-done.8.refs_3_, ...), custom_call_target="tpu_custom_call" | custom-call | flops 32768 | bytes 524288 | tf_op jit(solution)/shard_map/collect/pallas_call | solution.py:40
  (16 shorter events, 0.1 us)
Async XLA Ops:
  0.0 1.6 %copy-start.2 = (bf16[64,128]{1,0:T(8,128)(2,1)S(1)}, bf16[64,128]{1,0:T(8,128)(2,1)}, u32[]{:S(2)}) copy-start(bf16[64,128]{1,0:T(8,128)(2,1)} %proj_ref.5) | copy-start | bytes 49156
  0.0 1.6 %copy-start = (bf16[256,64]{0,1:T(8,128)(2,1)S(1)}, bf16[256,64]{0,1:T(8,128)(2,1)}, u32[]{:S(2)}) copy-start(bf16[256,64]{0,1:T(8,128)(2,1)} %param.9) | copy-start | bytes 98308
  2.0 4.7 %copy-start.3 = (bf16[256,256]{1,0:T(8,128)(2,1)S(1)}, bf16[256,256]{1,0:T(8,128)(2,1)}, u32[]{:S(2)}) copy-start(bf16[256,256]{1,0:T(8,128)(2,1)} %mix_ref.1) | copy-start | bytes 393220
  2.1 4.7 %copy-start.4 = (s32[4096]{0:T(1024)S(1)}, s32[4096]{0:T(1024)}, u32[]{:S(2)}) copy-start(s32[4096]{0:T(1024)} %param.13) | copy-start | bytes 49156
  2.1 1.7 %collective-permute-start.1 = (bf16[4,128,256]{2,1,0:T(8,128)(2,1)S(1)}, bf16[4,128,256]{2,1,0:T(8,128)(2,1)S(1)}, u32[]{:S(2)}, u32[]{:S(2)}) collective-permute-start(bf16[4,128,256]{2,1,0:T(8,128)(2,1)S(1)} %first_sums.1), channel_id=1, source_target_pairs={{0,1},{1,0},{2,3},{3,2},{4,5},{5,4},{6,7},{7,6},{8,9},{9,8},{10,11... | collective-permute-start | bytes 786440 | tf_op jit(solution)/shard_map/ppermute | solution.py:193
  3.2 10.2 %collective-permute-start = (f32[4,128,256]{2,1,0:T(8,128)S(1)}, f32[4,128,256]{2,1,0:T(8,128)S(1)}, u32[]{:S(2)}, u32[]{:S(2)}) collective-permute-start(f32[4,128,256]{2,1,0:T(8,128)S(1)} %get-tuple-element.27), channel_id=1, source_target_pairs={{0,1},{1,0},{2,3},{3,2},{4,5},{5,4},{6,7},{7,6},{8,9},{9,8},{10,11... | collective-permute-start | bytes 1572872 | tf_op jit(solution)/shard_map/ppermute | solution.py:193
  3.8 11.6 %copy-start.1 = (s32[4096,1]{0,1:T(1,128)S(1)}, s32[4096,1]{0,1:T(1,128)}, u32[]{:S(2)}) copy-start(s32[4096,1]{0,1:T(1,128)} %param.12) | copy-start | bytes 49156
  3.8 9.6 %collective-permute-start.2 = (bf16[4,128,256]{2,1,0:T(8,128)(2,1)S(1)}, bf16[4,128,256]{2,1,0:T(8,128)(2,1)S(1)}, u32[]{:S(2)}, u32[]{:S(2)}) collective-permute-start(bf16[4,128,256]{2,1,0:T(8,128)(2,1)S(1)} %add.1), channel_id=1, source_target_pairs={{0,2},{1,3},{2,0},{3,1},{4,6},{5,7},{6,4},{7,5},{8,10},{9,11},{10,... | collective-permute-start | bytes 786440 | tf_op jit(solution)/shard_map/ppermute | solution.py:193
  13.5 5.1 %collective-permute-start.3 = (bf16[4,64,256]{2,1,0:T(8,128)(2,1)S(1)}, bf16[4,64,256]{2,1,0:T(8,128)(2,1)S(1)}, u32[]{:S(2)}, u32[]{:S(2)}) collective-permute-start(bf16[4,64,256]{2,1,0:T(8,128)(2,1)S(1)} %layer_back.1.refs_5_), channel_id=1, source_target_pairs={{0,2},{1,3},{2,0},{3,1},{4,6},{5,7},{6,4},{7,5},{8,10},{9,11},{10,... | collective-permute-start | bytes 393224 | tf_op jit(solution)/shard_map/ppermute | solution.py:193
  15.4 3.3 %collective-permute-start.5 = (bf16[4,64,256]{2,1,0:T(8,128)(2,1)S(1)}, bf16[4,64,256]{2,1,0:T(8,128)(2,1)S(1)}, u32[]{:S(2)}, u32[]{:S(2)}) collective-permute-start(bf16[4,64,256]{2,1,0:T(8,128)(2,1)S(1)} %layer_back.1.refs_5_), channel_id=1, source_target_pairs={{0,1},{1,0},{2,3},{3,2},{4,5},{5,4},{6,7},{7,6},{8,9},{9,8},{10,11... | collective-permute-start | bytes 393224 | tf_op jit(solution)/shard_map/ppermute | solution.py:193
  18.6 1.8 %collective-permute-start.4 = (bf16[4,64,256]{2,1,0:T(8,128)(2,1)S(1)}, bf16[4,64,256]{2,1,0:T(8,128)(2,1)S(1)}, u32[]{:S(2)}, u32[]{:S(2)}) collective-permute-start(bf16[4,64,256]{2,1,0:T(8,128)(2,1)S(1)} %collective-permute-done.3.refs_6_), channel_id=1, source_target_pairs={{0,1},{1,0},{2,3},{3,2},{4,5},{5,4},{6,7},{7,6},{8,9},{9,8},{10,11... | collective-permute-start | bytes 393224 | tf_op jit(solution)/shard_map/ppermute | solution.py:193
  21.2 7.2 %collective-permute-start.9 = (bf16[128,256]{1,0:T(8,128)(2,1)S(1)}, bf16[128,256]{1,0:T(8,128)(2,1)S(1)}, u32[]{:S(2)}, u32[]{:S(2)}) collective-permute-start(bf16[128,256]{1,0:T(8,128)(2,1)S(1)} %get-tuple-element.36), channel_id=1, source_target_pairs={{0,12},{4,8},{8,4},{12,0},{16,28},{20,24},{24,20},{28,16},{1,13},{... | collective-permute-start | bytes 196616 | tf_op jit(solution)/shard_map/ppermute | solution.py:193
  24.0 4.8 %collective-permute-start.10 = (bf16[128,256]{1,0:T(8,128)(2,1)S(1)}, bf16[128,256]{1,0:T(8,128)(2,1)S(1)}, u32[]{:S(2)}, u32[]{:S(2)}) collective-permute-start(bf16[128,256]{1,0:T(8,128)(2,1)S(1)} %get-tuple-element.37), channel_id=1, source_target_pairs={{0,8},{4,12},{8,0},{12,4},{16,24},{20,28},{24,16},{28,20},{1,9},{5... | collective-permute-start | bytes 196616 | tf_op jit(solution)/shard_map/ppermute | solution.py:193
  24.4 5.0 %collective-permute-start.11 = (bf16[128,256]{1,0:T(8,128)(2,1)S(1)}, bf16[128,256]{1,0:T(8,128)(2,1)S(1)}, u32[]{:S(2)}, u32[]{:S(2)}) collective-permute-start(bf16[128,256]{1,0:T(8,128)(2,1)S(1)} %get-tuple-element.38), channel_id=1, source_target_pairs={{0,4},{4,0},{8,12},{12,8},{16,20},{20,16},{24,28},{28,24},{1,5},{5... | collective-permute-start | bytes 196616 | tf_op jit(solution)/shard_map/ppermute | solution.py:193
  25.2 6.4 %collective-permute-start.6 = (bf16[128,256]{1,0:T(8,128)(2,1)S(1)}, bf16[128,256]{1,0:T(8,128)(2,1)S(1)}, u32[]{:S(2)}, u32[]{:S(2)}) collective-permute-start(bf16[128,256]{1,0:T(8,128)(2,1)S(1)} %get-tuple-element.32), channel_id=1, source_target_pairs={{0,12},{4,8},{8,4},{12,0},{16,28},{20,24},{24,20},{28,16},{1,13},{... | collective-permute-start | bytes 196616 | tf_op jit(solution)/shard_map/ppermute | solution.py:193
  28.0 4.8 %collective-permute-start.7 = (bf16[128,256]{1,0:T(8,128)(2,1)S(1)}, bf16[128,256]{1,0:T(8,128)(2,1)S(1)}, u32[]{:S(2)}, u32[]{:S(2)}) collective-permute-start(bf16[128,256]{1,0:T(8,128)(2,1)S(1)} %get-tuple-element.33), channel_id=1, source_target_pairs={{0,8},{4,12},{8,0},{12,4},{16,24},{20,28},{24,16},{28,20},{1,9},{5... | collective-permute-start | bytes 196616 | tf_op jit(solution)/shard_map/ppermute | solution.py:193
  28.4 4.4 %collective-permute-start.8 = (bf16[128,256]{1,0:T(8,128)(2,1)S(1)}, bf16[128,256]{1,0:T(8,128)(2,1)S(1)}, u32[]{:S(2)}, u32[]{:S(2)}) collective-permute-start(bf16[128,256]{1,0:T(8,128)(2,1)S(1)} %get-tuple-element.34), channel_id=1, source_target_pairs={{0,4},{4,0},{8,12},{12,8},{16,20},{20,16},{24,28},{28,24},{1,5},{5... | collective-permute-start | bytes 196616 | tf_op jit(solution)/shard_map/ppermute | solution.py:193
  29.4 6.2 %collective-permute-start.12 = (bf16[128,256]{1,0:T(8,128)(2,1)S(1)}, bf16[128,256]{1,0:T(8,128)(2,1)S(1)}, u32[]{:S(2)}, u32[]{:S(2)}) collective-permute-start(bf16[128,256]{1,0:T(8,128)(2,1)S(1)} %collect.2), channel_id=1, source_target_pairs={{0,16},{4,20},{8,24},{12,28},{16,0},{20,4},{24,8},{28,12},{1,17},{... | collective-permute-start | bytes 196616 | tf_op jit(solution)/shard_map/ppermute | solution.py:193

commit v9 on v8

--- a/solution.py
+++ b/solution.py
@@ -290,10 +290,12 @@
         return call(collect_kernel, "collect", terms, [shape((width, SHARD), kind)], width * SHARD)[0]
 
     steps = near[:0:-1]
+    early = steps[:(len(steps) + 1) // 3]
     opposite = [opposite[0]] + [swap(opposite[m], m, "dp") for m in steps]
-    own = [own[0]] + [swap(own[m], m, "dp") for m in steps]
-    own.append(swap(collect(opposite, BF16), owners // 2, "dp"))
-    return collect(own, F32)
+    terms = [own[0]] + [swap(own[m], m, "dp") for m in early]
+    terms.append(swap(collect(opposite, BF16), owners // 2, "dp"))
+    terms = [collect(terms, F32)] + [swap(own[m], m, "dp") for m in steps[len(early):]]
+    return collect(terms, F32)
 
 
 def solution(mesh):

time: 36.5 us -> 38 us (1.041)
  starting transfers between devices: 14.7 us -> 16.3 us
    ppermute x13, starting transfers between devices: 14.7 us -> 16.3 us  [swap(): lax.ppermute(x, axis, [(i, i ^ bit) for i in range(lax.axis_size(axis))])]
    pallas_call x12 -> x13, Pallas kernels: 8.92 us -> 8.92 us  [call(): pl.pallas_call(kernel, in_specs=specs or [VMEM] * len(args), out_specs=[V...]
  transfers between devices with their start and end apart: 13 -> 13, of which waited for: 6 -> 8; matrix products, arithmetic and copies ran while one was open for 0% -> 0% of each run, Pallas kernels for 14% -> 14%
where the time goes in v9:
time: 38 us; the launch traced here: 37.9 us
  starting transfers between devices  16.3 us (43%)
  waiting for transfers between devices  12.5 us (33%)
  Pallas kernels  8.92 us (23%)
    ppermute x13, starting transfers between devices, swap(): lax.ppermute(x, axis, [(i, i ^ bit) for i in range(lax.axis_size(axis))])  16.3 us
    ppermute x13, waiting for transfers between devices, swap(): lax.ppermute(x, axis, [(i, i ^ bit) for i in range(lax.axis_size(axis))])  12.5 us
    pallas_call x13, Pallas kernels, call(): pl.pallas_call(kernel, in_specs=specs or [VMEM] * len(args), out_specs=[V...  8.92 us
  transfers between devices with their start and end apart: 13, of which 8 were waited for; matrix products, arithmetic and copies ran while one was open for 0% of the time, Pallas kernels for 14%

profile of v9, /device:TPU:0, one launch (start us, length us, event | category | flops | bytes accessed | tf_op | source)
XLA Modules:
  0.0 37.9 jit_solution(14797141487706355098)
XLA Ops:
  0.0 1.6 %load.1 = (bf16[16,128,256]{2,1,0:T(8,128)(2,1)S(1)}, bf16[16,128,256]{2,1,0:T(8,128)(2,1)S(1)}) custom-call(bf16[16,128,256]{2,1,0:T(8,128)(2,1)} %av_hbm.1, bf16[16,128,256]{2,1,0:T(8,128)(2,1)} %up_hbm.1), custom_call_target="tpu_custom_call" | custom-call | bytes 4194304 | tf_op jit(solution)/shard_map/load/pallas_call | solution.py:40
  1.6 0.4 %first_sums.1 = bf16[4,128,256]{2,1,0:T(8,128)(2,1)S(1)} custom-call(bf16[16,128,256]{2,1,0:T(8,128)(2,1)S(1)} %get-tuple-element.22.av_ref.refs_0_, bf16[16,128,256]{2,1,0:T(8,128)(2,1)S(1)} %get-tuple-element.23.up_ref, bf16[64,256]{1,0:T(8,128)(2,1)S(1)} %bitcast.3, bf16[64,128]{1,0:T(8,128)(2,1)S(1)} %copy-done.2), custom_call_target="tpu_custom_call" | custom-call | flops 50331648 | bytes 2408448 | tf_op jit(solution)/shard_map/first_sums/pallas_call | solution.py:40
  2.0 0.0 copy-start.3
  2.1 0.0 copy-start.4
  2.1 0.5 %collective-permute-start.1 = (bf16[4,128,256]{2,1,0:T(8,128)(2,1)S(1)}, bf16[4,128,256]{2,1,0:T(8,128)(2,1)S(1)}, u32[]{:S(2)}, u32[]{:S(2)}) collective-permute-start(bf16[4,128,256]{2,1,0:T(8,128)(2,1)S(1)} %first_sums.1), channel_id=1, source_target_pairs={{0,1},{1,0},{2,3},{3,2},{4,5},{5,4},{6,7},{7,6},{8,9},{9,8},{10,11... | collective-permute-start | bytes 786440 | tf_op jit(solution)/shard_map/ppermute | solution.py:193
  2.6 0.6 %sums.1 = (f32[4,128,256]{2,1,0:T(8,128)S(1)}, f32[4,128,256]{2,1,0:T(8,128)S(1)}) custom-call(bf16[16,128,256]{2,1,0:T(8,128)(2,1)S(1)} %get-tuple-element.22.av_ref.refs_0_, bf16[16,128,256]{2,1,0:T(8,128)(2,1)S(1)} %get-tuple-element.23.up_ref, bf16[64,256]{1,0:T(8,128)(2,1)S(1)} %bitcast.4, bf16[64,128]{1,0:T(8,128)(2,1)S(1)} %copy-done.2), custom_call_target="tpu_custom_call" | custom-call | flops 100663296 | bytes 3194880 | tf_op jit(solution)/shard_map/sums/pallas_call | solution.py:40
  3.2 0.1 collective-permute-start
  3.3 0.5 %collective-permute-done.1.got_ref = bf16[4,128,256]{2,1,0:T(8,128)(2,1)S(1)} collective-permute-done((bf16[4,128,256]{2,1,0:T(8,128)(2,1)S(1)}, bf16[4,128,256]{2,1,0:T(8,128)(2,1)S(1)}, u32[]{:S(2)}, u32[]{:S(2)}) %collective-permute-start.1) | collective-permute-done | bytes 262176 | tf_op jit(solution)/shard_map/ppermute | solution.py:193
  3.8 0.0 copy-start.1
  3.8 3.0 %collective-permute-start.2 = (bf16[4,128,256]{2,1,0:T(8,128)(2,1)S(1)}, bf16[4,128,256]{2,1,0:T(8,128)(2,1)S(1)}, u32[]{:S(2)}, u32[]{:S(2)}) collective-permute-start(bf16[4,128,256]{2,1,0:T(8,128)(2,1)S(1)} %add.1), channel_id=1, source_target_pairs={{0,2},{1,3},{2,0},{3,1},{4,6},{5,7},{6,4},{7,5},{8,10},{9,11},{10,... | collective-permute-start | bytes 786440 | tf_op jit(solution)/shard_map/ppermute | solution.py:193
  6.8 1.3 %prepare.1 = (f32[4,128,256]{2,1,0:T(8,128)S(1)}, f32[16,128,256]{2,1,0:T(8,128)S(1)}, bf16[4096,256]{1,0:T(8,128)(2,1)S(1)}) custom-call(bf16[16,128,256]{2,1,0:T(8,128)(2,1)S(1)} %get-tuple-element.22.av_ref.refs_0_, bf16[16,128,256]{2,1,0:T(8,128)(2,1)S(1)} %get-tuple-element.23.up_ref, bf16[64,256]{1,0:T(8,128)(2,1)S(1)} %bitcast.5, ...), custom_call_target="tpu_custom_call" | custom-call | flops 268435456 | bytes 7012352 | tf_op jit(solution)/shard_map/prepare/pallas_call | solution.py:40
  8.1 5.3 %collective-permute-done.2.refs_2_ = bf16[4,128,256]{2,1,0:T(8,128)(2,1)S(1)} collective-permute-done((bf16[4,128,256]{2,1,0:T(8,128)(2,1)S(1)}, bf16[4,128,256]{2,1,0:T(8,128)(2,1)S(1)}, u32[]{:S(2)}, u32[]{:S(2)}) %collective-permute-start.2) | collective-permute-done | bytes 262176 | tf_op jit(solution)/shard_map/ppermute | solution.py:193
  13.4 0.2 layer_back.1.refs_5_
  13.5 1.8 %collective-permute-start.3 = (bf16[4,64,256]{2,1,0:T(8,128)(2,1)S(1)}, bf16[4,64,256]{2,1,0:T(8,128)(2,1)S(1)}, u32[]{:S(2)}, u32[]{:S(2)}) collective-permute-start(bf16[4,64,256]{2,1,0:T(8,128)(2,1)S(1)} %layer_back.1.refs_5_), channel_id=1, source_target_pairs={{0,2},{1,3},{2,0},{3,1},{4,6},{5,7},{6,4},{7,5},{8,10},{9,11},{10,... | collective-permute-start | bytes 393224 | tf_op jit(solution)/shard_map/ppermute | solution.py:193
  15.4 1.1 %table_part.3.refs_7_ = f32[1024,256]{1,0:T(8,128)S(1)} custom-call(bf16[16,128,256]{2,1,0:T(8,128)(2,1)S(1)} %get-tuple-element.22.av_ref.refs_0_, bf16[64,256]{1,0:T(8,128)(2,1)S(1)} %bitcast.6, f32[16,128,256]{2,1,0:T(8,128)S(1)} %get-tuple-element.24.refs_2_, s32[1,4096]{1,0:T(1,128)S(1)} %bitcast.9, ...), custom_call_target="tpu_custom_call" | custom-call | flops 536870912 | bytes 6471680 | tf_op jit(solution)/shard_map/table_part/pallas_call | solution.py:40
  16.5 2.2 %collective-permute-done.3.refs_6_ = bf16[4,64,256]{2,1,0:T(8,128)(2,1)S(1)} collective-permute-done((bf16[4,64,256]{2,1,0:T(8,128)(2,1)S(1)}, bf16[4,64,256]{2,1,0:T(8,128)(2,1)S(1)}, u32[]{:S(2)}, u32[]{:S(2)}) %collective-permute-start.3) | collective-permute-done | bytes 131104 | tf_op jit(solution)/shard_map/ppermute | solution.py:193
  18.6 1.7 %table_part.4.refs_6_.total_ref = f32[1024,256]{1,0:T(8,128)S(1)} custom-call(bf16[16,128,256]{2,1,0:T(8,128)(2,1)S(1)} %get-tuple-element.22.av_ref.refs_0_, bf16[64,256]{1,0:T(8,128)(2,1)S(1)} %bitcast.7, f32[16,128,256]{2,1,0:T(8,128)S(1)} %get-tuple-element.24.refs_2_, s32[1,4096]{1,0:T(1,128)S(1)} %bitcast.10, ...), custom_call_target="tpu_custom_call" | custom-call | flops 1073741824 | bytes 7651328 | tf_op jit(solution)/shard_map/table_part/pallas_call | solution.py:40
  20.4 0.8 %table_part.5 = (f32[128,256]{1,0:T(8,128)S(1)}, bf16[128,256]{1,0:T(8,128)(2,1)S(1)}, bf16[128,256]{1,0:T(8,128)(2,1)S(1)}, bf16[128,256]{1,0:T(8,128)(2,1)S(1)}, bf16[4,128,256]{2,1,0:T(8,128)(2,1)S(1)}) custom-call(bf16[16,128,256]{2,1,0:T(8,128)(2,1)S(1)} %get-tuple-element.22.av_ref.refs_0_, bf16[64,256]{1,0:T(8,128)(2,1)S(1)} %bitcast.8, ...), custom_call_target="tpu_custom_call" | custom-call | flops 268435456 | bytes 7061504 | tf_op jit(solution)/shard_map/table_part/pallas_call | solution.py:40
  21.2 2.7 %collective-permute-start.7 = (bf16[128,256]{1,0:T(8,128)(2,1)S(1)}, bf16[128,256]{1,0:T(8,128)(2,1)S(1)}, u32[]{:S(2)}, u32[]{:S(2)}) collective-permute-start(bf16[128,256]{1,0:T(8,128)(2,1)S(1)} %get-tuple-element.34), channel_id=1, source_target_pairs={{0,12},{4,8},{8,4},{12,0},{16,28},{20,24},{24,20},{28,16},{1,13},{... | collective-permute-start | bytes 196616 | tf_op jit(solution)/shard_map/ppermute | solution.py:193
  24.0 0.4 %collective-permute-start.8 = (bf16[128,256]{1,0:T(8,128)(2,1)S(1)}, bf16[128,256]{1,0:T(8,128)(2,1)S(1)}, u32[]{:S(2)}, u32[]{:S(2)}) collective-permute-start(bf16[128,256]{1,0:T(8,128)(2,1)S(1)} %get-tuple-element.35), channel_id=1, source_target_pairs={{0,8},{4,12},{8,0},{12,4},{16,24},{20,28},{24,16},{28,20},{1,9},{5... | collective-permute-start | bytes 196616 | tf_op jit(solution)/shard_map/ppermute | solution.py:193
  24.4 0.4 collective-permute-start.9
  24.8 0.4 %near_part.1 = (f32[128,256]{1,0:T(8,128)S(1)}, bf16[128,256]{1,0:T(8,128)(2,1)S(1)}, bf16[128,256]{1,0:T(8,128)(2,1)S(1)}, bf16[128,256]{1,0:T(8,128)(2,1)S(1)}) custom-call(bf16[4,128,256]{2,1,0:T(8,128)(2,1)S(1)} %get-tuple-element.30.grad_ref, s32[1,4096]{1,0:T(1,128)S(1)} %bitcast.12, bf16[4096,256]{1,0:T(8,128)(2,1)S(1)} %get-tuple-element.25.refs_4_.onehot_ref, ...), custom_call_target="tpu_custom_call" | custom-call | flops 268435456 | bytes 3751936 | tf_op jit(solution)/shard_map/near_part/pallas_call | solution.py:40
  25.2 2.7 %collective-permute-start.6 = (bf16[128,256]{1,0:T(8,128)(2,1)S(1)}, bf16[128,256]{1,0:T(8,128)(2,1)S(1)}, u32[]{:S(2)}, u32[]{:S(2)}) collective-permute-start(bf16[128,256]{1,0:T(8,128)(2,1)S(1)} %get-tuple-element.32), channel_id=1, source_target_pairs={{0,12},{4,8},{8,4},{12,0},{16,28},{20,24},{24,20},{28,16},{1,13},{... | collective-permute-start | bytes 196616 | tf_op jit(solution)/shard_map/ppermute | solution.py:193
  28.0 0.3 collective-permute-done.8.refs_2_
  28.3 1.1 %collective-permute-done.9.refs_3_ = bf16[128,256]{1,0:T(8,128)(2,1)S(1)} collective-permute-done((bf16[128,256]{1,0:T(8,128)(2,1)S(1)}, bf16[128,256]{1,0:T(8,128)(2,1)S(1)}, u32[]{:S(2)}, u32[]{:S(2)}) %collective-permute-start.9) | collective-permute-done | bytes 65568 | tf_op jit(solution)/shard_map/ppermute | solution.py:193
  29.4 2.0 %collective-permute-start.10 = (bf16[128,256]{1,0:T(8,128)(2,1)S(1)}, bf16[128,256]{1,0:T(8,128)(2,1)S(1)}, u32[]{:S(2)}, u32[]{:S(2)}) collective-permute-start(bf16[128,256]{1,0:T(8,128)(2,1)S(1)} %collect.3), channel_id=1, source_target_pairs={{0,16},{4,20},{8,24},{12,28},{16,0},{20,4},{24,8},{28,12},{1,17},{... | collective-permute-start | bytes 196616 | tf_op jit(solution)/shard_map/ppermute | solution.py:193
  31.4 1.6 %collective-permute-start.11 = (bf16[128,256]{1,0:T(8,128)(2,1)S(1)}, bf16[128,256]{1,0:T(8,128)(2,1)S(1)}, u32[]{:S(2)}, u32[]{:S(2)}) collective-permute-start(bf16[128,256]{1,0:T(8,128)(2,1)S(1)} %get-tuple-element.37), channel_id=1, source_target_pairs={{0,8},{4,12},{8,0},{12,4},{16,24},{20,28},{24,16},{28,20},{1,9},{5... | collective-permute-start | bytes 196616 | tf_op jit(solution)/shard_map/ppermute | solution.py:193
  33.0 1.1 %collective-permute-start.12 = (bf16[128,256]{1,0:T(8,128)(2,1)S(1)}, bf16[128,256]{1,0:T(8,128)(2,1)S(1)}, u32[]{:S(2)}, u32[]{:S(2)}) collective-permute-start(bf16[128,256]{1,0:T(8,128)(2,1)S(1)} %get-tuple-element.38), channel_id=1, source_target_pairs={{0,4},{4,0},{8,12},{12,8},{16,20},{20,16},{24,28},{28,24},{1,5},{5... | collective-permute-start | bytes 196616 | tf_op jit(solution)/shard_map/ppermute | solution.py:193
  34.0 1.4 %collective-permute-done.10.refs_2_ = bf16[128,256]{1,0:T(8,128)(2,1)S(1)} collective-permute-done((bf16[128,256]{1,0:T(8,128)(2,1)S(1)}, bf16[128,256]{1,0:T(8,128)(2,1)S(1)}, u32[]{:S(2)}, u32[]{:S(2)}) %collective-permute-start.10) | collective-permute-done | bytes 65568 | tf_op jit(solution)/shard_map/ppermute | solution.py:193
  35.5 0.4 %collective-permute-done.11.refs_1_ = bf16[128,256]{1,0:T(8,128)(2,1)S(1)} collective-permute-done((bf16[128,256]{1,0:T(8,128)(2,1)S(1)}, bf16[128,256]{1,0:T(8,128)(2,1)S(1)}, u32[]{:S(2)}, u32[]{:S(2)}) %collective-permute-start.11) | collective-permute-done | bytes 65568 | tf_op jit(solution)/shard_map/ppermute | solution.py:193
  35.9 1.3 %collective-permute-done.12.refs_2_ = bf16[128,256]{1,0:T(8,128)(2,1)S(1)} collective-permute-done((bf16[128,256]{1,0:T(8,128)(2,1)S(1)}, bf16[128,256]{1,0:T(8,128)(2,1)S(1)}, u32[]{:S(2)}, u32[]{:S(2)}) %collective-permute-start.12) | collective-permute-done | bytes 65568 | tf_op jit(solution)/shard_map/ppermute | solution.py:193
  37.2 0.7 %collect.5 = f32[128,256]{1,0:T(8,128)} custom-call(f32[128,256]{1,0:T(8,128)S(1)} %collect.4.refs_0_, bf16[128,256]{1,0:T(8,128)(2,1)S(1)} %collective-permute-done.11.refs_1_, bf16[128,256]{1,0:T(8,128)(2,1)S(1)} %collective-permute-done.12.refs_2_), custom_call_target="tpu_custom_call" | custom-call | flops 32768 | bytes 393216 | tf_op jit(solution)/shard_map/collect/pallas_call | solution.py:40
  (17 shorter events, 0.1 us)
Async XLA Ops:
  0.0 1.6 %copy-start.2 = (bf16[64,128]{1,0:T(8,128)(2,1)S(1)}, bf16[64,128]{1,0:T(8,128)(2,1)}, u32[]{:S(2)}) copy-start(bf16[64,128]{1,0:T(8,128)(2,1)} %proj_ref.5) | copy-start | bytes 49156
  0.0 1.6 %copy-start = (bf16[256,64]{0,1:T(8,128)(2,1)S(1)}, bf16[256,64]{0,1:T(8,128)(2,1)}, u32[]{:S(2)}) copy-start(bf16[256,64]{0,1:T(8,128)(2,1)} %param.9) | copy-start | bytes 98308
  2.0 4.7 %copy-start.3 = (bf16[256,256]{1,0:T(8,128)(2,1)S(1)}, bf16[256,256]{1,0:T(8,128)(2,1)}, u32[]{:S(2)}) copy-start(bf16[256,256]{1,0:T(8,128)(2,1)} %mix_ref.1) | copy-start | bytes 393220
  2.1 4.7 %copy-start.4 = (s32[4096]{0:T(1024)S(1)}, s32[4096]{0:T(1024)}, u32[]{:S(2)}) copy-start(s32[4096]{0:T(1024)} %param.13) | copy-start | bytes 49156
  2.1 1.7 %collective-permute-start.1 = (bf16[4,128,256]{2,1,0:T(8,128)(2,1)S(1)}, bf16[4,128,256]{2,1,0:T(8,128)(2,1)S(1)}, u32[]{:S(2)}, u32[]{:S(2)}) collective-permute-start(bf16[4,128,256]{2,1,0:T(8,128)(2,1)S(1)} %first_sums.1), channel_id=1, source_target_pairs={{0,1},{1,0},{2,3},{3,2},{4,5},{5,4},{6,7},{7,6},{8,9},{9,8},{10,11... | collective-permute-start | bytes 786440 | tf_op jit(solution)/shard_map/ppermute | solution.py:193
  3.2 10.2 %collective-permute-start = (f32[4,128,256]{2,1,0:T(8,128)S(1)}, f32[4,128,256]{2,1,0:T(8,128)S(1)}, u32[]{:S(2)}, u32[]{:S(2)}) collective-permute-start(f32[4,128,256]{2,1,0:T(8,128)S(1)} %get-tuple-element.27), channel_id=1, source_target_pairs={{0,1},{1,0},{2,3},{3,2},{4,5},{5,4},{6,7},{7,6},{8,9},{9,8},{10,11... | collective-permute-start | bytes 1572872 | tf_op jit(solution)/shard_map/ppermute | solution.py:193
  3.8 11.6 %copy-start.1 = (s32[4096,1]{0,1:T(1,128)S(1)}, s32[4096,1]{0,1:T(1,128)}, u32[]{:S(2)}) copy-start(s32[4096,1]{0,1:T(1,128)} %param.12) | copy-start | bytes 49156
  3.8 9.6 %collective-permute-start.2 = (bf16[4,128,256]{2,1,0:T(8,128)(2,1)S(1)}, bf16[4,128,256]{2,1,0:T(8,128)(2,1)S(1)}, u32[]{:S(2)}, u32[]{:S(2)}) collective-permute-start(bf16[4,128,256]{2,1,0:T(8,128)(2,1)S(1)} %add.1), channel_id=1, source_target_pairs={{0,2},{1,3},{2,0},{3,1},{4,6},{5,7},{6,4},{7,5},{8,10},{9,11},{10,... | collective-permute-start | bytes 786440 | tf_op jit(solution)/shard_map/ppermute | solution.py:193
  13.5 5.1 %collective-permute-start.3 = (bf16[4,64,256]{2,1,0:T(8,128)(2,1)S(1)}, bf16[4,64,256]{2,1,0:T(8,128)(2,1)S(1)}, u32[]{:S(2)}, u32[]{:S(2)}) collective-permute-start(bf16[4,64,256]{2,1,0:T(8,128)(2,1)S(1)} %layer_back.1.refs_5_), channel_id=1, source_target_pairs={{0,2},{1,3},{2,0},{3,1},{4,6},{5,7},{6,4},{7,5},{8,10},{9,11},{10,... | collective-permute-start | bytes 393224 | tf_op jit(solution)/shard_map/ppermute | solution.py:193
  15.4 3.3 %collective-permute-start.5 = (bf16[4,64,256]{2,1,0:T(8,128)(2,1)S(1)}, bf16[4,64,256]{2,1,0:T(8,128)(2,1)S(1)}, u32[]{:S(2)}, u32[]{:S(2)}) collective-permute-start(bf16[4,64,256]{2,1,0:T(8,128)(2,1)S(1)} %layer_back.1.refs_5_), channel_id=1, source_target_pairs={{0,1},{1,0},{2,3},{3,2},{4,5},{5,4},{6,7},{7,6},{8,9},{9,8},{10,11... | collective-permute-start | bytes 393224 | tf_op jit(solution)/shard_map/ppermute | solution.py:193
  18.6 1.8 %collective-permute-start.4 = (bf16[4,64,256]{2,1,0:T(8,128)(2,1)S(1)}, bf16[4,64,256]{2,1,0:T(8,128)(2,1)S(1)}, u32[]{:S(2)}, u32[]{:S(2)}) collective-permute-start(bf16[4,64,256]{2,1,0:T(8,128)(2,1)S(1)} %collective-permute-done.3.refs_6_), channel_id=1, source_target_pairs={{0,1},{1,0},{2,3},{3,2},{4,5},{5,4},{6,7},{7,6},{8,9},{9,8},{10,11... | collective-permute-start | bytes 393224 | tf_op jit(solution)/shard_map/ppermute | solution.py:193
  21.2 6.7 %collective-permute-start.7 = (bf16[128,256]{1,0:T(8,128)(2,1)S(1)}, bf16[128,256]{1,0:T(8,128)(2,1)S(1)}, u32[]{:S(2)}, u32[]{:S(2)}) collective-permute-start(bf16[128,256]{1,0:T(8,128)(2,1)S(1)} %get-tuple-element.34), channel_id=1, source_target_pairs={{0,12},{4,8},{8,4},{12,0},{16,28},{20,24},{24,20},{28,16},{1,13},{... | collective-permute-start | bytes 196616 | tf_op jit(solution)/shard_map/ppermute | solution.py:193
  24.0 4.3 %collective-permute-start.8 = (bf16[128,256]{1,0:T(8,128)(2,1)S(1)}, bf16[128,256]{1,0:T(8,128)(2,1)S(1)}, u32[]{:S(2)}, u32[]{:S(2)}) collective-permute-start(bf16[128,256]{1,0:T(8,128)(2,1)S(1)} %get-tuple-element.35), channel_id=1, source_target_pairs={{0,8},{4,12},{8,0},{12,4},{16,24},{20,28},{24,16},{28,20},{1,9},{5... | collective-permute-start | bytes 196616 | tf_op jit(solution)/shard_map/ppermute | solution.py:193
  24.4 5.0 %collective-permute-start.9 = (bf16[128,256]{1,0:T(8,128)(2,1)S(1)}, bf16[128,256]{1,0:T(8,128)(2,1)S(1)}, u32[]{:S(2)}, u32[]{:S(2)}) collective-permute-start(bf16[128,256]{1,0:T(8,128)(2,1)S(1)} %get-tuple-element.36), channel_id=1, source_target_pairs={{0,4},{4,0},{8,12},{12,8},{16,20},{20,16},{24,28},{28,24},{1,5},{5... | collective-permute-start | bytes 196616 | tf_op jit(solution)/shard_map/ppermute | solution.py:193
  25.2 8.8 %collective-permute-start.6 = (bf16[128,256]{1,0:T(8,128)(2,1)S(1)}, bf16[128,256]{1,0:T(8,128)(2,1)S(1)}, u32[]{:S(2)}, u32[]{:S(2)}) collective-permute-start(bf16[128,256]{1,0:T(8,128)(2,1)S(1)} %get-tuple-element.32), channel_id=1, source_target_pairs={{0,12},{4,8},{8,4},{12,0},{16,28},{20,24},{24,20},{28,16},{1,13},{... | collective-permute-start | bytes 196616 | tf_op jit(solution)/shard_map/ppermute | solution.py:193
  29.4 6.0 %collective-permute-start.10 = (bf16[128,256]{1,0:T(8,128)(2,1)S(1)}, bf16[128,256]{1,0:T(8,128)(2,1)S(1)}, u32[]{:S(2)}, u32[]{:S(2)}) collective-permute-start(bf16[128,256]{1,0:T(8,128)(2,1)S(1)} %collect.3), channel_id=1, source_target_pairs={{0,16},{4,20},{8,24},{12,28},{16,0},{20,4},{24,8},{28,12},{1,17},{... | collective-permute-start | bytes 196616 | tf_op jit(solution)/shard_map/ppermute | solution.py:193
  31.4 4.5 %collective-permute-start.11 = (bf16[128,256]{1,0:T(8,128)(2,1)S(1)}, bf16[128,256]{1,0:T(8,128)(2,1)S(1)}, u32[]{:S(2)}, u32[]{:S(2)}) collective-permute-start(bf16[128,256]{1,0:T(8,128)(2,1)S(1)} %get-tuple-element.37), channel_id=1, source_target_pairs={{0,8},{4,12},{8,0},{12,4},{16,24},{20,28},{24,16},{28,20},{1,9},{5... | collective-permute-start | bytes 196616 | tf_op jit(solution)/shard_map/ppermute | solution.py:193
  33.0 4.3 %collective-permute-start.12 = (bf16[128,256]{1,0:T(8,128)(2,1)S(1)}, bf16[128,256]{1,0:T(8,128)(2,1)S(1)}, u32[]{:S(2)}, u32[]{:S(2)}) collective-permute-start(bf16[128,256]{1,0:T(8,128)(2,1)S(1)} %get-tuple-element.38), channel_id=1, source_target_pairs={{0,4},{4,0},{8,12},{12,8},{16,20},{20,16},{24,28},{28,24},{1,5},{5... | collective-permute-start | bytes 196616 | tf_op jit(solution)/shard_map/ppermute | solution.py:193

commit v10 on v8

--- a/solution.py
+++ b/solution.py
@@ -10,7 +10,8 @@
 SHARD = 256
 F32, BF16 = jnp.float32, jnp.bfloat16
 LIMIT = 20 * 2**20
-LOAD_LIMIT = 52600 * 2**10
+FIRST_LIMIT = 54400 * 2**10
+REST_LIMIT = 52600 * 2**10
 VMEM = pl.BlockSpec(memory_space=pltpu.VMEM)
 HBM = pl.BlockSpec(memory_space=pltpu.HBM)
 shape = jax.ShapeDtypeStruct
@@ -49,17 +50,32 @@
     )(*args)
 
 
-def load_kernel(piece, av_hbm, up_hbm, av_ref, up_ref, sems):
+def load_kernel(order, piece, av_hbm, up_hbm, *refs):
+    av_ref, up_ref, sems = refs[-3:]
     me = lax.axis_index("dim")
     copies = []
-    for j in range(av_ref.shape[0] // piece):
-        source, to = pl.ds((me ^ j) * piece, piece), pl.ds(j * piece, piece)
-        copies.append(pltpu.make_async_copy(av_hbm.at[source], av_ref.at[to], sems.at[2 * j]))
-        copies.append(pltpu.make_async_copy(up_hbm.at[source], up_ref.at[to], sems.at[2 * j + 1]))
+    for n, j in enumerate(order):
+        source, to = pl.ds((me ^ j) * piece, piece), pl.ds(n * piece, piece)
+        copies.append(pltpu.make_async_copy(av_hbm.at[source], av_ref.at[to], sems.at[2 * n]))
+        copies.append(pltpu.make_async_copy(up_hbm.at[source], up_ref.at[to], sems.at[2 * n + 1]))
     for copy in copies:
         copy.start()
     for copy in copies:
         copy.wait()
+
+
+def load(order, piece, av, up, limit, *others):
+    part = shape((len(order) * piece, *av.shape[1:]), BF16)
+    return call(
+        functools.partial(load_kernel, order, piece),
+        "load",
+        (av, up, *others),
+        [part] * 2,
+        0,
+        limit=limit,
+        specs=[HBM] * 2 + [pl.BlockSpec(memory_space=pl.ANY)] * len(others),
+        scratch=[pltpu.SemaphoreType.DMA((2 * len(order),))],
+    )
 
 
 def width_sums(comp_t_ref, proj_ref, av, up, out_ref, at):
@@ -72,24 +88,28 @@
     out_ref[at, rank:] = (grads - jnp.mean(grads, axis=0, keepdims=True)).astype(kind)
 
 
-def sums_kernel(orders, piece, av_ref, up_ref, comp_t_ref, proj_ref, *out_refs):
-    for order, out_ref in zip(orders, out_refs):
-        for n in range(len(order) * piece):
-            at = order[n // piece] * piece + n % piece
-            width_sums(comp_t_ref, proj_ref, av_ref[at], up_ref[at], out_ref, n)
-
-
-def prepare_kernel(low, piece, av_ref, up_ref, comp_t_ref, proj_ref, mix_ref, slot_ref, out_ref, linear_ref, onehot_ref):
-    sums_kernel([low], piece, av_ref, up_ref, comp_t_ref, proj_ref, out_ref)
+def sums_kernel(starts, av_ref, up_ref, comp_t_ref, proj_ref, *out_refs):
+    for start, out_ref in zip(starts, out_refs):
+        for n in range(out_ref.shape[0]):
+            width_sums(comp_t_ref, proj_ref, av_ref[start + n], up_ref[start + n], out_ref, n)
+
+
+def prepare_kernel(
+    order, piece, starts, first_ref, av_ref, up_ref, comp_t_ref, proj_ref, mix_ref, slot_ref, _,
+    send_ref, keep_ref, linear_ref, onehot_ref,
+):
+    sums_kernel(starts, av_ref, up_ref, comp_t_ref, proj_ref, send_ref, keep_ref)
     me = lax.axis_index("dim")
-    samples, _, features = up_ref.shape
+    count, _, features = up_ref.shape
     slots = lax.broadcasted_iota(jnp.int32, (SHARD, features), 0)
-    for at in range(samples):
-        b = at ^ (me * piece)
-        up = up_ref[at]
-        linear_ref[at] = up.astype(F32) + dot_nt(up, mix_ref[...])
-        hit = slots == slot_ref[:, pl.ds(pl.multiple_of(b * features, features), features)]
-        onehot_ref[at * features:(at + 1) * features] = jnp.where(hit, 1.0, 0.0).T.astype(BF16)
+    for n, j in enumerate(order):
+        for s in range(piece):
+            at, place = j * piece + s, n * piece + s
+            b = at ^ (me * piece)
+            up = up_ref[place] if place < count else first_ref[place - count]
+            linear_ref[at] = up.astype(F32) + dot_nt(up, mix_ref[...])
+            hit = slots == slot_ref[:, pl.ds(pl.multiple_of(b * features, features), features)]
+            onehot_ref[at * features:(at + 1) * features] = jnp.where(hit, 1.0, 0.0).T.astype(BF16)
 
 
 def add_kernel(keep_ref, got_ref, out_ref):
@@ -125,18 +145,20 @@
         masked[o * width:(o + 1) * width, n * features:(n + 1) * features] = grad * mask
 
 
-def table_kernel(start, piece, owners, far, count, has_total, *refs):
-    av_ref, comp_t_ref, linear_ref, owner_ref, onehot_ref = refs[:5]
-    pair_refs, refs = refs[5:5 + count], refs[5 + count:]
+def table_kernel(order, start, piece, owners, far, count, has_total, *refs):
+    rest_ref, first_ref, comp_t_ref, linear_ref, owner_ref, onehot_ref = refs[:6]
+    pair_refs, refs = refs[6:6 + count], refs[6 + count:]
     if has_total:
         total_ref, refs = refs[0], refs[1:]
     *outs, masked = refs
-    _, width, features = av_ref.shape
+    loaded, width, features = rest_ref.shape
     comp_t = comp_t_ref[...]
     for n in range(count * piece):
         at = start + n
+        place = order.index(at // piece) * piece + at % piece
+        av = rest_ref[place] if place < loaded else first_ref[place - loaded]
         back = pair_refs[n // piece][n % piece]
-        both = dot_nt(av_ref[at], jnp.concatenate([comp_t, back])).astype(BF16)
+        both = dot_nt(av, jnp.concatenate([comp_t, back])).astype(BF16)
         grad = linear_ref[at] + dot_nn(both, jnp.concatenate([back, comp_t]))
         grad = grad.astype(BF16)
         if far:
@@ -163,7 +185,7 @@
         out[...] = added[o * width:(o + 1) * width].astype(out.dtype)
 
 
-def table_part(j, piece, owners, far, arrays, pairs, total):
+def table_part(order, j, piece, owners, far, arrays, pairs, total):
     _, width, features = arrays[0].shape
     lookups = len(pairs) * piece * features
     if far:
@@ -171,7 +193,7 @@
     else:
         shapes = [shape((len(owners) * width, SHARD), F32)]
     return call(
-        functools.partial(table_kernel, j * piece, piece, owners, far, len(pairs), total is not None),
+        functools.partial(table_kernel, order, j * piece, piece, owners, far, len(pairs), total is not None),
         "table_part",
         [*arrays, *pairs] + ([] if total is None else [total]),
         shapes,
@@ -214,44 +236,36 @@
     owner, slot = row_owner.reshape(1, -1), row_slot.reshape(1, -1)
     part = shape((quarter, 2 * rank, features), F32)
     comp_t, proj = compress.T, interact_proj
-    av, up = call(
-        functools.partial(load_kernel, piece),
-        "load",
-        (attribute_vectors, upstream),
-        [shape(upstream.shape, BF16)] * 2,
-        0,
-        limit=LOAD_LIMIT,
-        specs=[HBM] * 2,
-        scratch=[pltpu.SemaphoreType.DMA((2 * peers,))],
-    )
-    args = (av, up, comp_t, proj)
+    first_order = [j ^ core for j in high]
+    order = high + [j ^ core for j in low] + low + first_order
+    first_av, first_up = load(first_order, piece, attribute_vectors, upstream, FIRST_LIMIT)
     (send_high,) = call(
-        functools.partial(sums_kernel, [[j ^ core for j in high]], piece),
+        functools.partial(sums_kernel, [0]),
         "first_sums",
-        args,
+        (first_av, first_up, comp_t, proj),
         [shape(part.shape, BF16)],
         quarter * sample_flops,
     )
     got_high = swap(send_high, core)
-    keep_high, send_low = call(
-        functools.partial(sums_kernel, [high, [j ^ core for j in low]], piece),
-        "sums",
-        args,
-        [part] * 2,
-        2 * quarter * sample_flops,
-    )
-    got_low = swap(send_low, core)
-    got = swap(add(keep_high, got_high), bits[1])
-    keep_low, linear, onehot = call(
-        functools.partial(prepare_kernel, low, piece),
+    av, up = load(order[:3 * count], piece, attribute_vectors, upstream, REST_LIMIT, send_high)
+    args = (av, up, comp_t, proj)
+    (keep_high,) = call(
+        functools.partial(sums_kernel, [0]), "sums", args, [part], quarter * sample_flops
+    )
+    sent = add(keep_high, got_high)
+    got = swap(sent, bits[1])
+    send_low, keep_low, linear, onehot = call(
+        functools.partial(prepare_kernel, order, piece, [quarter, 2 * quarter]),
         "prepare",
-        (*args, linear_mix, slot),
-        [part, shape(up.shape, F32), shape((samples * features, SHARD), BF16)],
+        (first_up, *args, linear_mix, slot, sent),
+        [shape(part.shape, BF16), part, shape(upstream.shape, F32), shape((samples * features, SHARD), BF16)],
         2 * samples * width * features * features,
     )
-    arrays = (av, comp_t, linear, owner, onehot)
-
-    terms = [keep_low, got_low, got]
+    got_low = swap(after(send_low, linear), core)
+    got = after(got, keep_low)
+    arrays = (av, first_av, comp_t, linear, owner, onehot)
+
+    terms = [keep_low, got, got_low]
     for bit in bits[2:]:
         keep = sum(term.astype(F32) for term in terms)
         half = keep.shape[0] // 2
@@ -267,16 +281,16 @@
     pairs = {0: pair}
     everyone = list(range(owners))
     near, far = everyone[:owners // 2], everyone[owners // 2:]
-    (total,) = table_part(0, piece, everyone, False, arrays, [pair], None)
+    (total,) = table_part(order, 0, piece, everyone, False, arrays, [pair], None)
     for bit in reversed(bits[1:]):
         pairs.update({j ^ bit: swap(got, bit) for j, got in pairs.items()})
     for j in list(pairs):
         pairs[j] = after(pairs[j], total) if j else pair
         pairs[j ^ core] = swap(pairs[j], core)
     middle = [pairs[j] for j in range(1, peers - 1)]
-    (total,) = table_part(1, piece, everyone, False, arrays, middle, total)
+    (total,) = table_part(order, 1, piece, everyone, False, arrays, middle, total)
     last = peers - 1
-    *opposite, grad = table_part(last, piece, far, True, arrays, [pairs[last]], total)
+    *opposite, grad = table_part(order, last, piece, far, True, arrays, [pairs[last]], total)
     own = call(
         functools.partial(near_kernel, last * piece, piece, near),
         "near_part",

time: 36.5 us -> 37.3 us (1.022)
  Pallas kernels: 8.92 us -> 9.81 us
    pallas_call x12 -> x13, Pallas kernels: 8.92 us -> 9.81 us  [call(): pl.pallas_call(kernel, in_specs=specs or [VMEM] * len(args), out_specs=[V...]
  transfers between devices with their start and end apart: 13 -> 13, of which waited for: 6 -> 4; matrix products, arithmetic and copies ran while one was open for 0% -> 0% of each run, Pallas kernels for 14% -> 18%
where the time goes in v10:
time: 37.3 us; the launch traced here: 37.2 us
  starting transfers between devices  14.9 us (40%)
  waiting for transfers between devices  12.3 us (33%)
  Pallas kernels  9.81 us (26%)
    ppermute x13, starting transfers between devices, swap(): lax.ppermute(x, axis, [(i, i ^ bit) for i in range(lax.axis_size(axis))])  14.9 us
    ppermute x13, waiting for transfers between devices, swap(): lax.ppermute(x, axis, [(i, i ^ bit) for i in range(lax.axis_size(axis))])  12.3 us
    pallas_call x13, Pallas kernels, call(): pl.pallas_call(kernel, in_specs=specs or [VMEM] * len(args), out_specs=[V...  9.81 us
  transfers between devices with their start and end apart: 13, of which 4 were waited for; matrix products, arithmetic and copies ran while one was open for 0% of the time, Pallas kernels for 18%

profile of v10, /device:TPU:0, one launch (start us, length us, event | category | flops | bytes accessed | tf_op | source)
XLA Modules:
  0.0 37.2 jit_solution(10042495764400182842)
XLA Ops:
  0.0 1.1 %load.2 = (bf16[4,128,256]{2,1,0:T(8,128)(2,1)S(1)}, bf16[4,128,256]{2,1,0:T(8,128)(2,1)S(1)}) custom-call(bf16[16,128,256]{2,1,0:T(8,128)(2,1)} %av_hbm.3, bf16[16,128,256]{2,1,0:T(8,128)(2,1)} %up_hbm.3), custom_call_target="tpu_custom_call" | custom-call | bytes 2621440 | tf_op jit(solution)/shard_map/load/pallas_call | solution.py:41
  1.1 0.4 %first_sums.1.refs_0_ = bf16[4,128,256]{2,1,0:T(8,128)(2,1)S(1)} custom-call(bf16[4,128,256]{2,1,0:T(8,128)(2,1)S(1)} %get-tuple-element.25.av_ref.refs_1_, bf16[4,128,256]{2,1,0:T(8,128)(2,1)S(1)} %get-tuple-element.26.up_ref.first_ref, bf16[64,256]{1,0:T(8,128)(2,1)S(1)} %bitcast.3, bf16[64,128]{1,0:T(8,128)(2,1)S(1)} %copy-done.2), custom_call_target="tpu_custom_call" | custom-call | flops 50331648 | bytes 835584 | tf_op jit(solution)/shard_map/first_sums/pallas_call | solution.py:41
  1.5 0.5 %collective-permute-start = (bf16[4,128,256]{2,1,0:T(8,128)(2,1)S(1)}, bf16[4,128,256]{2,1,0:T(8,128)(2,1)S(1)}, u32[]{:S(2)}, u32[]{:S(2)}) collective-permute-start(bf16[4,128,256]{2,1,0:T(8,128)(2,1)S(1)} %first_sums.1.refs_0_), channel_id=1, source_target_pairs={{0,1},{1,0},{2,3},{3,2},{4,5},{5,4},{6,7},{7,6},{8,9},{9,8},{10,11... | collective-permute-start | bytes 786440 | tf_op jit(solution)/shard_map/ppermute | solution.py:215
  2.0 1.4 %load.3 = (bf16[12,128,256]{2,1,0:T(8,128)(2,1)S(1)}, bf16[12,128,256]{2,1,0:T(8,128)(2,1)S(1)}) custom-call(bf16[16,128,256]{2,1,0:T(8,128)(2,1)} %av_hbm.3, bf16[16,128,256]{2,1,0:T(8,128)(2,1)} %up_hbm.3, bf16[4,128,256]{2,1,0:T(8,128)(2,1)S(1)} %first_sums.1.refs_0_), custom_call_target="tpu_custom_call" | custom-call | bytes 3932160 | tf_op jit(solution)/shard_map/load/pallas_call | solution.py:41
  3.4 0.0 copy-start.3
  3.4 0.0 copy-start.4
  3.5 0.4 %sums.1.keep_ref = f32[4,128,256]{2,1,0:T(8,128)S(1)} custom-call(bf16[12,128,256]{2,1,0:T(8,128)(2,1)S(1)} %get-tuple-element.27.av_ref.refs_0_, bf16[12,128,256]{2,1,0:T(8,128)(2,1)S(1)} %get-tuple-element.28.up_ref, bf16[64,256]{1,0:T(8,128)(2,1)S(1)} %bitcast.4, bf16[64,128]{1,0:T(8,128)(2,1)S(1)} %copy-done.2), custom_call_target="tpu_custom_call" | custom-call | flops 50331648 | bytes 2146304 | tf_op jit(solution)/shard_map/sums/pallas_call | solution.py:41
  3.9 0.0 copy-start.1
  3.9 0.1 add.1._
  4.0 2.6 %collective-permute-start.1 = (bf16[4,128,256]{2,1,0:T(8,128)(2,1)S(1)}, bf16[4,128,256]{2,1,0:T(8,128)(2,1)S(1)}, u32[]{:S(2)}, u32[]{:S(2)}) collective-permute-start(bf16[4,128,256]{2,1,0:T(8,128)(2,1)S(1)} %add.1._), channel_id=1, source_target_pairs={{0,2},{1,3},{2,0},{3,1},{4,6},{5,7},{6,4},{7,5},{8,10},{9,11},{10,... | collective-permute-start | bytes 786440 | tf_op jit(solution)/shard_map/ppermute | solution.py:215
  6.6 1.4 %prepare.1 = (bf16[4,128,256]{2,1,0:T(8,128)(2,1)S(1)}, f32[4,128,256]{2,1,0:T(8,128)S(1)}, f32[16,128,256]{2,1,0:T(8,128)S(1)}, bf16[4096,256]{1,0:T(8,128)(2,1)S(1)}) custom-call(bf16[4,128,256]{2,1,0:T(8,128)(2,1)S(1)} %get-tuple-element.26.up_ref.first_ref, bf16[12,128,256]{2,1,0:T(8,128)(2,1)S(1)} %get-tuple-element.27.av_ref.refs_0_, ...), custom_call_target="tpu_custom_call" | custom-call | flops 268435456 | bytes 7274496 | tf_op jit(solution)/shard_map/prepare/pallas_call | solution.py:41
  8.0 0.3 collective-permute-start.2
  8.3 5.2 %collective-permute-done.1.refs_1_ = bf16[4,128,256]{2,1,0:T(8,128)(2,1)S(1)} collective-permute-done((bf16[4,128,256]{2,1,0:T(8,128)(2,1)S(1)}, bf16[4,128,256]{2,1,0:T(8,128)(2,1)S(1)}, u32[]{:S(2)}, u32[]{:S(2)}) %collective-permute-start.1) | collective-permute-done | bytes 262176 | tf_op jit(solution)/shard_map/ppermute | solution.py:215
  13.5 0.2 layer_back.1.refs_6_
  13.7 1.8 %collective-permute-start.3 = (bf16[4,64,256]{2,1,0:T(8,128)(2,1)S(1)}, bf16[4,64,256]{2,1,0:T(8,128)(2,1)S(1)}, u32[]{:S(2)}, u32[]{:S(2)}) collective-permute-start(bf16[4,64,256]{2,1,0:T(8,128)(2,1)S(1)} %layer_back.1.refs_6_), channel_id=1, source_target_pairs={{0,2},{1,3},{2,0},{3,1},{4,6},{5,7},{6,4},{7,5},{8,10},{9,11},{10,... | collective-permute-start | bytes 393224 | tf_op jit(solution)/shard_map/ppermute | solution.py:215
  15.5 0.0 collective-permute-start.5
  15.5 1.1 %table_part.3.refs_8_ = f32[1024,256]{1,0:T(8,128)S(1)} custom-call(bf16[12,128,256]{2,1,0:T(8,128)(2,1)S(1)} %get-tuple-element.27.av_ref.refs_0_, bf16[4,128,256]{2,1,0:T(8,128)(2,1)S(1)} %get-tuple-element.25.av_ref.refs_1_, bf16[64,256]{1,0:T(8,128)(2,1)S(1)} %bitcast.6, f32[16,128,256]{2,1,0:T(8,128)S(1)} %get-tuple-element.29.refs_3_, ...), custom_call_target="tpu_custom_call" | custom-call | flops 536870912 | bytes 6471680 | tf_op jit(solution)/shard_map/table_part/pallas_call | solution.py:41
  16.6 2.5 %collective-permute-done.3.refs_7_ = bf16[4,64,256]{2,1,0:T(8,128)(2,1)S(1)} collective-permute-done((bf16[4,64,256]{2,1,0:T(8,128)(2,1)S(1)}, bf16[4,64,256]{2,1,0:T(8,128)(2,1)S(1)}, u32[]{:S(2)}, u32[]{:S(2)}) %collective-permute-start.3) | collective-permute-done | bytes 131104 | tf_op jit(solution)/shard_map/ppermute | solution.py:215
  19.1 1.7 %table_part.4.refs_7_.total_ref = f32[1024,256]{1,0:T(8,128)S(1)} custom-call(bf16[12,128,256]{2,1,0:T(8,128)(2,1)S(1)} %get-tuple-element.27.av_ref.refs_0_, bf16[4,128,256]{2,1,0:T(8,128)(2,1)S(1)} %get-tuple-element.25.av_ref.refs_1_, bf16[64,256]{1,0:T(8,128)(2,1)S(1)} %bitcast.7, f32[16,128,256]{2,1,0:T(8,128)S(1)} %get-tuple-element.29.refs_3_, ...), custom_call_target="tpu_custom_call" | custom-call | flops 1073741824 | bytes 7651328 | tf_op jit(solution)/shard_map/table_part/pallas_call | solution.py:41
  20.9 0.8 %table_part.5 = (f32[128,256]{1,0:T(8,128)S(1)}, bf16[128,256]{1,0:T(8,128)(2,1)S(1)}, bf16[128,256]{1,0:T(8,128)(2,1)S(1)}, bf16[128,256]{1,0:T(8,128)(2,1)S(1)}, bf16[4,128,256]{2,1,0:T(8,128)(2,1)S(1)}) custom-call(bf16[12,128,256]{2,1,0:T(8,128)(2,1)S(1)} %get-tuple-element.27.av_ref.refs_0_, bf16[4,128,256]{2,1,0:T(8,128)(2,1)S(1)} %get-tuple-element.25.av_ref.refs_1_, ...), custom_call_target="tpu_custom_call" | custom-call | flops 268435456 | bytes 7061504 | tf_op jit(solution)/shard_map/table_part/pallas_call | solution.py:41
  21.7 1.7 %collective-permute-start.10 = (bf16[128,256]{1,0:T(8,128)(2,1)S(1)}, bf16[128,256]{1,0:T(8,128)(2,1)S(1)}, u32[]{:S(2)}, u32[]{:S(2)}) collective-permute-start(bf16[128,256]{1,0:T(8,128)(2,1)S(1)} %get-tuple-element.43), channel_id=1, source_target_pairs={{0,8},{4,12},{8,0},{12,4},{16,24},{20,28},{24,16},{28,20},{1,9},{5... | collective-permute-start | bytes 196616 | tf_op jit(solution)/shard_map/ppermute | solution.py:215
  23.4 1.5 %collective-permute-start.11 = (bf16[128,256]{1,0:T(8,128)(2,1)S(1)}, bf16[128,256]{1,0:T(8,128)(2,1)S(1)}, u32[]{:S(2)}, u32[]{:S(2)}) collective-permute-start(bf16[128,256]{1,0:T(8,128)(2,1)S(1)} %get-tuple-element.44), channel_id=1, source_target_pairs={{0,4},{4,0},{8,12},{12,8},{16,20},{20,16},{24,28},{28,24},{1,5},{5... | collective-permute-start | bytes 196616 | tf_op jit(solution)/shard_map/ppermute | solution.py:215
  24.9 0.4 %collective-permute-start.9 = (bf16[128,256]{1,0:T(8,128)(2,1)S(1)}, bf16[128,256]{1,0:T(8,128)(2,1)S(1)}, u32[]{:S(2)}, u32[]{:S(2)}) collective-permute-start(bf16[128,256]{1,0:T(8,128)(2,1)S(1)} %get-tuple-element.42), channel_id=1, source_target_pairs={{0,12},{4,8},{8,4},{12,0},{16,28},{20,24},{24,20},{28,16},{1,13},{... | collective-permute-start | bytes 196616 | tf_op jit(solution)/shard_map/ppermute | solution.py:215
  25.2 0.4 %near_part.1 = (f32[128,256]{1,0:T(8,128)S(1)}, bf16[128,256]{1,0:T(8,128)(2,1)S(1)}, bf16[128,256]{1,0:T(8,128)(2,1)S(1)}, bf16[128,256]{1,0:T(8,128)(2,1)S(1)}) custom-call(bf16[4,128,256]{2,1,0:T(8,128)(2,1)S(1)} %get-tuple-element.36.grad_ref, s32[1,4096]{1,0:T(1,128)S(1)} %bitcast.12, bf16[4096,256]{1,0:T(8,128)(2,1)S(1)} %get-tuple-element.30.refs_5_.onehot_ref, ...), custom_call_target="tpu_custom_call" | custom-call | flops 268435456 | bytes 3751936 | tf_op jit(solution)/shard_map/near_part/pallas_call | solution.py:41
  25.7 2.6 %collective-permute-start.6 = (bf16[128,256]{1,0:T(8,128)(2,1)S(1)}, bf16[128,256]{1,0:T(8,128)(2,1)S(1)}, u32[]{:S(2)}, u32[]{:S(2)}) collective-permute-start(bf16[128,256]{1,0:T(8,128)(2,1)S(1)} %get-tuple-element.38), channel_id=1, source_target_pairs={{0,12},{4,8},{8,4},{12,0},{16,28},{20,24},{24,20},{28,16},{1,13},{... | collective-permute-start | bytes 196616 | tf_op jit(solution)/shard_map/ppermute | solution.py:215
  28.3 0.4 %collective-permute-start.7 = (bf16[128,256]{1,0:T(8,128)(2,1)S(1)}, bf16[128,256]{1,0:T(8,128)(2,1)S(1)}, u32[]{:S(2)}, u32[]{:S(2)}) collective-permute-start(bf16[128,256]{1,0:T(8,128)(2,1)S(1)} %get-tuple-element.39), channel_id=1, source_target_pairs={{0,8},{4,12},{8,0},{12,4},{16,24},{20,28},{24,16},{28,20},{1,9},{5... | collective-permute-start | bytes 196616 | tf_op jit(solution)/shard_map/ppermute | solution.py:215
  28.7 0.5 %collective-permute-start.8 = (bf16[128,256]{1,0:T(8,128)(2,1)S(1)}, bf16[128,256]{1,0:T(8,128)(2,1)S(1)}, u32[]{:S(2)}, u32[]{:S(2)}) collective-permute-start(bf16[128,256]{1,0:T(8,128)(2,1)S(1)} %get-tuple-element.40), channel_id=1, source_target_pairs={{0,4},{4,0},{8,12},{12,8},{16,20},{20,16},{24,28},{28,24},{1,5},{5... | collective-permute-start | bytes 196616 | tf_op jit(solution)/shard_map/ppermute | solution.py:215
  29.3 1.3 %collective-permute-done.9.refs_1_ = bf16[128,256]{1,0:T(8,128)(2,1)S(1)} collective-permute-done((bf16[128,256]{1,0:T(8,128)(2,1)S(1)}, bf16[128,256]{1,0:T(8,128)(2,1)S(1)}, u32[]{:S(2)}, u32[]{:S(2)}) %collective-permute-start.9) | collective-permute-done | bytes 65568 | tf_op jit(solution)/shard_map/ppermute | solution.py:215
  30.6 2.6 %collective-permute-start.12 = (bf16[128,256]{1,0:T(8,128)(2,1)S(1)}, bf16[128,256]{1,0:T(8,128)(2,1)S(1)}, u32[]{:S(2)}, u32[]{:S(2)}) collective-permute-start(bf16[128,256]{1,0:T(8,128)(2,1)S(1)} %collect.2), channel_id=1, source_target_pairs={{0,16},{4,20},{8,24},{12,28},{16,0},{20,4},{24,8},{28,12},{1,17},{... | collective-permute-start | bytes 196616 | tf_op jit(solution)/shard_map/ppermute | solution.py:215
  33.2 0.0 collective-permute-done.7.refs_2_
  33.3 3.2 %collective-permute-done.12.refs_4_ = bf16[128,256]{1,0:T(8,128)(2,1)S(1)} collective-permute-done((bf16[128,256]{1,0:T(8,128)(2,1)S(1)}, bf16[128,256]{1,0:T(8,128)(2,1)S(1)}, u32[]{:S(2)}, u32[]{:S(2)}) %collective-permute-start.12) | collective-permute-done | bytes 65568 | tf_op jit(solution)/shard_map/ppermute | solution.py:215
  36.5 0.7 %collect.3 = f32[128,256]{1,0:T(8,128)} custom-call(f32[128,256]{1,0:T(8,128)S(1)} %get-tuple-element.37.refs_0_, bf16[128,256]{1,0:T(8,128)(2,1)S(1)} %collective-permute-done.6.refs_1_, bf16[128,256]{1,0:T(8,128)(2,1)S(1)} %collective-permute-done.7.refs_2_, bf16[128,256]{1,0:T(8,128)(2,1)S(1)} %collective-permute-done.8.refs_3_, ...), custom_call_target="tpu_custom_call" | custom-call | flops 32768 | bytes 524288 | tf_op jit(solution)/shard_map/collect/pallas_call | solution.py:41
  (17 shorter events, 0.1 us)
Async XLA Ops:
  0.0 1.1 %copy-start = (bf16[256,64]{0,1:T(8,128)(2,1)S(1)}, bf16[256,64]{0,1:T(8,128)(2,1)}, u32[]{:S(2)}) copy-start(bf16[256,64]{0,1:T(8,128)(2,1)} %param.9) | copy-start | bytes 98308
  0.0 1.1 %copy-start.2 = (bf16[64,128]{1,0:T(8,128)(2,1)S(1)}, bf16[64,128]{1,0:T(8,128)(2,1)}, u32[]{:S(2)}) copy-start(bf16[64,128]{1,0:T(8,128)(2,1)} %proj_ref.5) | copy-start | bytes 49156
  1.5 2.4 %collective-permute-start = (bf16[4,128,256]{2,1,0:T(8,128)(2,1)S(1)}, bf16[4,128,256]{2,1,0:T(8,128)(2,1)S(1)}, u32[]{:S(2)}, u32[]{:S(2)}) collective-permute-start(bf16[4,128,256]{2,1,0:T(8,128)(2,1)S(1)} %first_sums.1.refs_0_), channel_id=1, source_target_pairs={{0,1},{1,0},{2,3},{3,2},{4,5},{5,4},{6,7},{7,6},{8,9},{9,8},{10,11... | collective-permute-start | bytes 786440 | tf_op jit(solution)/shard_map/ppermute | solution.py:215
  3.4 3.1 %copy-start.3 = (bf16[256,256]{1,0:T(8,128)(2,1)S(1)}, bf16[256,256]{1,0:T(8,128)(2,1)}, u32[]{:S(2)}) copy-start(bf16[256,256]{1,0:T(8,128)(2,1)} %mix_ref.1) | copy-start | bytes 393220
  3.4 3.1 %copy-start.4 = (s32[4096]{0:T(1024)S(1)}, s32[4096]{0:T(1024)}, u32[]{:S(2)}) copy-start(s32[4096]{0:T(1024)} %param.13) | copy-start | bytes 49156
  3.9 11.7 %copy-start.1 = (s32[4096,1]{0,1:T(1,128)S(1)}, s32[4096,1]{0,1:T(1,128)}, u32[]{:S(2)}) copy-start(s32[4096,1]{0,1:T(1,128)} %param.12) | copy-start | bytes 49156
  4.0 9.6 %collective-permute-start.1 = (bf16[4,128,256]{2,1,0:T(8,128)(2,1)S(1)}, bf16[4,128,256]{2,1,0:T(8,128)(2,1)S(1)}, u32[]{:S(2)}, u32[]{:S(2)}) collective-permute-start(bf16[4,128,256]{2,1,0:T(8,128)(2,1)S(1)} %add.1._), channel_id=1, source_target_pairs={{0,2},{1,3},{2,0},{3,1},{4,6},{5,7},{6,4},{7,5},{8,10},{9,11},{10,... | collective-permute-start | bytes 786440 | tf_op jit(solution)/shard_map/ppermute | solution.py:215
  8.0 5.5 %collective-permute-start.2 = (bf16[4,128,256]{2,1,0:T(8,128)(2,1)S(1)}, bf16[4,128,256]{2,1,0:T(8,128)(2,1)S(1)}, u32[]{:S(2)}, u32[]{:S(2)}) collective-permute-start(bf16[4,128,256]{2,1,0:T(8,128)(2,1)S(1)} %get-tuple-element.34), channel_id=1, source_target_pairs={{0,1},{1,0},{2,3},{3,2},{4,5},{5,4},{6,7},{7,6},{8,9},{9,8},{10,11... | collective-permute-start | bytes 786440 | tf_op jit(solution)/shard_map/ppermute | solution.py:215
  13.7 5.4 %collective-permute-start.3 = (bf16[4,64,256]{2,1,0:T(8,128)(2,1)S(1)}, bf16[4,64,256]{2,1,0:T(8,128)(2,1)S(1)}, u32[]{:S(2)}, u32[]{:S(2)}) collective-permute-start(bf16[4,64,256]{2,1,0:T(8,128)(2,1)S(1)} %layer_back.1.refs_6_), channel_id=1, source_target_pairs={{0,2},{1,3},{2,0},{3,1},{4,6},{5,7},{6,4},{7,5},{8,10},{9,11},{10,... | collective-permute-start | bytes 393224 | tf_op jit(solution)/shard_map/ppermute | solution.py:215
  15.5 3.6 %collective-permute-start.5 = (bf16[4,64,256]{2,1,0:T(8,128)(2,1)S(1)}, bf16[4,64,256]{2,1,0:T(8,128)(2,1)S(1)}, u32[]{:S(2)}, u32[]{:S(2)}) collective-permute-start(bf16[4,64,256]{2,1,0:T(8,128)(2,1)S(1)} %layer_back.1.refs_6_), channel_id=1, source_target_pairs={{0,1},{1,0},{2,3},{3,2},{4,5},{5,4},{6,7},{7,6},{8,9},{9,8},{10,11... | collective-permute-start | bytes 393224 | tf_op jit(solution)/shard_map/ppermute | solution.py:215
  19.1 1.8 %collective-permute-start.4 = (bf16[4,64,256]{2,1,0:T(8,128)(2,1)S(1)}, bf16[4,64,256]{2,1,0:T(8,128)(2,1)S(1)}, u32[]{:S(2)}, u32[]{:S(2)}) collective-permute-start(bf16[4,64,256]{2,1,0:T(8,128)(2,1)S(1)} %collective-permute-done.3.refs_7_), channel_id=1, source_target_pairs={{0,1},{1,0},{2,3},{3,2},{4,5},{5,4},{6,7},{7,6},{8,9},{9,8},{10,11... | collective-permute-start | bytes 393224 | tf_op jit(solution)/shard_map/ppermute | solution.py:215
  21.7 7.0 %collective-permute-start.10 = (bf16[128,256]{1,0:T(8,128)(2,1)S(1)}, bf16[128,256]{1,0:T(8,128)(2,1)S(1)}, u32[]{:S(2)}, u32[]{:S(2)}) collective-permute-start(bf16[128,256]{1,0:T(8,128)(2,1)S(1)} %get-tuple-element.43), channel_id=1, source_target_pairs={{0,8},{4,12},{8,0},{12,4},{16,24},{20,28},{24,16},{28,20},{1,9},{5... | collective-permute-start | bytes 196616 | tf_op jit(solution)/shard_map/ppermute | solution.py:215
  23.4 5.9 %collective-permute-start.11 = (bf16[128,256]{1,0:T(8,128)(2,1)S(1)}, bf16[128,256]{1,0:T(8,128)(2,1)S(1)}, u32[]{:S(2)}, u32[]{:S(2)}) collective-permute-start(bf16[128,256]{1,0:T(8,128)(2,1)S(1)} %get-tuple-element.44), channel_id=1, source_target_pairs={{0,4},{4,0},{8,12},{12,8},{16,20},{20,16},{24,28},{28,24},{1,5},{5... | collective-permute-start | bytes 196616 | tf_op jit(solution)/shard_map/ppermute | solution.py:215
  24.9 5.7 %collective-permute-start.9 = (bf16[128,256]{1,0:T(8,128)(2,1)S(1)}, bf16[128,256]{1,0:T(8,128)(2,1)S(1)}, u32[]{:S(2)}, u32[]{:S(2)}) collective-permute-start(bf16[128,256]{1,0:T(8,128)(2,1)S(1)} %get-tuple-element.42), channel_id=1, source_target_pairs={{0,12},{4,8},{8,4},{12,0},{16,28},{20,24},{24,20},{28,16},{1,13},{... | collective-permute-start | bytes 196616 | tf_op jit(solution)/shard_map/ppermute | solution.py:215
  25.7 7.5 %collective-permute-start.6 = (bf16[128,256]{1,0:T(8,128)(2,1)S(1)}, bf16[128,256]{1,0:T(8,128)(2,1)S(1)}, u32[]{:S(2)}, u32[]{:S(2)}) collective-permute-start(bf16[128,256]{1,0:T(8,128)(2,1)S(1)} %get-tuple-element.38), channel_id=1, source_target_pairs={{0,12},{4,8},{8,4},{12,0},{16,28},{20,24},{24,20},{28,16},{1,13},{... | collective-permute-start | bytes 196616 | tf_op jit(solution)/shard_map/ppermute | solution.py:215
  28.3 5.0 %collective-permute-start.7 = (bf16[128,256]{1,0:T(8,128)(2,1)S(1)}, bf16[128,256]{1,0:T(8,128)(2,1)S(1)}, u32[]{:S(2)}, u32[]{:S(2)}) collective-permute-start(bf16[128,256]{1,0:T(8,128)(2,1)S(1)} %get-tuple-element.39), channel_id=1, source_target_pairs={{0,8},{4,12},{8,0},{12,4},{16,24},{20,28},{24,16},{28,20},{1,9},{5... | collective-permute-start | bytes 196616 | tf_op jit(solution)/shard_map/ppermute | solution.py:215
  28.7 4.5 %collective-permute-start.8 = (bf16[128,256]{1,0:T(8,128)(2,1)S(1)}, bf16[128,256]{1,0:T(8,128)(2,1)S(1)}, u32[]{:S(2)}, u32[]{:S(2)}) collective-permute-start(bf16[128,256]{1,0:T(8,128)(2,1)S(1)} %get-tuple-element.40), channel_id=1, source_target_pairs={{0,4},{4,0},{8,12},{12,8},{16,20},{20,16},{24,28},{28,24},{1,5},{5... | collective-permute-start | bytes 196616 | tf_op jit(solution)/shard_map/ppermute | solution.py:215
  30.6 5.9 %collective-permute-start.12 = (bf16[128,256]{1,0:T(8,128)(2,1)S(1)}, bf16[128,256]{1,0:T(8,128)(2,1)S(1)}, u32[]{:S(2)}, u32[]{:S(2)}) collective-permute-start(bf16[128,256]{1,0:T(8,128)(2,1)S(1)} %collect.2), channel_id=1, source_target_pairs={{0,16},{4,20},{8,24},{12,28},{16,0},{20,4},{24,8},{28,12},{1,17},{... | collective-permute-start | bytes 196616 | tf_op jit(solution)/shard_map/ppermute | solution.py:215

commit v11 on v9

--- a/solution.py
+++ b/solution.py
@@ -290,7 +290,7 @@
         return call(collect_kernel, "collect", terms, [shape((width, SHARD), kind)], width * SHARD)[0]
 
     steps = near[:0:-1]
-    early = steps[:(len(steps) + 1) // 3]
+    early = steps[:-1]
     opposite = [opposite[0]] + [swap(opposite[m], m, "dp") for m in steps]
     terms = [own[0]] + [swap(own[m], m, "dp") for m in early]
     terms.append(swap(collect(opposite, BF16), owners // 2, "dp"))

time: 38 us -> 36.5 us (0.961)
  starting transfers between devices: 16.3 us -> 15.2 us
  waiting for transfers between devices: 12.5 us -> 12.1 us
    ppermute x13, starting transfers between devices: 16.3 us -> 15.2 us  [swap(): lax.ppermute(x, axis, [(i, i ^ bit) for i in range(lax.axis_size(axis))])]
    ppermute x13, waiting for transfers between devices: 12.5 us -> 12.1 us  [swap(): lax.ppermute(x, axis, [(i, i ^ bit) for i in range(lax.axis_size(axis))])]
  transfers between devices with their start and end apart: 13 -> 13, of which waited for: 8 -> 6; matrix products, arithmetic and copies ran while one was open for 0% -> 0% of each run, Pallas kernels for 14% -> 14%
where the time goes in v11:
time: 36.5 us; the launch traced here: 36.4 us
  starting transfers between devices  15.2 us (42%)
  waiting for transfers between devices  12.1 us (33%)
  Pallas kernels  8.92 us (24%)
    ppermute x13, starting transfers between devices, swap(): lax.ppermute(x, axis, [(i, i ^ bit) for i in range(lax.axis_size(axis))])  15.2 us
    ppermute x13, waiting for transfers between devices, swap(): lax.ppermute(x, axis, [(i, i ^ bit) for i in range(lax.axis_size(axis))])  12.1 us
    pallas_call x13, Pallas kernels, call(): pl.pallas_call(kernel, in_specs=specs or [VMEM] * len(args), out_specs=[V...  8.92 us
  transfers between devices with their start and end apart: 13, of which 6 were waited for; matrix products, arithmetic and copies ran while one was open for 0% of the time, Pallas kernels for 14%

profile of v11, /device:TPU:0, one launch (start us, length us, event | category | flops | bytes accessed | tf_op | source)
XLA Modules:
  0.0 36.4 jit_solution(8691953507812105552)
XLA Ops:
  0.0 1.6 %load.1 = (bf16[16,128,256]{2,1,0:T(8,128)(2,1)S(1)}, bf16[16,128,256]{2,1,0:T(8,128)(2,1)S(1)}) custom-call(bf16[16,128,256]{2,1,0:T(8,128)(2,1)} %av_hbm.1, bf16[16,128,256]{2,1,0:T(8,128)(2,1)} %up_hbm.1), custom_call_target="tpu_custom_call" | custom-call | bytes 4194304 | tf_op jit(solution)/shard_map/load/pallas_call | solution.py:40
  1.6 0.4 %first_sums.1 = bf16[4,128,256]{2,1,0:T(8,128)(2,1)S(1)} custom-call(bf16[16,128,256]{2,1,0:T(8,128)(2,1)S(1)} %get-tuple-element.22.av_ref.refs_0_, bf16[16,128,256]{2,1,0:T(8,128)(2,1)S(1)} %get-tuple-element.23.up_ref, bf16[64,256]{1,0:T(8,128)(2,1)S(1)} %bitcast.3, bf16[64,128]{1,0:T(8,128)(2,1)S(1)} %copy-done.2), custom_call_target="tpu_custom_call" | custom-call | flops 50331648 | bytes 2408448 | tf_op jit(solution)/shard_map/first_sums/pallas_call | solution.py:40
  2.0 0.0 copy-start.3
  2.1 0.0 copy-start.4
  2.1 0.5 %collective-permute-start.1 = (bf16[4,128,256]{2,1,0:T(8,128)(2,1)S(1)}, bf16[4,128,256]{2,1,0:T(8,128)(2,1)S(1)}, u32[]{:S(2)}, u32[]{:S(2)}) collective-permute-start(bf16[4,128,256]{2,1,0:T(8,128)(2,1)S(1)} %first_sums.1), channel_id=1, source_target_pairs={{0,1},{1,0},{2,3},{3,2},{4,5},{5,4},{6,7},{7,6},{8,9},{9,8},{10,11... | collective-permute-start | bytes 786440 | tf_op jit(solution)/shard_map/ppermute | solution.py:193
  2.6 0.6 %sums.1 = (f32[4,128,256]{2,1,0:T(8,128)S(1)}, f32[4,128,256]{2,1,0:T(8,128)S(1)}) custom-call(bf16[16,128,256]{2,1,0:T(8,128)(2,1)S(1)} %get-tuple-element.22.av_ref.refs_0_, bf16[16,128,256]{2,1,0:T(8,128)(2,1)S(1)} %get-tuple-element.23.up_ref, bf16[64,256]{1,0:T(8,128)(2,1)S(1)} %bitcast.4, bf16[64,128]{1,0:T(8,128)(2,1)S(1)} %copy-done.2), custom_call_target="tpu_custom_call" | custom-call | flops 100663296 | bytes 3194880 | tf_op jit(solution)/shard_map/sums/pallas_call | solution.py:40
  3.2 0.1 collective-permute-start
  3.3 0.5 %collective-permute-done.1.got_ref = bf16[4,128,256]{2,1,0:T(8,128)(2,1)S(1)} collective-permute-done((bf16[4,128,256]{2,1,0:T(8,128)(2,1)S(1)}, bf16[4,128,256]{2,1,0:T(8,128)(2,1)S(1)}, u32[]{:S(2)}, u32[]{:S(2)}) %collective-permute-start.1) | collective-permute-done | bytes 262176 | tf_op jit(solution)/shard_map/ppermute | solution.py:193
  3.8 0.0 copy-start.1
  3.8 3.0 %collective-permute-start.2 = (bf16[4,128,256]{2,1,0:T(8,128)(2,1)S(1)}, bf16[4,128,256]{2,1,0:T(8,128)(2,1)S(1)}, u32[]{:S(2)}, u32[]{:S(2)}) collective-permute-start(bf16[4,128,256]{2,1,0:T(8,128)(2,1)S(1)} %add.1), channel_id=1, source_target_pairs={{0,2},{1,3},{2,0},{3,1},{4,6},{5,7},{6,4},{7,5},{8,10},{9,11},{10,... | collective-permute-start | bytes 786440 | tf_op jit(solution)/shard_map/ppermute | solution.py:193
  6.8 1.3 %prepare.1 = (f32[4,128,256]{2,1,0:T(8,128)S(1)}, f32[16,128,256]{2,1,0:T(8,128)S(1)}, bf16[4096,256]{1,0:T(8,128)(2,1)S(1)}) custom-call(bf16[16,128,256]{2,1,0:T(8,128)(2,1)S(1)} %get-tuple-element.22.av_ref.refs_0_, bf16[16,128,256]{2,1,0:T(8,128)(2,1)S(1)} %get-tuple-element.23.up_ref, bf16[64,256]{1,0:T(8,128)(2,1)S(1)} %bitcast.5, ...), custom_call_target="tpu_custom_call" | custom-call | flops 268435456 | bytes 7012352 | tf_op jit(solution)/shard_map/prepare/pallas_call | solution.py:40
  8.1 5.3 %collective-permute-done.2.refs_2_ = bf16[4,128,256]{2,1,0:T(8,128)(2,1)S(1)} collective-permute-done((bf16[4,128,256]{2,1,0:T(8,128)(2,1)S(1)}, bf16[4,128,256]{2,1,0:T(8,128)(2,1)S(1)}, u32[]{:S(2)}, u32[]{:S(2)}) %collective-permute-start.2) | collective-permute-done | bytes 262176 | tf_op jit(solution)/shard_map/ppermute | solution.py:193
  13.4 0.2 layer_back.1.refs_5_
  13.5 1.8 %collective-permute-start.3 = (bf16[4,64,256]{2,1,0:T(8,128)(2,1)S(1)}, bf16[4,64,256]{2,1,0:T(8,128)(2,1)S(1)}, u32[]{:S(2)}, u32[]{:S(2)}) collective-permute-start(bf16[4,64,256]{2,1,0:T(8,128)(2,1)S(1)} %layer_back.1.refs_5_), channel_id=1, source_target_pairs={{0,2},{1,3},{2,0},{3,1},{4,6},{5,7},{6,4},{7,5},{8,10},{9,11},{10,... | collective-permute-start | bytes 393224 | tf_op jit(solution)/shard_map/ppermute | solution.py:193
  15.4 1.1 %table_part.3.refs_7_ = f32[1024,256]{1,0:T(8,128)S(1)} custom-call(bf16[16,128,256]{2,1,0:T(8,128)(2,1)S(1)} %get-tuple-element.22.av_ref.refs_0_, bf16[64,256]{1,0:T(8,128)(2,1)S(1)} %bitcast.6, f32[16,128,256]{2,1,0:T(8,128)S(1)} %get-tuple-element.24.refs_2_, s32[1,4096]{1,0:T(1,128)S(1)} %bitcast.9, ...), custom_call_target="tpu_custom_call" | custom-call | flops 536870912 | bytes 6471680 | tf_op jit(solution)/shard_map/table_part/pallas_call | solution.py:40
  16.5 2.2 %collective-permute-done.3.refs_6_ = bf16[4,64,256]{2,1,0:T(8,128)(2,1)S(1)} collective-permute-done((bf16[4,64,256]{2,1,0:T(8,128)(2,1)S(1)}, bf16[4,64,256]{2,1,0:T(8,128)(2,1)S(1)}, u32[]{:S(2)}, u32[]{:S(2)}) %collective-permute-start.3) | collective-permute-done | bytes 131104 | tf_op jit(solution)/shard_map/ppermute | solution.py:193
  18.6 0.0 collective-permute-start.4
  18.6 0.0 collective-permute-done.5.refs_5_
  18.6 1.7 %table_part.4.refs_6_.total_ref = f32[1024,256]{1,0:T(8,128)S(1)} custom-call(bf16[16,128,256]{2,1,0:T(8,128)(2,1)S(1)} %get-tuple-element.22.av_ref.refs_0_, bf16[64,256]{1,0:T(8,128)(2,1)S(1)} %bitcast.7, f32[16,128,256]{2,1,0:T(8,128)S(1)} %get-tuple-element.24.refs_2_, s32[1,4096]{1,0:T(1,128)S(1)} %bitcast.10, ...), custom_call_target="tpu_custom_call" | custom-call | flops 1073741824 | bytes 7651328 | tf_op jit(solution)/shard_map/table_part/pallas_call | solution.py:40
  20.4 0.8 %table_part.5 = (f32[128,256]{1,0:T(8,128)S(1)}, bf16[128,256]{1,0:T(8,128)(2,1)S(1)}, bf16[128,256]{1,0:T(8,128)(2,1)S(1)}, bf16[128,256]{1,0:T(8,128)(2,1)S(1)}, bf16[4,128,256]{2,1,0:T(8,128)(2,1)S(1)}) custom-call(bf16[16,128,256]{2,1,0:T(8,128)(2,1)S(1)} %get-tuple-element.22.av_ref.refs_0_, bf16[64,256]{1,0:T(8,128)(2,1)S(1)} %bitcast.8, ...), custom_call_target="tpu_custom_call" | custom-call | flops 268435456 | bytes 7061504 | tf_op jit(solution)/shard_map/table_part/pallas_call | solution.py:40
  21.2 2.7 %collective-permute-start.8 = (bf16[128,256]{1,0:T(8,128)(2,1)S(1)}, bf16[128,256]{1,0:T(8,128)(2,1)S(1)}, u32[]{:S(2)}, u32[]{:S(2)}) collective-permute-start(bf16[128,256]{1,0:T(8,128)(2,1)S(1)} %get-tuple-element.35), channel_id=1, source_target_pairs={{0,12},{4,8},{8,4},{12,0},{16,28},{20,24},{24,20},{28,16},{1,13},{... | collective-permute-start | bytes 196616 | tf_op jit(solution)/shard_map/ppermute | solution.py:193
  24.0 0.4 %collective-permute-start.9 = (bf16[128,256]{1,0:T(8,128)(2,1)S(1)}, bf16[128,256]{1,0:T(8,128)(2,1)S(1)}, u32[]{:S(2)}, u32[]{:S(2)}) collective-permute-start(bf16[128,256]{1,0:T(8,128)(2,1)S(1)} %get-tuple-element.36), channel_id=1, source_target_pairs={{0,8},{4,12},{8,0},{12,4},{16,24},{20,28},{24,16},{28,20},{1,9},{5... | collective-permute-start | bytes 196616 | tf_op jit(solution)/shard_map/ppermute | solution.py:193
  24.4 0.4 %collective-permute-start.10 = (bf16[128,256]{1,0:T(8,128)(2,1)S(1)}, bf16[128,256]{1,0:T(8,128)(2,1)S(1)}, u32[]{:S(2)}, u32[]{:S(2)}) collective-permute-start(bf16[128,256]{1,0:T(8,128)(2,1)S(1)} %get-tuple-element.37), channel_id=1, source_target_pairs={{0,4},{4,0},{8,12},{12,8},{16,20},{20,16},{24,28},{28,24},{1,5},{5... | collective-permute-start | bytes 196616 | tf_op jit(solution)/shard_map/ppermute | solution.py:193
  24.8 0.4 %near_part.1 = (f32[128,256]{1,0:T(8,128)S(1)}, bf16[128,256]{1,0:T(8,128)(2,1)S(1)}, bf16[128,256]{1,0:T(8,128)(2,1)S(1)}, bf16[128,256]{1,0:T(8,128)(2,1)S(1)}) custom-call(bf16[4,128,256]{2,1,0:T(8,128)(2,1)S(1)} %get-tuple-element.30.grad_ref, s32[1,4096]{1,0:T(1,128)S(1)} %bitcast.12, bf16[4096,256]{1,0:T(8,128)(2,1)S(1)} %get-tuple-element.25.refs_4_.onehot_ref, ...), custom_call_target="tpu_custom_call" | custom-call | flops 268435456 | bytes 3751936 | tf_op jit(solution)/shard_map/near_part/pallas_call | solution.py:40
  25.2 2.7 %collective-permute-start.6 = (bf16[128,256]{1,0:T(8,128)(2,1)S(1)}, bf16[128,256]{1,0:T(8,128)(2,1)S(1)}, u32[]{:S(2)}, u32[]{:S(2)}) collective-permute-start(bf16[128,256]{1,0:T(8,128)(2,1)S(1)} %get-tuple-element.32), channel_id=1, source_target_pairs={{0,12},{4,8},{8,4},{12,0},{16,28},{20,24},{24,20},{28,16},{1,13},{... | collective-permute-start | bytes 196616 | tf_op jit(solution)/shard_map/ppermute | solution.py:193
  28.0 0.4 %collective-permute-start.7 = (bf16[128,256]{1,0:T(8,128)(2,1)S(1)}, bf16[128,256]{1,0:T(8,128)(2,1)S(1)}, u32[]{:S(2)}, u32[]{:S(2)}) collective-permute-start(bf16[128,256]{1,0:T(8,128)(2,1)S(1)} %get-tuple-element.33), channel_id=1, source_target_pairs={{0,8},{4,12},{8,0},{12,4},{16,24},{20,28},{24,16},{28,20},{1,9},{5... | collective-permute-start | bytes 196616 | tf_op jit(solution)/shard_map/ppermute | solution.py:193
  28.4 1.0 %collective-permute-done.10.refs_3_ = bf16[128,256]{1,0:T(8,128)(2,1)S(1)} collective-permute-done((bf16[128,256]{1,0:T(8,128)(2,1)S(1)}, bf16[128,256]{1,0:T(8,128)(2,1)S(1)}, u32[]{:S(2)}, u32[]{:S(2)}) %collective-permute-start.10) | collective-permute-done | bytes 65568 | tf_op jit(solution)/shard_map/ppermute | solution.py:193
  29.4 2.0 %collective-permute-start.11 = (bf16[128,256]{1,0:T(8,128)(2,1)S(1)}, bf16[128,256]{1,0:T(8,128)(2,1)S(1)}, u32[]{:S(2)}, u32[]{:S(2)}) collective-permute-start(bf16[128,256]{1,0:T(8,128)(2,1)S(1)} %collect.3), channel_id=1, source_target_pairs={{0,16},{4,20},{8,24},{12,28},{16,0},{20,4},{24,8},{28,12},{1,17},{... | collective-permute-start | bytes 196616 | tf_op jit(solution)/shard_map/ppermute | solution.py:193
  31.4 1.1 %collective-permute-start.12 = (bf16[128,256]{1,0:T(8,128)(2,1)S(1)}, bf16[128,256]{1,0:T(8,128)(2,1)S(1)}, u32[]{:S(2)}, u32[]{:S(2)}) collective-permute-start(bf16[128,256]{1,0:T(8,128)(2,1)S(1)} %get-tuple-element.38), channel_id=1, source_target_pairs={{0,4},{4,0},{8,12},{12,8},{16,20},{20,16},{24,28},{28,24},{1,5},{5... | collective-permute-start | bytes 196616 | tf_op jit(solution)/shard_map/ppermute | solution.py:193
  32.5 0.4 collective-permute-done.7.refs_2_
  32.8 2.8 %collective-permute-done.11.refs_3_ = bf16[128,256]{1,0:T(8,128)(2,1)S(1)} collective-permute-done((bf16[128,256]{1,0:T(8,128)(2,1)S(1)}, bf16[128,256]{1,0:T(8,128)(2,1)S(1)}, u32[]{:S(2)}, u32[]{:S(2)}) %collective-permute-start.11) | collective-permute-done | bytes 65568 | tf_op jit(solution)/shard_map/ppermute | solution.py:193
  35.7 0.7 %collect.5 = f32[128,256]{1,0:T(8,128)} custom-call(f32[128,256]{1,0:T(8,128)S(1)} %collect.4.refs_0_, bf16[128,256]{1,0:T(8,128)(2,1)S(1)} %collective-permute-done.12.refs_1_), custom_call_target="tpu_custom_call" | custom-call | flops 32768 | bytes 327680 | tf_op jit(solution)/shard_map/collect/pallas_call | solution.py:40
  (17 shorter events, 0.1 us)
Async XLA Ops:
  0.0 1.6 %copy-start.2 = (bf16[64,128]{1,0:T(8,128)(2,1)S(1)}, bf16[64,128]{1,0:T(8,128)(2,1)}, u32[]{:S(2)}) copy-start(bf16[64,128]{1,0:T(8,128)(2,1)} %proj_ref.5) | copy-start | bytes 49156
  0.0 1.6 %copy-start = (bf16[256,64]{0,1:T(8,128)(2,1)S(1)}, bf16[256,64]{0,1:T(8,128)(2,1)}, u32[]{:S(2)}) copy-start(bf16[256,64]{0,1:T(8,128)(2,1)} %param.9) | copy-start | bytes 98308
  2.0 4.7 %copy-start.3 = (bf16[256,256]{1,0:T(8,128)(2,1)S(1)}, bf16[256,256]{1,0:T(8,128)(2,1)}, u32[]{:S(2)}) copy-start(bf16[256,256]{1,0:T(8,128)(2,1)} %mix_ref.1) | copy-start | bytes 393220
  2.1 4.7 %copy-start.4 = (s32[4096]{0:T(1024)S(1)}, s32[4096]{0:T(1024)}, u32[]{:S(2)}) copy-start(s32[4096]{0:T(1024)} %param.13) | copy-start | bytes 49156
  2.1 1.7 %collective-permute-start.1 = (bf16[4,128,256]{2,1,0:T(8,128)(2,1)S(1)}, bf16[4,128,256]{2,1,0:T(8,128)(2,1)S(1)}, u32[]{:S(2)}, u32[]{:S(2)}) collective-permute-start(bf16[4,128,256]{2,1,0:T(8,128)(2,1)S(1)} %first_sums.1), channel_id=1, source_target_pairs={{0,1},{1,0},{2,3},{3,2},{4,5},{5,4},{6,7},{7,6},{8,9},{9,8},{10,11... | collective-permute-start | bytes 786440 | tf_op jit(solution)/shard_map/ppermute | solution.py:193
  3.2 10.2 %collective-permute-start = (f32[4,128,256]{2,1,0:T(8,128)S(1)}, f32[4,128,256]{2,1,0:T(8,128)S(1)}, u32[]{:S(2)}, u32[]{:S(2)}) collective-permute-start(f32[4,128,256]{2,1,0:T(8,128)S(1)} %get-tuple-element.27), channel_id=1, source_target_pairs={{0,1},{1,0},{2,3},{3,2},{4,5},{5,4},{6,7},{7,6},{8,9},{9,8},{10,11... | collective-permute-start | bytes 1572872 | tf_op jit(solution)/shard_map/ppermute | solution.py:193
  3.8 11.6 %copy-start.1 = (s32[4096,1]{0,1:T(1,128)S(1)}, s32[4096,1]{0,1:T(1,128)}, u32[]{:S(2)}) copy-start(s32[4096,1]{0,1:T(1,128)} %param.12) | copy-start | bytes 49156
  3.8 9.6 %collective-permute-start.2 = (bf16[4,128,256]{2,1,0:T(8,128)(2,1)S(1)}, bf16[4,128,256]{2,1,0:T(8,128)(2,1)S(1)}, u32[]{:S(2)}, u32[]{:S(2)}) collective-permute-start(bf16[4,128,256]{2,1,0:T(8,128)(2,1)S(1)} %add.1), channel_id=1, source_target_pairs={{0,2},{1,3},{2,0},{3,1},{4,6},{5,7},{6,4},{7,5},{8,10},{9,11},{10,... | collective-permute-start | bytes 786440 | tf_op jit(solution)/shard_map/ppermute | solution.py:193
  13.5 5.1 %collective-permute-start.3 = (bf16[4,64,256]{2,1,0:T(8,128)(2,1)S(1)}, bf16[4,64,256]{2,1,0:T(8,128)(2,1)S(1)}, u32[]{:S(2)}, u32[]{:S(2)}) collective-permute-start(bf16[4,64,256]{2,1,0:T(8,128)(2,1)S(1)} %layer_back.1.refs_5_), channel_id=1, source_target_pairs={{0,2},{1,3},{2,0},{3,1},{4,6},{5,7},{6,4},{7,5},{8,10},{9,11},{10,... | collective-permute-start | bytes 393224 | tf_op jit(solution)/shard_map/ppermute | solution.py:193
  15.4 3.3 %collective-permute-start.5 = (bf16[4,64,256]{2,1,0:T(8,128)(2,1)S(1)}, bf16[4,64,256]{2,1,0:T(8,128)(2,1)S(1)}, u32[]{:S(2)}, u32[]{:S(2)}) collective-permute-start(bf16[4,64,256]{2,1,0:T(8,128)(2,1)S(1)} %layer_back.1.refs_5_), channel_id=1, source_target_pairs={{0,1},{1,0},{2,3},{3,2},{4,5},{5,4},{6,7},{7,6},{8,9},{9,8},{10,11... | collective-permute-start | bytes 393224 | tf_op jit(solution)/shard_map/ppermute | solution.py:193
  18.6 1.8 %collective-permute-start.4 = (bf16[4,64,256]{2,1,0:T(8,128)(2,1)S(1)}, bf16[4,64,256]{2,1,0:T(8,128)(2,1)S(1)}, u32[]{:S(2)}, u32[]{:S(2)}) collective-permute-start(bf16[4,64,256]{2,1,0:T(8,128)(2,1)S(1)} %collective-permute-done.3.refs_6_), channel_id=1, source_target_pairs={{0,1},{1,0},{2,3},{3,2},{4,5},{5,4},{6,7},{7,6},{8,9},{9,8},{10,11... | collective-permute-start | bytes 393224 | tf_op jit(solution)/shard_map/ppermute | solution.py:193
  21.2 7.2 %collective-permute-start.8 = (bf16[128,256]{1,0:T(8,128)(2,1)S(1)}, bf16[128,256]{1,0:T(8,128)(2,1)S(1)}, u32[]{:S(2)}, u32[]{:S(2)}) collective-permute-start(bf16[128,256]{1,0:T(8,128)(2,1)S(1)} %get-tuple-element.35), channel_id=1, source_target_pairs={{0,12},{4,8},{8,4},{12,0},{16,28},{20,24},{24,20},{28,16},{1,13},{... | collective-permute-start | bytes 196616 | tf_op jit(solution)/shard_map/ppermute | solution.py:193
  24.0 4.5 %collective-permute-start.9 = (bf16[128,256]{1,0:T(8,128)(2,1)S(1)}, bf16[128,256]{1,0:T(8,128)(2,1)S(1)}, u32[]{:S(2)}, u32[]{:S(2)}) collective-permute-start(bf16[128,256]{1,0:T(8,128)(2,1)S(1)} %get-tuple-element.36), channel_id=1, source_target_pairs={{0,8},{4,12},{8,0},{12,4},{16,24},{20,28},{24,16},{28,20},{1,9},{5... | collective-permute-start | bytes 196616 | tf_op jit(solution)/shard_map/ppermute | solution.py:193
  24.4 5.0 %collective-permute-start.10 = (bf16[128,256]{1,0:T(8,128)(2,1)S(1)}, bf16[128,256]{1,0:T(8,128)(2,1)S(1)}, u32[]{:S(2)}, u32[]{:S(2)}) collective-permute-start(bf16[128,256]{1,0:T(8,128)(2,1)S(1)} %get-tuple-element.37), channel_id=1, source_target_pairs={{0,4},{4,0},{8,12},{12,8},{16,20},{20,16},{24,28},{28,24},{1,5},{5... | collective-permute-start | bytes 196616 | tf_op jit(solution)/shard_map/ppermute | solution.py:193
  25.2 7.2 %collective-permute-start.6 = (bf16[128,256]{1,0:T(8,128)(2,1)S(1)}, bf16[128,256]{1,0:T(8,128)(2,1)S(1)}, u32[]{:S(2)}, u32[]{:S(2)}) collective-permute-start(bf16[128,256]{1,0:T(8,128)(2,1)S(1)} %get-tuple-element.32), channel_id=1, source_target_pairs={{0,12},{4,8},{8,4},{12,0},{16,28},{20,24},{24,20},{28,16},{1,13},{... | collective-permute-start | bytes 196616 | tf_op jit(solution)/shard_map/ppermute | solution.py:193
  28.0 4.8 %collective-permute-start.7 = (bf16[128,256]{1,0:T(8,128)(2,1)S(1)}, bf16[128,256]{1,0:T(8,128)(2,1)S(1)}, u32[]{:S(2)}, u32[]{:S(2)}) collective-permute-start(bf16[128,256]{1,0:T(8,128)(2,1)S(1)} %get-tuple-element.33), channel_id=1, source_target_pairs={{0,8},{4,12},{8,0},{12,4},{16,24},{20,28},{24,16},{28,20},{1,9},{5... | collective-permute-start | bytes 196616 | tf_op jit(solution)/shard_map/ppermute | solution.py:193
  29.4 6.2 %collective-permute-start.11 = (bf16[128,256]{1,0:T(8,128)(2,1)S(1)}, bf16[128,256]{1,0:T(8,128)(2,1)S(1)}, u32[]{:S(2)}, u32[]{:S(2)}) collective-permute-start(bf16[128,256]{1,0:T(8,128)(2,1)S(1)} %collect.3), channel_id=1, source_target_pairs={{0,16},{4,20},{8,24},{12,28},{16,0},{20,4},{24,8},{28,12},{1,17},{... | collective-permute-start | bytes 196616 | tf_op jit(solution)/shard_map/ppermute | solution.py:193
  31.4 4.3 %collective-permute-start.12 = (bf16[128,256]{1,0:T(8,128)(2,1)S(1)}, bf16[128,256]{1,0:T(8,128)(2,1)S(1)}, u32[]{:S(2)}, u32[]{:S(2)}) collective-permute-start(bf16[128,256]{1,0:T(8,128)(2,1)S(1)} %get-tuple-element.38), channel_id=1, source_target_pairs={{0,4},{4,0},{8,12},{12,8},{16,20},{20,16},{24,28},{28,24},{1,5},{5... | collective-permute-start | bytes 196616 | tf_op jit(solution)/shard_map/ppermute | solution.py:193

commit v12 on v8

--- a/solution.py
+++ b/solution.py
@@ -139,8 +139,6 @@
         both = dot_nt(av_ref[at], jnp.concatenate([comp_t, back])).astype(BF16)
         grad = linear_ref[at] + dot_nn(both, jnp.concatenate([back, comp_t]))
         grad = grad.astype(BF16)
-        if far:
-            outs[-1][n] = grad
         spread(grad, lookup_mask(owner_ref, piece, features, at), owners, masked, n)
     added = dot_nn(masked[...], onehot_ref[start * features:(start + count * piece) * features])
     if has_total:
@@ -148,26 +146,23 @@
     if not far:
         outs[0][...] = added
         return
-    for o in range(len(owners)):
-        outs[o][...] = added[o * width:(o + 1) * width].astype(outs[o].dtype)
-
-
-def near_kernel(start, piece, owners, grad_ref, owner_ref, onehot_ref, total_ref, *refs):
-    *outs, masked = refs
-    count, width, features = grad_ref.shape
-    for n in range(count):
-        spread(grad_ref[n], lookup_mask(owner_ref, piece, features, start + n), owners, masked, n)
-    added = dot_nn(masked[...], onehot_ref[start * features:(start + count) * features])
-    added = added + total_ref[owners[0] * width:(owners[-1] + 1) * width]
-    for o, out in enumerate(outs):
-        out[...] = added[o * width:(o + 1) * width].astype(out.dtype)
+    half = len(owners) // 2
+    for o in range(half):
+        mine, opposite = (added[m * width:(m + 1) * width] for m in (o, half + o))
+        if o:
+            outs[o + 1][0] = opposite.astype(BF16)
+            outs[o + 1][1] = mine.astype(BF16)
+        else:
+            outs[0][...] = mine
+            outs[1][...] = opposite
 
 
 def table_part(j, piece, owners, far, arrays, pairs, total):
     _, width, features = arrays[0].shape
     lookups = len(pairs) * piece * features
     if far:
-        shapes = blocks(width, owners) + [shape((piece, width, features), BF16)]
+        kept, sent = shape((width, SHARD), F32), shape((2, width, SHARD), BF16)
+        shapes = [kept] * 2 + [sent] * (len(owners) // 2 - 1)
     else:
         shapes = [shape((len(owners) * width, SHARD), F32)]
     return call(
@@ -180,13 +175,10 @@
     )
 
 
-def blocks(width, owners):
-    return [shape((width, SHARD), BF16 if o else F32) for o in range(len(owners))]
-
-
-def collect_kernel(*refs):
+def collect_kernel(at, *refs):
     *terms, out_ref = refs
-    out_ref[...] = sum(term[...].astype(F32) for term in terms).astype(out_ref.dtype)
+    terms = [(term[at] if len(term.shape) == 3 else term[...]).astype(F32) for term in terms]
+    out_ref[...] = sum(terms).astype(out_ref.dtype)
 
 
 def swap(x, bit, axis="dim"):
@@ -266,7 +258,6 @@
 
     pairs = {0: pair}
     everyone = list(range(owners))
-    near, far = everyone[:owners // 2], everyone[owners // 2:]
     (total,) = table_part(0, piece, everyone, False, arrays, [pair], None)
     for bit in reversed(bits[1:]):
         pairs.update({j ^ bit: swap(got, bit) for j, got in pairs.items()})
@@ -276,24 +267,15 @@
     middle = [pairs[j] for j in range(1, peers - 1)]
     (total,) = table_part(1, piece, everyone, False, arrays, middle, total)
     last = peers - 1
-    *opposite, grad = table_part(last, piece, far, True, arrays, [pairs[last]], total)
-    own = call(
-        functools.partial(near_kernel, last * piece, piece, near),
-        "near_part",
-        (grad, owner, onehot, total),
-        blocks(width, near),
-        2 * piece * features * width * len(near) * SHARD,
-        scratch=[pltpu.VMEM((len(near) * width, piece * features), BF16)],
-    )
-
-    def collect(terms, kind):
-        return call(collect_kernel, "collect", terms, [shape((width, SHARD), kind)], width * SHARD)[0]
-
-    steps = near[:0:-1]
-    opposite = [opposite[0]] + [swap(opposite[m], m, "dp") for m in steps]
-    own = [own[0]] + [swap(own[m], m, "dp") for m in steps]
-    own.append(swap(collect(opposite, BF16), owners // 2, "dp"))
-    return collect(own, F32)
+    own, opposite, *sent = table_part(last, piece, everyone, True, arrays, [pairs[last]], total)
+
+    def collect(at, terms, kind):
+        kernel = functools.partial(collect_kernel, at)
+        return call(kernel, "collect", terms, [shape((width, SHARD), kind)], width * SHARD)[0]
+
+    got = [swap(sent[m - 1], m, "dp") for m in range(owners // 2 - 1, 0, -1)]
+    across = swap(collect(0, [opposite, *got], BF16), owners // 2, "dp")
+    return collect(1, [own, *got, across], F32)
 
 
 def solution(mesh):

time: 36.5 us -> 38.9 us (1.066)
  waiting for transfers between devices: 12.5 us -> 18.3 us
  starting transfers between devices: 14.7 us -> 11.6 us
    ppermute x13 -> x10, waiting for transfers between devices: 12.5 us -> 18.3 us  [swap(): lax.ppermute(x, axis, [(i, i ^ bit) for i in range(lax.axis_size(axis))])]
    ppermute x13 -> x10, starting transfers between devices: 14.7 us -> 11.6 us  [swap(): lax.ppermute(x, axis, [(i, i ^ bit) for i in range(lax.axis_size(axis))])]
    pallas_call x12 -> x11, Pallas kernels: 8.92 us -> 8.75 us  [call(): pl.pallas_call(kernel, in_specs=specs or [VMEM] * len(args), out_specs=[V...]
  transfers between devices with their start and end apart: 13 -> 10, of which waited for: 6 -> 6; matrix products, arithmetic and copies ran while one was open for 0% -> 0% of each run, Pallas kernels for 14% -> 12%
where the time goes in v12:
time: 38.9 us; the launch traced here: 38.8 us
  waiting for transfers between devices  18.3 us (47%)
  starting transfers between devices  11.6 us (30%)
  Pallas kernels  8.75 us (22%)
    ppermute x10, waiting for transfers between devices, swap(): lax.ppermute(x, axis, [(i, i ^ bit) for i in range(lax.axis_size(axis))])  18.3 us
    ppermute x10, starting transfers between devices, swap(): lax.ppermute(x, axis, [(i, i ^ bit) for i in range(lax.axis_size(axis))])  11.6 us
    pallas_call x11, Pallas kernels, call(): pl.pallas_call(kernel, in_specs=specs or [VMEM] * len(args), out_specs=[V...  8.75 us
  transfers between devices with their start and end apart: 10, of which 6 were waited for; matrix products, arithmetic and copies ran while one was open for 0% of the time, Pallas kernels for 12%

profile of v12, /device:TPU:0, one launch (start us, length us, event | category | flops | bytes accessed | tf_op | source)
XLA Modules:
  0.0 38.8 jit_solution(13200225007686277258)
XLA Ops:
  0.0 1.6 %load.1 = (bf16[16,128,256]{2,1,0:T(8,128)(2,1)S(1)}, bf16[16,128,256]{2,1,0:T(8,128)(2,1)S(1)}) custom-call(bf16[16,128,256]{2,1,0:T(8,128)(2,1)} %av_hbm.1, bf16[16,128,256]{2,1,0:T(8,128)(2,1)} %up_hbm.1), custom_call_target="tpu_custom_call" | custom-call | bytes 4194304 | tf_op jit(solution)/shard_map/load/pallas_call | solution.py:40
  1.6 0.4 %first_sums.1 = bf16[4,128,256]{2,1,0:T(8,128)(2,1)S(1)} custom-call(bf16[16,128,256]{2,1,0:T(8,128)(2,1)S(1)} %get-tuple-element.18.av_ref.refs_0_, bf16[16,128,256]{2,1,0:T(8,128)(2,1)S(1)} %get-tuple-element.19.up_ref, bf16[64,256]{1,0:T(8,128)(2,1)S(1)} %bitcast.3, bf16[64,128]{1,0:T(8,128)(2,1)S(1)} %copy-done.1), custom_call_target="tpu_custom_call" | custom-call | flops 50331648 | bytes 2408448 | tf_op jit(solution)/shard_map/first_sums/pallas_call | solution.py:40
  2.0 0.0 copy-start.3
  2.1 0.0 copy-start.4
  2.1 0.5 %collective-permute-start.1 = (bf16[4,128,256]{2,1,0:T(8,128)(2,1)S(1)}, bf16[4,128,256]{2,1,0:T(8,128)(2,1)S(1)}, u32[]{:S(2)}, u32[]{:S(2)}) collective-permute-start(bf16[4,128,256]{2,1,0:T(8,128)(2,1)S(1)} %first_sums.1), channel_id=1, source_target_pairs={{0,1},{1,0},{2,3},{3,2},{4,5},{5,4},{6,7},{7,6},{8,9},{9,8},{10,11... | collective-permute-start | bytes 786440 | tf_op jit(solution)/shard_map/ppermute | solution.py:185
  2.6 0.6 %sums.1 = (f32[4,128,256]{2,1,0:T(8,128)S(1)}, f32[4,128,256]{2,1,0:T(8,128)S(1)}) custom-call(bf16[16,128,256]{2,1,0:T(8,128)(2,1)S(1)} %get-tuple-element.18.av_ref.refs_0_, bf16[16,128,256]{2,1,0:T(8,128)(2,1)S(1)} %get-tuple-element.19.up_ref, bf16[64,256]{1,0:T(8,128)(2,1)S(1)} %bitcast.4, bf16[64,128]{1,0:T(8,128)(2,1)S(1)} %copy-done.1), custom_call_target="tpu_custom_call" | custom-call | flops 100663296 | bytes 3194880 | tf_op jit(solution)/shard_map/sums/pallas_call | solution.py:40
  3.2 0.1 collective-permute-start
  3.3 0.5 %collective-permute-done.1.got_ref = bf16[4,128,256]{2,1,0:T(8,128)(2,1)S(1)} collective-permute-done((bf16[4,128,256]{2,1,0:T(8,128)(2,1)S(1)}, bf16[4,128,256]{2,1,0:T(8,128)(2,1)S(1)}, u32[]{:S(2)}, u32[]{:S(2)}) %collective-permute-start.1) | collective-permute-done | bytes 262176 | tf_op jit(solution)/shard_map/ppermute | solution.py:185
  3.8 0.0 copy-start.2
  3.8 3.0 %collective-permute-start.2 = (bf16[4,128,256]{2,1,0:T(8,128)(2,1)S(1)}, bf16[4,128,256]{2,1,0:T(8,128)(2,1)S(1)}, u32[]{:S(2)}, u32[]{:S(2)}) collective-permute-start(bf16[4,128,256]{2,1,0:T(8,128)(2,1)S(1)} %add.1), channel_id=1, source_target_pairs={{0,2},{1,3},{2,0},{3,1},{4,6},{5,7},{6,4},{7,5},{8,10},{9,11},{10,... | collective-permute-start | bytes 786440 | tf_op jit(solution)/shard_map/ppermute | solution.py:185
  6.8 1.3 %prepare.1 = (f32[4,128,256]{2,1,0:T(8,128)S(1)}, f32[16,128,256]{2,1,0:T(8,128)S(1)}, bf16[4096,256]{1,0:T(8,128)(2,1)S(1)}) custom-call(bf16[16,128,256]{2,1,0:T(8,128)(2,1)S(1)} %get-tuple-element.18.av_ref.refs_0_, bf16[16,128,256]{2,1,0:T(8,128)(2,1)S(1)} %get-tuple-element.19.up_ref, bf16[64,256]{1,0:T(8,128)(2,1)S(1)} %bitcast.5, ...), custom_call_target="tpu_custom_call" | custom-call | flops 268435456 | bytes 7012352 | tf_op jit(solution)/shard_map/prepare/pallas_call | solution.py:40
  8.1 5.3 %collective-permute-done.2.refs_2_ = bf16[4,128,256]{2,1,0:T(8,128)(2,1)S(1)} collective-permute-done((bf16[4,128,256]{2,1,0:T(8,128)(2,1)S(1)}, bf16[4,128,256]{2,1,0:T(8,128)(2,1)S(1)}, u32[]{:S(2)}, u32[]{:S(2)}) %collective-permute-start.2) | collective-permute-done | bytes 262176 | tf_op jit(solution)/shard_map/ppermute | solution.py:185
  13.4 0.0 collective-permute-done.refs_1_
  13.4 0.2 layer_back.1.refs_5_
  13.5 1.8 %collective-permute-start.3 = (bf16[4,64,256]{2,1,0:T(8,128)(2,1)S(1)}, bf16[4,64,256]{2,1,0:T(8,128)(2,1)S(1)}, u32[]{:S(2)}, u32[]{:S(2)}) collective-permute-start(bf16[4,64,256]{2,1,0:T(8,128)(2,1)S(1)} %layer_back.1.refs_5_), channel_id=1, source_target_pairs={{0,2},{1,3},{2,0},{3,1},{4,6},{5,7},{6,4},{7,5},{8,10},{9,11},{10,... | collective-permute-start | bytes 393224 | tf_op jit(solution)/shard_map/ppermute | solution.py:185
  15.4 0.0 collective-permute-start.5
  15.4 1.1 %table_part.3.refs_7_ = f32[1024,256]{1,0:T(8,128)S(1)} custom-call(bf16[16,128,256]{2,1,0:T(8,128)(2,1)S(1)} %get-tuple-element.18.av_ref.refs_0_, bf16[64,256]{1,0:T(8,128)(2,1)S(1)} %bitcast.6, f32[16,128,256]{2,1,0:T(8,128)S(1)} %get-tuple-element.20.refs_2_, s32[1,4096]{1,0:T(1,128)S(1)} %bitcast.9, bf16[4096,256]{1,0:T(8,128)(2,1)S(1)} %get-tuple-element.21.refs_4_, ...), custom_call_target="tpu_custom_call" | custom-call | flops 536870912 | bytes 6471680 | tf_op jit(solution)/shard_map/table_part/pallas_call | solution.py:40
  16.5 2.2 %collective-permute-done.3.refs_6_ = bf16[4,64,256]{2,1,0:T(8,128)(2,1)S(1)} collective-permute-done((bf16[4,64,256]{2,1,0:T(8,128)(2,1)S(1)}, bf16[4,64,256]{2,1,0:T(8,128)(2,1)S(1)}, u32[]{:S(2)}, u32[]{:S(2)}) %collective-permute-start.3) | collective-permute-done | bytes 131104 | tf_op jit(solution)/shard_map/ppermute | solution.py:185
  18.6 0.0 collective-permute-start.4
  18.6 0.0 collective-permute-done.5.refs_5_
  18.6 1.7 %table_part.4.refs_6_ = f32[1024,256]{1,0:T(8,128)S(1)} custom-call(bf16[16,128,256]{2,1,0:T(8,128)(2,1)S(1)} %get-tuple-element.18.av_ref.refs_0_, bf16[64,256]{1,0:T(8,128)(2,1)S(1)} %bitcast.7, f32[16,128,256]{2,1,0:T(8,128)S(1)} %get-tuple-element.20.refs_2_, s32[1,4096]{1,0:T(1,128)S(1)} %bitcast.10, bf16[4096,256]{1,0:T(8,128)(2,1)S(1)} %get-tuple-element.21.refs_4_, ...), custom_call_target="tpu_custom_call" | custom-call | flops 1073741824 | bytes 7651328 | tf_op jit(solution)/shard_map/table_part/pallas_call | solution.py:40
  20.4 0.0 collective-permute-done.4.refs_5_
  20.4 1.1 %table_part.5 = (f32[128,256]{1,0:T(8,128)S(1)}, f32[128,256]{1,0:T(8,128)S(1)}, bf16[2,128,256]{2,1,0:T(8,128)(2,1)S(1)}, bf16[2,128,256]{2,1,0:T(8,128)(2,1)S(1)}, bf16[2,128,256]{2,1,0:T(8,128)(2,1)S(1)}) custom-call(bf16[16,128,256]{2,1,0:T(8,128)(2,1)S(1)} %get-tuple-element.18.av_ref.refs_0_, bf16[64,256]{1,0:T(8,128)(2,1)S(1)} %bitcast.8, ...), custom_call_target="tpu_custom_call" | custom-call | flops 536870912 | bytes 7127040 | tf_op jit(solution)/shard_map/table_part/pallas_call | solution.py:40
  21.5 2.7 %collective-permute-start.6 = (bf16[2,128,256]{2,1,0:T(8,128)(2,1)S(1)}, bf16[2,128,256]{2,1,0:T(8,128)(2,1)S(1)}, u32[]{:S(2)}, u32[]{:S(2)}) collective-permute-start(bf16[2,128,256]{2,1,0:T(8,128)(2,1)S(1)} %get-tuple-element.27), channel_id=1, source_target_pairs={{0,12},{4,8},{8,4},{12,0},{16,28},{20,24},{24,20},{28,16},{1,13},{... | collective-permute-start | bytes 393224 | tf_op jit(solution)/shard_map/ppermute | solution.py:185
  24.2 0.4 %collective-permute-start.7 = (bf16[2,128,256]{2,1,0:T(8,128)(2,1)S(1)}, bf16[2,128,256]{2,1,0:T(8,128)(2,1)S(1)}, u32[]{:S(2)}, u32[]{:S(2)}) collective-permute-start(bf16[2,128,256]{2,1,0:T(8,128)(2,1)S(1)} %get-tuple-element.28), channel_id=1, source_target_pairs={{0,8},{4,12},{8,0},{12,4},{16,24},{20,28},{24,16},{28,20},{1,9},{5... | collective-permute-start | bytes 393224 | tf_op jit(solution)/shard_map/ppermute | solution.py:185
  24.7 0.4 collective-permute-start.8
  25.1 3.7 %collective-permute-done.6.refs_1_ = bf16[2,128,256]{2,1,0:T(8,128)(2,1)S(1)} collective-permute-done((bf16[2,128,256]{2,1,0:T(8,128)(2,1)S(1)}, bf16[2,128,256]{2,1,0:T(8,128)(2,1)S(1)}, u32[]{:S(2)}, u32[]{:S(2)}) %collective-permute-start.6) | collective-permute-done | bytes 131104 | tf_op jit(solution)/shard_map/ppermute | solution.py:185
  28.8 2.7 %collective-permute-done.7.refs_2_ = bf16[2,128,256]{2,1,0:T(8,128)(2,1)S(1)} collective-permute-done((bf16[2,128,256]{2,1,0:T(8,128)(2,1)S(1)}, bf16[2,128,256]{2,1,0:T(8,128)(2,1)S(1)}, u32[]{:S(2)}, u32[]{:S(2)}) %collective-permute-start.7) | collective-permute-done | bytes 131104 | tf_op jit(solution)/shard_map/ppermute | solution.py:185
  31.4 0.0 collective-permute-done.8.refs_3_
  31.5 2.7 %collective-permute-start.9 = (bf16[128,256]{1,0:T(8,128)(2,1)S(1)}, bf16[128,256]{1,0:T(8,128)(2,1)S(1)}, u32[]{:S(2)}, u32[]{:S(2)}) collective-permute-start(bf16[128,256]{1,0:T(8,128)(2,1)S(1)} %collect.2), channel_id=1, source_target_pairs={{0,16},{4,20},{8,24},{12,28},{16,0},{20,4},{24,8},{28,12},{1,17},{... | collective-permute-start | bytes 196616 | tf_op jit(solution)/shard_map/ppermute | solution.py:185
  34.1 4.0 %collective-permute-done.9.refs_4_ = bf16[128,256]{1,0:T(8,128)(2,1)S(1)} collective-permute-done((bf16[128,256]{1,0:T(8,128)(2,1)S(1)}, bf16[128,256]{1,0:T(8,128)(2,1)S(1)}, u32[]{:S(2)}, u32[]{:S(2)}) %collective-permute-start.9) | collective-permute-done | bytes 65568 | tf_op jit(solution)/shard_map/ppermute | solution.py:185
  38.1 0.7 %collect.3 = f32[128,256]{1,0:T(8,128)} custom-call(f32[128,256]{1,0:T(8,128)S(1)} %get-tuple-element.26.refs_0_, bf16[2,128,256]{2,1,0:T(8,128)(2,1)S(1)} %collective-permute-done.6.refs_1_, bf16[2,128,256]{2,1,0:T(8,128)(2,1)S(1)} %collective-permute-done.7.refs_2_, bf16[2,128,256]{2,1,0:T(8,128)(2,1)S(1)} %collective-permute-done.8.refs_3_, ...), custom_call_target="tpu_custom_call" | custom-call | flops 32768 | bytes 720896 | tf_op jit(solution)/shard_map/collect/pallas_call | solution.py:40
  (9 shorter events, 0.1 us)
Async XLA Ops:
  0.0 1.6 %copy-start.1 = (bf16[64,128]{1,0:T(8,128)(2,1)S(1)}, bf16[64,128]{1,0:T(8,128)(2,1)}, u32[]{:S(2)}) copy-start(bf16[64,128]{1,0:T(8,128)(2,1)} %proj_ref.5) | copy-start | bytes 49156
  0.0 1.6 %copy-start = (bf16[256,64]{0,1:T(8,128)(2,1)S(1)}, bf16[256,64]{0,1:T(8,128)(2,1)}, u32[]{:S(2)}) copy-start(bf16[256,64]{0,1:T(8,128)(2,1)} %param.9) | copy-start | bytes 98308
  2.0 4.7 %copy-start.3 = (bf16[256,256]{1,0:T(8,128)(2,1)S(1)}, bf16[256,256]{1,0:T(8,128)(2,1)}, u32[]{:S(2)}) copy-start(bf16[256,256]{1,0:T(8,128)(2,1)} %mix_ref.1) | copy-start | bytes 393220
  2.1 4.7 %copy-start.4 = (s32[4096]{0:T(1024)S(1)}, s32[4096]{0:T(1024)}, u32[]{:S(2)}) copy-start(s32[4096]{0:T(1024)} %param.13) | copy-start | bytes 49156
  2.1 1.7 %collective-permute-start.1 = (bf16[4,128,256]{2,1,0:T(8,128)(2,1)S(1)}, bf16[4,128,256]{2,1,0:T(8,128)(2,1)S(1)}, u32[]{:S(2)}, u32[]{:S(2)}) collective-permute-start(bf16[4,128,256]{2,1,0:T(8,128)(2,1)S(1)} %first_sums.1), channel_id=1, source_target_pairs={{0,1},{1,0},{2,3},{3,2},{4,5},{5,4},{6,7},{7,6},{8,9},{9,8},{10,11... | collective-permute-start | bytes 786440 | tf_op jit(solution)/shard_map/ppermute | solution.py:185
  3.2 10.2 %collective-permute-start = (f32[4,128,256]{2,1,0:T(8,128)S(1)}, f32[4,128,256]{2,1,0:T(8,128)S(1)}, u32[]{:S(2)}, u32[]{:S(2)}) collective-permute-start(f32[4,128,256]{2,1,0:T(8,128)S(1)} %get-tuple-element.23), channel_id=1, source_target_pairs={{0,1},{1,0},{2,3},{3,2},{4,5},{5,4},{6,7},{7,6},{8,9},{9,8},{10,11... | collective-permute-start | bytes 1572872 | tf_op jit(solution)/shard_map/ppermute | solution.py:185
  3.8 11.6 %copy-start.2 = (s32[4096,1]{0,1:T(1,128)S(1)}, s32[4096,1]{0,1:T(1,128)}, u32[]{:S(2)}) copy-start(s32[4096,1]{0,1:T(1,128)} %param.12) | copy-start | bytes 49156
  3.8 9.6 %collective-permute-start.2 = (bf16[4,128,256]{2,1,0:T(8,128)(2,1)S(1)}, bf16[4,128,256]{2,1,0:T(8,128)(2,1)S(1)}, u32[]{:S(2)}, u32[]{:S(2)}) collective-permute-start(bf16[4,128,256]{2,1,0:T(8,128)(2,1)S(1)} %add.1), channel_id=1, source_target_pairs={{0,2},{1,3},{2,0},{3,1},{4,6},{5,7},{6,4},{7,5},{8,10},{9,11},{10,... | collective-permute-start | bytes 786440 | tf_op jit(solution)/shard_map/ppermute | solution.py:185
  13.5 5.1 %collective-permute-start.3 = (bf16[4,64,256]{2,1,0:T(8,128)(2,1)S(1)}, bf16[4,64,256]{2,1,0:T(8,128)(2,1)S(1)}, u32[]{:S(2)}, u32[]{:S(2)}) collective-permute-start(bf16[4,64,256]{2,1,0:T(8,128)(2,1)S(1)} %layer_back.1.refs_5_), channel_id=1, source_target_pairs={{0,2},{1,3},{2,0},{3,1},{4,6},{5,7},{6,4},{7,5},{8,10},{9,11},{10,... | collective-permute-start | bytes 393224 | tf_op jit(solution)/shard_map/ppermute | solution.py:185
  15.4 3.3 %collective-permute-start.5 = (bf16[4,64,256]{2,1,0:T(8,128)(2,1)S(1)}, bf16[4,64,256]{2,1,0:T(8,128)(2,1)S(1)}, u32[]{:S(2)}, u32[]{:S(2)}) collective-permute-start(bf16[4,64,256]{2,1,0:T(8,128)(2,1)S(1)} %layer_back.1.refs_5_), channel_id=1, source_target_pairs={{0,1},{1,0},{2,3},{3,2},{4,5},{5,4},{6,7},{7,6},{8,9},{9,8},{10,11... | collective-permute-start | bytes 393224 | tf_op jit(solution)/shard_map/ppermute | solution.py:185
  18.6 1.8 %collective-permute-start.4 = (bf16[4,64,256]{2,1,0:T(8,128)(2,1)S(1)}, bf16[4,64,256]{2,1,0:T(8,128)(2,1)S(1)}, u32[]{:S(2)}, u32[]{:S(2)}) collective-permute-start(bf16[4,64,256]{2,1,0:T(8,128)(2,1)S(1)} %collective-permute-done.3.refs_6_), channel_id=1, source_target_pairs={{0,1},{1,0},{2,3},{3,2},{4,5},{5,4},{6,7},{7,6},{8,9},{9,8},{10,11... | collective-permute-start | bytes 393224 | tf_op jit(solution)/shard_map/ppermute | solution.py:185
  21.5 7.3 %collective-permute-start.6 = (bf16[2,128,256]{2,1,0:T(8,128)(2,1)S(1)}, bf16[2,128,256]{2,1,0:T(8,128)(2,1)S(1)}, u32[]{:S(2)}, u32[]{:S(2)}) collective-permute-start(bf16[2,128,256]{2,1,0:T(8,128)(2,1)S(1)} %get-tuple-element.27), channel_id=1, source_target_pairs={{0,12},{4,8},{8,4},{12,0},{16,28},{20,24},{24,20},{28,16},{1,13},{... | collective-permute-start | bytes 393224 | tf_op jit(solution)/shard_map/ppermute | solution.py:185
  24.2 7.2 %collective-permute-start.7 = (bf16[2,128,256]{2,1,0:T(8,128)(2,1)S(1)}, bf16[2,128,256]{2,1,0:T(8,128)(2,1)S(1)}, u32[]{:S(2)}, u32[]{:S(2)}) collective-permute-start(bf16[2,128,256]{2,1,0:T(8,128)(2,1)S(1)} %get-tuple-element.28), channel_id=1, source_target_pairs={{0,8},{4,12},{8,0},{12,4},{16,24},{20,28},{24,16},{28,20},{1,9},{5... | collective-permute-start | bytes 393224 | tf_op jit(solution)/shard_map/ppermute | solution.py:185
  24.7 6.7 %collective-permute-start.8 = (bf16[2,128,256]{2,1,0:T(8,128)(2,1)S(1)}, bf16[2,128,256]{2,1,0:T(8,128)(2,1)S(1)}, u32[]{:S(2)}, u32[]{:S(2)}) collective-permute-start(bf16[2,128,256]{2,1,0:T(8,128)(2,1)S(1)} %get-tuple-element.29), channel_id=1, source_target_pairs={{0,4},{4,0},{8,12},{12,8},{16,20},{20,16},{24,28},{28,24},{1,5},{5... | collective-permute-start | bytes 393224 | tf_op jit(solution)/shard_map/ppermute | solution.py:185
  31.5 6.6 %collective-permute-start.9 = (bf16[128,256]{1,0:T(8,128)(2,1)S(1)}, bf16[128,256]{1,0:T(8,128)(2,1)S(1)}, u32[]{:S(2)}, u32[]{:S(2)}) collective-permute-start(bf16[128,256]{1,0:T(8,128)(2,1)S(1)} %collect.2), channel_id=1, source_target_pairs={{0,16},{4,20},{8,24},{12,28},{16,0},{20,4},{24,8},{28,12},{1,17},{... | collective-permute-start | bytes 196616 | tf_op jit(solution)/shard_map/ppermute | solution.py:185
